TPU v7x, 32 devices: a whole 2x2x4 slice. The times are simulated.
32 devices in a mesh: ctx: 8 (over z, x), grp: 4 (over y, core).
Axes of the slice: x: 2, y: 2, z: 4, core: 2. Of those that a mesh axis runs over, the one named last changes fastest.
Arguments:
- query: bfloat16 [1024, 8192], P('ctx', 'grp'), may hold values from -6 to 6
- keys: bfloat16 [1024, 8192], P('ctx', 'grp'), may hold values from -6 to 6
- values: bfloat16 [1024, 8192], P('ctx', 'grp'), may hold values from -6 to 6
- cotangent: bfloat16 [1024, 8192], P('ctx', 'grp'), may hold values from -6 to 6
- filter_taps: bfloat16 [64, 384], P('grp'), may hold values from -5 to 5, as said below
Outputs:
- gated: bfloat16 [1024, 8192], P('ctx', 'grp')
- key_grad: bfloat16 [1024, 8192], P('ctx', 'grp')
- value_grad: bfloat16 [1024, 8192], P('ctx', 'grp')
- filter_grad: float32 [64, 384], P('grp')
Inputs may be any that keep to these rules, and one draw needn't show every extreme that they name: `filter_taps`: each tap is a random value times a decay along the taps whose length differs from group to group.
All inputs are finite; a program needn't handle non-finite values.
Results may differ from a plain program's by a relative error of at most 0.005.
Values may be sent and summed in bfloat16 or wider, within the bound.
No kernel may reach another device: no remote copies, remote signals or barrier semaphores. Data moves between devices by JAX's collectives and lax.ppermute only.
A program may use at most 64 MiB of HBM per device.

v0:
```python
import math

import jax
import jax.numpy as jnp
from jax import lax
from jax.sharding import PartitionSpec as P

REACH = 3


def shifted(block, axis, distance):
    devices = range(lax.axis_size(axis))
    route = [(i - distance, i) for i in devices if i - distance in devices]
    return lax.ppermute(block, axis, route)


def make_tiles(padded, distance, block_rows, group_count):
    window = padded[:, distance * block_rows : (distance + 2) * block_rows]
    mirror = window[:, ::-1]
    flattened = jnp.tile(mirror, (1, block_rows))[
        :, block_rows - 1 : block_rows - 1 + block_rows * (2 * block_rows - 1)
    ]
    return flattened.reshape(group_count, block_rows, 2 * block_rows - 1)[:, :, :block_rows]


def diagonal_sums(outer_sum, block_rows, group_count):
    widened = jnp.pad(outer_sum, ((0, 0), (0, 0), (0, block_rows)))
    skewed = widened.reshape(group_count, 2 * block_rows * block_rows)[
        :, : block_rows * (2 * block_rows - 1)
    ]
    antidiag = jnp.sum(skewed.reshape(group_count, block_rows, 2 * block_rows - 1), axis=1)
    return jnp.concatenate([jnp.zeros((group_count, 1), jnp.float32), antidiag], axis=1)


def shards(query, keys, values, cotangent, filter_taps):
    block_rows, local_width = query.shape
    group_count = filter_taps.shape[0]
    group_width = local_width // group_count
    prod = (keys.astype(jnp.float32) * values.astype(jnp.float32)).astype(jnp.bfloat16)
    grad_gate = (cotangent.astype(jnp.float32) * query.astype(jnp.float32)).astype(jnp.bfloat16)
    prod_major = prod.reshape(block_rows, group_count, group_width).transpose(1, 0, 2)
    grad_major = grad_gate.reshape(block_rows, group_count, group_width).transpose(1, 0, 2)
    padded = jnp.concatenate(
        [jnp.zeros((group_count, block_rows), jnp.bfloat16), filter_taps], axis=1
    )
    convolved = jnp.zeros((group_count, block_rows, group_width), jnp.float32)
    backward = jnp.zeros((group_count, block_rows, group_width), jnp.float32)
    filter_acc = jnp.zeros((group_count, (REACH + 1) * block_rows), jnp.float32)
    early = prod_major
    late = grad_major
    for distance in range(REACH):
        if distance > 0:
            early = shifted(prod_major, "ctx", distance)
            late = shifted(grad_major, "ctx", -distance)
        toeplitz = make_tiles(padded, distance, block_rows, group_count)
        convolved = convolved + jnp.einsum(
            "grs,gsc->grc", toeplitz, early, preferred_element_type=jnp.float32
        )
        backward = backward + jnp.einsum(
            "grs,grc->gsc", toeplitz, late, preferred_element_type=jnp.float32
        )
        outer_sum = jnp.einsum(
            "grc,gsc->grs", grad_major, early[:, ::-1], preferred_element_type=jnp.float32
        )
        diagonal = diagonal_sums(outer_sum, block_rows, group_count)
        filter_acc = filter_acc.at[:, distance * block_rows : (distance + 2) * block_rows].add(
            diagonal
        )
    convolved = convolved.transpose(1, 0, 2).reshape(block_rows, local_width)
    backward = backward.transpose(1, 0, 2).reshape(block_rows, local_width)
    gated = (query.astype(jnp.float32) * convolved).astype(jnp.bfloat16)
    key_grad = (backward * values.astype(jnp.float32)).astype(jnp.bfloat16)
    value_grad = (backward * keys.astype(jnp.float32)).astype(jnp.bfloat16)
    factor = 1.0 / math.sqrt(block_rows * lax.axis_size("ctx") * group_width)
    filter_grad = lax.psum(filter_acc[:, block_rows:] * factor, "ctx")
    return (gated, key_grad, value_grad, filter_grad)


def solution(mesh):
    in_specs = (P("ctx", "grp"), P("ctx", "grp"), P("ctx", "grp"), P("ctx", "grp"), P("grp", None))
    out_specs = (P("ctx", "grp"), P("ctx", "grp"), P("ctx", "grp"), P("grp", None))
    return jax.shard_map(shards, mesh=mesh, in_specs=in_specs, out_specs=out_specs, check_vma=False)
```

profile of v0, /device:TPU:0, one launch (start us, length us, event | category | flops | bytes accessed | tf_op | source)
XLA Modules:
  0.0 134.6 jit_solution(16475089342390926085)
XLA Ops:
  0.6 1.3 fusion.5
  6.1 3.4 %reshape.131 = bf16[16,128,255]{2,1,0:T(8,128)(2,1)S(1)} reshape(bf16[16,32640]{1,0:T(8,128)(2,1)S(1)} %slice.108) | data formatting | bytes 2088960 | tf_op jit(solution)/shard_map/reshape | solution.py:23
  10.3 1.3 slice.110
  11.6 4.6 %reshape.133 = bf16[16,128,255]{2,1,0:T(8,128)(2,1)S(1)} reshape(bf16[16,32640]{1,0:T(8,128)(2,1)} %slice.110) | data formatting | bytes 2088960 | tf_op jit(solution)/shard_map/reshape | solution.py:23
  17.1 1.3 slice.112
  18.5 5.6 %reshape.134 = bf16[16,128,255]{2,1,0:T(8,128)(2,1)} reshape(bf16[16,32640]{1,0:T(8,128)(2,1)} %slice.112) | data formatting | bytes 2088960 | tf_op jit(solution)/shard_map/reshape | solution.py:23
  26.0 5.5 %collective-permute-done.3 = bf16[16,128,128]{1,2,0:T(8,128)(2,1)} collective-permute-done((bf16[16,128,128]{1,2,0:T(8,128)(2,1)S(1)}, bf16[16,128,128]{1,2,0:T(8,128)(2,1)}, u32[]{:S(2)}, u32[]{:S(2)}) %collective-permute-start.3) | collective-permute-done | bytes 524320 | tf_op jit(solution)/shard_map/ppermute | solution.py:14
  31.5 1.3 fusion
  33.2 2.4 %fusion.6 = (bf16[128,2048]{1,0:T(8,128)(2,1)}, bf16[128,2048]{1,0:T(8,128)(2,1)}, bf16[128,2048]{1,0:T(8,128)(2,1)S(1)}) fusion(f32[128,2048]{1,0:T(8,128)S(1)} %copy.23, bf16[128,2048]{1,0:T(8,128)(2,1)S(1)} %copy-done.6, bf16[128,2048]{1,0:T(8,128)(2,1)} %param.13), kind=kLoop, calls=%fused_computation.17 | loop fusion | flops 2097152 | bytes 3670016 | tf_op jit(solution)/shard_map/convert_element_type | solution.py:73
  35.9 2.1 %collective-permute-start = (bf16[16,128,128]{1,2,0:T(8,128)(2,1)S(1)}, bf16[16,128,128]{1,2,0:T(8,128)(2,1)}, u32[]{:S(2)}, u32[]{:S(2)}) collective-permute-start(bf16[16,128,128]{1,2,0:T(8,128)(2,1)S(1)} %bitcast.64), channel_id=1, source_target_pairs={{0,4},{4,8},{8,12},{12,16},{16,20},{20,24},{24,28},{1,5},{5,9},{9,... | collective-permute-start | bytes 1572872 | tf_op jit(solution)/shard_map/ppermute | solution.py:14
  38.0 4.1 %collective-permute-start.1 = (bf16[16,128,128]{1,2,0:T(8,128)(2,1)S(1)}, bf16[16,128,128]{1,2,0:T(8,128)(2,1)}, u32[]{:S(2)}, u32[]{:S(2)}) collective-permute-start(bf16[16,128,128]{1,2,0:T(8,128)(2,1)S(1)} %bitcast.65), channel_id=1, source_target_pairs={{0,8},{4,12},{8,16},{12,20},{16,24},{20,28},{1,9},{5,13},{9,17},{1... | collective-permute-start | bytes 1572872 | tf_op jit(solution)/shard_map/ppermute | solution.py:14
  42.1 1.5 %rev.21 = bf16[16,128,128]{1,2,0:T(8,128)(2,1)S(1)} reverse(bf16[16,128,128]{1,2,0:T(8,128)(2,1)S(1)} %bitcast.66), dimensions={1} | reverse | bytes 1048576 | tf_op jit(solution)/shard_map/rev | solution.py:63
  45.4 1.5 %slice.114 = f32[16,32640]{1,0:T(8,128)} slice(f32[16,32768]{1,0:T(8,128)S(1)} %bitcast.61), slice={[0:16], [0:32640]} | slice | bytes 4177920 | tf_op jit(solution)/shard_map/slice | solution.py:28
  46.8 4.8 %reshape.139 = f32[16,128,255]{2,1,0:T(8,128)S(1)} reshape(f32[16,32640]{1,0:T(8,128)} %slice.114) | data formatting | bytes 4177920 | tf_op jit(solution)/shard_map/reshape | solution.py:31
  52.7 1.5 %convolution_bitcast_fusion.5 = f32[128,16,128]{0,2,1:T(8,128)S(1)} fusion(bf16[16,128,128]{1,2,0:T(8,128)(2,1)S(1)} %bitcast.67, bf16[16,128,255]{2,1,0:T(8,128)(2,1)} %copy-done), kind=kOutput, calls=%fused_computation.9 | convolution fusion | flops 67108864 | bytes 2097152 | tf_op jit(solution)/shard_map/grs,gsc->grc/dot_general | solution.py:56
  54.2 1.6 %fusion.3 = f32[128,16,128]{0,2,1:T(8,128)S(1)} fusion(f32[128,16,128]{0,2,1:T(8,128)S(1)} %convolution_bitcast_fusion.5, bf16[16,128,128]{1,2,0:T(8,128)(2,1)} %collective-permute-done, bf16[16,128,255]{2,1,0:T(8,128)(2,1)S(1)} %copy-done.2), kind=kOutput, calls=%fused_computation.8 | convolution fusion | flops 67371008 | bytes 3145728 | tf_op jit(solution)/shard_map/grs,gsc->grc/dot_general | solution.py:56
  55.8 1.6 %fusion.2 = f32[128,16,128]{0,2,1:T(8,128)S(1)} fusion(f32[128,16,128]{0,2,1:T(8,128)S(1)} %fusion.3, bf16[16,128,128]{1,2,0:T(8,128)(2,1)} %collective-permute-done.1, bf16[16,128,255]{2,1,0:T(8,128)(2,1)S(1)} %copy-done.4), kind=kOutput, calls=%fused_computation.6 | convolution fusion | flops 67371008 | bytes 3145728 | tf_op jit(solution)/shard_map/grs,gsc->grc/dot_general | solution.py:56
  58.7 6.9 %rev.22 = bf16[16,128,128]{1,2,0:T(8,128)(2,1)S(1)} reverse(bf16[16,128,128]{1,2,0:T(8,128)(2,1)} %collective-permute-done), dimensions={1} | reverse | bytes 1048576 | tf_op jit(solution)/shard_map/rev | solution.py:63
  67.4 1.5 %slice.115 = f32[16,32640]{1,0:T(8,128)} slice(f32[16,32768]{1,0:T(8,128)S(1)} %bitcast.62), slice={[0:16], [0:32640]} | slice | bytes 4177920 | tf_op jit(solution)/shard_map/slice | solution.py:28
  68.9 4.8 %reshape.141 = f32[16,128,255]{2,1,0:T(8,128)S(1)} reshape(f32[16,32640]{1,0:T(8,128)} %slice.115) | data formatting | bytes 4177920 | tf_op jit(solution)/shard_map/reshape | solution.py:31
  73.8 7.1 %rev.23 = bf16[16,128,128]{1,2,0:T(8,128)(2,1)S(1)} reverse(bf16[16,128,128]{1,2,0:T(8,128)(2,1)} %collective-permute-done.1), dimensions={1} | reverse | bytes 1048576 | tf_op jit(solution)/shard_map/rev | solution.py:63
  82.8 1.5 %slice.117 = f32[16,32640]{1,0:T(8,128)} slice(f32[16,32768]{1,0:T(8,128)S(1)} %bitcast.63), slice={[0:16], [0:32640]} | slice | bytes 4177920 | tf_op jit(solution)/shard_map/slice | solution.py:28
  84.2 4.8 %reshape.143 = f32[16,128,255]{2,1,0:T(8,128)S(1)} reshape(f32[16,32640]{1,0:T(8,128)} %slice.117) | data formatting | bytes 4177920 | tf_op jit(solution)/shard_map/reshape | solution.py:31
  90.0 44.6 %psum.7 = f32[16,384]{1,0:T(8,128)} all-reduce(f32[16,384]{1,0:T(8,128)S(1)} %slice_multiply_fusion), channel_id=1, replica_groups=mesh['ctx'=8,'grp'=4] {'ctx'}, use_global_device_ids=true, to_apply=%region_5.6 | all-reduce | flops 6144 | bytes 49152 | tf_op jit(solution)/shard_map/psum | solution.py:75
  (58 shorter events, 16.9 us)
Async XLA Ops:
  0.6 4.2 %copy-start.7 = (bf16[16,384]{1,0:T(8,128)(2,1)S(1)}, bf16[16,384]{1,0:T(8,128)(2,1)}, u32[]{:S(2)}) copy-start(bf16[16,384]{1,0:T(8,128)(2,1)} %param.15) | copy-start | bytes 36868
  2.3 23.4 %collective-permute-start.2 = (bf16[16,128,128]{1,2,0:T(8,128)(2,1)S(1)}, bf16[16,128,128]{1,2,0:T(8,128)(2,1)S(1)}, u32[]{:S(2)}, u32[]{:S(2)}) collective-permute-start(bf16[16,128,128]{1,2,0:T(8,128)(2,1)S(1)} %bitcast.52), channel_id=1, source_target_pairs={{4,0},{8,4},{12,8},{16,12},{20,16},{24,20},{28,24},{5,1},{9,5},{13... | collective-permute-start | bytes 1572872 | tf_op jit(solution)/shard_map/ppermute | solution.py:14
  3.6 28.0 %collective-permute-start.3 = (bf16[16,128,128]{1,2,0:T(8,128)(2,1)S(1)}, bf16[16,128,128]{1,2,0:T(8,128)(2,1)}, u32[]{:S(2)}, u32[]{:S(2)}) collective-permute-start(bf16[16,128,128]{1,2,0:T(8,128)(2,1)S(1)} %bitcast.53), channel_id=1, source_target_pairs={{8,0},{12,4},{16,8},{20,12},{24,16},{28,20},{9,1},{13,5},{17,9},{2... | collective-permute-start | bytes 1572872 | tf_op jit(solution)/shard_map/ppermute | solution.py:14
  9.4 15.9 %copy-start = (bf16[16,128,255]{2,1,0:T(8,128)(2,1)}, bf16[16,128,255]{2,1,0:T(8,128)(2,1)S(1)}, u32[]{:S(2)}) copy-start(bf16[16,128,255]{2,1,0:T(8,128)(2,1)S(1)} %reshape.131) | copy-start | bytes 3133444
  16.3 9.4 %copy-start.1 = (bf16[16,128,255]{2,1,0:T(8,128)(2,1)}, bf16[16,128,255]{2,1,0:T(8,128)(2,1)S(1)}, u32[]{:S(2)}) copy-start(bf16[16,128,255]{2,1,0:T(8,128)(2,1)S(1)} %reshape.133) | copy-start | bytes 3133444
  25.4 6.2 %copy-start.3 = (bf16[16,128,255]{2,1,0:T(8,128)(2,1)S(1)}, bf16[16,128,255]{2,1,0:T(8,128)(2,1)}, u32[]{:S(2)}) copy-start(bf16[16,128,255]{2,1,0:T(8,128)(2,1)} %reshape.134) | copy-start | bytes 3133444
  26.0 7.2 %copy-start.6 = (bf16[128,2048]{1,0:T(8,128)(2,1)S(1)}, bf16[128,2048]{1,0:T(8,128)(2,1)}, u32[]{:S(2)}) copy-start(bf16[128,2048]{1,0:T(8,128)(2,1)} %param.12) | copy-start | bytes 1572868
  35.9 18.3 %collective-permute-start = (bf16[16,128,128]{1,2,0:T(8,128)(2,1)S(1)}, bf16[16,128,128]{1,2,0:T(8,128)(2,1)}, u32[]{:S(2)}, u32[]{:S(2)}) collective-permute-start(bf16[16,128,128]{1,2,0:T(8,128)(2,1)S(1)} %bitcast.64), channel_id=1, source_target_pairs={{0,4},{4,8},{8,12},{12,16},{16,20},{20,24},{24,28},{1,5},{5,9},{9,... | collective-permute-start | bytes 1572872 | tf_op jit(solution)/shard_map/ppermute | solution.py:14
  38.0 17.9 %collective-permute-start.1 = (bf16[16,128,128]{1,2,0:T(8,128)(2,1)S(1)}, bf16[16,128,128]{1,2,0:T(8,128)(2,1)}, u32[]{:S(2)}, u32[]{:S(2)}) collective-permute-start(bf16[16,128,128]{1,2,0:T(8,128)(2,1)S(1)} %bitcast.65), channel_id=1, source_target_pairs={{0,8},{4,12},{8,16},{12,20},{16,24},{20,28},{1,9},{5,13},{9,17},{1... | collective-permute-start | bytes 1572872 | tf_op jit(solution)/shard_map/ppermute | solution.py:14
  51.8 2.4 %copy-start.2 = (bf16[16,128,255]{2,1,0:T(8,128)(2,1)S(1)}, bf16[16,128,255]{2,1,0:T(8,128)(2,1)}, u32[]{:S(2)}) copy-start(bf16[16,128,255]{2,1,0:T(8,128)(2,1)} %copy-done.1) | copy-start | bytes 3133444
  54.2 1.7 %copy-start.4 = (bf16[16,128,255]{2,1,0:T(8,128)(2,1)S(1)}, bf16[16,128,255]{2,1,0:T(8,128)(2,1)}, u32[]{:S(2)}) copy-start(bf16[16,128,255]{2,1,0:T(8,128)(2,1)} %reshape.134) | copy-start | bytes 3133444
  55.8 2.0 %copy-start.5 = (bf16[128,2048]{1,0:T(8,128)(2,1)S(1)}, bf16[128,2048]{1,0:T(8,128)(2,1)}, u32[]{:S(2)}) copy-start(bf16[128,2048]{1,0:T(8,128)(2,1)} %param.11) | copy-start | bytes 1572868
where the time goes:
time: 136 us; the launch traced here: 135 us
  local copies, waits for them, and re-layouts  59 us (43%)
  blocking collectives  44.6 us (33%)
  starting transfers between devices  8.81 us (6%)
  other arithmetic  7.92 us (6%)
  matrix products  7.65 us (6%)
  waiting for transfers between devices  5.55 us (4%)
    psum x1, blocking collectives, shards(): filter_grad = lax.psum(filter_acc[:, block_rows:] * factor, 'ctx')  44.6 us
    rev x3, local copies, waits for them, and re-layouts, shards(): early[:, ::-1]  15.4 us
    reshape x3, local copies, waits for them, and re-layouts, diagonal_sums(): skewed.reshape(group_count, block_rows, 2 * block_rows - 1)  14.4 us
    reshape x3, local copies, waits for them, and re-layouts, make_tiles(): flattened.reshape(group_count, block_rows, 2 * block_rows - 1)  13.6 us
    ppermute x4, starting transfers between devices, shifted(): return lax.ppermute(block, axis, route)  8.81 us
    ppermute x4, waiting for transfers between devices, shifted(): return lax.ppermute(block, axis, route)  5.55 us
    unnamed x22, local copies, waits for them, and re-layouts  5.45 us
    dot_general x3, matrix products, shards(): jnp.einsum('grs,gsc->grc', toeplitz, early, preferred_element_type=jnp.fl...  4.68 us
  transfers between devices with their start and end apart: 4, of which 1 were waited for; matrix products, arithmetic and copies ran while one was open for 26% of the time, Pallas kernels for 0%

commit v1 on v0

v1 whole, which is shorter than its diff:
```python
import functools
import math

import jax
import jax.numpy as jnp
from jax import lax
from jax.experimental import pallas as pl
from jax.experimental.pallas import tpu as pltpu
from jax.sharding import PartitionSpec as P

SUBLANES = 8
VMEM_LIMIT = 32 * 1024 * 1024


def shifted(block, axis, distance):
    devices = range(lax.axis_size(axis))
    route = [(i - distance, i) for i in devices if i - distance in devices]
    return lax.ppermute(block, axis, route)


def summed(partial, axis):
    size = lax.axis_size(axis)
    if size & (size - 1):
        return lax.psum(partial, axis)
    stride = 1
    while stride < size:
        route = [(i, i ^ stride) for i in range(size)]
        partial = partial + lax.ppermute(partial, axis, route)
        stride *= 2
    return partial


def tiles_kernel(rows, reach, taps_ref, back_ref, conv_ref):
    width = reach * rows
    for group in range(taps_ref.shape[0]):
        row = taps_ref[group : group + 1, :].astype(jnp.float32)
        spread = jnp.concatenate(
            [jnp.zeros((SUBLANES, rows), jnp.float32), jnp.broadcast_to(row, (SUBLANES, width))],
            axis=1,
        )
        spread = pltpu.roll(spread, 0, 1, stride=1, stride_axis=0)
        bands = [
            pltpu.roll(spread, start, 1)[:, rows:] if start else spread[:, rows:]
            for start in range(0, rows, SUBLANES)
        ]
        band = jnp.concatenate(bands, axis=0)
        back_ref[group] = band.astype(jnp.bfloat16)
        turned = [band[:, d * rows : (d + 1) * rows].T for d in range(reach)]
        conv_ref[group] = jnp.concatenate(turned, axis=1).astype(jnp.bfloat16)


def taps_kernel(rows, reach, factor, prod_ref, early_ref, grad_ref, late_ref, out_ref):
    width = reach * rows
    contract = (((1,), (1,)), ((), ()))
    group_count = out_ref.shape[0]
    group_width = prod_ref.shape[1] // group_count
    sums = []
    for group in range(group_count):
        columns = slice(group * group_width, (group + 1) * group_width)
        prod = prod_ref[:, columns]
        grad = grad_ref[:, columns]
        dot = functools.partial(
            lax.dot_general, dimension_numbers=contract, preferred_element_type=jnp.float32
        )
        near = dot(prod, grad)
        middle = dot(early_ref[:, columns], grad)
        far = dot(prod, late_ref[:, columns])
        outer = jnp.concatenate([near, middle, far, jnp.zeros((rows, rows), jnp.float32)], axis=1)
        total = outer[:SUBLANES]
        for start in range(SUBLANES, rows, SUBLANES):
            total = total + pltpu.roll(
                outer[start : start + SUBLANES], width + rows - start, 1
            )
        total = jnp.concatenate(
            [pltpu.roll(total[s : s + 1], (width + rows - s) % (width + rows), 1) for s in range(SUBLANES)],
            axis=0,
        )
        sums.append(jnp.sum(total, axis=0, keepdims=True)[:, :width])
    out_ref[...] = jnp.concatenate(sums, axis=0) * factor


def outputs_kernel(
    rows, group_width, conv_ref, back_ref, p0, p1, p2, g0, g1, g2, query, keys, values, gated, key_grad, value_grad
):
    for group in range(conv_ref.shape[0]):
        columns = slice(group * group_width, (group + 1) * group_width)
        early = jnp.concatenate([ref[:, columns] for ref in (p0, p1, p2)], axis=0)
        late = jnp.concatenate([ref[:, columns] for ref in (g0, g1, g2)], axis=0)
        convolved = jnp.dot(conv_ref[group], early, preferred_element_type=jnp.float32)
        backward = jnp.dot(back_ref[group], late, preferred_element_type=jnp.float32)
        gated[:, columns] = (query[:, columns].astype(jnp.float32) * convolved).astype(gated.dtype)
        key_grad[:, columns] = (backward * values[:, columns].astype(jnp.float32)).astype(key_grad.dtype)
        value_grad[:, columns] = (backward * keys[:, columns].astype(jnp.float32)).astype(value_grad.dtype)


def shards(query, keys, values, cotangent, filter_taps):
    rows, local_width = query.shape
    group_count, taps = filter_taps.shape
    group_width = local_width // group_count
    reach = taps // rows
    params = pltpu.CompilerParams(vmem_limit_bytes=VMEM_LIMIT)
    step = min(group_count, 8)
    grid = (group_count // step,)

    prod = (keys.astype(jnp.float32) * values.astype(jnp.float32)).astype(jnp.bfloat16)
    p1 = shifted(prod, "ctx", 1)
    grad_gate = (cotangent.astype(jnp.float32) * query.astype(jnp.float32)).astype(jnp.bfloat16)
    g2 = shifted(grad_gate, "ctx", -2)

    tile_shape = jax.ShapeDtypeStruct((group_count, rows, taps), jnp.bfloat16)
    tile_spec = pl.BlockSpec((step, rows, taps), lambda i: (i, 0, 0))
    taps_spec = pl.BlockSpec((step, taps), lambda i: (i, 0))
    block_spec = pl.BlockSpec((rows, step * group_width), lambda i: (0, i))
    back_tiles, conv_tiles = pl.pallas_call(
        functools.partial(tiles_kernel, rows, reach),
        grid=grid,
        in_specs=[taps_spec],
        out_specs=[tile_spec, tile_spec],
        out_shape=[tile_shape, tile_shape],
        compiler_params=params,
        cost_estimate=pl.CostEstimate(flops=10**9, bytes_accessed=10**7, transcendentals=0),
        name="tiles",
    )(filter_taps)

    p1, g2, late_p, late_g = lax.optimization_barrier((p1, g2, prod, grad_gate))
    p2 = shifted(late_p, "ctx", 2)
    g1 = shifted(late_g, "ctx", -1)

    factor = 1.0 / math.sqrt(rows * lax.axis_size("ctx") * group_width)
    partial = pl.pallas_call(
        functools.partial(taps_kernel, rows, reach, factor),
        grid=grid,
        in_specs=[block_spec] * 4,
        out_specs=taps_spec,
        out_shape=jax.ShapeDtypeStruct((group_count, taps), jnp.float32),
        compiler_params=params,
        cost_estimate=pl.CostEstimate(flops=10**9, bytes_accessed=10**7, transcendentals=0),
        name="taps",
    )(prod, p1, grad_gate, g2)
    filter_grad = summed(partial, "ctx")

    out_shape = jax.ShapeDtypeStruct((rows, local_width), jnp.bfloat16)
    gated, key_grad, value_grad = pl.pallas_call(
        functools.partial(outputs_kernel, rows, group_width),
        grid=grid,
        in_specs=[tile_spec, tile_spec] + [block_spec] * 9,
        out_specs=[block_spec] * 3,
        out_shape=[out_shape] * 3,
        compiler_params=params,
        cost_estimate=pl.CostEstimate(flops=10**9, bytes_accessed=10**7, transcendentals=0),
        name="outputs",
    )(conv_tiles, back_tiles, prod, p1, p2, grad_gate, g1, g2, query, keys, values)
    return (gated, key_grad, value_grad, filter_grad)


def solution(mesh):
    in_specs = (P("ctx", "grp"), P("ctx", "grp"), P("ctx", "grp"), P("ctx", "grp"), P("grp", None))
    out_specs = (P("ctx", "grp"), P("ctx", "grp"), P("ctx", "grp"), P("grp", None))
    return jax.shard_map(shards, mesh=mesh, in_specs=in_specs, out_specs=out_specs, check_vma=False)
```

time: 136 us -> 52.6 us (0.39)
  local copies, waits for them, and re-layouts: 59 us -> 0.02 us
  blocking collectives: 44.6 us -> 0 us
  waiting for transfers between devices: 5.55 us -> 25.7 us
  starting transfers between devices: 8.81 us -> 16.5 us
  matrix products: 7.65 us -> 0 us
  Pallas kernels: 0 us -> 7.2 us
  other arithmetic: 7.92 us -> 2.16 us
    psum x1 -> x0, blocking collectives: 44.6 us -> none  [shards(): filter_grad = lax.psum(filter_acc[:, block_rows:] * factor, 'ctx')]
    reshape x8 -> x0, local copies, waits for them, and re-layouts: 28.7 us -> none  [the longest x3 14.4 us: diagonal_sums(): skewed.reshape(group_count, block_rows, 2 * block_rows - 1)]
    rev x6 -> x0, local copies, waits for them, and re-layouts: 16 us -> none  [the longest x3 15.4 us: shards(): early[:, ::-1]]
    ppermute x0 -> x3, waiting for transfers between devices: none -> 11.7 us  [summed(): partial = partial + lax.ppermute(partial, axis, route)]
    ppermute x4, waiting for transfers between devices: 5.55 us -> 14 us  [shifted(): return lax.ppermute(block, axis, route)]
    dot_general x9 -> x0, matrix products: 7.65 us -> none  [the longest x3 4.68 us: shards(): jnp.einsum('grs,gsc->grc', toeplitz, early, preferred_element_type=jnp.fl...]
    slice x7 -> x0, local copies, waits for them, and re-layouts: 7.47 us -> none  [the longest x3 4.46 us: diagonal_sums(): widened.reshape(group_count, 2 * block_rows * block_rows)]
    pallas_call x0 -> x3, Pallas kernels: none -> 7.2 us  [the longest x1 2.56 us: shards(): pl.pallas_call(functools.partial(outputs_kernel, rows, group_width), grid...]
  transfers between devices with their start and end apart: 4 -> 7, of which waited for: 1 -> 5; matrix products, arithmetic and copies ran while one was open for 26% -> 1% of each run, Pallas kernels for 0% -> 9%
where the time goes in v1:
time: 52.6 us; the launch traced here: 52.3 us
  waiting for transfers between devices  25.7 us (49%)
  starting transfers between devices  16.5 us (31%)
  Pallas kernels  7.2 us (14%)
  other arithmetic  2.16 us (4%)
  between operations  0.76 us (1%)
    ppermute x4, waiting for transfers between devices, shifted(): return lax.ppermute(block, axis, route)  14 us
    ppermute x3, waiting for transfers between devices, summed(): partial = partial + lax.ppermute(partial, axis, route)  11.7 us
    ppermute x4, starting transfers between devices, shifted(): return lax.ppermute(block, axis, route)  10.9 us
    ppermute x3, starting transfers between devices, summed(): partial = partial + lax.ppermute(partial, axis, route)  5.6 us
    pallas_call x1, Pallas kernels, shards(): pl.pallas_call(functools.partial(outputs_kernel, rows, group_width), grid...  2.56 us
    pallas_call x1, Pallas kernels, shards(): pl.pallas_call(functools.partial(taps_kernel, rows, reach, factor), grid=...  2.4 us
    pallas_call x1, Pallas kernels, shards(): pl.pallas_call(functools.partial(tiles_kernel, rows, reach), grid=grid, i...  2.23 us
    convert_element_type x1, other arithmetic, shards(): (keys.astype(jnp.float32) * values.astype(jnp.float32)).astype(jnp.bfloat16)  1.41 us
  transfers between devices with their start and end apart: 7, of which 5 were waited for; matrix products, arithmetic and copies ran while one was open for 1% of the time, Pallas kernels for 9%

profile of v1, /device:TPU:0, one launch (start us, length us, event | category | flops | bytes accessed | tf_op | source)
XLA Modules:
  0.0 52.3 jit_solution(7894606981825152791)
XLA Ops:
  0.6 0.0 copy-start.2
  0.6 0.0 copy-start.4
  0.7 1.4 %multiply_convert_fusion.1.p0.prod_ref = bf16[128,2048]{1,0:T(8,128)(2,1)S(1)} fusion(bf16[128,2048]{1,0:T(8,128)(2,1)} %values.1, bf16[128,2048]{1,0:T(8,128)(2,1)} %keys.1), kind=kLoop, calls=%fused_computation.1 | loop fusion | flops 1048576 | bytes 1572864 | tf_op jit(solution)/shard_map/convert_element_type | solution.py:105
  2.1 4.9 %collective-permute-start = (bf16[128,2048]{1,0:T(8,128)(2,1)S(1)}, bf16[128,2048]{1,0:T(8,128)(2,1)S(1)}, u32[]{:S(2)}, u32[]{:S(2)}) collective-permute-start(bf16[128,2048]{1,0:T(8,128)(2,1)S(1)} %multiply_convert_fusion.1.p0.prod_ref), channel_id=1, source_target_pairs={{0,4},{4,8},{8,12},{12,16},{16,20},{20,24},{24,28},{1,5},{5,9},{9,... | collective-permute-start | bytes 1572872 | tf_op jit(solution)/shard_map/ppermute | solution.py:18
  7.0 0.0 copy-done.2
  7.0 0.1 multiply_convert_fusion.g0.grad_ref
  7.1 0.0 copy-start.3
  7.1 1.3 %collective-permute-start.1 = (bf16[128,2048]{1,0:T(8,128)(2,1)S(1)}, bf16[128,2048]{1,0:T(8,128)(2,1)S(1)}, u32[]{:S(2)}, u32[]{:S(2)}) collective-permute-start(bf16[128,2048]{1,0:T(8,128)(2,1)S(1)} %multiply_convert_fusion.g0.grad_ref), channel_id=1, source_target_pairs={{8,0},{12,4},{16,8},{20,12},{24,16},{28,20},{9,1},{13,5},{17,9},{2... | collective-permute-start | bytes 1572872 | tf_op jit(solution)/shard_map/ppermute | solution.py:18
  8.4 9.7 %collective-permute-done.p1.early_ref = bf16[128,2048]{1,0:T(8,128)(2,1)S(1)} collective-permute-done((bf16[128,2048]{1,0:T(8,128)(2,1)S(1)}, bf16[128,2048]{1,0:T(8,128)(2,1)S(1)}, u32[]{:S(2)}, u32[]{:S(2)}) %collective-permute-start) | collective-permute-done | bytes 524320 | tf_op jit(solution)/shard_map/ppermute | solution.py:18
  18.1 4.3 %collective-permute-done.1.g2.late_ref = bf16[128,2048]{1,0:T(8,128)(2,1)S(1)} collective-permute-done((bf16[128,2048]{1,0:T(8,128)(2,1)S(1)}, bf16[128,2048]{1,0:T(8,128)(2,1)S(1)}, u32[]{:S(2)}, u32[]{:S(2)}) %collective-permute-start.1) | collective-permute-done | bytes 524320 | tf_op jit(solution)/shard_map/ppermute | solution.py:18
  22.4 3.5 %collective-permute-start.2 = (bf16[128,2048]{1,0:T(8,128)(2,1)S(1)}, bf16[128,2048]{1,0:T(8,128)(2,1)S(1)}, u32[]{:S(2)}, u32[]{:S(2)}) collective-permute-start(bf16[128,2048]{1,0:T(8,128)(2,1)S(1)} %multiply_convert_fusion.1.p0.prod_ref), channel_id=1, source_target_pairs={{0,8},{4,12},{8,16},{12,20},{16,24},{20,28},{1,9},{5,13},{9,17},{1... | collective-permute-start | bytes 1572872 | tf_op jit(solution)/shard_map/ppermute | solution.py:18
  25.9 1.3 %collective-permute-start.3 = (bf16[128,2048]{1,0:T(8,128)(2,1)S(1)}, bf16[128,2048]{1,0:T(8,128)(2,1)S(1)}, u32[]{:S(2)}, u32[]{:S(2)}) collective-permute-start(bf16[128,2048]{1,0:T(8,128)(2,1)S(1)} %multiply_convert_fusion.g0.grad_ref), channel_id=1, source_target_pairs={{4,0},{8,4},{12,8},{16,12},{20,16},{24,20},{28,24},{5,1},{9,5},{13... | collective-permute-start | bytes 1572872 | tf_op jit(solution)/shard_map/ppermute | solution.py:18
  27.2 2.4 %taps.1 = f32[16,384]{1,0:T(8,128)S(1)} custom-call(bf16[128,2048]{1,0:T(8,128)(2,1)S(1)} %multiply_convert_fusion.1.p0.prod_ref, bf16[128,2048]{1,0:T(8,128)(2,1)S(1)} %collective-permute-done.p1.early_ref, bf16[128,2048]{1,0:T(8,128)(2,1)S(1)} %multiply_convert_fusion.g0.grad_ref, bf16[128,2048]{1,0:T(8,128)(2,1)S(1)} %collective-permute-done.1.g2.late_ref), custom_call_target="tpu_custom_call" | custom-call | flops 1000000000 | bytes 10000000 | tf_op jit(solution)/shard_map/taps/pallas_call | solution.py:130
  29.6 2.7 %collective-permute-start.4 = (f32[16,384]{1,0:T(8,128)S(1)}, f32[16,384]{1,0:T(8,128)S(1)}, u32[]{:S(2)}, u32[]{:S(2)}) collective-permute-start(f32[16,384]{1,0:T(8,128)S(1)} %taps.1), channel_id=1, source_target_pairs={{0,4},{4,0},{8,12},{12,8},{16,20},{20,16},{24,28},{28,24},{1,5},{5... | collective-permute-start | bytes 73736 | tf_op jit(solution)/shard_map/ppermute | solution.py:28
  32.3 8.2 %collective-permute-done.4 = f32[16,384]{1,0:T(8,128)S(1)} collective-permute-done((f32[16,384]{1,0:T(8,128)S(1)}, f32[16,384]{1,0:T(8,128)S(1)}, u32[]{:S(2)}, u32[]{:S(2)}) %collective-permute-start.4) | collective-permute-done | bytes 24608 | tf_op jit(solution)/shard_map/ppermute | solution.py:28
  40.5 1.5 %collective-permute-start.5 = (f32[16,384]{1,0:T(8,128)S(1)}, f32[16,384]{1,0:T(8,128)S(1)}, u32[]{:S(2)}, u32[]{:S(2)}) collective-permute-start(f32[16,384]{1,0:T(8,128)S(1)} %add.9), channel_id=1, source_target_pairs={{0,8},{4,12},{8,0},{12,4},{16,24},{20,28},{24,16},{28,20},{1,9},{5... | collective-permute-start | bytes 73736 | tf_op jit(solution)/shard_map/ppermute | solution.py:28
  42.0 2.3 %collective-permute-done.5 = f32[16,384]{1,0:T(8,128)S(1)} collective-permute-done((f32[16,384]{1,0:T(8,128)S(1)}, f32[16,384]{1,0:T(8,128)S(1)}, u32[]{:S(2)}, u32[]{:S(2)}) %collective-permute-start.5) | collective-permute-done | bytes 24608 | tf_op jit(solution)/shard_map/ppermute | solution.py:28
  44.3 1.3 %collective-permute-start.6 = (f32[16,384]{1,0:T(8,128)S(1)}, f32[16,384]{1,0:T(8,128)S(1)}, u32[]{:S(2)}, u32[]{:S(2)}) collective-permute-start(f32[16,384]{1,0:T(8,128)S(1)} %add.10), channel_id=1, source_target_pairs={{0,16},{4,20},{8,24},{12,28},{16,0},{20,4},{24,8},{28,12},{1,17},{... | collective-permute-start | bytes 73736 | tf_op jit(solution)/shard_map/ppermute | solution.py:28
  45.7 2.2 %tiles.1 = (bf16[16,128,384]{2,1,0:T(8,128)(2,1)S(1)}, bf16[16,128,384]{2,1,0:T(8,128)(2,1)S(1)}) custom-call(bf16[16,384]{1,0:T(8,128)(2,1)S(1)} %copy-done.3), custom_call_target="tpu_custom_call" | custom-call | flops 1000000000 | bytes 10000000 | tf_op jit(solution)/shard_map/tiles/pallas_call | solution.py:114
  47.9 1.2 %collective-permute-done.6 = f32[16,384]{1,0:T(8,128)S(1)} collective-permute-done((f32[16,384]{1,0:T(8,128)S(1)}, f32[16,384]{1,0:T(8,128)S(1)}, u32[]{:S(2)}, u32[]{:S(2)}) %collective-permute-start.6) | collective-permute-done | bytes 24608 | tf_op jit(solution)/shard_map/ppermute | solution.py:28
  49.1 0.6 %add.11 = f32[16,384]{1,0:T(8,128)} add(f32[16,384]{1,0:T(8,128)S(1)} %add.10, f32[16,384]{1,0:T(8,128)S(1)} %collective-permute-done.6) | non-fusion elementwise | flops 6144 | bytes 73728 | tf_op jit(solution)/shard_map/add | solution.py:28
  49.7 0.0 collective-permute-done.2.p2
  49.7 0.0 collective-permute-done.3.g1
  49.8 2.6 %outputs.1 = (bf16[128,2048]{1,0:T(8,128)(2,1)}, bf16[128,2048]{1,0:T(8,128)(2,1)}, bf16[128,2048]{1,0:T(8,128)(2,1)}) custom-call(bf16[16,128,384]{2,1,0:T(8,128)(2,1)S(1)} %get-tuple-element.13.conv_ref, bf16[16,128,384]{2,1,0:T(8,128)(2,1)S(1)} %get-tuple-element.14.back_ref, bf16[128,2048]{1,0:T(8,128)(2,1)S(1)} %multiply_convert_fusion.1.p0.prod_ref, ...), custom_call_target="tpu_custom_call" | custom-call | flops 1000000000 | bytes 10000000 | tf_op jit(solution)/shard_map/outputs/pallas_call | solution.py:143
  (8 shorter events, 0.0 us)
Async XLA Ops:
  0.6 6.3 %copy-start.2 = (bf16[128,2048]{1,0:T(8,128)(2,1)S(1)}, bf16[128,2048]{1,0:T(8,128)(2,1)}, u32[]{:S(2)}) copy-start(bf16[128,2048]{1,0:T(8,128)(2,1)} %query.1) | copy-start | bytes 1572868
  0.6 6.3 %copy-start.4 = (bf16[128,2048]{1,0:T(8,128)(2,1)S(1)}, bf16[128,2048]{1,0:T(8,128)(2,1)}, u32[]{:S(2)}) copy-start(bf16[128,2048]{1,0:T(8,128)(2,1)} %param.8) | copy-start | bytes 1572868
  2.1 16.0 %collective-permute-start = (bf16[128,2048]{1,0:T(8,128)(2,1)S(1)}, bf16[128,2048]{1,0:T(8,128)(2,1)S(1)}, u32[]{:S(2)}, u32[]{:S(2)}) collective-permute-start(bf16[128,2048]{1,0:T(8,128)(2,1)S(1)} %multiply_convert_fusion.1.p0.prod_ref), channel_id=1, source_target_pairs={{0,4},{4,8},{8,12},{12,16},{16,20},{20,24},{24,28},{1,5},{5,9},{9,... | collective-permute-start | bytes 1572872 | tf_op jit(solution)/shard_map/ppermute | solution.py:18
  7.1 38.6 %copy-start.3 = (bf16[16,384]{1,0:T(8,128)(2,1)S(1)}, bf16[16,384]{1,0:T(8,128)(2,1)}, u32[]{:S(2)}) copy-start(bf16[16,384]{1,0:T(8,128)(2,1)} %taps_ref.1) | copy-start | bytes 36868
  7.1 15.3 %collective-permute-start.1 = (bf16[128,2048]{1,0:T(8,128)(2,1)S(1)}, bf16[128,2048]{1,0:T(8,128)(2,1)S(1)}, u32[]{:S(2)}, u32[]{:S(2)}) collective-permute-start(bf16[128,2048]{1,0:T(8,128)(2,1)S(1)} %multiply_convert_fusion.g0.grad_ref), channel_id=1, source_target_pairs={{8,0},{12,4},{16,8},{20,12},{24,16},{28,20},{9,1},{13,5},{17,9},{2... | collective-permute-start | bytes 1572872 | tf_op jit(solution)/shard_map/ppermute | solution.py:18
  22.4 27.3 %collective-permute-start.2 = (bf16[128,2048]{1,0:T(8,128)(2,1)S(1)}, bf16[128,2048]{1,0:T(8,128)(2,1)S(1)}, u32[]{:S(2)}, u32[]{:S(2)}) collective-permute-start(bf16[128,2048]{1,0:T(8,128)(2,1)S(1)} %multiply_convert_fusion.1.p0.prod_ref), channel_id=1, source_target_pairs={{0,8},{4,12},{8,16},{12,20},{16,24},{20,28},{1,9},{5,13},{9,17},{1... | collective-permute-start | bytes 1572872 | tf_op jit(solution)/shard_map/ppermute | solution.py:18
  25.9 23.9 %collective-permute-start.3 = (bf16[128,2048]{1,0:T(8,128)(2,1)S(1)}, bf16[128,2048]{1,0:T(8,128)(2,1)S(1)}, u32[]{:S(2)}, u32[]{:S(2)}) collective-permute-start(bf16[128,2048]{1,0:T(8,128)(2,1)S(1)} %multiply_convert_fusion.g0.grad_ref), channel_id=1, source_target_pairs={{4,0},{8,4},{12,8},{16,12},{20,16},{24,20},{28,24},{5,1},{9,5},{13... | collective-permute-start | bytes 1572872 | tf_op jit(solution)/shard_map/ppermute | solution.py:18
  29.6 10.9 %collective-permute-start.4 = (f32[16,384]{1,0:T(8,128)S(1)}, f32[16,384]{1,0:T(8,128)S(1)}, u32[]{:S(2)}, u32[]{:S(2)}) collective-permute-start(f32[16,384]{1,0:T(8,128)S(1)} %taps.1), channel_id=1, source_target_pairs={{0,4},{4,0},{8,12},{12,8},{16,20},{20,16},{24,28},{28,24},{1,5},{5... | collective-permute-start | bytes 73736 | tf_op jit(solution)/shard_map/ppermute | solution.py:28
  40.5 3.8 %collective-permute-start.5 = (f32[16,384]{1,0:T(8,128)S(1)}, f32[16,384]{1,0:T(8,128)S(1)}, u32[]{:S(2)}, u32[]{:S(2)}) collective-permute-start(f32[16,384]{1,0:T(8,128)S(1)} %add.9), channel_id=1, source_target_pairs={{0,8},{4,12},{8,0},{12,4},{16,24},{20,28},{24,16},{28,20},{1,9},{5... | collective-permute-start | bytes 73736 | tf_op jit(solution)/shard_map/ppermute | solution.py:28
  44.3 5.4 %copy-start = (bf16[128,2048]{1,0:T(8,128)(2,1)S(1)}, bf16[128,2048]{1,0:T(8,128)(2,1)}, u32[]{:S(2)}) copy-start(bf16[128,2048]{1,0:T(8,128)(2,1)} %values.1) | copy-start | bytes 1572868
  44.3 5.4 %copy-start.1 = (bf16[128,2048]{1,0:T(8,128)(2,1)S(1)}, bf16[128,2048]{1,0:T(8,128)(2,1)}, u32[]{:S(2)}) copy-start(bf16[128,2048]{1,0:T(8,128)(2,1)} %keys.1) | copy-start | bytes 1572868
  44.3 4.8 %collective-permute-start.6 = (f32[16,384]{1,0:T(8,128)S(1)}, f32[16,384]{1,0:T(8,128)S(1)}, u32[]{:S(2)}, u32[]{:S(2)}) collective-permute-start(f32[16,384]{1,0:T(8,128)S(1)} %add.10), channel_id=1, source_target_pairs={{0,16},{4,20},{8,24},{12,28},{16,0},{20,4},{24,8},{28,12},{1,17},{... | collective-permute-start | bytes 73736 | tf_op jit(solution)/shard_map/ppermute | solution.py:28

commit v2 on v1

--- a/solution.py
+++ b/solution.py
@@ -19,15 +19,7 @@
 
 
 def summed(partial, axis):
-    size = lax.axis_size(axis)
-    if size & (size - 1):
-        return lax.psum(partial, axis)
-    stride = 1
-    while stride < size:
-        route = [(i, i ^ stride) for i in range(size)]
-        partial = partial + lax.ppermute(partial, axis, route)
-        stride *= 2
-    return partial
+    return jnp.sum(lax.all_gather(partial, axis), axis=0)
 
 
 def tiles_kernel(rows, reach, taps_ref, back_ref, conv_ref):
@@ -122,10 +114,10 @@
         name="tiles",
     )(filter_taps)
 
-    p1, g2, late_p, late_g = lax.optimization_barrier((p1, g2, prod, grad_gate))
-    p2 = shifted(late_p, "ctx", 2)
-    g1 = shifted(late_g, "ctx", -1)
+    g1 = shifted(grad_gate, "ctx", -1)
+    p2 = shifted(prod, "ctx", 2)
 
+    back_tiles, conv_tiles, ready = lax.optimization_barrier((back_tiles, conv_tiles, grad_gate))
     factor = 1.0 / math.sqrt(rows * lax.axis_size("ctx") * group_width)
     partial = pl.pallas_call(
         functools.partial(taps_kernel, rows, reach, factor),
@@ -136,7 +128,7 @@
         compiler_params=params,
         cost_estimate=pl.CostEstimate(flops=10**9, bytes_accessed=10**7, transcendentals=0),
         name="taps",
-    )(prod, p1, grad_gate, g2)
+    )(prod, p1, ready, g2)
     filter_grad = summed(partial, "ctx")
 
     out_shape = jax.ShapeDtypeStruct((rows, local_width), jnp.bfloat16)

time: 52.6 us -> 64.9 us (1.23)
  blocking collectives: 0 us -> 30.6 us
  waiting for transfers between devices: 25.7 us -> 4.22 us
  local copies, waits for them, and re-layouts: 0.02 us -> 6.17 us
  starting transfers between devices: 16.5 us -> 12.8 us
    all_gather x0 -> x1, blocking collectives: none -> 30.6 us  [summed(): return jnp.sum(lax.all_gather(partial, axis), axis=0)]
    ppermute x3 -> x0, waiting for transfers between devices: 11.7 us -> none  [summed(): partial = partial + lax.ppermute(partial, axis, route)]
    ppermute x4, waiting for transfers between devices: 14 us -> 4.22 us  [shifted(): return lax.ppermute(block, axis, route)]
    unnamed x10 -> x22, local copies, waits for them, and re-layouts: 0.02 us -> 6.17 us
    ppermute x3 -> x0, starting transfers between devices: 5.6 us -> none  [summed(): partial = partial + lax.ppermute(partial, axis, route)]
    ppermute x4, starting transfers between devices: 10.9 us -> 12.8 us  [shifted(): return lax.ppermute(block, axis, route)]
  transfers between devices with their start and end apart: 7 -> 4, of which waited for: 5 -> 1; matrix products, arithmetic and copies ran while one was open for 1% -> 1% of each run, Pallas kernels for 9% -> 7%
where the time goes in v2:
time: 64.9 us; the launch traced here: 64.6 us
  blocking collectives  30.6 us (47%)
  starting transfers between devices  12.8 us (20%)
  Pallas kernels  7.81 us (12%)
  local copies, waits for them, and re-layouts  6.17 us (10%)
  waiting for transfers between devices  4.22 us (7%)
  other arithmetic  2.16 us (3%)
  between operations  0.78 us (1%)
    all_gather x1, blocking collectives, summed(): return jnp.sum(lax.all_gather(partial, axis), axis=0)  30.6 us
    ppermute x4, starting transfers between devices, shifted(): return lax.ppermute(block, axis, route)  12.8 us
    unnamed x22, local copies, waits for them, and re-layouts  6.17 us
    ppermute x4, waiting for transfers between devices, shifted(): return lax.ppermute(block, axis, route)  4.22 us
    pallas_call x1, Pallas kernels, shards(): pl.pallas_call(functools.partial(outputs_kernel, rows, group_width), grid...  3.18 us
    pallas_call x1, Pallas kernels, shards(): pl.pallas_call(functools.partial(taps_kernel, rows, reach, factor), grid=...  2.39 us
    pallas_call x1, Pallas kernels, shards(): pl.pallas_call(functools.partial(tiles_kernel, rows, reach), grid=grid, i...  2.25 us
    convert_element_type x1, other arithmetic, shards(): (keys.astype(jnp.float32) * values.astype(jnp.float32)).astype(jnp.bfloat16)  1.41 us
  transfers between devices with their start and end apart: 4, of which 1 were waited for; matrix products, arithmetic and copies ran while one was open for 1% of the time, Pallas kernels for 7%

profile of v2, /device:TPU:0, one launch (start us, length us, event | category | flops | bytes accessed | tf_op | source)
XLA Modules:
  0.0 64.6 jit_solution(13413309049889709850)
XLA Ops:
  0.6 0.0 copy-start.2
  0.7 1.4 %multiply_convert_fusion.p0.prod_ref = bf16[128,2048]{1,0:T(8,128)(2,1)S(1)} fusion(bf16[128,2048]{1,0:T(8,128)(2,1)} %values.1, bf16[128,2048]{1,0:T(8,128)(2,1)} %keys.1), kind=kLoop, calls=%fused_computation | loop fusion | flops 1048576 | bytes 1572864 | tf_op jit(solution)/shard_map/convert_element_type | solution.py:97
  2.1 4.9 %collective-permute-start = (bf16[128,2048]{1,0:T(8,128)(2,1)S(1)}, bf16[128,2048]{1,0:T(8,128)(2,1)S(1)}, u32[]{:S(2)}, u32[]{:S(2)}) collective-permute-start(bf16[128,2048]{1,0:T(8,128)(2,1)S(1)} %multiply_convert_fusion.p0.prod_ref), channel_id=1, source_target_pairs={{0,4},{4,8},{8,12},{12,16},{16,20},{20,24},{24,28},{1,5},{5,9},{9,... | collective-permute-start | bytes 1572872 | tf_op jit(solution)/shard_map/ppermute | solution.py:18
  7.0 0.1 multiply_convert_fusion.1.g0.grad_ref
  7.1 1.3 %collective-permute-start.3 = (bf16[128,2048]{1,0:T(8,128)(2,1)S(1)}, bf16[128,2048]{1,0:T(8,128)(2,1)S(1)}, u32[]{:S(2)}, u32[]{:S(2)}) collective-permute-start(bf16[128,2048]{1,0:T(8,128)(2,1)S(1)} %multiply_convert_fusion.1.g0.grad_ref), channel_id=1, source_target_pairs={{8,0},{12,4},{16,8},{20,12},{24,16},{28,20},{9,1},{13,5},{17,9},{2... | collective-permute-start | bytes 1572872 | tf_op jit(solution)/shard_map/ppermute | solution.py:18
  8.4 5.4 %collective-permute-start.1 = (bf16[128,2048]{1,0:T(8,128)(2,1)S(1)}, bf16[128,2048]{1,0:T(8,128)(2,1)}, u32[]{:S(2)}, u32[]{:S(2)}) collective-permute-start(bf16[128,2048]{1,0:T(8,128)(2,1)S(1)} %multiply_convert_fusion.p0.prod_ref), channel_id=1, source_target_pairs={{0,8},{4,12},{8,16},{12,20},{16,24},{20,28},{1,9},{5,13},{9,17},{1... | collective-permute-start | bytes 1572872 | tf_op jit(solution)/shard_map/ppermute | solution.py:18
  13.8 1.3 %collective-permute-start.2 = (bf16[128,2048]{1,0:T(8,128)(2,1)S(1)}, bf16[128,2048]{1,0:T(8,128)(2,1)}, u32[]{:S(2)}, u32[]{:S(2)}) collective-permute-start(bf16[128,2048]{1,0:T(8,128)(2,1)S(1)} %multiply_convert_fusion.1.g0.grad_ref), channel_id=1, source_target_pairs={{4,0},{8,4},{12,8},{16,12},{20,16},{24,20},{28,24},{5,1},{9,5},{13... | collective-permute-start | bytes 1572872 | tf_op jit(solution)/shard_map/ppermute | solution.py:18
  15.1 0.0 copy-done.9
  15.1 2.2 %tiles.1 = (bf16[16,128,384]{2,1,0:T(8,128)(2,1)S(1)}, bf16[16,128,384]{2,1,0:T(8,128)(2,1)S(1)}) custom-call(bf16[16,384]{1,0:T(8,128)(2,1)S(1)} %copy-done.9), custom_call_target="tpu_custom_call" | custom-call | flops 1000000000 | bytes 10000000 | tf_op jit(solution)/shard_map/tiles/pallas_call | solution.py:106
  17.3 1.1 %copy-done.3 = bf16[16,128,384]{2,1,0:T(8,128)(2,1)} copy-done((bf16[16,128,384]{2,1,0:T(8,128)(2,1)}, bf16[16,128,384]{2,1,0:T(8,128)(2,1)S(1)}, u32[]{:S(2)}) %copy-start.3) | copy-done | bytes 1572888
  18.5 1.2 %copy-done.5 = bf16[16,128,384]{2,1,0:T(8,128)(2,1)} copy-done((bf16[16,128,384]{2,1,0:T(8,128)(2,1)}, bf16[16,128,384]{2,1,0:T(8,128)(2,1)S(1)}, u32[]{:S(2)}) %copy-start.5) | copy-done | bytes 1572888
  19.6 0.0 collective-permute-done.p1.early_ref
  19.6 4.2 %collective-permute-done.3.g2.late_ref = bf16[128,2048]{1,0:T(8,128)(2,1)S(1)} collective-permute-done((bf16[128,2048]{1,0:T(8,128)(2,1)S(1)}, bf16[128,2048]{1,0:T(8,128)(2,1)S(1)}, u32[]{:S(2)}, u32[]{:S(2)}) %collective-permute-start.3) | collective-permute-done | bytes 524320 | tf_op jit(solution)/shard_map/ppermute | solution.py:18
  23.9 2.4 %taps.1 = f32[16,384]{1,0:T(8,128)S(1)} custom-call(bf16[128,2048]{1,0:T(8,128)(2,1)S(1)} %multiply_convert_fusion.p0.prod_ref, bf16[128,2048]{1,0:T(8,128)(2,1)S(1)} %collective-permute-done.p1.early_ref, bf16[128,2048]{1,0:T(8,128)(2,1)S(1)} %multiply_convert_fusion.1.g0.grad_ref, bf16[128,2048]{1,0:T(8,128)(2,1)S(1)} %collective-permute-done.3.g2.late_ref), custom_call_target="tpu_custom_call" | custom-call | flops 1000000000 | bytes 10000000 | tf_op jit(solution)/shard_map/taps/pallas_call | solution.py:122
  26.3 30.6 %all-gather = f32[128,384]{1,0:T(8,128)S(1)} all-gather(f32[16,384]{1,0:T(8,128)S(1)} %taps.1), channel_id=2, replica_groups=mesh['ctx'=8,'grp'=4] {'ctx'}, dimensions={0}, use_global_device_ids=true | all-gather | bytes 221184 | tf_op jit(solution)/shard_map/all_gather | solution.py:22
  56.9 0.6 reduce_sum.9
  57.5 0.0 collective-permute-done.1.p2
  57.5 0.0 collective-permute-done.2.g1
  57.5 0.0 copy-done.1
  57.6 0.0 copy-start.4
  57.6 1.4 %copy-done.4 = bf16[16,128,384]{2,1,0:T(8,128)(2,1)S(1)} copy-done((bf16[16,128,384]{2,1,0:T(8,128)(2,1)S(1)}, bf16[16,128,384]{2,1,0:T(8,128)(2,1)}, u32[]{:S(2)}) %copy-start.4) | copy-done | bytes 1572888
  59.0 1.4 %copy-done.6 = bf16[16,128,384]{2,1,0:T(8,128)(2,1)S(1)} copy-done((bf16[16,128,384]{2,1,0:T(8,128)(2,1)S(1)}, bf16[16,128,384]{2,1,0:T(8,128)(2,1)}, u32[]{:S(2)}) %copy-start.6) | copy-done | bytes 1572888
  60.4 1.0 %copy-done.8 = bf16[128,2048]{1,0:T(8,128)(2,1)S(1)} copy-done((bf16[128,2048]{1,0:T(8,128)(2,1)S(1)}, bf16[128,2048]{1,0:T(8,128)(2,1)}, u32[]{:S(2)}) %copy-start.8) | copy-done | bytes 524312
  61.4 3.2 %outputs.1 = (bf16[128,2048]{1,0:T(8,128)(2,1)}, bf16[128,2048]{1,0:T(8,128)(2,1)}, bf16[128,2048]{1,0:T(8,128)(2,1)}) custom-call(bf16[16,128,384]{2,1,0:T(8,128)(2,1)S(1)} %copy-done.6, bf16[16,128,384]{2,1,0:T(8,128)(2,1)S(1)} %copy-done.4, bf16[128,2048]{1,0:T(8,128)(2,1)S(1)} %multiply_convert_fusion.p0.prod_ref, ...), custom_call_target="tpu_custom_call" | custom-call | flops 1000000000 | bytes 10000000 | tf_op jit(solution)/shard_map/outputs/pallas_call | solution.py:135
  (13 shorter events, 0.0 us)
Async XLA Ops:
  0.6 6.3 %copy-start.2 = (bf16[128,2048]{1,0:T(8,128)(2,1)S(1)}, bf16[128,2048]{1,0:T(8,128)(2,1)}, u32[]{:S(2)}) copy-start(bf16[128,2048]{1,0:T(8,128)(2,1)} %query.1) | copy-start | bytes 1572868
  0.6 6.3 %copy-start.10 = (bf16[128,2048]{1,0:T(8,128)(2,1)S(1)}, bf16[128,2048]{1,0:T(8,128)(2,1)}, u32[]{:S(2)}) copy-start(bf16[128,2048]{1,0:T(8,128)(2,1)} %param.8) | copy-start | bytes 1572868
  0.7 14.4 %copy-start.9 = (bf16[16,384]{1,0:T(8,128)(2,1)S(1)}, bf16[16,384]{1,0:T(8,128)(2,1)}, u32[]{:S(2)}) copy-start(bf16[16,384]{1,0:T(8,128)(2,1)} %taps_ref.1) | copy-start | bytes 36868
  2.1 17.6 %collective-permute-start = (bf16[128,2048]{1,0:T(8,128)(2,1)S(1)}, bf16[128,2048]{1,0:T(8,128)(2,1)S(1)}, u32[]{:S(2)}, u32[]{:S(2)}) collective-permute-start(bf16[128,2048]{1,0:T(8,128)(2,1)S(1)} %multiply_convert_fusion.p0.prod_ref), channel_id=1, source_target_pairs={{0,4},{4,8},{8,12},{12,16},{16,20},{20,24},{24,28},{1,5},{5,9},{9,... | collective-permute-start | bytes 1572872 | tf_op jit(solution)/shard_map/ppermute | solution.py:18
  7.1 16.7 %collective-permute-start.3 = (bf16[128,2048]{1,0:T(8,128)(2,1)S(1)}, bf16[128,2048]{1,0:T(8,128)(2,1)S(1)}, u32[]{:S(2)}, u32[]{:S(2)}) collective-permute-start(bf16[128,2048]{1,0:T(8,128)(2,1)S(1)} %multiply_convert_fusion.1.g0.grad_ref), channel_id=1, source_target_pairs={{8,0},{12,4},{16,8},{20,12},{24,16},{28,20},{9,1},{13,5},{17,9},{2... | collective-permute-start | bytes 1572872 | tf_op jit(solution)/shard_map/ppermute | solution.py:18
  8.4 49.1 %collective-permute-start.1 = (bf16[128,2048]{1,0:T(8,128)(2,1)S(1)}, bf16[128,2048]{1,0:T(8,128)(2,1)}, u32[]{:S(2)}, u32[]{:S(2)}) collective-permute-start(bf16[128,2048]{1,0:T(8,128)(2,1)S(1)} %multiply_convert_fusion.p0.prod_ref), channel_id=1, source_target_pairs={{0,8},{4,12},{8,16},{12,20},{16,24},{20,28},{1,9},{5,13},{9,17},{1... | collective-permute-start | bytes 1572872 | tf_op jit(solution)/shard_map/ppermute | solution.py:18
  13.8 43.8 %collective-permute-start.2 = (bf16[128,2048]{1,0:T(8,128)(2,1)S(1)}, bf16[128,2048]{1,0:T(8,128)(2,1)}, u32[]{:S(2)}, u32[]{:S(2)}) collective-permute-start(bf16[128,2048]{1,0:T(8,128)(2,1)S(1)} %multiply_convert_fusion.1.g0.grad_ref), channel_id=1, source_target_pairs={{4,0},{8,4},{12,8},{16,12},{20,16},{24,20},{28,24},{5,1},{9,5},{13... | collective-permute-start | bytes 1572872 | tf_op jit(solution)/shard_map/ppermute | solution.py:18
  17.3 1.1 %copy-start.3 = (bf16[16,128,384]{2,1,0:T(8,128)(2,1)}, bf16[16,128,384]{2,1,0:T(8,128)(2,1)S(1)}, u32[]{:S(2)}) copy-start(bf16[16,128,384]{2,1,0:T(8,128)(2,1)S(1)} %get-tuple-element.15.back_ref) | copy-start | bytes 4718596
  18.5 1.2 %copy-start.5 = (bf16[16,128,384]{2,1,0:T(8,128)(2,1)}, bf16[16,128,384]{2,1,0:T(8,128)(2,1)S(1)}, u32[]{:S(2)}) copy-start(bf16[16,128,384]{2,1,0:T(8,128)(2,1)S(1)} %get-tuple-element.14.conv_ref) | copy-start | bytes 4718596
  19.6 37.9 %copy-start = (bf16[128,2048]{1,0:T(8,128)(2,1)S(1)}, bf16[128,2048]{1,0:T(8,128)(2,1)}, u32[]{:S(2)}) copy-start(bf16[128,2048]{1,0:T(8,128)(2,1)} %values.1) | copy-start | bytes 1572868
  19.6 37.9 %copy-start.1 = (bf16[128,2048]{1,0:T(8,128)(2,1)S(1)}, bf16[128,2048]{1,0:T(8,128)(2,1)}, u32[]{:S(2)}) copy-start(bf16[128,2048]{1,0:T(8,128)(2,1)} %keys.1) | copy-start | bytes 1572868
  23.9 2.4 %copy-start.7 = (bf16[128,2048]{1,0:T(8,128)(2,1)}, bf16[128,2048]{1,0:T(8,128)(2,1)S(1)}, u32[]{:S(2)}) copy-start(bf16[128,2048]{1,0:T(8,128)(2,1)S(1)} %collective-permute-done.3.g2.late_ref) | copy-start | bytes 1572868
  57.6 1.4 %copy-start.4 = (bf16[16,128,384]{2,1,0:T(8,128)(2,1)S(1)}, bf16[16,128,384]{2,1,0:T(8,128)(2,1)}, u32[]{:S(2)}) copy-start(bf16[16,128,384]{2,1,0:T(8,128)(2,1)} %copy-done.3) | copy-start | bytes 4718596
  59.0 1.4 %copy-start.6 = (bf16[16,128,384]{2,1,0:T(8,128)(2,1)S(1)}, bf16[16,128,384]{2,1,0:T(8,128)(2,1)}, u32[]{:S(2)}) copy-start(bf16[16,128,384]{2,1,0:T(8,128)(2,1)} %copy-done.5) | copy-start | bytes 4718596
  60.4 1.0 %copy-start.8 = (bf16[128,2048]{1,0:T(8,128)(2,1)S(1)}, bf16[128,2048]{1,0:T(8,128)(2,1)}, u32[]{:S(2)}) copy-start(bf16[128,2048]{1,0:T(8,128)(2,1)} %copy-done.7) | copy-start | bytes 1572868

commit v3 on v2

--- a/solution.py
+++ b/solution.py
@@ -19,7 +19,8 @@
 
 
 def summed(partial, axis):
-    return jnp.sum(lax.all_gather(partial, axis), axis=0)
+    copies = jnp.broadcast_to(partial[None], (lax.axis_size(axis), *partial.shape))
+    return jnp.sum(lax.all_to_all(copies, axis, 0, 0), axis=0)
 
 
 def tiles_kernel(rows, reach, taps_ref, back_ref, conv_ref):
@@ -117,7 +118,6 @@
     g1 = shifted(grad_gate, "ctx", -1)
     p2 = shifted(prod, "ctx", 2)
 
-    back_tiles, conv_tiles, ready = lax.optimization_barrier((back_tiles, conv_tiles, grad_gate))
     factor = 1.0 / math.sqrt(rows * lax.axis_size("ctx") * group_width)
     partial = pl.pallas_call(
         functools.partial(taps_kernel, rows, reach, factor),
@@ -128,7 +128,7 @@
         compiler_params=params,
         cost_estimate=pl.CostEstimate(flops=10**9, bytes_accessed=10**7, transcendentals=0),
         name="taps",
-    )(prod, p1, ready, g2)
+    )(prod, p1, grad_gate, g2)
     filter_grad = summed(partial, "ctx")
 
     out_shape = jax.ShapeDtypeStruct((rows, local_width), jnp.bfloat16)

time: 64.9 us -> 39.8 us (0.61)
  blocking collectives: 30.6 us -> 0 us
  waiting for transfers between devices: 4.22 us -> 12.1 us
  local copies, waits for them, and re-layouts: 6.17 us -> 0.72 us
  starting transfers between devices: 12.8 us -> 15.9 us
    all_gather x1 -> x0, blocking collectives: 30.6 us -> none  [summed(): return jnp.sum(lax.all_gather(partial, axis), axis=0)]
    unnamed x22 -> x10, local copies, waits for them, and re-layouts: 6.17 us -> 0.03 us
    ppermute x4, waiting for transfers between devices: 4.22 us -> 9.56 us  [shifted(): return lax.ppermute(block, axis, route)]
    all_to_all x0 -> x1, starting transfers between devices: none -> 3.84 us  [summed(): return jnp.sum(lax.all_to_all(copies, axis, 0, 0), axis=0)]
    all_to_all x0 -> x1, waiting for transfers between devices: none -> 2.5 us  [summed(): return jnp.sum(lax.all_to_all(copies, axis, 0, 0), axis=0)]
    ppermute x4, starting transfers between devices: 12.8 us -> 12 us  [shifted(): return lax.ppermute(block, axis, route)]
    broadcast_in_dim x0 -> x1, local copies, waits for them, and re-layouts: none -> 0.69 us  [summed(): jnp.broadcast_to(partial[None], (lax.axis_size(axis), *partial.shape))]
  transfers between devices with their start and end apart: 4 -> 5, of which waited for: 1 -> 3; matrix products, arithmetic and copies ran while one was open for 1% -> 2% of each run, Pallas kernels for 7% -> 20%
where the time goes in v3:
time: 39.8 us; the launch traced here: 39.5 us
  starting transfers between devices  15.9 us (40%)
  waiting for transfers between devices  12.1 us (30%)
  Pallas kernels  7.85 us (20%)
  other arithmetic  2.16 us (5%)
  between operations  0.78 us (2%)
  local copies, waits for them, and re-layouts  0.72 us (2%)
    ppermute x4, starting transfers between devices, shifted(): return lax.ppermute(block, axis, route)  12 us
    ppermute x4, waiting for transfers between devices, shifted(): return lax.ppermute(block, axis, route)  9.56 us
    all_to_all x1, starting transfers between devices, summed(): return jnp.sum(lax.all_to_all(copies, axis, 0, 0), axis=0)  3.84 us
    pallas_call x1, Pallas kernels, shards(): pl.pallas_call(functools.partial(outputs_kernel, rows, group_width), grid...  3.21 us
    all_to_all x1, waiting for transfers between devices, summed(): return jnp.sum(lax.all_to_all(copies, axis, 0, 0), axis=0)  2.5 us
    pallas_call x1, Pallas kernels, shards(): pl.pallas_call(functools.partial(taps_kernel, rows, reach, factor), grid=...  2.39 us
    pallas_call x1, Pallas kernels, shards(): pl.pallas_call(functools.partial(tiles_kernel, rows, reach), grid=grid, i...  2.25 us
    convert_element_type x1, other arithmetic, shards(): (keys.astype(jnp.float32) * values.astype(jnp.float32)).astype(jnp.bfloat16)  1.41 us
  transfers between devices with their start and end apart: 5, of which 3 were waited for; matrix products, arithmetic and copies ran while one was open for 2% of the time, Pallas kernels for 20%

profile of v3, /device:TPU:0, one launch (start us, length us, event | category | flops | bytes accessed | tf_op | source)
XLA Modules:
  0.0 39.5 jit_solution(6203665159396028926)
XLA Ops:
  0.6 0.0 copy-start.2
  0.6 0.0 copy-start.4
  0.7 1.4 %multiply_convert_fusion.1.p0.prod_ref = bf16[128,2048]{1,0:T(8,128)(2,1)S(1)} fusion(bf16[128,2048]{1,0:T(8,128)(2,1)} %values.1, bf16[128,2048]{1,0:T(8,128)(2,1)} %keys.1), kind=kLoop, calls=%fused_computation.1 | loop fusion | flops 1048576 | bytes 1572864 | tf_op jit(solution)/shard_map/convert_element_type | solution.py:98
  2.1 4.9 %collective-permute-start = (bf16[128,2048]{1,0:T(8,128)(2,1)S(1)}, bf16[128,2048]{1,0:T(8,128)(2,1)S(1)}, u32[]{:S(2)}, u32[]{:S(2)}) collective-permute-start(bf16[128,2048]{1,0:T(8,128)(2,1)S(1)} %multiply_convert_fusion.1.p0.prod_ref), channel_id=1, source_target_pairs={{0,4},{4,8},{8,12},{12,16},{16,20},{20,24},{24,28},{1,5},{5,9},{9,... | collective-permute-start | bytes 1572872 | tf_op jit(solution)/shard_map/ppermute | solution.py:18
  7.0 0.0 copy-done.2
  7.0 0.0 copy-done.4
  7.0 0.1 multiply_convert_fusion.g0.grad_ref
  7.1 0.0 copy-start.3
  7.1 1.3 %collective-permute-start.3 = (bf16[128,2048]{1,0:T(8,128)(2,1)S(1)}, bf16[128,2048]{1,0:T(8,128)(2,1)S(1)}, u32[]{:S(2)}, u32[]{:S(2)}) collective-permute-start(bf16[128,2048]{1,0:T(8,128)(2,1)S(1)} %multiply_convert_fusion.g0.grad_ref), channel_id=1, source_target_pairs={{8,0},{12,4},{16,8},{20,12},{24,16},{28,20},{9,1},{13,5},{17,9},{2... | collective-permute-start | bytes 1572872 | tf_op jit(solution)/shard_map/ppermute | solution.py:18
  8.4 4.6 %collective-permute-start.1 = (bf16[128,2048]{1,0:T(8,128)(2,1)S(1)}, bf16[128,2048]{1,0:T(8,128)(2,1)S(1)}, u32[]{:S(2)}, u32[]{:S(2)}) collective-permute-start(bf16[128,2048]{1,0:T(8,128)(2,1)S(1)} %multiply_convert_fusion.1.p0.prod_ref), channel_id=1, source_target_pairs={{0,8},{4,12},{8,16},{12,20},{16,24},{20,28},{1,9},{5,13},{9,17},{1... | collective-permute-start | bytes 1572872 | tf_op jit(solution)/shard_map/ppermute | solution.py:18
  13.0 1.3 %collective-permute-start.2 = (bf16[128,2048]{1,0:T(8,128)(2,1)S(1)}, bf16[128,2048]{1,0:T(8,128)(2,1)}, u32[]{:S(2)}, u32[]{:S(2)}) collective-permute-start(bf16[128,2048]{1,0:T(8,128)(2,1)S(1)} %multiply_convert_fusion.g0.grad_ref), channel_id=1, source_target_pairs={{4,0},{8,4},{12,8},{16,12},{20,16},{24,20},{28,24},{5,1},{9,5},{13... | collective-permute-start | bytes 1572872 | tf_op jit(solution)/shard_map/ppermute | solution.py:18
  14.3 3.8 %collective-permute-done.p1.early_ref = bf16[128,2048]{1,0:T(8,128)(2,1)S(1)} collective-permute-done((bf16[128,2048]{1,0:T(8,128)(2,1)S(1)}, bf16[128,2048]{1,0:T(8,128)(2,1)S(1)}, u32[]{:S(2)}, u32[]{:S(2)}) %collective-permute-start) | collective-permute-done | bytes 524320 | tf_op jit(solution)/shard_map/ppermute | solution.py:18
  18.1 5.8 %collective-permute-done.3.g2.late_ref = bf16[128,2048]{1,0:T(8,128)(2,1)S(1)} collective-permute-done((bf16[128,2048]{1,0:T(8,128)(2,1)S(1)}, bf16[128,2048]{1,0:T(8,128)(2,1)S(1)}, u32[]{:S(2)}, u32[]{:S(2)}) %collective-permute-start.3) | collective-permute-done | bytes 524320 | tf_op jit(solution)/shard_map/ppermute | solution.py:18
  23.9 2.4 %taps.1 = f32[16,384]{1,0:T(8,128)S(1)} custom-call(bf16[128,2048]{1,0:T(8,128)(2,1)S(1)} %multiply_convert_fusion.1.p0.prod_ref, bf16[128,2048]{1,0:T(8,128)(2,1)S(1)} %collective-permute-done.p1.early_ref, bf16[128,2048]{1,0:T(8,128)(2,1)S(1)} %multiply_convert_fusion.g0.grad_ref, bf16[128,2048]{1,0:T(8,128)(2,1)S(1)} %collective-permute-done.3.g2.late_ref), custom_call_target="tpu_custom_call" | custom-call | flops 1000000000 | bytes 10000000 | tf_op jit(solution)/shard_map/taps/pallas_call | solution.py:122
  26.3 0.7 %broadcast_in_dim.2 = f32[8,16,384]{2,1,0:T(8,128)} broadcast(f32[16,384]{1,0:T(8,128)S(1)} %taps.1), dimensions={1,2} | broadcast | bytes 221184 | tf_op jit(solution)/shard_map/broadcast_in_dim | solution.py:22
  26.9 3.8 %all-to-all-start = ((f32[8,16,384]{2,1,0:T(8,128)}), f32[8,16,384]{2,1,0:T(8,128)S(1)}, u32[]{:S(2)}, u32[]{:S(2)}) async-start(f32[8,16,384]{2,1,0:T(8,128)} %broadcast_in_dim.2), calls=%async_computation | async-start | bytes 393216 | tf_op jit(solution)/shard_map/all_to_all | solution.py:23
  30.8 0.0 copy-start
  30.8 0.0 copy-start.1
  30.8 2.2 %tiles.1 = (bf16[16,128,384]{2,1,0:T(8,128)(2,1)S(1)}, bf16[16,128,384]{2,1,0:T(8,128)(2,1)S(1)}) custom-call(bf16[16,384]{1,0:T(8,128)(2,1)S(1)} %copy-done.3), custom_call_target="tpu_custom_call" | custom-call | flops 1000000000 | bytes 10000000 | tf_op jit(solution)/shard_map/tiles/pallas_call | solution.py:107
  33.1 0.0 collective-permute-done.1.p2
  33.1 0.0 collective-permute-done.2.g1
  33.1 3.2 %outputs.1 = (bf16[128,2048]{1,0:T(8,128)(2,1)}, bf16[128,2048]{1,0:T(8,128)(2,1)}, bf16[128,2048]{1,0:T(8,128)(2,1)}) custom-call(bf16[16,128,384]{2,1,0:T(8,128)(2,1)S(1)} %get-tuple-element.9.conv_ref, bf16[16,128,384]{2,1,0:T(8,128)(2,1)S(1)} %get-tuple-element.10.back_ref, bf16[128,2048]{1,0:T(8,128)(2,1)S(1)} %multiply_convert_fusion.1.p0.prod_ref, ...), custom_call_target="tpu_custom_call" | custom-call | flops 1000000000 | bytes 10000000 | tf_op jit(solution)/shard_map/outputs/pallas_call | solution.py:135
  36.3 2.5 %all-to-all-done = f32[8,16,384]{2,1,0:T(8,128)S(1)} async-done(((f32[8,16,384]{2,1,0:T(8,128)}), f32[8,16,384]{2,1,0:T(8,128)S(1)}, u32[]{:S(2)}, u32[]{:S(2)}) %all-to-all-start) | async-done | bytes 196640 | tf_op jit(solution)/shard_map/all_to_all | solution.py:23
  38.8 0.6 %reduce_sum.9 = f32[16,384]{1,0:T(8,128)} reduce(f32[8,16,384]{2,1,0:T(8,128)S(1)} %all-to-all-done, f32[]{:T(128)} %constant.0.clone.1), dimensions={0}, to_apply=%region_0.0 | reduce | flops 43008 | bytes 221188 | tf_op jit(solution)/shard_map/reduce_sum | solution.py:23
  (3 shorter events, 0.0 us)
Async XLA Ops:
  0.6 6.3 %copy-start.2 = (bf16[128,2048]{1,0:T(8,128)(2,1)S(1)}, bf16[128,2048]{1,0:T(8,128)(2,1)}, u32[]{:S(2)}) copy-start(bf16[128,2048]{1,0:T(8,128)(2,1)} %query.1) | copy-start | bytes 1572868
  0.6 6.3 %copy-start.4 = (bf16[128,2048]{1,0:T(8,128)(2,1)S(1)}, bf16[128,2048]{1,0:T(8,128)(2,1)}, u32[]{:S(2)}) copy-start(bf16[128,2048]{1,0:T(8,128)(2,1)} %param.8) | copy-start | bytes 1572868
  2.1 16.0 %collective-permute-start = (bf16[128,2048]{1,0:T(8,128)(2,1)S(1)}, bf16[128,2048]{1,0:T(8,128)(2,1)S(1)}, u32[]{:S(2)}, u32[]{:S(2)}) collective-permute-start(bf16[128,2048]{1,0:T(8,128)(2,1)S(1)} %multiply_convert_fusion.1.p0.prod_ref), channel_id=1, source_target_pairs={{0,4},{4,8},{8,12},{12,16},{16,20},{20,24},{24,28},{1,5},{5,9},{9,... | collective-permute-start | bytes 1572872 | tf_op jit(solution)/shard_map/ppermute | solution.py:18
  7.1 23.7 %copy-start.3 = (bf16[16,384]{1,0:T(8,128)(2,1)S(1)}, bf16[16,384]{1,0:T(8,128)(2,1)}, u32[]{:S(2)}) copy-start(bf16[16,384]{1,0:T(8,128)(2,1)} %taps_ref.1) | copy-start | bytes 36868
  7.1 16.7 %collective-permute-start.3 = (bf16[128,2048]{1,0:T(8,128)(2,1)S(1)}, bf16[128,2048]{1,0:T(8,128)(2,1)S(1)}, u32[]{:S(2)}, u32[]{:S(2)}) collective-permute-start(bf16[128,2048]{1,0:T(8,128)(2,1)S(1)} %multiply_convert_fusion.g0.grad_ref), channel_id=1, source_target_pairs={{8,0},{12,4},{16,8},{20,12},{24,16},{28,20},{9,1},{13,5},{17,9},{2... | collective-permute-start | bytes 1572872 | tf_op jit(solution)/shard_map/ppermute | solution.py:18
  8.4 24.7 %collective-permute-start.1 = (bf16[128,2048]{1,0:T(8,128)(2,1)S(1)}, bf16[128,2048]{1,0:T(8,128)(2,1)S(1)}, u32[]{:S(2)}, u32[]{:S(2)}) collective-permute-start(bf16[128,2048]{1,0:T(8,128)(2,1)S(1)} %multiply_convert_fusion.1.p0.prod_ref), channel_id=1, source_target_pairs={{0,8},{4,12},{8,16},{12,20},{16,24},{20,28},{1,9},{5,13},{9,17},{1... | collective-permute-start | bytes 1572872 | tf_op jit(solution)/shard_map/ppermute | solution.py:18
  13.0 20.1 %collective-permute-start.2 = (bf16[128,2048]{1,0:T(8,128)(2,1)S(1)}, bf16[128,2048]{1,0:T(8,128)(2,1)}, u32[]{:S(2)}, u32[]{:S(2)}) collective-permute-start(bf16[128,2048]{1,0:T(8,128)(2,1)S(1)} %multiply_convert_fusion.g0.grad_ref), channel_id=1, source_target_pairs={{4,0},{8,4},{12,8},{16,12},{20,16},{24,20},{28,24},{5,1},{9,5},{13... | collective-permute-start | bytes 1572872 | tf_op jit(solution)/shard_map/ppermute | solution.py:18
  26.9 11.9 %all-to-all-start = ((f32[8,16,384]{2,1,0:T(8,128)}), f32[8,16,384]{2,1,0:T(8,128)S(1)}, u32[]{:S(2)}, u32[]{:S(2)}) async-start(f32[8,16,384]{2,1,0:T(8,128)} %broadcast_in_dim.2), calls=%async_computation | async-start | bytes 393216 | tf_op jit(solution)/shard_map/all_to_all | solution.py:23
  30.8 2.3 %copy-start = (bf16[128,2048]{1,0:T(8,128)(2,1)S(1)}, bf16[128,2048]{1,0:T(8,128)(2,1)}, u32[]{:S(2)}) copy-start(bf16[128,2048]{1,0:T(8,128)(2,1)} %values.1) | copy-start | bytes 1572868
  30.8 2.3 %copy-start.1 = (bf16[128,2048]{1,0:T(8,128)(2,1)S(1)}, bf16[128,2048]{1,0:T(8,128)(2,1)}, u32[]{:S(2)}) copy-start(bf16[128,2048]{1,0:T(8,128)(2,1)} %keys.1) | copy-start | bytes 1572868

commit v4 on v3

v4 whole, which is shorter than its diff:
```python
import functools
import math

import jax
import jax.numpy as jnp
from jax import lax
from jax.experimental import pallas as pl
from jax.experimental.pallas import tpu as pltpu
from jax.sharding import PartitionSpec as P

SUBLANES = 8
VMEM_LIMIT = 32 * 1024 * 1024
WHOLE = pl.BlockSpec(memory_space=pltpu.VMEM)


def moved(block, axis, distances):
    size = lax.axis_size(axis)
    route = [(i, i + distances[i % 2]) for i in range(size)]
    return lax.ppermute(block, axis, [pair for pair in route if 0 <= pair[1] < size])


def tiles_kernel(rows, reach, taps_ref, back_ref, conv_ref):
    width = reach * rows
    for group in range(taps_ref.shape[0]):
        row = taps_ref[group : group + 1, :].astype(jnp.float32)
        spread = jnp.concatenate(
            [jnp.zeros((SUBLANES, rows), jnp.float32), jnp.broadcast_to(row, (SUBLANES, width))],
            axis=1,
        )
        spread = pltpu.roll(spread, 0, 1, stride=1, stride_axis=0)
        bands = [
            pltpu.roll(spread, start, 1)[:, rows:] if start else spread[:, rows:]
            for start in range(0, rows, SUBLANES)
        ]
        band = jnp.concatenate(bands, axis=0)
        back_ref[group] = band.astype(jnp.bfloat16)
        turned = [band[:, d * rows : (d + 1) * rows].T for d in range(reach)]
        conv_ref[group] = jnp.concatenate(turned, axis=1).astype(jnp.bfloat16)


def skewed_sum(outer, rows):
    width = outer.shape[1]
    total = outer[:SUBLANES]
    for start in range(SUBLANES, rows, SUBLANES):
        total = total + pltpu.roll(outer[start : start + SUBLANES], width - start, 1)
    lines = [total[:1]] + [pltpu.roll(total[s : s + 1], width - s, 1) for s in range(1, SUBLANES)]
    return functools.reduce(jnp.add, lines)


DOT_ROWS = functools.partial(
    lax.dot_general,
    dimension_numbers=(((1,), (1,)), ((), ())),
    preferred_element_type=jnp.float32,
)


def most_taps_kernel(rows, even_ref, odd_ref, diagonal_ref, two_ref, out_ref):
    odd = lax.rem(lax.axis_index("ctx"), 2) == 1
    group_count, width = out_ref.shape
    group_width = even_ref.shape[1] // group_count
    half = group_count // 2

    def columns(group):
        return slice(group * group_width, (group + 1) * group_width)

    def held(ref, group):
        return ref[:, columns(group)]

    middles = []
    for group in range(half):
        across = lax.select(odd, held(diagonal_ref, group + half), held(diagonal_ref, group))
        own = lax.select(odd, held(odd_ref, group + half), held(odd_ref, group))
        middles.append(DOT_ROWS(lax.select(odd, own, across), lax.select(odd, across, own)))
    blank = jnp.zeros((rows, rows), jnp.float32)
    sums = []
    for group in range(group_count):
        near = DOT_ROWS(
            lax.select(odd, held(odd_ref, group), held(even_ref, group)),
            lax.select(odd, held(even_ref, group), held(odd_ref, group)),
        )
        far = DOT_ROWS(
            lax.select(odd, held(odd_ref, group), held(two_ref, group)),
            lax.select(odd, held(two_ref, group), held(odd_ref, group)),
        )
        if group < half:
            middle = lax.select(odd, blank, middles[group])
        else:
            middle = lax.select(odd, middles[group - half], blank)
        outer = jnp.concatenate([near, middle, far, blank], axis=1)
        sums.append(skewed_sum(outer, rows)[:, :width])
    out_ref[...] = jnp.concatenate(sums, axis=0)


def last_taps_kernel(rows, factor, partial_ref, even_ref, first_ref, out_ref):
    odd = lax.rem(lax.axis_index("ctx"), 2) == 1
    copies, group_count, width = out_ref.shape
    group_width = even_ref.shape[1] // group_count
    half = group_count // 2
    blank = jnp.zeros((rows, rows), jnp.float32)
    sums = []
    for group in range(half):
        columns = slice(group * group_width, (group + 1) * group_width)
        other = slice((group + half) * group_width, (group + half + 1) * group_width)
        own = lax.select(odd, even_ref[:, columns], even_ref[:, other])
        across = first_ref[:, columns]
        outer = DOT_ROWS(lax.select(odd, across, own), lax.select(odd, own, across))
        sums.append(skewed_sum(jnp.concatenate([blank, outer], axis=1), rows))
    rest = jnp.concatenate(
        [jnp.concatenate(sums, axis=0), jnp.zeros((half, width - 2 * rows), jnp.float32)], axis=1
    )
    low = partial_ref[:half] + lax.select(odd, rest, jnp.zeros_like(rest))
    high = partial_ref[half:] + lax.select(odd, jnp.zeros_like(rest), rest)
    for copy in range(copies):
        out_ref[copy, :half] = low * factor
        out_ref[copy, half:] = high * factor


def outputs_kernel(
    conv_ref, back_ref, even_ref, odd_ref, diagonal_ref, two_ref, first_ref, far_ref, last_ref,
    query_ref, keys_ref, values_ref, gated_out, key_out, value_out, gated, key_grad, value_grad, sems,
):
    odd = lax.rem(lax.axis_index("ctx"), 2) == 1
    group_count = conv_ref.shape[0]
    group_width = even_ref.shape[1] // group_count
    half = group_count // 2
    step = max(1, group_count // 4)
    copies = []
    for group in range(group_count):
        columns = slice(group * group_width, (group + 1) * group_width)
        inner = slice((group % half) * group_width, (group % half + 1) * group_width)
        diagonal = diagonal_ref[:, columns]
        first = first_ref[:, inner]
        last = last_ref[:, inner]
        even_kept, odd_kept = even_ref[:, columns], odd_ref[:, columns]
        two, far = two_ref[:, columns], far_ref[:, columns]
        low = group < half
        early = [
            lax.select(odd, odd_kept, even_kept),
            lax.select(odd, first if low else last, diagonal),
            lax.select(odd, far, two),
        ]
        late = [
            lax.select(odd, even_kept, odd_kept),
            lax.select(odd, diagonal, last if low else first),
            lax.select(odd, two, far),
        ]
        convolved = jnp.dot(
            conv_ref[group], jnp.concatenate(early, axis=0), preferred_element_type=jnp.float32
        )
        backward = jnp.dot(
            back_ref[group], jnp.concatenate(late, axis=0), preferred_element_type=jnp.float32
        )
        gated[:, columns] = (query_ref[:, columns].astype(jnp.float32) * convolved).astype(gated.dtype)
        key_grad[:, columns] = (backward * values_ref[:, columns].astype(jnp.float32)).astype(key_grad.dtype)
        value_grad[:, columns] = (backward * keys_ref[:, columns].astype(jnp.float32)).astype(value_grad.dtype)
        if (group + 1) % step == 0:
            part = pl.ds((group + 1 - step) * group_width, step * group_width)
            for kept, out in ((gated, gated_out), (key_grad, key_out), (value_grad, value_out)):
                copy = pltpu.make_async_copy(kept.at[:, part], out.at[:, part], sems.at[len(copies)])
                copy.start()
                copies.append(copy)
    for copy in copies:
        copy.wait()


def shards(query, keys, values, cotangent, filter_taps):
    rows, local_width = query.shape
    group_count, taps = filter_taps.shape
    group_width = local_width // group_count
    reach = taps // rows
    size = lax.axis_size("ctx")
    odd = lax.axis_index("ctx") % 2 == 1
    half = local_width // 2
    params = pltpu.CompilerParams(vmem_limit_bytes=VMEM_LIMIT)
    cost = pl.CostEstimate(flops=5 * 10**8, bytes_accessed=8 * 10**6, transcendentals=0)

    prod = (keys.astype(jnp.float32) * values.astype(jnp.float32)).astype(jnp.bfloat16)
    grad = (cotangent.astype(jnp.float32) * query.astype(jnp.float32)).astype(jnp.bfloat16)
    odd_kept = jnp.where(odd, prod, grad)
    diagonal = moved(odd_kept, "ctx", (-1, 1))
    even_kept = jnp.where(odd, grad, prod)
    two = moved(even_kept, "ctx", (2, -2))
    first = moved(jnp.where(odd, grad[:, half:], prod[:, :half]), "ctx", (1, -1))
    far = moved(odd_kept, "ctx", (-2, 2))
    last = moved(jnp.where(odd, grad[:, :half], prod[:, half:]), "ctx", (1, -1))

    step = min(group_count, 8)
    tile_shape = jax.ShapeDtypeStruct((group_count, rows, taps), jnp.bfloat16)
    tile_spec = pl.BlockSpec((step, rows, taps), lambda i: (i, 0, 0))
    back_tiles, conv_tiles = pl.pallas_call(
        functools.partial(tiles_kernel, rows, reach),
        grid=(group_count // step,),
        in_specs=[pl.BlockSpec((step, taps), lambda i: (i, 0))],
        out_specs=[tile_spec, tile_spec],
        out_shape=[tile_shape, tile_shape],
        compiler_params=params,
        cost_estimate=cost,
        name="tiles",
    )(filter_taps)

    factor = 1.0 / math.sqrt(rows * size * group_width)
    most = pl.pallas_call(
        functools.partial(most_taps_kernel, rows),
        in_specs=[WHOLE] * 4,
        out_specs=WHOLE,
        out_shape=jax.ShapeDtypeStruct((group_count, taps), jnp.float32),
        compiler_params=params,
        cost_estimate=cost,
        name="most_taps",
    )(even_kept, odd_kept, diagonal, two)
    partial = pl.pallas_call(
        functools.partial(last_taps_kernel, rows, factor),
        in_specs=[WHOLE] * 3,
        out_specs=WHOLE,
        out_shape=jax.ShapeDtypeStruct((size, group_count, taps), jnp.float32),
        compiler_params=params,
        cost_estimate=cost,
        name="last_taps",
    )(most, even_kept, first)
    filter_grad = jnp.sum(lax.all_to_all(partial, "ctx", 0, 0), axis=0)

    out_shape = jax.ShapeDtypeStruct((rows, local_width), jnp.bfloat16)
    gated, key_grad, value_grad = pl.pallas_call(
        outputs_kernel,
        in_specs=[WHOLE] * 12,
        out_specs=[pl.BlockSpec(memory_space=pl.ANY)] * 3,
        out_shape=[out_shape] * 3,
        scratch_shapes=[pltpu.VMEM((rows, local_width), jnp.bfloat16)] * 3 + [pltpu.SemaphoreType.DMA((12,))],
        compiler_params=params,
        cost_estimate=cost,
        name="outputs",
    )(
        conv_tiles, back_tiles, even_kept, odd_kept, diagonal, two, first, far, last, query, keys, values
    )
    return (gated, key_grad, value_grad, filter_grad)


def solution(mesh):
    in_specs = (P("ctx", "grp"), P("ctx", "grp"), P("ctx", "grp"), P("ctx", "grp"), P("grp", None))
    out_specs = (P("ctx", "grp"), P("ctx", "grp"), P("ctx", "grp"), P("grp", None))
    return jax.shard_map(shards, mesh=mesh, in_specs=in_specs, out_specs=out_specs, check_vma=False)
```

time: 39.8 us -> 48 us (1.21)
  waiting for transfers between devices: 12.1 us -> 15.8 us
  other arithmetic: 2.16 us -> 4.28 us
  starting transfers between devices: 15.9 us -> 17.5 us
  Pallas kernels: 7.85 us -> 8.47 us
    ppermute x4 -> x5, waiting for transfers between devices: 9.56 us -> 15.8 us  [moved(): lax.ppermute(block, axis, [pair for pair in route if 0 <= pair[1] < size])]
    select_n x0 -> x3, other arithmetic: none -> 2.72 us  [the longest x1 1.91 us: shards(): odd_kept = jnp.where(odd, prod, grad)]
    all_to_all x1, waiting for transfers between devices: 2.5 us -> 0.01 us  [shards(): filter_grad = jnp.sum(lax.all_to_all(partial, 'ctx', 0, 0), axis=0)]
    all_to_all x1, starting transfers between devices: 3.84 us -> 6 us  [shards(): filter_grad = jnp.sum(lax.all_to_all(partial, 'ctx', 0, 0), axis=0)]
    convert_element_type x2 -> x0, other arithmetic: 1.54 us -> none  [the longest x1 1.41 us: shards(): (keys.astype(jnp.float32) * values.astype(jnp.float32)).astype(jnp.bfloat16)]
    reduce_sum x1, other arithmetic: 0.62 us -> 1.55 us  [shards(): filter_grad = jnp.sum(lax.all_to_all(partial, 'ctx', 0, 0), axis=0)]
    broadcast_in_dim x1 -> x0, local copies, waits for them, and re-layouts: 0.69 us -> none  [summed(): jnp.broadcast_to(partial[None], (lax.axis_size(axis), *partial.shape))]
    unnamed x10 -> x14, local copies, waits for them, and re-layouts: 0.03 us -> 0.69 us
  transfers between devices with their start and end apart: 5 -> 6, of which waited for: 3 -> 3; matrix products, arithmetic and copies ran while one was open for 2% -> 2% of each run, Pallas kernels for 20% -> 18%
where the time goes in v4:
time: 48 us; the launch traced here: 47.6 us
  starting transfers between devices  17.5 us (36%)
  waiting for transfers between devices  15.8 us (33%)
  Pallas kernels  8.47 us (18%)
  other arithmetic  4.28 us (9%)
  between operations  0.78 us (2%)
  local copies, waits for them, and re-layouts  0.69 us (1%)
    ppermute x5, waiting for transfers between devices, moved(): lax.ppermute(block, axis, [pair for pair in route if 0 <= pair[1] < size])  15.8 us
    ppermute x5, starting transfers between devices, moved(): lax.ppermute(block, axis, [pair for pair in route if 0 <= pair[1] < size])  11.5 us
    all_to_all x1, starting transfers between devices, shards(): filter_grad = jnp.sum(lax.all_to_all(partial, 'ctx', 0, 0), axis=0)  6 us
    pallas_call x1, Pallas kernels, shards(): pl.pallas_call(outputs_kernel, in_specs=[WHOLE] * 12, out_specs=[pl.Block...  3.39 us
    pallas_call x1, Pallas kernels, shards(): pl.pallas_call(functools.partial(most_taps_kernel, rows), in_specs=[WHOLE...  2.3 us
    pallas_call x1, Pallas kernels, shards(): pl.pallas_call(functools.partial(tiles_kernel, rows, reach), grid=(group_...  2.23 us
    select_n x1, other arithmetic, shards(): odd_kept = jnp.where(odd, prod, grad)  1.91 us
    reduce_sum x1, other arithmetic, shards(): filter_grad = jnp.sum(lax.all_to_all(partial, 'ctx', 0, 0), axis=0)  1.55 us
  transfers between devices with their start and end apart: 6, of which 3 were waited for; matrix products, arithmetic and copies ran while one was open for 2% of the time, Pallas kernels for 18%

profile of v4, /device:TPU:0, one launch (start us, length us, event | category | flops | bytes accessed | tf_op | source)
XLA Modules:
  0.0 47.6 jit_solution(15451994513498300790)
XLA Ops:
  0.6 1.9 %broadcast_select_fusion = (bf16[128,2048]{1,0:T(8,128)(2,1)S(1)}, bf16[128,2048]{1,0:T(8,128)(2,1)S(1)}, bf16[128,2048]{1,0:T(8,128)(2,1)S(1)}) fusion(pred[]{:T(512)S(6)} %eq.5, bf16[128,2048]{1,0:T(8,128)(2,1)} %values_ref.1, bf16[128,2048]{1,0:T(8,128)(2,1)} %keys_ref.1, bf16[128,2048]{1,0:T(8,128)(2,1)} %query_ref.1, bf16[128,2048]{1,0:T(8,128)(2,1)} %param.8), kind=kLoop, calls=%fused_computation.2 | loop fusion | flops 2359296 | bytes 3670017 | tf_op jit(solution)/shard_map/jit(_where)/select_n | solution.py:179
  2.6 0.7 %collective-permute-start = (bf16[128,2048]{1,0:T(8,128)(2,1)S(1)}, bf16[128,2048]{1,0:T(8,128)(2,1)S(1)}, u32[]{:S(2)}, u32[]{:S(2)}) collective-permute-start(bf16[128,2048]{1,0:T(8,128)(2,1)S(1)} %get-tuple-element.14.odd_ref), channel_id=1, source_target_pairs={{4,8},{8,4},{12,16},{16,12},{20,24},{24,20},{5,9},{9,5},{13,17},{1... | collective-permute-start | bytes 1572872 | tf_op jit(solution)/shard_map/ppermute | solution.py:19
  3.3 0.1 broadcast_select_fusion.1.even_ref
  3.3 7.6 %collective-permute-start.1 = (bf16[128,2048]{1,0:T(8,128)(2,1)S(1)}, bf16[128,2048]{1,0:T(8,128)(2,1)S(1)}, u32[]{:S(2)}, u32[]{:S(2)}) collective-permute-start(bf16[128,2048]{1,0:T(8,128)(2,1)S(1)} %broadcast_select_fusion.1.even_ref), channel_id=1, source_target_pairs={{0,8},{8,16},{12,4},{16,24},{20,12},{28,20},{1,9},{9,17},{13,5},{1... | collective-permute-start | bytes 1572872 | tf_op jit(solution)/shard_map/ppermute | solution.py:19
  10.9 0.8 %slice_select_fusion = (bf16[128,1024]{1,0:T(8,128)(2,1)}, bf16[128,1024]{1,0:T(8,128)(2,1)S(1)}) fusion(bf16[128,2048]{1,0:T(8,128)(2,1)S(1)} %get-tuple-element.15, bf16[128,2048]{1,0:T(8,128)(2,1)S(1)} %get-tuple-element.16, pred[]{:T(512)S(6)} %eq.5), kind=kLoop, calls=%fused_computation.4 | loop fusion | flops 262144 | bytes 1572865 | tf_op jit(solution)/shard_map/jit(_where)/select_n | solution.py:185
  11.6 0.0 collective-permute-start.2
  11.6 1.3 %collective-permute-start.3 = (bf16[128,2048]{1,0:T(8,128)(2,1)S(1)}, bf16[128,2048]{1,0:T(8,128)(2,1)}, u32[]{:S(2)}, u32[]{:S(2)}) collective-permute-start(bf16[128,2048]{1,0:T(8,128)(2,1)S(1)} %get-tuple-element.14.odd_ref), channel_id=1, source_target_pairs={{4,12},{8,0},{12,20},{16,8},{20,28},{24,16},{5,13},{9,1},{13,21},{... | collective-permute-start | bytes 1572872 | tf_op jit(solution)/shard_map/ppermute | solution.py:19
  12.9 0.0 collective-permute-done.diagonal_ref
  12.9 8.8 %collective-permute-done.1.two_ref = bf16[128,2048]{1,0:T(8,128)(2,1)S(1)} collective-permute-done((bf16[128,2048]{1,0:T(8,128)(2,1)S(1)}, bf16[128,2048]{1,0:T(8,128)(2,1)S(1)}, u32[]{:S(2)}, u32[]{:S(2)}) %collective-permute-start.1) | collective-permute-done | bytes 524320 | tf_op jit(solution)/shard_map/ppermute | solution.py:19
  21.7 2.3 %most_taps.1.partial_ref = f32[16,384]{1,0:T(8,128)S(1)} custom-call(bf16[128,2048]{1,0:T(8,128)(2,1)S(1)} %broadcast_select_fusion.1.even_ref, bf16[128,2048]{1,0:T(8,128)(2,1)S(1)} %get-tuple-element.14.odd_ref, bf16[128,2048]{1,0:T(8,128)(2,1)S(1)} %collective-permute-done.diagonal_ref, bf16[128,2048]{1,0:T(8,128)(2,1)S(1)} %collective-permute-done.1.two_ref), custom_call_target="tpu_custom_call" | custom-call | flops 500000000 | bytes 8000000 | tf_op jit(solution)/shard_map/most_taps/pallas_call | solution.py:202
  24.0 0.0 copy-start.6
  24.1 1.0 %collective-permute-done.2.first_ref = bf16[128,1024]{1,0:T(8,128)(2,1)S(1)} collective-permute-done((bf16[128,1024]{1,0:T(8,128)(2,1)S(1)}, bf16[128,1024]{1,0:T(8,128)(2,1)S(1)}, u32[]{:S(2)}, u32[]{:S(2)}) %collective-permute-start.2) | collective-permute-done | bytes 262176 | tf_op jit(solution)/shard_map/ppermute | solution.py:19
  25.1 0.0 copy-done.3
  25.1 0.6 %last_taps.1 = f32[8,16,384]{2,1,0:T(8,128)S(1)} custom-call(f32[16,384]{1,0:T(8,128)S(1)} %most_taps.1.partial_ref, bf16[128,2048]{1,0:T(8,128)(2,1)S(1)} %broadcast_select_fusion.1.even_ref, bf16[128,1024]{1,0:T(8,128)(2,1)S(1)} %collective-permute-done.2.first_ref), custom_call_target="tpu_custom_call" | custom-call | flops 500000000 | bytes 8000000 | tf_op jit(solution)/shard_map/last_taps/pallas_call | solution.py:211
  25.7 0.0 copy-start.5
  25.7 0.7 %copy-done.5 = f32[8,16,384]{2,1,0:T(8,128)} copy-done((f32[8,16,384]{2,1,0:T(8,128)}, f32[8,16,384]{2,1,0:T(8,128)S(1)}, u32[]{:S(2)}) %copy-start.5) | copy-done | bytes 196632
  26.3 6.0 %all-to-all-start = ((f32[8,16,384]{2,1,0:T(8,128)}), f32[8,16,384]{2,1,0:T(8,128)}, u32[]{:S(2)}, u32[]{:S(2)}) async-start(f32[8,16,384]{2,1,0:T(8,128)} %copy-done.5), calls=%async_computation | async-start | bytes 393216 | tf_op jit(solution)/shard_map/all_to_all | solution.py:220
  32.3 2.0 %collective-permute-start.4 = (bf16[128,1024]{1,0:T(8,128)(2,1)}, bf16[128,1024]{1,0:T(8,128)(2,1)S(1)}, u32[]{:S(2)}, u32[]{:S(2)}) collective-permute-start(bf16[128,1024]{1,0:T(8,128)(2,1)} %get-tuple-element.17), channel_id=1, source_target_pairs={{0,4},{4,0},{8,12},{12,8},{16,20},{20,16},{24,28},{28,24},{1,5},{5... | collective-permute-start | bytes 786440 | tf_op jit(solution)/shard_map/ppermute | solution.py:19
  34.4 2.2 %tiles.1 = (bf16[16,128,384]{2,1,0:T(8,128)(2,1)S(1)}, bf16[16,128,384]{2,1,0:T(8,128)(2,1)S(1)}) custom-call(bf16[16,384]{1,0:T(8,128)(2,1)S(1)} %copy-done.6), custom_call_target="tpu_custom_call" | custom-call | flops 500000000 | bytes 8000000 | tf_op jit(solution)/shard_map/tiles/pallas_call | solution.py:190
  36.6 6.0 %collective-permute-done.4.last_ref = bf16[128,1024]{1,0:T(8,128)(2,1)S(1)} collective-permute-done((bf16[128,1024]{1,0:T(8,128)(2,1)}, bf16[128,1024]{1,0:T(8,128)(2,1)S(1)}, u32[]{:S(2)}, u32[]{:S(2)}) %collective-permute-start.4) | collective-permute-done | bytes 262176 | tf_op jit(solution)/shard_map/ppermute | solution.py:19
  42.6 0.0 collective-permute-done.3.far_ref
  42.6 3.4 %outputs.1 = (bf16[128,2048]{1,0:T(8,128)(2,1)}, bf16[128,2048]{1,0:T(8,128)(2,1)}, bf16[128,2048]{1,0:T(8,128)(2,1)}) custom-call(bf16[16,128,384]{2,1,0:T(8,128)(2,1)S(1)} %get-tuple-element.9.conv_ref, bf16[16,128,384]{2,1,0:T(8,128)(2,1)S(1)} %get-tuple-element.10.back_ref, bf16[128,2048]{1,0:T(8,128)(2,1)S(1)} %broadcast_select_fusion.1.even_ref, ...), custom_call_target="tpu_custom_call" | custom-call | flops 500000000 | bytes 8000000 | tf_op jit(solution)/shard_map/outputs/pallas_call | solution.py:223
  46.0 0.0 all-to-all-done
  46.0 1.6 %reduce_sum.9 = f32[16,384]{1,0:T(8,128)} reduce(f32[8,16,384]{2,1,0:T(8,128)} %all-to-all-done, f32[]{:T(128)} %constant.21.clone.1), dimensions={0}, to_apply=%region_0.1 | reduce | flops 43008 | bytes 221188 | tf_op jit(solution)/shard_map/reduce_sum | solution.py:220
  (10 shorter events, 0.0 us)
Async XLA Ops:
  2.6 10.4 %collective-permute-start = (bf16[128,2048]{1,0:T(8,128)(2,1)S(1)}, bf16[128,2048]{1,0:T(8,128)(2,1)S(1)}, u32[]{:S(2)}, u32[]{:S(2)}) collective-permute-start(bf16[128,2048]{1,0:T(8,128)(2,1)S(1)} %get-tuple-element.14.odd_ref), channel_id=1, source_target_pairs={{4,8},{8,4},{12,16},{16,12},{20,24},{24,20},{5,9},{9,5},{13,17},{1... | collective-permute-start | bytes 1572872 | tf_op jit(solution)/shard_map/ppermute | solution.py:19
  3.3 18.4 %collective-permute-start.1 = (bf16[128,2048]{1,0:T(8,128)(2,1)S(1)}, bf16[128,2048]{1,0:T(8,128)(2,1)S(1)}, u32[]{:S(2)}, u32[]{:S(2)}) collective-permute-start(bf16[128,2048]{1,0:T(8,128)(2,1)S(1)} %broadcast_select_fusion.1.even_ref), channel_id=1, source_target_pairs={{0,8},{8,16},{12,4},{16,24},{20,12},{28,20},{1,9},{9,17},{13,5},{1... | collective-permute-start | bytes 1572872 | tf_op jit(solution)/shard_map/ppermute | solution.py:19
  11.6 13.4 %collective-permute-start.2 = (bf16[128,1024]{1,0:T(8,128)(2,1)S(1)}, bf16[128,1024]{1,0:T(8,128)(2,1)S(1)}, u32[]{:S(2)}, u32[]{:S(2)}) collective-permute-start(bf16[128,1024]{1,0:T(8,128)(2,1)S(1)} %get-tuple-element.18), channel_id=1, source_target_pairs={{0,4},{4,0},{8,12},{12,8},{16,20},{20,16},{24,28},{28,24},{1,5},{5... | collective-permute-start | bytes 786440 | tf_op jit(solution)/shard_map/ppermute | solution.py:19
  11.6 31.0 %collective-permute-start.3 = (bf16[128,2048]{1,0:T(8,128)(2,1)S(1)}, bf16[128,2048]{1,0:T(8,128)(2,1)}, u32[]{:S(2)}, u32[]{:S(2)}) collective-permute-start(bf16[128,2048]{1,0:T(8,128)(2,1)S(1)} %get-tuple-element.14.odd_ref), channel_id=1, source_target_pairs={{4,12},{8,0},{12,20},{16,8},{20,28},{24,16},{5,13},{9,1},{13,21},{... | collective-permute-start | bytes 1572872 | tf_op jit(solution)/shard_map/ppermute | solution.py:19
  21.7 3.4 %copy-start.3 = (bf16[128,2048]{1,0:T(8,128)(2,1)}, bf16[128,2048]{1,0:T(8,128)(2,1)S(1)}, u32[]{:S(2)}) copy-start(bf16[128,2048]{1,0:T(8,128)(2,1)S(1)} %collective-permute-done.1.two_ref) | copy-start | bytes 1572868
  24.0 10.3 %copy-start.6 = (bf16[16,384]{1,0:T(8,128)(2,1)S(1)}, bf16[16,384]{1,0:T(8,128)(2,1)}, u32[]{:S(2)}) copy-start(bf16[16,384]{1,0:T(8,128)(2,1)} %taps_ref.1) | copy-start | bytes 36868
  25.7 0.7 %copy-start.5 = (f32[8,16,384]{2,1,0:T(8,128)}, f32[8,16,384]{2,1,0:T(8,128)S(1)}, u32[]{:S(2)}) copy-start(f32[8,16,384]{2,1,0:T(8,128)S(1)} %last_taps.1) | copy-start | bytes 589828
  26.3 16.3 %copy-start = (bf16[128,2048]{1,0:T(8,128)(2,1)S(1)}, bf16[128,2048]{1,0:T(8,128)(2,1)}, u32[]{:S(2)}) copy-start(bf16[128,2048]{1,0:T(8,128)(2,1)} %values_ref.1) | copy-start | bytes 1572868
  26.3 16.3 %copy-start.1 = (bf16[128,2048]{1,0:T(8,128)(2,1)S(1)}, bf16[128,2048]{1,0:T(8,128)(2,1)}, u32[]{:S(2)}) copy-start(bf16[128,2048]{1,0:T(8,128)(2,1)} %keys_ref.1) | copy-start | bytes 1572868
  26.3 16.3 %copy-start.2 = (bf16[128,2048]{1,0:T(8,128)(2,1)S(1)}, bf16[128,2048]{1,0:T(8,128)(2,1)}, u32[]{:S(2)}) copy-start(bf16[128,2048]{1,0:T(8,128)(2,1)} %query_ref.1) | copy-start | bytes 1572868
  26.3 19.7 %all-to-all-start = ((f32[8,16,384]{2,1,0:T(8,128)}), f32[8,16,384]{2,1,0:T(8,128)}, u32[]{:S(2)}, u32[]{:S(2)}) async-start(f32[8,16,384]{2,1,0:T(8,128)} %copy-done.5), calls=%async_computation | async-start | bytes 393216 | tf_op jit(solution)/shard_map/all_to_all | solution.py:220
  32.3 10.3 %copy-start.4 = (bf16[128,2048]{1,0:T(8,128)(2,1)S(1)}, bf16[128,2048]{1,0:T(8,128)(2,1)}, u32[]{:S(2)}) copy-start(bf16[128,2048]{1,0:T(8,128)(2,1)} %copy-done.3) | copy-start | bytes 1572868
  32.3 10.3 %collective-permute-start.4 = (bf16[128,1024]{1,0:T(8,128)(2,1)}, bf16[128,1024]{1,0:T(8,128)(2,1)S(1)}, u32[]{:S(2)}, u32[]{:S(2)}) collective-permute-start(bf16[128,1024]{1,0:T(8,128)(2,1)} %get-tuple-element.17), channel_id=1, source_target_pairs={{0,4},{4,0},{8,12},{12,8},{16,20},{20,16},{24,28},{28,24},{1,5},{5... | collective-permute-start | bytes 786440 | tf_op jit(solution)/shard_map/ppermute | solution.py:19

commit v5 on v4

v5 whole, which is shorter than its diff:
```python
import functools
import math

import jax
import jax.numpy as jnp
from jax import lax
from jax.experimental import pallas as pl
from jax.experimental.pallas import tpu as pltpu
from jax.sharding import PartitionSpec as P

SUBLANES = 8
PARTS = 4
VMEM_LIMIT = 16 * 1024 * 1024
WHOLE = pl.BlockSpec(memory_space=pltpu.VMEM)


def moved(block, axis, distances):
    size = lax.axis_size(axis)
    route = [(i, i + distances[i % 2]) for i in range(size)]
    return lax.ppermute(block, axis, [pair for pair in route if 0 <= pair[1] < size])


def tiles_kernel(rows, reach, taps_ref, ready_ref, late_ref):
    odd = lax.rem(lax.axis_index("ctx"), 2) == 1
    width = reach * rows
    for group in range(taps_ref.shape[0]):
        row = taps_ref[group : group + 1, :].astype(jnp.float32)
        spread = jnp.concatenate(
            [jnp.zeros((SUBLANES, rows), jnp.float32), jnp.broadcast_to(row, (SUBLANES, width))],
            axis=1,
        )
        spread = pltpu.roll(spread, 0, 1, stride=1, stride_axis=0)
        bands = [
            pltpu.roll(spread, start, 1)[:, rows:] if start else spread[:, rows:]
            for start in range(0, rows, SUBLANES)
        ]
        band = jnp.concatenate(bands, axis=0)
        turned = [band[:, d * rows : (d + 1) * rows].T for d in range(reach)]
        turned = jnp.concatenate(turned, axis=1)
        ready_ref[group] = lax.select(odd, band, turned).astype(jnp.bfloat16)
        late_ref[group] = lax.select(odd, turned, band).astype(jnp.bfloat16)


def skewed_sum(outer, rows):
    width = outer.shape[1]
    total = outer[:SUBLANES]
    for start in range(SUBLANES, rows, SUBLANES):
        total = total + pltpu.roll(outer[start : start + SUBLANES], width - start, 1)
    lines = [total[:1]] + [pltpu.roll(total[s : s + 1], width - s, 1) for s in range(1, SUBLANES)]
    return functools.reduce(jnp.add, lines)


DOT_ROWS = functools.partial(
    lax.dot_general,
    dimension_numbers=(((1,), (1,)), ((), ())),
    preferred_element_type=jnp.float32,
)


def write_out(odd, held, outs, part, sems, place):
    copies = []
    for block, places in zip(held, outs):
        for parity, out in enumerate(places):
            if out is not None:
                copies.append((parity, block.at[:, part], out.at[:, part], sems.at[place + len(copies)]))
    for parity, source, target, sem in copies:
        @pl.when(odd == (parity == 1))
        def _():
            pltpu.make_async_copy(source, target, sem).start()
    return copies


def wait_out(odd, copies):
    for parity, source, target, sem in copies:
        @pl.when(odd == (parity == 1))
        def _():
            pltpu.make_async_copy(source, target, sem).wait()


def ready_kernel(
    rows, tile_ref, even_ref, odd_ref, diagonal_ref, two_ref, query_ref, keys_ref, values_ref,
    sum_ref, gated_out, key_out, value_out, one, other, sems,
):
    odd = lax.rem(lax.axis_index("ctx"), 2) == 1
    group_count, width = sum_ref.shape
    group_width = even_ref.shape[1] // group_count
    half = group_count // 2
    step = max(1, group_count // PARTS)

    def columns(group):
        return slice(group * group_width, (group + 1) * group_width)

    def held(ref, group):
        return ref[:, columns(group)]

    copies = []
    for group in range(group_count):
        ready = jnp.dot(
            tile_ref[group],
            jnp.concatenate([held(ref, group) for ref in (even_ref, diagonal_ref, two_ref)], axis=0),
            preferred_element_type=jnp.float32,
        )
        factor = lax.select(odd, held(values_ref, group), held(query_ref, group))
        one[:, columns(group)] = (ready * factor.astype(jnp.float32)).astype(one.dtype)
        other[:, columns(group)] = (ready * held(keys_ref, group).astype(jnp.float32)).astype(other.dtype)
        if (group + 1) % step == 0:
            part = pl.ds((group + 1 - step) * group_width, step * group_width)
            copies += write_out(
                odd, (one, other), ((gated_out, key_out), (None, value_out)), part, sems, len(copies)
            )

    middles = []
    for group in range(half):
        across = lax.select(odd, held(diagonal_ref, group + half), held(diagonal_ref, group))
        own = lax.select(odd, held(odd_ref, group + half), held(odd_ref, group))
        middles.append(DOT_ROWS(lax.select(odd, own, across), lax.select(odd, across, own)))
    blank = jnp.zeros((rows, rows), jnp.float32)
    sums = []
    for group in range(group_count):
        near = DOT_ROWS(
            lax.select(odd, held(odd_ref, group), held(even_ref, group)),
            lax.select(odd, held(even_ref, group), held(odd_ref, group)),
        )
        far = DOT_ROWS(
            lax.select(odd, held(odd_ref, group), held(two_ref, group)),
            lax.select(odd, held(two_ref, group), held(odd_ref, group)),
        )
        if group < half:
            middle = lax.select(odd, blank, middles[group])
        else:
            middle = lax.select(odd, middles[group - half], blank)
        outer = jnp.concatenate([near, middle, far, blank], axis=1)
        sums.append(skewed_sum(outer, rows)[:, :width])
    sum_ref[...] = jnp.concatenate(sums, axis=0)
    wait_out(odd, copies)


def first_kernel(rows, factor, sum_ref, tile_ref, even_ref, odd_ref, first_ref, out_ref, late_ref):
    odd = lax.rem(lax.axis_index("ctx"), 2) == 1
    copies, group_count, width = out_ref.shape
    group_width = even_ref.shape[1] // group_count
    half = group_count // 2
    blank = jnp.zeros((rows, rows), jnp.float32)
    sums = []
    for group in range(half):
        columns = slice(group * group_width, (group + 1) * group_width)
        other = slice((group + half) * group_width, (group + half + 1) * group_width)
        own = lax.select(odd, even_ref[:, columns], even_ref[:, other])
        across = first_ref[:, columns]
        outer = DOT_ROWS(lax.select(odd, across, own), lax.select(odd, own, across))
        sums.append(skewed_sum(jnp.concatenate([blank, outer], axis=1), rows))
        low = jnp.dot(tile_ref[group, :, :rows], odd_ref[:, columns], preferred_element_type=jnp.float32)
        high = jnp.dot(tile_ref[group + half, :, :rows], odd_ref[:, other], preferred_element_type=jnp.float32)
        tile = lax.select(
            odd, tile_ref[group, :, rows : 2 * rows], tile_ref[group + half, :, rows : 2 * rows]
        )
        more = jnp.dot(tile, across, preferred_element_type=jnp.float32)
        late_ref[:, columns] = low + lax.select(odd, more, blank)
        late_ref[:, other] = high + lax.select(odd, blank, more)
    rest = jnp.concatenate(
        [jnp.concatenate(sums, axis=0), jnp.zeros((half, width - 2 * rows), jnp.float32)], axis=1
    )
    low = (sum_ref[:half] + lax.select(odd, rest, jnp.zeros_like(rest))) * factor
    high = (sum_ref[half:] + lax.select(odd, jnp.zeros_like(rest), rest)) * factor
    for copy in range(copies):
        out_ref[copy, :half] = low
        out_ref[copy, half:] = high


def late_kernel(
    tile_ref, late_ref, far_ref, last_ref, query_ref, keys_ref, values_ref, gated_in, key_in, value_in,
    gated_out, key_out, value_out, one, other, sems,
):
    odd = lax.rem(lax.axis_index("ctx"), 2) == 1
    group_count, rows, _ = tile_ref.shape
    group_width = far_ref.shape[1] // group_count
    half = group_count // 2
    step = max(1, group_count // PARTS)
    blank = jnp.zeros((rows, group_width), jnp.float32)
    copies = []
    for group in range(group_count):
        columns = slice(group * group_width, (group + 1) * group_width)
        inner = slice((group % half) * group_width, (group % half + 1) * group_width)
        late = late_ref[:, columns] + jnp.dot(
            tile_ref[group, :, 2 * rows :], far_ref[:, columns], preferred_element_type=jnp.float32
        )
        more = jnp.dot(
            tile_ref[group, :, rows : 2 * rows], last_ref[:, inner], preferred_element_type=jnp.float32
        )
        late = late + (lax.select(odd, blank, more) if group < half else lax.select(odd, more, blank))
        factor = lax.select(odd, query_ref[:, columns], values_ref[:, columns])
        one[:, columns] = (late * factor.astype(jnp.float32)).astype(one.dtype)
        other[:, columns] = (late * keys_ref[:, columns].astype(jnp.float32)).astype(other.dtype)
        if (group + 1) % step == 0:
            part = pl.ds((group + 1 - step) * group_width, step * group_width)
            copies += write_out(
                odd, (one, other), ((key_out, gated_out), (value_out, None)), part, sems, len(copies)
            )
    wait_out(odd, copies)


def shards(query, keys, values, cotangent, filter_taps):
    rows, local_width = query.shape
    group_count, taps = filter_taps.shape
    group_width = local_width // group_count
    reach = taps // rows
    size = lax.axis_size("ctx")
    odd = lax.axis_index("ctx") % 2 == 1
    half = local_width // 2
    params = pltpu.CompilerParams(vmem_limit_bytes=VMEM_LIMIT)
    cost = pl.CostEstimate(flops=5 * 10**8, bytes_accessed=8 * 10**6, transcendentals=0)

    prod = (keys.astype(jnp.float32) * values.astype(jnp.float32)).astype(jnp.bfloat16)
    grad = (cotangent.astype(jnp.float32) * query.astype(jnp.float32)).astype(jnp.bfloat16)
    odd_kept = jnp.where(odd, prod, grad)
    diagonal = moved(odd_kept, "ctx", (-1, 1))
    even_kept = jnp.where(odd, grad, prod)
    two = moved(even_kept, "ctx", (2, -2))
    first = moved(jnp.where(odd, grad[:, half:], prod[:, :half]), "ctx", (1, -1))
    far = moved(odd_kept, "ctx", (-2, 2))
    rest = jnp.where(odd, grad[:, :half], prod[:, half:])
    rest, diagonal = lax.optimization_barrier((rest, diagonal))
    last = moved(rest, "ctx", (1, -1))

    step = min(group_count, 8)
    tile_shape = jax.ShapeDtypeStruct((group_count, rows, taps), jnp.bfloat16)
    tile_spec = pl.BlockSpec((step, rows, taps), lambda i: (i, 0, 0))
    ready_tiles, late_tiles = pl.pallas_call(
        functools.partial(tiles_kernel, rows, reach),
        grid=(group_count // step,),
        in_specs=[pl.BlockSpec((step, taps), lambda i: (i, 0))],
        out_specs=[tile_spec, tile_spec],
        out_shape=[tile_shape, tile_shape],
        compiler_params=params,
        cost_estimate=cost,
        name="tiles",
    )(filter_taps)

    out_shape = jax.ShapeDtypeStruct((rows, local_width), jnp.bfloat16)
    out_scratch = [pltpu.VMEM((rows, local_width), jnp.bfloat16)] * 2 + [pltpu.SemaphoreType.DMA((3 * PARTS,))]
    anywhere = pl.BlockSpec(memory_space=pl.ANY)
    sums, gated, key_grad, value_grad = pl.pallas_call(
        functools.partial(ready_kernel, rows),
        in_specs=[WHOLE] * 8,
        out_specs=[WHOLE] + [anywhere] * 3,
        out_shape=[jax.ShapeDtypeStruct((group_count, taps), jnp.float32)] + [out_shape] * 3,
        scratch_shapes=out_scratch,
        compiler_params=params,
        cost_estimate=cost,
        name="ready",
    )(ready_tiles, even_kept, odd_kept, diagonal, two, query, keys, values)

    factor = 1.0 / math.sqrt(rows * size * group_width)
    partial, late = pl.pallas_call(
        functools.partial(first_kernel, rows, factor),
        in_specs=[WHOLE] * 5,
        out_specs=[WHOLE] * 2,
        out_shape=[
            jax.ShapeDtypeStruct((size, group_count, taps), jnp.float32),
            jax.ShapeDtypeStruct((rows, local_width), jnp.float32),
        ],
        compiler_params=params,
        cost_estimate=cost,
        name="first",
    )(sums, late_tiles, even_kept, odd_kept, first)
    filter_grad = jnp.sum(lax.all_to_all(partial, "ctx", 0, 0), axis=0)

    gated, key_grad, value_grad = pl.pallas_call(
        late_kernel,
        in_specs=[WHOLE] * 7 + [anywhere] * 3,
        out_specs=[anywhere] * 3,
        out_shape=[out_shape] * 3,
        input_output_aliases={7: 0, 8: 1, 9: 2},
        scratch_shapes=out_scratch,
        compiler_params=params,
        cost_estimate=cost,
        name="late",
    )(late_tiles, late, far, last, query, keys, values, gated, key_grad, value_grad)
    return (gated, key_grad, value_grad, filter_grad)


def solution(mesh):
    in_specs = (P("ctx", "grp"), P("ctx", "grp"), P("ctx", "grp"), P("ctx", "grp"), P("grp", None))
    out_specs = (P("ctx", "grp"), P("ctx", "grp"), P("ctx", "grp"), P("grp", None))
    return jax.shard_map(shards, mesh=mesh, in_specs=in_specs, out_specs=out_specs, check_vma=False)
```

time: 48 us -> 50.5 us (1.052)
  Pallas kernels: 8.47 us -> 11 us
  waiting for transfers between devices: 15.8 us -> 14.2 us
  local copies, waits for them, and re-layouts: 0.69 us -> 2.22 us
    pallas_call x3, Pallas kernels: 6.23 us -> 8.68 us  [the longest x1 3.78 us: shards(): pl.pallas_call(functools.partial(ready_kernel, rows), in_specs=[WHOLE] *...]
    ppermute x5, waiting for transfers between devices: 15.8 us -> 14.2 us  [moved(): lax.ppermute(block, axis, [pair for pair in route if 0 <= pair[1] < size])]
    unnamed x14 -> x12, local copies, waits for them, and re-layouts: 0.69 us -> 2.22 us
    reduce_sum x1, other arithmetic: 1.55 us -> 0.62 us  [shards(): filter_grad = jnp.sum(lax.all_to_all(partial, 'ctx', 0, 0), axis=0)]
    select_n x1, other arithmetic: 1.91 us -> 2.74 us  [shards(): odd_kept = jnp.where(odd, prod, grad)]
  transfers between devices with their start and end apart: 6 -> 6, of which waited for: 3 -> 2; matrix products, arithmetic and copies ran while one was open for 2% -> 2% of each run, Pallas kernels for 18% -> 22%
where the time goes in v5:
time: 50.5 us; the launch traced here: 50 us
  starting transfers between devices  17.7 us (35%)
  waiting for transfers between devices  14.2 us (28%)
  Pallas kernels  11 us (22%)
  other arithmetic  4.19 us (8%)
  local copies, waits for them, and re-layouts  2.22 us (4%)
  between operations  0.77 us (2%)
    ppermute x5, waiting for transfers between devices, moved(): lax.ppermute(block, axis, [pair for pair in route if 0 <= pair[1] < size])  14.2 us
    ppermute x5, starting transfers between devices, moved(): lax.ppermute(block, axis, [pair for pair in route if 0 <= pair[1] < size])  11.7 us
    all_to_all x1, starting transfers between devices, shards(): filter_grad = jnp.sum(lax.all_to_all(partial, 'ctx', 0, 0), axis=0)  6.01 us
    pallas_call x1, Pallas kernels, shards(): pl.pallas_call(functools.partial(ready_kernel, rows), in_specs=[WHOLE] *...  3.78 us
    select_n x1, other arithmetic, shards(): odd_kept = jnp.where(odd, prod, grad)  2.74 us
    pallas_call x1, Pallas kernels, shards(): pl.pallas_call(late_kernel, in_specs=[WHOLE] * 7 + [anywhere] * 3, out_sp...  2.47 us
    pallas_call x1, Pallas kernels, shards(): pl.pallas_call(functools.partial(first_kernel, rows, factor), in_specs=[W...  2.43 us
    pallas_call x1, Pallas kernels, shards(): pl.pallas_call(functools.partial(tiles_kernel, rows, reach), grid=(group_...  2.28 us
  transfers between devices with their start and end apart: 6, of which 2 were waited for; matrix products, arithmetic and copies ran while one was open for 2% of the time, Pallas kernels for 22%

profile of v5, /device:TPU:0, one launch (start us, length us, event | category | flops | bytes accessed | tf_op | source)
XLA Modules:
  0.0 50.0 jit_solution(4389249462076495623)
XLA Ops:
  0.6 2.7 %broadcast_select_fusion = (bf16[128,2048]{1,0:T(8,128)(2,1)}, bf16[128,2048]{1,0:T(8,128)(2,1)S(1)}, bf16[128,2048]{1,0:T(8,128)(2,1)S(1)}) fusion(pred[]{:T(512)S(6)} %eq.5, bf16[128,2048]{1,0:T(8,128)(2,1)} %values_ref.3, bf16[128,2048]{1,0:T(8,128)(2,1)} %keys_ref.3, bf16[128,2048]{1,0:T(8,128)(2,1)} %query_ref.3, bf16[128,2048]{1,0:T(8,128)(2,1)} %param.8), kind=kLoop, calls=%fused_computation.2 | loop fusion | flops 2359296 | bytes 3670017 | tf_op jit(solution)/shard_map/jit(_where)/select_n | solution.py:215
  3.4 0.7 %collective-permute-start = (bf16[128,2048]{1,0:T(8,128)(2,1)}, bf16[128,2048]{1,0:T(8,128)(2,1)S(1)}, u32[]{:S(2)}, u32[]{:S(2)}) collective-permute-start(bf16[128,2048]{1,0:T(8,128)(2,1)} %get-tuple-element.30.odd_ref), channel_id=1, source_target_pairs={{4,8},{8,4},{12,16},{16,12},{20,24},{24,20},{5,9},{9,5},{13,17},{1... | collective-permute-start | bytes 1572872 | tf_op jit(solution)/shard_map/ppermute | solution.py:20
  4.1 0.0 copy-start.5
  4.1 0.1 broadcast_select_fusion.1.even_ref
  4.1 0.0 copy-start
  4.2 0.0 copy-start.1
  4.2 0.0 copy-start.2
  4.2 7.7 %collective-permute-start.1 = (bf16[128,2048]{1,0:T(8,128)(2,1)S(1)}, bf16[128,2048]{1,0:T(8,128)(2,1)S(1)}, u32[]{:S(2)}, u32[]{:S(2)}) collective-permute-start(bf16[128,2048]{1,0:T(8,128)(2,1)S(1)} %broadcast_select_fusion.1.even_ref), channel_id=1, source_target_pairs={{0,8},{8,16},{12,4},{16,24},{20,12},{28,20},{1,9},{9,17},{13,5},{1... | collective-permute-start | bytes 1572872 | tf_op jit(solution)/shard_map/ppermute | solution.py:20
  11.9 0.8 %slice_select_fusion = (bf16[128,1024]{1,0:T(8,128)(2,1)S(1)}, bf16[128,1024]{1,0:T(8,128)(2,1)}) fusion(bf16[128,2048]{1,0:T(8,128)(2,1)S(1)} %get-tuple-element.31, bf16[128,2048]{1,0:T(8,128)(2,1)S(1)} %get-tuple-element.32, pred[]{:T(512)S(6)} %eq.5), kind=kLoop, calls=%fused_computation.4 | loop fusion | flops 262144 | bytes 1572865 | tf_op jit(solution)/shard_map/jit(_where)/select_n | solution.py:219
  12.6 0.0 collective-permute-start.2
  12.6 1.3 %collective-permute-start.3 = (bf16[128,2048]{1,0:T(8,128)(2,1)}, bf16[128,2048]{1,0:T(8,128)(2,1)}, u32[]{:S(2)}, u32[]{:S(2)}) collective-permute-start(bf16[128,2048]{1,0:T(8,128)(2,1)} %get-tuple-element.30.odd_ref), channel_id=1, source_target_pairs={{4,12},{8,0},{12,20},{16,8},{20,28},{24,16},{5,13},{9,1},{13,21},{... | collective-permute-start | bytes 1572872 | tf_op jit(solution)/shard_map/ppermute | solution.py:20
  13.9 2.3 %tiles.1 = (bf16[16,128,384]{2,1,0:T(8,128)(2,1)S(1)}, bf16[16,128,384]{2,1,0:T(8,128)(2,1)S(1)}) custom-call(bf16[16,384]{1,0:T(8,128)(2,1)S(1)} %copy-done.5), custom_call_target="tpu_custom_call" | custom-call | flops 500000000 | bytes 8000000 | tf_op jit(solution)/shard_map/tiles/pallas_call | solution.py:228
  16.2 0.0 collective-permute-done.diagonal_ref
  16.2 6.5 %collective-permute-done.1.two_ref = bf16[128,2048]{1,0:T(8,128)(2,1)S(1)} collective-permute-done((bf16[128,2048]{1,0:T(8,128)(2,1)S(1)}, bf16[128,2048]{1,0:T(8,128)(2,1)S(1)}, u32[]{:S(2)}, u32[]{:S(2)}) %collective-permute-start.1) | collective-permute-done | bytes 524320 | tf_op jit(solution)/shard_map/ppermute | solution.py:20
  22.7 3.8 %ready.1 = (f32[16,384]{1,0:T(8,128)S(1)}, bf16[128,2048]{1,0:T(8,128)(2,1)}, bf16[128,2048]{1,0:T(8,128)(2,1)}, bf16[128,2048]{1,0:T(8,128)(2,1)}) custom-call(bf16[16,128,384]{2,1,0:T(8,128)(2,1)S(1)} %get-tuple-element.18.tile_ref, bf16[128,2048]{1,0:T(8,128)(2,1)S(1)} %broadcast_select_fusion.1.even_ref, bf16[128,2048]{1,0:T(8,128)(2,1)} %get-tuple-element.30.odd_ref, ...), custom_call_target="tpu_custom_call" | custom-call | flops 500000000 | bytes 8000000 | tf_op jit(solution)/shard_map/ready/pallas_call | solution.py:242
  26.5 0.0 collective-permute-done.2.first_ref
  26.5 2.4 %first.1 = (f32[8,16,384]{2,1,0:T(8,128)}, f32[128,2048]{1,0:T(8,128)S(1)}) custom-call(f32[16,384]{1,0:T(8,128)S(1)} %get-tuple-element.20.sum_ref, bf16[16,128,384]{2,1,0:T(8,128)(2,1)S(1)} %get-tuple-element.17.tile_ref, bf16[128,2048]{1,0:T(8,128)(2,1)S(1)} %broadcast_select_fusion.1.even_ref, bf16[128,2048]{1,0:T(8,128)(2,1)} %get-tuple-element.30.odd_ref, ...), custom_call_target="tpu_custom_call" | custom-call | flops 500000000 | bytes 8000000 | tf_op jit(solution)/shard_map/first/pallas_call | solution.py:254
  29.0 1.0 %copy-done.3 = f32[128,2048]{1,0:T(8,128)} copy-done((f32[128,2048]{1,0:T(8,128)}, f32[128,2048]{1,0:T(8,128)S(1)}, u32[]{:S(2)}) %copy-start.3) | copy-done | bytes 1048600
  29.9 6.0 %all-to-all-start = ((f32[8,16,384]{2,1,0:T(8,128)}), f32[8,16,384]{2,1,0:T(8,128)S(1)}, u32[]{:S(2)}, u32[]{:S(2)}) async-start(f32[8,16,384]{2,1,0:T(8,128)} %get-tuple-element.29), calls=%async_computation | async-start | bytes 393216 | tf_op jit(solution)/shard_map/all_to_all | solution.py:266
  36.0 2.0 %collective-permute-start.4 = (bf16[128,1024]{1,0:T(8,128)(2,1)}, bf16[128,1024]{1,0:T(8,128)(2,1)S(1)}, u32[]{:S(2)}, u32[]{:S(2)}) collective-permute-start(bf16[128,1024]{1,0:T(8,128)(2,1)} %get-tuple-element.22), channel_id=1, source_target_pairs={{0,4},{4,0},{8,12},{12,8},{16,20},{20,16},{24,28},{28,24},{1,5},{5... | collective-permute-start | bytes 786440 | tf_op jit(solution)/shard_map/ppermute | solution.py:20
  38.0 7.7 %collective-permute-done.4.last_ref = bf16[128,1024]{1,0:T(8,128)(2,1)S(1)} collective-permute-done((bf16[128,1024]{1,0:T(8,128)(2,1)}, bf16[128,1024]{1,0:T(8,128)(2,1)S(1)}, u32[]{:S(2)}, u32[]{:S(2)}) %collective-permute-start.4) | collective-permute-done | bytes 262176 | tf_op jit(solution)/shard_map/ppermute | solution.py:20
  45.7 1.2 %copy-done.4 = f32[128,2048]{1,0:T(8,128)S(1)} copy-done((f32[128,2048]{1,0:T(8,128)S(1)}, f32[128,2048]{1,0:T(8,128)}, u32[]{:S(2)}) %copy-start.4) | copy-done | bytes 1048600
  46.9 2.5 %late.1 = (bf16[128,2048]{1,0:T(8,128)(2,1)}, bf16[128,2048]{1,0:T(8,128)(2,1)}, bf16[128,2048]{1,0:T(8,128)(2,1)}) custom-call(bf16[16,128,384]{2,1,0:T(8,128)(2,1)S(1)} %get-tuple-element.17.tile_ref, f32[128,2048]{1,0:T(8,128)S(1)} %copy-done.4, ...), custom_call_target="tpu_custom_call", output_to_operand_aliasing={{0}: (7, {}), {1}: (8, {}), {2}: (9, {})} | custom-call | flops 500000000 | bytes 8000000 | tf_op jit(solution)/shard_map/late/pallas_call | solution.py:268
  49.4 0.6 %reduce_sum.9 = f32[16,384]{1,0:T(8,128)} reduce(f32[8,16,384]{2,1,0:T(8,128)S(1)} %all-to-all-done, f32[]{:T(128)} %constant.21.clone.1), dimensions={0}, to_apply=%region_0.1 | reduce | flops 43008 | bytes 221188 | tf_op jit(solution)/shard_map/reduce_sum | solution.py:266
  (8 shorter events, 0.0 us)
Async XLA Ops:
  3.4 12.9 %collective-permute-start = (bf16[128,2048]{1,0:T(8,128)(2,1)}, bf16[128,2048]{1,0:T(8,128)(2,1)S(1)}, u32[]{:S(2)}, u32[]{:S(2)}) collective-permute-start(bf16[128,2048]{1,0:T(8,128)(2,1)} %get-tuple-element.30.odd_ref), channel_id=1, source_target_pairs={{4,8},{8,4},{12,16},{16,12},{20,24},{24,20},{5,9},{9,5},{13,17},{1... | collective-permute-start | bytes 1572872 | tf_op jit(solution)/shard_map/ppermute | solution.py:20
  4.1 9.9 %copy-start.5 = (bf16[16,384]{1,0:T(8,128)(2,1)S(1)}, bf16[16,384]{1,0:T(8,128)(2,1)}, u32[]{:S(2)}) copy-start(bf16[16,384]{1,0:T(8,128)(2,1)} %taps_ref.1) | copy-start | bytes 36868
  4.1 18.6 %copy-start = (bf16[128,2048]{1,0:T(8,128)(2,1)S(1)}, bf16[128,2048]{1,0:T(8,128)(2,1)}, u32[]{:S(2)}) copy-start(bf16[128,2048]{1,0:T(8,128)(2,1)} %values_ref.3) | copy-start | bytes 1572868
  4.2 18.6 %copy-start.1 = (bf16[128,2048]{1,0:T(8,128)(2,1)S(1)}, bf16[128,2048]{1,0:T(8,128)(2,1)}, u32[]{:S(2)}) copy-start(bf16[128,2048]{1,0:T(8,128)(2,1)} %keys_ref.3) | copy-start | bytes 1572868
  4.2 18.6 %copy-start.2 = (bf16[128,2048]{1,0:T(8,128)(2,1)S(1)}, bf16[128,2048]{1,0:T(8,128)(2,1)}, u32[]{:S(2)}) copy-start(bf16[128,2048]{1,0:T(8,128)(2,1)} %query_ref.3) | copy-start | bytes 1572868
  4.2 18.5 %collective-permute-start.1 = (bf16[128,2048]{1,0:T(8,128)(2,1)S(1)}, bf16[128,2048]{1,0:T(8,128)(2,1)S(1)}, u32[]{:S(2)}, u32[]{:S(2)}) collective-permute-start(bf16[128,2048]{1,0:T(8,128)(2,1)S(1)} %broadcast_select_fusion.1.even_ref), channel_id=1, source_target_pairs={{0,8},{8,16},{12,4},{16,24},{20,12},{28,20},{1,9},{9,17},{13,5},{1... | collective-permute-start | bytes 1572872 | tf_op jit(solution)/shard_map/ppermute | solution.py:20
  12.6 13.9 %collective-permute-start.2 = (bf16[128,1024]{1,0:T(8,128)(2,1)S(1)}, bf16[128,1024]{1,0:T(8,128)(2,1)S(1)}, u32[]{:S(2)}, u32[]{:S(2)}) collective-permute-start(bf16[128,1024]{1,0:T(8,128)(2,1)S(1)} %get-tuple-element.33), channel_id=1, source_target_pairs={{0,4},{4,0},{8,12},{12,8},{16,20},{20,16},{24,28},{28,24},{1,5},{5... | collective-permute-start | bytes 786440 | tf_op jit(solution)/shard_map/ppermute | solution.py:20
  12.6 25.3 %collective-permute-start.3 = (bf16[128,2048]{1,0:T(8,128)(2,1)}, bf16[128,2048]{1,0:T(8,128)(2,1)}, u32[]{:S(2)}, u32[]{:S(2)}) collective-permute-start(bf16[128,2048]{1,0:T(8,128)(2,1)} %get-tuple-element.30.odd_ref), channel_id=1, source_target_pairs={{4,12},{8,0},{12,20},{16,8},{20,28},{24,16},{5,13},{9,1},{13,21},{... | collective-permute-start | bytes 1572872 | tf_op jit(solution)/shard_map/ppermute | solution.py:20
  29.0 1.0 %copy-start.3 = (f32[128,2048]{1,0:T(8,128)}, f32[128,2048]{1,0:T(8,128)S(1)}, u32[]{:S(2)}) copy-start(f32[128,2048]{1,0:T(8,128)S(1)} %get-tuple-element.21.late_ref) | copy-start | bytes 3145732
  29.9 19.4 %all-to-all-start = ((f32[8,16,384]{2,1,0:T(8,128)}), f32[8,16,384]{2,1,0:T(8,128)S(1)}, u32[]{:S(2)}, u32[]{:S(2)}) async-start(f32[8,16,384]{2,1,0:T(8,128)} %get-tuple-element.29), calls=%async_computation | async-start | bytes 393216 | tf_op jit(solution)/shard_map/all_to_all | solution.py:266
  36.0 9.7 %collective-permute-start.4 = (bf16[128,1024]{1,0:T(8,128)(2,1)}, bf16[128,1024]{1,0:T(8,128)(2,1)S(1)}, u32[]{:S(2)}, u32[]{:S(2)}) collective-permute-start(bf16[128,1024]{1,0:T(8,128)(2,1)} %get-tuple-element.22), channel_id=1, source_target_pairs={{0,4},{4,0},{8,12},{12,8},{16,20},{20,16},{24,28},{28,24},{1,5},{5... | collective-permute-start | bytes 786440 | tf_op jit(solution)/shard_map/ppermute | solution.py:20
  45.7 1.2 %copy-start.4 = (f32[128,2048]{1,0:T(8,128)S(1)}, f32[128,2048]{1,0:T(8,128)}, u32[]{:S(2)}) copy-start(f32[128,2048]{1,0:T(8,128)} %copy-done.3) | copy-start | bytes 3145732

commit v6 on v5

--- a/solution.py
+++ b/solution.py
@@ -12,6 +12,10 @@
 PARTS = 4
 VMEM_LIMIT = 16 * 1024 * 1024
 WHOLE = pl.BlockSpec(memory_space=pltpu.VMEM)
+
+
+def in_vmem(*arrays):
+    return [pltpu.with_memory_space_constraint(array, pltpu.VMEM) for array in arrays]
 
 
 def moved(block, axis, distances):
@@ -208,7 +212,8 @@
     odd = lax.axis_index("ctx") % 2 == 1
     half = local_width // 2
     params = pltpu.CompilerParams(vmem_limit_bytes=VMEM_LIMIT)
-    cost = pl.CostEstimate(flops=5 * 10**8, bytes_accessed=8 * 10**6, transcendentals=0)
+    small = pl.CostEstimate(flops=10**6, bytes_accessed=10**5, transcendentals=0)
+    large = pl.CostEstimate(flops=10**11, bytes_accessed=10**8, transcendentals=0)
 
     prod = (keys.astype(jnp.float32) * values.astype(jnp.float32)).astype(jnp.bfloat16)
     grad = (cotangent.astype(jnp.float32) * query.astype(jnp.float32)).astype(jnp.bfloat16)
@@ -222,17 +227,13 @@
     rest, diagonal = lax.optimization_barrier((rest, diagonal))
     last = moved(rest, "ctx", (1, -1))
 
-    step = min(group_count, 8)
-    tile_shape = jax.ShapeDtypeStruct((group_count, rows, taps), jnp.bfloat16)
-    tile_spec = pl.BlockSpec((step, rows, taps), lambda i: (i, 0, 0))
     ready_tiles, late_tiles = pl.pallas_call(
         functools.partial(tiles_kernel, rows, reach),
-        grid=(group_count // step,),
-        in_specs=[pl.BlockSpec((step, taps), lambda i: (i, 0))],
-        out_specs=[tile_spec, tile_spec],
-        out_shape=[tile_shape, tile_shape],
-        compiler_params=params,
-        cost_estimate=cost,
+        in_specs=[WHOLE],
+        out_specs=[WHOLE] * 2,
+        out_shape=[pltpu.VMEM((group_count, rows, taps), jnp.bfloat16)] * 2,
+        compiler_params=params,
+        cost_estimate=small,
         name="tiles",
     )(filter_taps)
 
@@ -243,12 +244,12 @@
         functools.partial(ready_kernel, rows),
         in_specs=[WHOLE] * 8,
         out_specs=[WHOLE] + [anywhere] * 3,
-        out_shape=[jax.ShapeDtypeStruct((group_count, taps), jnp.float32)] + [out_shape] * 3,
+        out_shape=[pltpu.VMEM((group_count, taps), jnp.float32)] + [out_shape] * 3,
         scratch_shapes=out_scratch,
         compiler_params=params,
-        cost_estimate=cost,
+        cost_estimate=small,
         name="ready",
-    )(ready_tiles, even_kept, odd_kept, diagonal, two, query, keys, values)
+    )(*in_vmem(ready_tiles, even_kept, odd_kept, diagonal, two, query, keys, values))
 
     factor = 1.0 / math.sqrt(rows * size * group_width)
     partial, late = pl.pallas_call(
@@ -257,12 +258,12 @@
         out_specs=[WHOLE] * 2,
         out_shape=[
             jax.ShapeDtypeStruct((size, group_count, taps), jnp.float32),
-            jax.ShapeDtypeStruct((rows, local_width), jnp.float32),
+            pltpu.VMEM((rows, local_width), jnp.float32),
         ],
         compiler_params=params,
-        cost_estimate=cost,
+        cost_estimate=small,
         name="first",
-    )(sums, late_tiles, even_kept, odd_kept, first)
+    )(*in_vmem(sums, late_tiles, even_kept, odd_kept, first))
     filter_grad = jnp.sum(lax.all_to_all(partial, "ctx", 0, 0), axis=0)
 
     gated, key_grad, value_grad = pl.pallas_call(
@@ -273,9 +274,9 @@
         input_output_aliases={7: 0, 8: 1, 9: 2},
         scratch_shapes=out_scratch,
         compiler_params=params,
-        cost_estimate=cost,
+        cost_estimate=large,
         name="late",
-    )(late_tiles, late, far, last, query, keys, values, gated, key_grad, value_grad)
+    )(*in_vmem(late_tiles, late, far, last, query, keys, values), gated, key_grad, value_grad)
     return (gated, key_grad, value_grad, filter_grad)
 
 

time: 50.5 us -> 44.4 us (0.88)
  waiting for transfers between devices: 14.2 us -> 4 us
  starting transfers between devices: 17.7 us -> 24.7 us
  Pallas kernels: 11 us -> 8.85 us
  local copies, waits for them, and re-layouts: 2.22 us -> 1.43 us
    ppermute x5, waiting for transfers between devices: 14.2 us -> 0.01 us  [moved(): lax.ppermute(block, axis, [pair for pair in route if 0 <= pair[1] < size])]
    ppermute x5, starting transfers between devices: 11.7 us -> 19.7 us  [moved(): lax.ppermute(block, axis, [pair for pair in route if 0 <= pair[1] < size])]
    all_to_all x1, waiting for transfers between devices: 0.01 us -> 3.99 us  [shards(): filter_grad = jnp.sum(lax.all_to_all(partial, 'ctx', 0, 0), axis=0)]
    pallas_call x1, Pallas kernels: 3.78 us -> 2.74 us  [shards(): pl.pallas_call(functools.partial(ready_kernel, rows), in_specs=[WHOLE] *...]
    all_to_all x1, starting transfers between devices: 6.01 us -> 4.98 us  [shards(): filter_grad = jnp.sum(lax.all_to_all(partial, 'ctx', 0, 0), axis=0)]
    pallas_call x1, Pallas kernels: 2.43 us -> 1.42 us  [shards(): pl.pallas_call(functools.partial(first_kernel, rows, factor), in_specs=[W...]
    reduce_sum x1, other arithmetic: 0.62 us -> 1.55 us  [shards(): filter_grad = jnp.sum(lax.all_to_all(partial, 'ctx', 0, 0), axis=0)]
    select_n x1, other arithmetic: 2.74 us -> 1.91 us  [shards(): odd_kept = jnp.where(odd, prod, grad)]
  transfers between devices with their start and end apart: 6 -> 6, of which waited for: 2 -> 1; matrix products, arithmetic and copies ran while one was open for 2% -> 2% of each run, Pallas kernels for 22% -> 20%
where the time goes in v6:
time: 44.4 us; the launch traced here: 44 us
  starting transfers between devices  24.7 us (56%)
  Pallas kernels  8.85 us (20%)
  other arithmetic  4.29 us (10%)
  waiting for transfers between devices  4 us (9%)
  local copies, waits for them, and re-layouts  1.43 us (3%)
  between operations  0.82 us (2%)
    ppermute x5, starting transfers between devices, moved(): lax.ppermute(block, axis, [pair for pair in route if 0 <= pair[1] < size])  19.7 us
    all_to_all x1, starting transfers between devices, shards(): filter_grad = jnp.sum(lax.all_to_all(partial, 'ctx', 0, 0), axis=0)  4.98 us
    all_to_all x1, waiting for transfers between devices, shards(): filter_grad = jnp.sum(lax.all_to_all(partial, 'ctx', 0, 0), axis=0)  3.99 us
    pallas_call x1, Pallas kernels, shards(): pl.pallas_call(functools.partial(ready_kernel, rows), in_specs=[WHOLE] *...  2.74 us
    pallas_call x1, Pallas kernels, shards(): pl.pallas_call(late_kernel, in_specs=[WHOLE] * 7 + [anywhere] * 3, out_sp...  2.47 us
    pallas_call x1, Pallas kernels, shards(): pl.pallas_call(functools.partial(tiles_kernel, rows, reach), in_specs=[WH...  2.22 us
    select_n x1, other arithmetic, shards(): odd_kept = jnp.where(odd, prod, grad)  1.91 us
    reduce_sum x1, other arithmetic, shards(): filter_grad = jnp.sum(lax.all_to_all(partial, 'ctx', 0, 0), axis=0)  1.55 us
  transfers between devices with their start and end apart: 6, of which 1 were waited for; matrix products, arithmetic and copies ran while one was open for 2% of the time, Pallas kernels for 20%

profile of v6, /device:TPU:0, one launch (start us, length us, event | category | flops | bytes accessed | tf_op | source)
XLA Modules:
  0.0 44.0 jit_solution(16406342657935671526)
XLA Ops:
  0.6 1.9 %broadcast_select_fusion = (bf16[128,2048]{1,0:T(8,128)(2,1)S(1)}, bf16[128,2048]{1,0:T(8,128)(2,1)S(1)}, bf16[128,2048]{1,0:T(8,128)(2,1)S(1)}) fusion(pred[]{:T(512)S(6)} %eq.5, bf16[128,2048]{1,0:T(8,128)(2,1)} %values_ref.3, bf16[128,2048]{1,0:T(8,128)(2,1)} %keys_ref.3, bf16[128,2048]{1,0:T(8,128)(2,1)} %query_ref.3, bf16[128,2048]{1,0:T(8,128)(2,1)} %param.8), kind=kLoop, calls=%fused_computation.2 | loop fusion | flops 2359296 | bytes 3670017 | tf_op jit(solution)/shard_map/jit(_where)/select_n | solution.py:220
  2.6 0.7 %collective-permute-start = (bf16[128,2048]{1,0:T(8,128)(2,1)S(1)}, bf16[128,2048]{1,0:T(8,128)(2,1)S(1)}, u32[]{:S(2)}, u32[]{:S(2)}) collective-permute-start(bf16[128,2048]{1,0:T(8,128)(2,1)S(1)} %get-tuple-element.30.odd_ref), channel_id=1, source_target_pairs={{4,8},{8,4},{12,16},{16,12},{20,24},{24,20},{5,9},{9,5},{13,17},{1... | collective-permute-start | bytes 1572872 | tf_op jit(solution)/shard_map/ppermute | solution.py:24
  3.3 0.0 copy-start.5
  3.3 0.0 copy-start
  3.3 0.0 copy-start.1
  3.3 0.0 copy-start.2
  3.3 0.1 broadcast_select_fusion.1.even_ref
  3.4 7.7 %collective-permute-start.1 = (bf16[128,2048]{1,0:T(8,128)(2,1)S(1)}, bf16[128,2048]{1,0:T(8,128)(2,1)S(1)}, u32[]{:S(2)}, u32[]{:S(2)}) collective-permute-start(bf16[128,2048]{1,0:T(8,128)(2,1)S(1)} %broadcast_select_fusion.1.even_ref), channel_id=1, source_target_pairs={{0,8},{8,16},{12,4},{16,24},{20,12},{28,20},{1,9},{9,17},{13,5},{1... | collective-permute-start | bytes 1572872 | tf_op jit(solution)/shard_map/ppermute | solution.py:24
  11.1 1.3 %collective-permute-start.3 = (bf16[128,2048]{1,0:T(8,128)(2,1)S(1)}, bf16[128,2048]{1,0:T(8,128)(2,1)}, u32[]{:S(2)}, u32[]{:S(2)}) collective-permute-start(bf16[128,2048]{1,0:T(8,128)(2,1)S(1)} %get-tuple-element.30.odd_ref), channel_id=1, source_target_pairs={{4,12},{8,0},{12,20},{16,8},{20,28},{24,16},{5,13},{9,1},{13,21},{... | collective-permute-start | bytes 1572872 | tf_op jit(solution)/shard_map/ppermute | solution.py:24
  12.4 0.8 %slice_select_fusion = (bf16[128,1024]{1,0:T(8,128)(2,1)S(1)}, bf16[128,1024]{1,0:T(8,128)(2,1)}) fusion(bf16[128,2048]{1,0:T(8,128)(2,1)S(1)} %get-tuple-element.31, bf16[128,2048]{1,0:T(8,128)(2,1)S(1)} %get-tuple-element.32, pred[]{:T(512)S(6)} %eq.5), kind=kLoop, calls=%fused_computation.4 | loop fusion | flops 262144 | bytes 1572865 | tf_op jit(solution)/shard_map/jit(_where)/select_n | solution.py:224
  13.1 3.5 %collective-permute-start.2 = (bf16[128,1024]{1,0:T(8,128)(2,1)S(1)}, bf16[128,1024]{1,0:T(8,128)(2,1)S(1)}, u32[]{:S(2)}, u32[]{:S(2)}) collective-permute-start(bf16[128,1024]{1,0:T(8,128)(2,1)S(1)} %get-tuple-element.33), channel_id=1, source_target_pairs={{0,4},{4,0},{8,12},{12,8},{16,20},{20,16},{24,28},{28,24},{1,5},{5... | collective-permute-start | bytes 786440 | tf_op jit(solution)/shard_map/ppermute | solution.py:24
  16.7 0.0 collective-permute-done.diagonal_ref
  16.7 6.5 %collective-permute-start.4 = (bf16[128,1024]{1,0:T(8,128)(2,1)}, bf16[128,1024]{1,0:T(8,128)(2,1)S(1)}, u32[]{:S(2)}, u32[]{:S(2)}) collective-permute-start(bf16[128,1024]{1,0:T(8,128)(2,1)} %get-tuple-element.22), channel_id=1, source_target_pairs={{0,4},{4,0},{8,12},{12,8},{16,20},{20,16},{24,28},{28,24},{1,5},{5... | collective-permute-start | bytes 786440 | tf_op jit(solution)/shard_map/ppermute | solution.py:24
  23.1 2.2 %tiles.1 = (bf16[16,128,384]{2,1,0:T(8,128)(2,1)S(1)}, bf16[16,128,384]{2,1,0:T(8,128)(2,1)S(1)}) custom-call(bf16[16,384]{1,0:T(8,128)(2,1)S(1)} %copy-done.5), custom_call_target="tpu_custom_call" | custom-call | flops 1000000 | bytes 100000 | tf_op jit(solution)/shard_map/tiles/pallas_call | solution.py:230
  25.4 0.0 collective-permute-done.1.two_ref
  25.4 2.7 %ready.1 = (f32[16,384]{1,0:T(8,128)S(1)}, bf16[128,2048]{1,0:T(8,128)(2,1)}, bf16[128,2048]{1,0:T(8,128)(2,1)}, bf16[128,2048]{1,0:T(8,128)(2,1)}) custom-call(bf16[16,128,384]{2,1,0:T(8,128)(2,1)S(1)} %get-tuple-element.18.tile_ref, bf16[128,2048]{1,0:T(8,128)(2,1)S(1)} %broadcast_select_fusion.1.even_ref, ...), custom_call_target="tpu_custom_call" | custom-call | flops 1000000 | bytes 100000 | tf_op jit(solution)/shard_map/ready/pallas_call | solution.py:243
  28.2 0.0 collective-permute-done.2.first_ref
  28.2 1.4 %first.1 = (f32[8,16,384]{2,1,0:T(8,128)}, f32[128,2048]{1,0:T(8,128)S(1)}) custom-call(f32[16,384]{1,0:T(8,128)S(1)} %get-tuple-element.20.sum_ref, bf16[16,128,384]{2,1,0:T(8,128)(2,1)S(1)} %get-tuple-element.17.tile_ref, bf16[128,2048]{1,0:T(8,128)(2,1)S(1)} %broadcast_select_fusion.1.even_ref, bf16[128,2048]{1,0:T(8,128)(2,1)S(1)} %get-tuple-element.30.odd_ref, ...), custom_call_target="tpu_custom_call" | custom-call | flops 1000000 | bytes 100000 | tf_op jit(solution)/shard_map/first/pallas_call | solution.py:255
  29.6 5.0 %all-to-all-start = ((f32[8,16,384]{2,1,0:T(8,128)}), f32[8,16,384]{2,1,0:T(8,128)}, u32[]{:S(2)}, u32[]{:S(2)}) async-start(f32[8,16,384]{2,1,0:T(8,128)} %get-tuple-element.29), calls=%async_computation | async-start | bytes 393216 | tf_op jit(solution)/shard_map/all_to_all | solution.py:267
  34.6 0.0 collective-permute-done.4.last_ref
  34.6 1.4 %copy-done.4 = bf16[16,128,384]{2,1,0:T(8,128)(2,1)S(1)} copy-done((bf16[16,128,384]{2,1,0:T(8,128)(2,1)S(1)}, bf16[16,128,384]{2,1,0:T(8,128)(2,1)}, u32[]{:S(2)}) %copy-start.4) | copy-done | bytes 1572888
  36.0 2.5 %late.1 = (bf16[128,2048]{1,0:T(8,128)(2,1)}, bf16[128,2048]{1,0:T(8,128)(2,1)}, bf16[128,2048]{1,0:T(8,128)(2,1)}) custom-call(bf16[16,128,384]{2,1,0:T(8,128)(2,1)S(1)} %copy-done.4, f32[128,2048]{1,0:T(8,128)S(1)} %get-tuple-element.21.late_ref, ...), custom_call_target="tpu_custom_call", output_to_operand_aliasing={{0}: (7, {}), {1}: (8, {}), {2}: (9, {})} | custom-call | flops 99999997952 | bytes 100000000 | tf_op jit(solution)/shard_map/late/pallas_call | solution.py:269
  38.5 4.0 %all-to-all-done = f32[8,16,384]{2,1,0:T(8,128)} async-done(((f32[8,16,384]{2,1,0:T(8,128)}), f32[8,16,384]{2,1,0:T(8,128)}, u32[]{:S(2)}, u32[]{:S(2)}) %all-to-all-start) | async-done | bytes 196640 | tf_op jit(solution)/shard_map/all_to_all | solution.py:267
  42.5 1.6 %reduce_sum.9 = f32[16,384]{1,0:T(8,128)} reduce(f32[8,16,384]{2,1,0:T(8,128)} %all-to-all-done, f32[]{:T(128)} %constant.21.clone.1), dimensions={0}, to_apply=%region_0.1 | reduce | flops 43008 | bytes 221188 | tf_op jit(solution)/shard_map/reduce_sum | solution.py:267
  (8 shorter events, 0.0 us)
Async XLA Ops:
  2.6 14.1 %collective-permute-start = (bf16[128,2048]{1,0:T(8,128)(2,1)S(1)}, bf16[128,2048]{1,0:T(8,128)(2,1)S(1)}, u32[]{:S(2)}, u32[]{:S(2)}) collective-permute-start(bf16[128,2048]{1,0:T(8,128)(2,1)S(1)} %get-tuple-element.30.odd_ref), channel_id=1, source_target_pairs={{4,8},{8,4},{12,16},{16,12},{20,24},{24,20},{5,9},{9,5},{13,17},{1... | collective-permute-start | bytes 1572872 | tf_op jit(solution)/shard_map/ppermute | solution.py:24
  3.3 19.9 %copy-start.5 = (bf16[16,384]{1,0:T(8,128)(2,1)S(1)}, bf16[16,384]{1,0:T(8,128)(2,1)}, u32[]{:S(2)}) copy-start(bf16[16,384]{1,0:T(8,128)(2,1)} %taps_ref.1) | copy-start | bytes 36868
  3.3 22.1 %copy-start = (bf16[128,2048]{1,0:T(8,128)(2,1)S(1)}, bf16[128,2048]{1,0:T(8,128)(2,1)}, u32[]{:S(2)}) copy-start(bf16[128,2048]{1,0:T(8,128)(2,1)} %values_ref.3) | copy-start | bytes 1572868
  3.3 22.1 %copy-start.1 = (bf16[128,2048]{1,0:T(8,128)(2,1)S(1)}, bf16[128,2048]{1,0:T(8,128)(2,1)}, u32[]{:S(2)}) copy-start(bf16[128,2048]{1,0:T(8,128)(2,1)} %keys_ref.3) | copy-start | bytes 1572868
  3.3 22.1 %copy-start.2 = (bf16[128,2048]{1,0:T(8,128)(2,1)S(1)}, bf16[128,2048]{1,0:T(8,128)(2,1)}, u32[]{:S(2)}) copy-start(bf16[128,2048]{1,0:T(8,128)(2,1)} %query_ref.3) | copy-start | bytes 1572868
  3.4 22.0 %collective-permute-start.1 = (bf16[128,2048]{1,0:T(8,128)(2,1)S(1)}, bf16[128,2048]{1,0:T(8,128)(2,1)S(1)}, u32[]{:S(2)}, u32[]{:S(2)}) collective-permute-start(bf16[128,2048]{1,0:T(8,128)(2,1)S(1)} %broadcast_select_fusion.1.even_ref), channel_id=1, source_target_pairs={{0,8},{8,16},{12,4},{16,24},{20,12},{28,20},{1,9},{9,17},{13,5},{1... | collective-permute-start | bytes 1572872 | tf_op jit(solution)/shard_map/ppermute | solution.py:24
  11.1 23.5 %collective-permute-start.3 = (bf16[128,2048]{1,0:T(8,128)(2,1)S(1)}, bf16[128,2048]{1,0:T(8,128)(2,1)}, u32[]{:S(2)}, u32[]{:S(2)}) collective-permute-start(bf16[128,2048]{1,0:T(8,128)(2,1)S(1)} %get-tuple-element.30.odd_ref), channel_id=1, source_target_pairs={{4,12},{8,0},{12,20},{16,8},{20,28},{24,16},{5,13},{9,1},{13,21},{... | collective-permute-start | bytes 1572872 | tf_op jit(solution)/shard_map/ppermute | solution.py:24
  13.1 15.0 %collective-permute-start.2 = (bf16[128,1024]{1,0:T(8,128)(2,1)S(1)}, bf16[128,1024]{1,0:T(8,128)(2,1)S(1)}, u32[]{:S(2)}, u32[]{:S(2)}) collective-permute-start(bf16[128,1024]{1,0:T(8,128)(2,1)S(1)} %get-tuple-element.33), channel_id=1, source_target_pairs={{0,4},{4,0},{8,12},{12,8},{16,20},{20,16},{24,28},{28,24},{1,5},{5... | collective-permute-start | bytes 786440 | tf_op jit(solution)/shard_map/ppermute | solution.py:24
  16.7 17.9 %collective-permute-start.4 = (bf16[128,1024]{1,0:T(8,128)(2,1)}, bf16[128,1024]{1,0:T(8,128)(2,1)S(1)}, u32[]{:S(2)}, u32[]{:S(2)}) collective-permute-start(bf16[128,1024]{1,0:T(8,128)(2,1)} %get-tuple-element.22), channel_id=1, source_target_pairs={{0,4},{4,0},{8,12},{12,8},{16,20},{20,16},{24,28},{28,24},{1,5},{5... | collective-permute-start | bytes 786440 | tf_op jit(solution)/shard_map/ppermute | solution.py:24
  25.4 2.8 %copy-start.3 = (bf16[16,128,384]{2,1,0:T(8,128)(2,1)}, bf16[16,128,384]{2,1,0:T(8,128)(2,1)S(1)}, u32[]{:S(2)}) copy-start(bf16[16,128,384]{2,1,0:T(8,128)(2,1)S(1)} %get-tuple-element.17.tile_ref) | copy-start | bytes 4718596
  29.6 12.9 %all-to-all-start = ((f32[8,16,384]{2,1,0:T(8,128)}), f32[8,16,384]{2,1,0:T(8,128)}, u32[]{:S(2)}, u32[]{:S(2)}) async-start(f32[8,16,384]{2,1,0:T(8,128)} %get-tuple-element.29), calls=%async_computation | async-start | bytes 393216 | tf_op jit(solution)/shard_map/all_to_all | solution.py:267
  34.6 1.4 %copy-start.4 = (bf16[16,128,384]{2,1,0:T(8,128)(2,1)S(1)}, bf16[16,128,384]{2,1,0:T(8,128)(2,1)}, u32[]{:S(2)}) copy-start(bf16[16,128,384]{2,1,0:T(8,128)(2,1)} %copy-done.3) | copy-start | bytes 4718596

commit v7 on v0

v7 whole, which is shorter than its diff:
```python
import functools
import math

import jax
import jax.numpy as jnp
from jax import lax
from jax.experimental import pallas as pl
from jax.experimental.pallas import tpu as pltpu
from jax.sharding import PartitionSpec as P

SUBLANES = 8
PARTS = 4
VMEM_LIMIT = 16 * 1024 * 1024
WHOLE = pl.BlockSpec(memory_space=pltpu.VMEM)
ANYWHERE = pl.BlockSpec(memory_space=pl.ANY)
DOT_ROWS = functools.partial(
    lax.dot_general,
    dimension_numbers=(((1,), (1,)), ((), ())),
    preferred_element_type=jnp.float32,
)
DOT = functools.partial(jnp.dot, preferred_element_type=jnp.float32)


def in_vmem(*arrays):
    return [pltpu.with_memory_space_constraint(array, pltpu.VMEM) for array in arrays]


def in_hbm(*arrays):
    return [pltpu.with_memory_space_constraint(array, pltpu.HBM) for array in arrays]


def moved(block, axis, distances):
    size = lax.axis_size(axis)
    route = [(i, i + distances[i % 2]) for i in range(size)]
    return lax.ppermute(block, axis, [pair for pair in route if 0 <= pair[1] < size])


def summed(pair_sum, axis, add, add_last):
    size = lax.axis_size(axis)
    if size & (size - 1):
        even = lax.axis_index(axis) % 2 == 0
        return lax.psum(jnp.where(even, pair_sum, 0.0), axis)
    stride = 2
    while stride < size:
        route = [(i, i ^ stride) for i in range(size)]
        arrived = lax.ppermute(pair_sum, axis, route)
        stride *= 2
        pair_sum = (add if stride < size else add_last)(pair_sum, arrived)
    return pair_sum


def is_odd():
    return lax.rem(lax.axis_index("ctx"), 2) == 1


def product(left, right):
    return (left.astype(jnp.float32) * right.astype(jnp.float32)).astype(jnp.bfloat16)


def scaled(value, factor):
    return (value * factor.astype(jnp.float32)).astype(jnp.bfloat16)


def columns_of(group, width):
    return slice(group * width, (group + 1) * width)


def launch(odd, moves, sems, used):
    copies = [(*move, sems.at[used + place]) for place, move in enumerate(moves)]
    for parity, source, target, sem in copies:
        @pl.when(odd if parity else jnp.logical_not(odd))
        def _():
            pltpu.make_async_copy(source, target, sem).start()
    return copies


def finish(odd, copies):
    for parity, source, target, sem in copies:
        @pl.when(odd if parity else jnp.logical_not(odd))
        def _():
            pltpu.make_async_copy(source, target, sem).wait()


def skewed_sum(outer, rows):
    width = outer.shape[1]
    total = outer[:SUBLANES]
    for start in range(SUBLANES, rows, SUBLANES):
        total = total + pltpu.roll(outer[start : start + SUBLANES], width - start, 1)
    lines = [total[:1]] + [pltpu.roll(total[s : s + 1], width - s, 1) for s in range(1, SUBLANES)]
    return functools.reduce(jnp.add, lines)


def diagonal_kernel(query_hbm, keys_hbm, values_hbm, cotangent_hbm, out_ref, left, right, sems):
    odd = is_odd()
    half = out_ref.shape[1]
    low, high = pl.ds(0, half), pl.ds(half, half)
    copies = launch(
        odd,
        [
            (1, keys_hbm.at[:, low], left),
            (1, values_hbm.at[:, low], right),
            (0, cotangent_hbm.at[:, high], left),
            (0, query_hbm.at[:, high], right),
        ],
        sems,
        0,
    )
    finish(odd, copies)
    out_ref[...] = product(left[...], right[...])


def products_kernel(query_ref, keys_ref, values_ref, cotangent_ref, sent_ref, near_ref, across_ref):
    odd = is_odd()
    prod = product(keys_ref[...], values_ref[...])
    grad = product(cotangent_ref[...], query_ref[...])
    near_ref[...] = lax.select(odd, prod, grad)
    across_ref[...] = lax.select(odd, grad, prod)


def tiles_kernel(rows, taps_ref, ready_tiles, late_tiles):
    odd = is_odd()
    group_count, width = taps_ref.shape
    for group in range(group_count):
        row = taps_ref[group : group + 1, :].astype(jnp.float32)
        spread = jnp.concatenate(
            [jnp.zeros((SUBLANES, rows), jnp.float32), jnp.broadcast_to(row, (SUBLANES, width))],
            axis=1,
        )
        spread = pltpu.roll(spread, 0, 1, stride=1, stride_axis=0)
        bands = [
            pltpu.roll(spread, start, 1)[:, rows:] if start else spread[:, rows:]
            for start in range(0, rows, SUBLANES)
        ]
        band = jnp.concatenate(bands, axis=0)
        turned = [band[:, start : start + rows].T for start in range(0, width, rows)]
        turned = jnp.concatenate(turned, axis=1)
        ready_tiles[group] = lax.select(odd, band, turned).astype(jnp.bfloat16)
        late_tiles[group] = lax.select(odd, turned, band).astype(jnp.bfloat16)


def own_kernel(
    rows, ready_tiles, late_tiles, near_ref, across_ref, diagonal_ref, sum_ref, late_ref, ready_ref
):
    odd = is_odd()
    group_count, width = sum_ref.shape
    group_width = near_ref.shape[1] // group_count
    half = group_count // 2
    blank = jnp.zeros((rows, rows), jnp.float32)
    for group in range(group_count):
        columns = columns_of(group, group_width)
        late_ref[:, columns] = DOT(late_tiles[group, :, :rows], near_ref[:, columns])
        ready_ref[:, columns] = DOT(ready_tiles[group, :, :rows], across_ref[:, columns])
    middles = []
    for group in range(half):
        low, high = columns_of(group, group_width), columns_of(group + half, group_width)
        arrived = diagonal_ref[:, low]
        own = lax.select(odd, near_ref[:, high], near_ref[:, low])
        middles.append(DOT_ROWS(lax.select(odd, own, arrived), lax.select(odd, arrived, own)))
        tile = lax.select(
            odd, ready_tiles[group + half, :, rows : 2 * rows], ready_tiles[group, :, rows : 2 * rows]
        )
        more = DOT(tile, arrived)
        ready_ref[:, low] += lax.select(odd, blank, more)
        ready_ref[:, high] += lax.select(odd, more, blank)
    sums = []
    for group in range(group_count):
        columns = columns_of(group, group_width)
        near, across = near_ref[:, columns], across_ref[:, columns]
        outer = DOT_ROWS(lax.select(odd, near, across), lax.select(odd, across, near))
        if group < half:
            middle = lax.select(odd, blank, middles[group])
        else:
            middle = lax.select(odd, middles[group - half], blank)
        sums.append(skewed_sum(jnp.concatenate([outer, middle, blank], axis=1), rows)[:, : 2 * rows])
    sums = jnp.concatenate(sums, axis=0)
    sum_ref[...] = jnp.concatenate([sums, jnp.zeros((group_count, width - 2 * rows), jnp.float32)], axis=1)


def two_kernel(rows, sum_ref, near_ref, two_ref, out_ref):
    odd = is_odd()
    group_count, width = out_ref.shape
    group_width = near_ref.shape[1] // group_count
    blank = jnp.zeros((rows, rows), jnp.float32)
    sums = []
    for group in range(group_count):
        columns = columns_of(group, group_width)
        near, two = near_ref[:, columns], two_ref[:, columns]
        outer = DOT_ROWS(lax.select(odd, near, two), lax.select(odd, two, near))
        sums.append(skewed_sum(jnp.concatenate([blank, outer], axis=1), rows))
    sums = jnp.concatenate(sums, axis=0)
    out_ref[...] = sum_ref[...] + jnp.concatenate(
        [jnp.zeros((group_count, width - 2 * rows), jnp.float32), sums], axis=1
    )


def pair_kernel(rows, factor, sum_ref, other_ref, across_ref, swap_ref, out_ref):
    odd = is_odd()
    group_count, width = out_ref.shape
    group_width = across_ref.shape[1] // group_count
    blank = jnp.zeros((rows, rows), jnp.float32)
    sums = []
    for group in range(group_count):
        columns = columns_of(group, group_width)
        across, swap = across_ref[:, columns], swap_ref[:, columns]
        outer = DOT_ROWS(lax.select(odd, swap, across), lax.select(odd, across, swap))
        sums.append(skewed_sum(jnp.concatenate([blank, outer], axis=1), rows))
    sums = jnp.concatenate(sums, axis=0)
    rest = jnp.concatenate([sums, jnp.zeros((group_count, width - 2 * rows), jnp.float32)], axis=1)
    out_ref[...] = (sum_ref[...] + other_ref[...] + rest) * factor


def add_kernel(left_ref, right_ref, known_ref, out_ref):
    out_ref[...] = left_ref[...] + right_ref[...]


def forward_kernel(far_ref, rest_ref, out_ref):
    half = out_ref.shape[1]
    out_ref[...] = lax.select(is_odd(), far_ref[:, half:], far_ref[:, :half])


def ready_kernel(
    tiles_ref, ready_ref, two_ref, query_ref, keys_ref, values_ref, sum_ref,
    gated_out, key_out, value_out, rest_ref, one, other, sems,
):
    odd = is_odd()
    group_count, rows, _ = tiles_ref.shape
    group_width = two_ref.shape[1] // group_count
    half = group_count // 2
    step = max(1, half // 2)
    copies = []
    for group in range(half):
        low, high = columns_of(group, group_width), columns_of(group + half, group_width)
        first = ready_ref[:, low] + DOT(tiles_ref[group, :, 2 * rows :], two_ref[:, low])
        second = ready_ref[:, high] + DOT(tiles_ref[group + half, :, 2 * rows :], two_ref[:, high])
        rest_ref[:, low] = lax.select(odd, first, second)
        known = lax.select(odd, second, first)
        one[:, low] = scaled(known, lax.select(odd, values_ref[:, high], query_ref[:, low]))
        other[:, low] = scaled(known, keys_ref[:, high])
        if (group + 1) % step == 0:
            start, size = (group + 1 - step) * group_width, step * group_width
            part, place = pl.ds(start, size), pl.ds(start + half * group_width, size)
            moves = [
                (0, one.at[:, part], gated_out.at[:, part]),
                (1, one.at[:, part], key_out.at[:, place]),
                (1, other.at[:, part], value_out.at[:, place]),
            ]
            copies += launch(odd, moves, sems, len(copies))
    finish(odd, copies)


def known_kernel(
    tiles_ref, late_ref, swap_ref, far_ref, query_ref, keys_ref, values_ref, gated_in, key_in, value_in,
    gated_out, key_out, value_out, done_ref, one, other, sems,
):
    odd = is_odd()
    done_ref[...] = jnp.zeros_like(done_ref)
    group_count, rows, _ = tiles_ref.shape
    group_width = far_ref.shape[1] // group_count
    step = max(1, group_count // PARTS)
    copies = []
    for group in range(group_count):
        columns = columns_of(group, group_width)
        arrived = jnp.concatenate([swap_ref[:, columns], far_ref[:, columns]], axis=0)
        late = late_ref[:, columns] + DOT(tiles_ref[group, :, rows:], arrived)
        one[:, columns] = scaled(late, lax.select(odd, query_ref[:, columns], values_ref[:, columns]))
        other[:, columns] = scaled(late, keys_ref[:, columns])
        if (group + 1) % step == 0:
            part = pl.ds((group + 1 - step) * group_width, step * group_width)
            moves = [
                (0, one.at[:, part], key_out.at[:, part]),
                (0, other.at[:, part], value_out.at[:, part]),
                (1, one.at[:, part], gated_out.at[:, part]),
            ]
            copies += launch(odd, moves, sems, len(copies))
    finish(odd, copies)


def last_kernel(
    tiles_ref, rest_ref, forwarded_ref, query_ref, keys_ref, values_ref, gated_in, key_in, value_in,
    gated_out, key_out, value_out, done_ref, one, other, sems,
):
    odd = is_odd()
    done_ref[...] = jnp.zeros_like(done_ref)
    group_count, rows, _ = tiles_ref.shape
    half = group_count // 2
    group_width = forwarded_ref.shape[1] // half
    step = max(1, half // 2)
    copies = []
    for group in range(half):
        low, high = columns_of(group, group_width), columns_of(group + half, group_width)
        tile = lax.select(
            odd, tiles_ref[group, :, rows : 2 * rows], tiles_ref[group + half, :, rows : 2 * rows]
        )
        ready = rest_ref[:, low] + DOT(tile, forwarded_ref[:, low])
        one[:, low] = scaled(ready, lax.select(odd, values_ref[:, low], query_ref[:, high]))
        other[:, low] = scaled(ready, keys_ref[:, low])
        if (group + 1) % step == 0:
            start, size = (group + 1 - step) * group_width, step * group_width
            part, place = pl.ds(start, size), pl.ds(start + half * group_width, size)
            moves = [
                (0, one.at[:, part], gated_out.at[:, place]),
                (1, one.at[:, part], key_out.at[:, part]),
                (1, other.at[:, part], value_out.at[:, part]),
            ]
            copies += launch(odd, moves, sems, len(copies))
    finish(odd, copies)


def shards(query, keys, values, cotangent, filter_taps):
    rows, local_width = query.shape
    group_count, taps = filter_taps.shape
    group_width = local_width // group_count
    half_width = local_width // 2
    factor = 1.0 / math.sqrt(rows * lax.axis_size("ctx") * group_width)

    def call(kernel, name, flops=10**6, **options):
        return pl.pallas_call(
            kernel,
            compiler_params=pltpu.CompilerParams(vmem_limit_bytes=VMEM_LIMIT),
            cost_estimate=pl.CostEstimate(flops=flops, bytes_accessed=10**5, transcendentals=0),
            name=name,
            **options,
        )

    def out_scratch(width, parts):
        return [pltpu.VMEM((rows, width), jnp.bfloat16)] * 2 + [pltpu.SemaphoreType.DMA((3 * parts,))]

    bf16, f32 = jnp.bfloat16, jnp.float32
    block, half_block = pltpu.VMEM((rows, local_width), bf16), pltpu.VMEM((rows, half_width), bf16)
    wide, half_wide = pltpu.VMEM((rows, local_width), f32), pltpu.VMEM((rows, half_width), f32)
    tiles, sums = pltpu.VMEM((group_count, rows, taps), bf16), pltpu.VMEM((group_count, taps), f32)
    mark = pltpu.VMEM((SUBLANES, group_width), f32)
    outs = [jax.ShapeDtypeStruct((rows, local_width), bf16)] * 3

    sent = call(
        diagonal_kernel,
        "diagonal",
        in_specs=[ANYWHERE] * 4,
        out_specs=WHOLE,
        out_shape=half_block,
        scratch_shapes=[half_block] * 2 + [pltpu.SemaphoreType.DMA((4,))],
    )(*in_hbm(query, keys, values, cotangent))
    diagonal = moved(sent, "ctx", (-1, 1))
    near, across = call(
        products_kernel,
        "products",
        in_specs=[WHOLE] * 4 + [ANYWHERE],
        out_specs=[WHOLE] * 2,
        out_shape=[block] * 2,
    )(*in_vmem(query, keys, values, cotangent), sent)
    two = moved(across, "ctx", (2, -2))
    far = moved(near, "ctx", (-2, 2))
    swap = moved(across, "ctx", (1, -1))

    ready_tiles, late_tiles = call(
        functools.partial(tiles_kernel, rows),
        "tiles",
        in_specs=[WHOLE],
        out_specs=[WHOLE] * 2,
        out_shape=[tiles] * 2,
    )(*in_vmem(filter_taps))
    partial, late, ready = call(
        functools.partial(own_kernel, rows),
        "own",
        flops=4 * 10**9,
        in_specs=[WHOLE] * 5,
        out_specs=[WHOLE] * 3,
        out_shape=[sums, wide, wide],
    )(*in_vmem(ready_tiles, late_tiles, near, across, diagonal))

    partial = call(
        functools.partial(two_kernel, rows),
        "two",
        in_specs=[WHOLE] * 3,
        out_specs=WHOLE,
        out_shape=sums,
    )(*in_vmem(partial, near, two))
    other = moved(partial, "ctx", (1, -1))

    gated, key_grad, value_grad, rest = call(
        ready_kernel,
        "ready",
        in_specs=[WHOLE] * 6 + [ANYWHERE],
        out_specs=[ANYWHERE] * 3 + [WHOLE],
        out_shape=outs + [half_wide],
        scratch_shapes=out_scratch(half_width, 2),
    )(*in_vmem(ready_tiles, ready, two, query, keys, values), partial)

    forwarded = call(
        forward_kernel,
        "forward",
        in_specs=[WHOLE, ANYWHERE],
        out_specs=WHOLE,
        out_shape=half_block,
    )(*in_vmem(far), rest)
    forwarded = moved(forwarded, "ctx", (1, -1))

    pair_sum = call(
        functools.partial(pair_kernel, rows, factor),
        "pair",
        in_specs=[WHOLE] * 4,
        out_specs=WHOLE,
        out_shape=sums,
    )(*in_vmem(partial, other, across, swap))
    gated, key_grad, value_grad, known_done = call(
        known_kernel,
        "known",
        flops=4 * 10**9,
        in_specs=[WHOLE] * 7 + [ANYWHERE] * 3,
        out_specs=[ANYWHERE] * 3 + [WHOLE],
        out_shape=outs + [mark],
        input_output_aliases={7: 0, 8: 1, 9: 2},
        scratch_shapes=out_scratch(local_width, PARTS),
    )(*in_vmem(late_tiles, late, swap, far, query, keys, values), gated, key_grad, value_grad)

    gated, key_grad, value_grad, last_done = call(
        last_kernel,
        "last",
        in_specs=[WHOLE] * 6 + [ANYWHERE] * 3,
        out_specs=[ANYWHERE] * 3 + [WHOLE],
        out_shape=outs + [mark],
        input_output_aliases={6: 0, 7: 1, 8: 2},
        scratch_shapes=out_scratch(half_width, 2),
    )(*in_vmem(ready_tiles, rest, forwarded, query, keys, values), gated, key_grad, value_grad)

    def adder(out_shape, after):
        add = call(
            add_kernel,
            "add",
            in_specs=[WHOLE] * 2 + [ANYWHERE],
            out_specs=WHOLE,
            out_shape=out_shape,
        )
        return lambda left, right: add(*in_vmem(left, right), after)

    whole_sums = jax.ShapeDtypeStruct((group_count, taps), f32)
    filter_grad = summed(pair_sum, "ctx", adder(sums, known_done), adder(whole_sums, last_done))
    return (gated, key_grad, value_grad, filter_grad)


def solution(mesh):
    in_specs = (P("ctx", "grp"), P("ctx", "grp"), P("ctx", "grp"), P("ctx", "grp"), P("grp", None))
    out_specs = (P("ctx", "grp"), P("ctx", "grp"), P("ctx", "grp"), P("grp", None))
    return jax.shard_map(shards, mesh=mesh, in_specs=in_specs, out_specs=out_specs, check_vma=False)
```

time: 136 us -> 37.4 us (0.27)
  local copies, waits for them, and re-layouts: 59 us -> 0.02 us
  blocking collectives: 44.6 us -> 0 us
  Pallas kernels: 0 us -> 11.4 us
  starting transfers between devices: 8.81 us -> 20.2 us
  other arithmetic: 7.92 us -> 0 us
  matrix products: 7.65 us -> 0 us
    psum x1 -> x0, blocking collectives: 44.6 us -> none  [shards(): filter_grad = lax.psum(filter_acc[:, block_rows:] * factor, 'ctx')]
    reshape x8 -> x0, local copies, waits for them, and re-layouts: 28.7 us -> none  [the longest x3 14.4 us: diagonal_sums(): skewed.reshape(group_count, block_rows, 2 * block_rows - 1)]
    rev x6 -> x0, local copies, waits for them, and re-layouts: 16 us -> none  [the longest x3 15.4 us: shards(): early[:, ::-1]]
    ppermute x4 -> x8, starting transfers between devices: 8.81 us -> 20.2 us  [the longest x6 15.1 us: moved(): lax.ppermute(block, axis, [pair for pair in route if 0 <= pair[1] < size])]
    pallas_call x0 -> x12, Pallas kernels: none -> 11.4 us  [the longest x1 2.22 us: shards(): call(functools.partial(tiles_kernel, rows), 'tiles', in_specs=[WHOLE], ou...]
    dot_general x9 -> x0, matrix products: 7.65 us -> none  [the longest x3 4.68 us: shards(): jnp.einsum('grs,gsc->grc', toeplitz, early, preferred_element_type=jnp.fl...]
    slice x7 -> x0, local copies, waits for them, and re-layouts: 7.47 us -> none  [the longest x3 4.46 us: diagonal_sums(): widened.reshape(group_count, 2 * block_rows * block_rows)]
    unnamed x22 -> x10, local copies, waits for them, and re-layouts: 5.45 us -> 0.02 us
  transfers between devices with their start and end apart: 4 -> 8, of which waited for: 1 -> 4; matrix products, arithmetic and copies ran while one was open for 26% -> 0% of each run, Pallas kernels for 0% -> 25%
where the time goes in v7:
time: 37.4 us; the launch traced here: 37.2 us
  starting transfers between devices  20.2 us (54%)
  Pallas kernels  11.4 us (30%)
  waiting for transfers between devices  4.7 us (13%)
  between operations  0.82 us (2%)
    ppermute x6, starting transfers between devices, moved(): lax.ppermute(block, axis, [pair for pair in route if 0 <= pair[1] < size])  15.1 us
    ppermute x2, starting transfers between devices, summed(): arrived = lax.ppermute(pair_sum, axis, route)  5.16 us
    ppermute x6, waiting for transfers between devices, moved(): lax.ppermute(block, axis, [pair for pair in route if 0 <= pair[1] < size])  3.43 us
    pallas_call x1, Pallas kernels, shards(): call(functools.partial(tiles_kernel, rows), 'tiles', in_specs=[WHOLE], ou...  2.22 us
    pallas_call x1, Pallas kernels, shards(): call(functools.partial(own_kernel, rows), 'own', flops=4 * 10 ** 9, in_sp...  1.61 us
    pallas_call x1, Pallas kernels, shards(): call(known_kernel, 'known', flops=4 * 10 ** 9, in_specs=[WHOLE] * 7 + [AN...  1.4 us
    pallas_call x1, Pallas kernels, shards(): call(diagonal_kernel, 'diagonal', in_specs=[ANYWHERE] * 4, out_specs=WHOL...  1.28 us
    ppermute x2, waiting for transfers between devices, summed(): arrived = lax.ppermute(pair_sum, axis, route)  1.27 us
  transfers between devices with their start and end apart: 8, of which 4 were waited for; matrix products, arithmetic and copies ran while one was open for 0% of the time, Pallas kernels for 25%

profile of v7, /device:TPU:0, one launch (start us, length us, event | category | flops | bytes accessed | tf_op | source)
XLA Modules:
  0.0 37.2 jit_solution(14704004909576005433)
XLA Ops:
  0.7 1.3 %diagonal.1.sent_ref = bf16[128,1024]{1,0:T(8,128)(2,1)S(1)} custom-call(bf16[128,2048]{1,0:T(8,128)(2,1)} %query_ref.7, bf16[128,2048]{1,0:T(8,128)(2,1)} %keys_ref.7, bf16[128,2048]{1,0:T(8,128)(2,1)} %values_ref.7, bf16[128,2048]{1,0:T(8,128)(2,1)} %cotangent_ref.1), custom_call_target="tpu_custom_call" | custom-call | flops 1000000 | bytes 100000 | tf_op jit(solution)/shard_map/diagonal/pallas_call | solution.py:335
  2.0 0.0 copy-start.4
  2.0 0.7 %collective-permute-start = (bf16[128,1024]{1,0:T(8,128)(2,1)S(1)}, bf16[128,1024]{1,0:T(8,128)(2,1)S(1)}, u32[]{:S(2)}, u32[]{:S(2)}) collective-permute-start(bf16[128,1024]{1,0:T(8,128)(2,1)S(1)} %diagonal.1.sent_ref), channel_id=1, source_target_pairs={{4,8},{8,4},{12,16},{16,12},{20,24},{24,20},{5,9},{9,5},{13,17},{1... | collective-permute-start | bytes 786440 | tf_op jit(solution)/shard_map/ppermute | solution.py:35
  2.7 0.3 products.1
  3.0 7.6 %collective-permute-start.1 = (bf16[128,2048]{1,0:T(8,128)(2,1)S(1)}, bf16[128,2048]{1,0:T(8,128)(2,1)S(1)}, u32[]{:S(2)}, u32[]{:S(2)}) collective-permute-start(bf16[128,2048]{1,0:T(8,128)(2,1)S(1)} %get-tuple-element.26.across_ref), channel_id=1, source_target_pairs={{0,8},{8,16},{12,4},{16,24},{20,12},{28,20},{1,9},{9,17},{13,5},{1... | collective-permute-start | bytes 1572872 | tf_op jit(solution)/shard_map/ppermute | solution.py:35
  10.6 1.3 %collective-permute-start.2 = (bf16[128,2048]{1,0:T(8,128)(2,1)S(1)}, bf16[128,2048]{1,0:T(8,128)(2,1)S(1)}, u32[]{:S(2)}, u32[]{:S(2)}) collective-permute-start(bf16[128,2048]{1,0:T(8,128)(2,1)S(1)} %get-tuple-element.25.near_ref), channel_id=1, source_target_pairs={{4,12},{8,0},{12,20},{16,8},{20,28},{24,16},{5,13},{9,1},{13,21},{... | collective-permute-start | bytes 1572872 | tf_op jit(solution)/shard_map/ppermute | solution.py:35
  11.9 2.8 %collective-permute-start.4 = (bf16[128,2048]{1,0:T(8,128)(2,1)S(1)}, bf16[128,2048]{1,0:T(8,128)(2,1)S(1)}, u32[]{:S(2)}, u32[]{:S(2)}) collective-permute-start(bf16[128,2048]{1,0:T(8,128)(2,1)S(1)} %get-tuple-element.26.across_ref), channel_id=1, source_target_pairs={{0,4},{4,0},{8,12},{12,8},{16,20},{20,16},{24,28},{28,24},{1,5},{5... | collective-permute-start | bytes 1572872 | tf_op jit(solution)/shard_map/ppermute | solution.py:35
  14.7 2.2 %tiles.1 = (bf16[16,128,384]{2,1,0:T(8,128)(2,1)S(1)}, bf16[16,128,384]{2,1,0:T(8,128)(2,1)S(1)}) custom-call(bf16[16,384]{1,0:T(8,128)(2,1)S(1)} %copy-done.4), custom_call_target="tpu_custom_call" | custom-call | flops 1000000 | bytes 100000 | tf_op jit(solution)/shard_map/tiles/pallas_call | solution.py:355
  16.9 0.0 collective-permute-done.diagonal_ref
  16.9 1.6 %own.1 = (f32[16,384]{1,0:T(8,128)S(1)}, f32[128,2048]{1,0:T(8,128)S(1)}, f32[128,2048]{1,0:T(8,128)S(1)}) custom-call(bf16[16,128,384]{2,1,0:T(8,128)(2,1)S(1)} %get-tuple-element.23.ready_tiles.tiles_ref, bf16[16,128,384]{2,1,0:T(8,128)(2,1)S(1)} %get-tuple-element.24.late_tiles.tiles_ref, bf16[128,2048]{1,0:T(8,128)(2,1)S(1)} %get-tuple-element.25.near_ref, ...), custom_call_target="tpu_custom_call" | custom-call | flops 4000000000 | bytes 100000 | tf_op jit(solution)/shard_map/own/pallas_call | solution.py:362
  18.6 2.9 %collective-permute-done.1.two_ref = bf16[128,2048]{1,0:T(8,128)(2,1)S(1)} collective-permute-done((bf16[128,2048]{1,0:T(8,128)(2,1)S(1)}, bf16[128,2048]{1,0:T(8,128)(2,1)S(1)}, u32[]{:S(2)}, u32[]{:S(2)}) %collective-permute-start.1) | collective-permute-done | bytes 524320 | tf_op jit(solution)/shard_map/ppermute | solution.py:35
  21.5 0.9 %two.1.sum_ref = f32[16,384]{1,0:T(8,128)S(1)} custom-call(f32[16,384]{1,0:T(8,128)S(1)} %get-tuple-element.28.sum_ref, bf16[128,2048]{1,0:T(8,128)(2,1)S(1)} %get-tuple-element.25.near_ref, bf16[128,2048]{1,0:T(8,128)(2,1)S(1)} %collective-permute-done.1.two_ref), custom_call_target="tpu_custom_call" | custom-call | flops 1000000 | bytes 100000 | tf_op jit(solution)/shard_map/two/pallas_call | solution.py:371
  22.3 2.6 %collective-permute-start.5 = (f32[16,384]{1,0:T(8,128)S(1)}, f32[16,384]{1,0:T(8,128)S(1)}, u32[]{:S(2)}, u32[]{:S(2)}) collective-permute-start(f32[16,384]{1,0:T(8,128)S(1)} %two.1.sum_ref), channel_id=1, source_target_pairs={{0,4},{4,0},{8,12},{12,8},{16,20},{20,16},{24,28},{28,24},{1,5},{5... | collective-permute-start | bytes 73736 | tf_op jit(solution)/shard_map/ppermute | solution.py:35
  25.0 1.1 %ready.1 = (bf16[128,2048]{1,0:T(8,128)(2,1)}, bf16[128,2048]{1,0:T(8,128)(2,1)}, bf16[128,2048]{1,0:T(8,128)(2,1)}, f32[128,1024]{1,0:T(8,128)S(1)}) custom-call(bf16[16,128,384]{2,1,0:T(8,128)(2,1)S(1)} %get-tuple-element.23.ready_tiles.tiles_ref, f32[128,2048]{1,0:T(8,128)S(1)} %get-tuple-element.27.ready_ref, ...), custom_call_target="tpu_custom_call" | custom-call | flops 1000000 | bytes 100000 | tf_op jit(solution)/shard_map/ready/pallas_call | solution.py:380
  26.1 0.1 collective-permute-start.3
  26.3 0.5 %collective-permute-done.5.other_ref = f32[16,384]{1,0:T(8,128)S(1)} collective-permute-done((f32[16,384]{1,0:T(8,128)S(1)}, f32[16,384]{1,0:T(8,128)S(1)}, u32[]{:S(2)}, u32[]{:S(2)}) %collective-permute-start.5) | collective-permute-done | bytes 24608 | tf_op jit(solution)/shard_map/ppermute | solution.py:35
  26.8 0.9 %pair.1.left_ref = f32[16,384]{1,0:T(8,128)S(1)} custom-call(f32[16,384]{1,0:T(8,128)S(1)} %two.1.sum_ref, f32[16,384]{1,0:T(8,128)S(1)} %collective-permute-done.5.other_ref, bf16[128,2048]{1,0:T(8,128)(2,1)S(1)} %get-tuple-element.26.across_ref, bf16[128,2048]{1,0:T(8,128)(2,1)S(1)} %collective-permute-done.4.swap_ref), custom_call_target="tpu_custom_call" | custom-call | flops 1000000 | bytes 100000 | tf_op jit(solution)/shard_map/pair/pallas_call | solution.py:398
  27.7 2.0 %collective-permute-start.6 = (f32[16,384]{1,0:T(8,128)S(1)}, f32[16,384]{1,0:T(8,128)S(1)}, u32[]{:S(2)}, u32[]{:S(2)}) collective-permute-start(f32[16,384]{1,0:T(8,128)S(1)} %pair.1.left_ref), channel_id=1, source_target_pairs={{0,8},{4,12},{8,0},{12,4},{16,24},{20,28},{24,16},{28,20},{1,9},{5... | collective-permute-start | bytes 73736 | tf_op jit(solution)/shard_map/ppermute | solution.py:46
  29.7 1.4 %known.1 = (bf16[128,2048]{1,0:T(8,128)(2,1)}, bf16[128,2048]{1,0:T(8,128)(2,1)}, bf16[128,2048]{1,0:T(8,128)(2,1)}, f32[8,128]{1,0:T(8,128)S(1)}) custom-call(bf16[16,128,384]{2,1,0:T(8,128)(2,1)S(1)} %get-tuple-element.24.late_tiles.tiles_ref, ...), custom_call_target="tpu_custom_call", output_to_operand_aliasing={{0}: (7, {}), {1}: (8, {}), {2}: (9, {})} | custom-call | flops 4000000000 | bytes 100000 | tf_op jit(solution)/shard_map/known/pallas_call | solution.py:405
  31.1 0.5 %collective-permute-done.6.right_ref = f32[16,384]{1,0:T(8,128)S(1)} collective-permute-done((f32[16,384]{1,0:T(8,128)S(1)}, f32[16,384]{1,0:T(8,128)S(1)}, u32[]{:S(2)}, u32[]{:S(2)}) %collective-permute-start.6) | collective-permute-done | bytes 24608 | tf_op jit(solution)/shard_map/ppermute | solution.py:46
  31.6 3.2 %collective-permute-start.7 = (f32[16,384]{1,0:T(8,128)S(1)}, f32[16,384]{1,0:T(8,128)S(1)}, u32[]{:S(2)}, u32[]{:S(2)}) collective-permute-start(f32[16,384]{1,0:T(8,128)S(1)} %add.2.left_ref), channel_id=1, source_target_pairs={{0,16},{4,20},{8,24},{12,28},{16,0},{20,4},{24,8},{28,12},{1,17},{... | collective-permute-start | bytes 73736 | tf_op jit(solution)/shard_map/ppermute | solution.py:46
  34.7 1.0 %last.1 = (bf16[128,2048]{1,0:T(8,128)(2,1)}, bf16[128,2048]{1,0:T(8,128)(2,1)}, bf16[128,2048]{1,0:T(8,128)(2,1)}, f32[8,128]{1,0:T(8,128)S(1)}) custom-call(bf16[16,128,384]{2,1,0:T(8,128)(2,1)S(1)} %get-tuple-element.23.ready_tiles.tiles_ref, ...), custom_call_target="tpu_custom_call", output_to_operand_aliasing={{0}: (6, {}), {1}: (7, {}), {2}: (8, {})} | custom-call | flops 1000000 | bytes 100000 | tf_op jit(solution)/shard_map/last/pallas_call | solution.py:416
  35.8 0.8 %collective-permute-done.7.right_ref = f32[16,384]{1,0:T(8,128)S(1)} collective-permute-done((f32[16,384]{1,0:T(8,128)S(1)}, f32[16,384]{1,0:T(8,128)S(1)}, u32[]{:S(2)}, u32[]{:S(2)}) %collective-permute-start.7) | collective-permute-done | bytes 24608 | tf_op jit(solution)/shard_map/ppermute | solution.py:46
  36.5 0.6 %add.3 = f32[16,384]{1,0:T(8,128)} custom-call(f32[16,384]{1,0:T(8,128)S(1)} %add.2.left_ref, f32[16,384]{1,0:T(8,128)S(1)} %collective-permute-done.7.right_ref, f32[8,128]{1,0:T(8,128)S(1)} %get-tuple-element.41.known_ref), custom_call_target="tpu_custom_call" | custom-call | flops 1000000 | bytes 100000 | tf_op jit(solution)/shard_map/add/pallas_call | solution.py:434
  (14 shorter events, 0.1 us)
Async XLA Ops:
  0.6 2.0 %copy-start.2 = (bf16[128,2048]{1,0:T(8,128)(2,1)S(1)}, bf16[128,2048]{1,0:T(8,128)(2,1)}, u32[]{:S(2)}) copy-start(bf16[128,2048]{1,0:T(8,128)(2,1)} %values_ref.7) | copy-start | bytes 1572868
  0.6 2.0 %copy-start.1 = (bf16[128,2048]{1,0:T(8,128)(2,1)S(1)}, bf16[128,2048]{1,0:T(8,128)(2,1)}, u32[]{:S(2)}) copy-start(bf16[128,2048]{1,0:T(8,128)(2,1)} %keys_ref.7) | copy-start | bytes 1572868
  0.7 2.0 %copy-start = (bf16[128,2048]{1,0:T(8,128)(2,1)S(1)}, bf16[128,2048]{1,0:T(8,128)(2,1)}, u32[]{:S(2)}) copy-start(bf16[128,2048]{1,0:T(8,128)(2,1)} %query_ref.7) | copy-start | bytes 1572868
  0.7 2.0 %copy-start.3 = (bf16[128,2048]{1,0:T(8,128)(2,1)S(1)}, bf16[128,2048]{1,0:T(8,128)(2,1)}, u32[]{:S(2)}) copy-start(bf16[128,2048]{1,0:T(8,128)(2,1)} %cotangent_ref.1) | copy-start | bytes 1572868
  2.0 12.7 %copy-start.4 = (bf16[16,384]{1,0:T(8,128)(2,1)S(1)}, bf16[16,384]{1,0:T(8,128)(2,1)}, u32[]{:S(2)}) copy-start(bf16[16,384]{1,0:T(8,128)(2,1)} %taps_ref.1) | copy-start | bytes 36868
  2.0 15.0 %collective-permute-start = (bf16[128,1024]{1,0:T(8,128)(2,1)S(1)}, bf16[128,1024]{1,0:T(8,128)(2,1)S(1)}, u32[]{:S(2)}, u32[]{:S(2)}) collective-permute-start(bf16[128,1024]{1,0:T(8,128)(2,1)S(1)} %diagonal.1.sent_ref), channel_id=1, source_target_pairs={{4,8},{8,4},{12,16},{16,12},{20,24},{24,20},{5,9},{9,5},{13,17},{1... | collective-permute-start | bytes 786440 | tf_op jit(solution)/shard_map/ppermute | solution.py:35
  3.0 18.4 %collective-permute-start.1 = (bf16[128,2048]{1,0:T(8,128)(2,1)S(1)}, bf16[128,2048]{1,0:T(8,128)(2,1)S(1)}, u32[]{:S(2)}, u32[]{:S(2)}) collective-permute-start(bf16[128,2048]{1,0:T(8,128)(2,1)S(1)} %get-tuple-element.26.across_ref), channel_id=1, source_target_pairs={{0,8},{8,16},{12,4},{16,24},{20,12},{28,20},{1,9},{9,17},{13,5},{1... | collective-permute-start | bytes 1572872 | tf_op jit(solution)/shard_map/ppermute | solution.py:35
  10.6 15.5 %collective-permute-start.2 = (bf16[128,2048]{1,0:T(8,128)(2,1)S(1)}, bf16[128,2048]{1,0:T(8,128)(2,1)S(1)}, u32[]{:S(2)}, u32[]{:S(2)}) collective-permute-start(bf16[128,2048]{1,0:T(8,128)(2,1)S(1)} %get-tuple-element.25.near_ref), channel_id=1, source_target_pairs={{4,12},{8,0},{12,20},{16,8},{20,28},{24,16},{5,13},{9,1},{13,21},{... | collective-permute-start | bytes 1572872 | tf_op jit(solution)/shard_map/ppermute | solution.py:35
  11.9 14.4 %collective-permute-start.4 = (bf16[128,2048]{1,0:T(8,128)(2,1)S(1)}, bf16[128,2048]{1,0:T(8,128)(2,1)S(1)}, u32[]{:S(2)}, u32[]{:S(2)}) collective-permute-start(bf16[128,2048]{1,0:T(8,128)(2,1)S(1)} %get-tuple-element.26.across_ref), channel_id=1, source_target_pairs={{0,4},{4,0},{8,12},{12,8},{16,20},{20,16},{24,28},{28,24},{1,5},{5... | collective-permute-start | bytes 1572872 | tf_op jit(solution)/shard_map/ppermute | solution.py:35
  22.3 4.4 %collective-permute-start.5 = (f32[16,384]{1,0:T(8,128)S(1)}, f32[16,384]{1,0:T(8,128)S(1)}, u32[]{:S(2)}, u32[]{:S(2)}) collective-permute-start(f32[16,384]{1,0:T(8,128)S(1)} %two.1.sum_ref), channel_id=1, source_target_pairs={{0,4},{4,0},{8,12},{12,8},{16,20},{20,16},{24,28},{28,24},{1,5},{5... | collective-permute-start | bytes 73736 | tf_op jit(solution)/shard_map/ppermute | solution.py:35
  26.1 8.6 %collective-permute-start.3 = (bf16[128,1024]{1,0:T(8,128)(2,1)S(1)}, bf16[128,1024]{1,0:T(8,128)(2,1)S(1)}, u32[]{:S(2)}, u32[]{:S(2)}) collective-permute-start(bf16[128,1024]{1,0:T(8,128)(2,1)S(1)} %forward.1), channel_id=1, source_target_pairs={{0,4},{4,0},{8,12},{12,8},{16,20},{20,16},{24,28},{28,24},{1,5},{5... | collective-permute-start | bytes 786440 | tf_op jit(solution)/shard_map/ppermute | solution.py:35
  27.7 3.9 %collective-permute-start.6 = (f32[16,384]{1,0:T(8,128)S(1)}, f32[16,384]{1,0:T(8,128)S(1)}, u32[]{:S(2)}, u32[]{:S(2)}) collective-permute-start(f32[16,384]{1,0:T(8,128)S(1)} %pair.1.left_ref), channel_id=1, source_target_pairs={{0,8},{4,12},{8,0},{12,4},{16,24},{20,28},{24,16},{28,20},{1,9},{5... | collective-permute-start | bytes 73736 | tf_op jit(solution)/shard_map/ppermute | solution.py:46
  31.6 5.0 %collective-permute-start.7 = (f32[16,384]{1,0:T(8,128)S(1)}, f32[16,384]{1,0:T(8,128)S(1)}, u32[]{:S(2)}, u32[]{:S(2)}) collective-permute-start(f32[16,384]{1,0:T(8,128)S(1)} %add.2.left_ref), channel_id=1, source_target_pairs={{0,16},{4,20},{8,24},{12,28},{16,0},{20,4},{24,8},{28,12},{1,17},{... | collective-permute-start | bytes 73736 | tf_op jit(solution)/shard_map/ppermute | solution.py:46

commit v8 on v7

--- a/solution.py
+++ b/solution.py
@@ -42,10 +42,11 @@
         return lax.psum(jnp.where(even, pair_sum, 0.0), axis)
     stride = 2
     while stride < size:
-        route = [(i, i ^ stride) for i in range(size)]
-        arrived = lax.ppermute(pair_sum, axis, route)
-        stride *= 2
-        pair_sum = (add if stride < size else add_last)(pair_sum, arrived)
+        hops = (stride, 2 * stride, 3 * stride) if 4 * stride <= size else (stride,)
+        routes = [[(i, i ^ hop) for i in range(size)] for hop in hops]
+        arrived = [lax.ppermute(pair_sum, axis, route) for route in routes]
+        stride *= len(hops) + 1
+        pair_sum = (add if stride < size else add_last)(pair_sum, *arrived)
     return pair_sum
 
 
@@ -193,7 +194,7 @@
     )
 
 
-def pair_kernel(rows, factor, sum_ref, other_ref, across_ref, swap_ref, out_ref):
+def cross_kernel(rows, across_ref, swap_ref, out_ref):
     odd = is_odd()
     group_count, width = out_ref.shape
     group_width = across_ref.shape[1] // group_count
@@ -205,15 +206,19 @@
         outer = DOT_ROWS(lax.select(odd, swap, across), lax.select(odd, across, swap))
         sums.append(skewed_sum(jnp.concatenate([blank, outer], axis=1), rows))
     sums = jnp.concatenate(sums, axis=0)
-    rest = jnp.concatenate([sums, jnp.zeros((group_count, width - 2 * rows), jnp.float32)], axis=1)
-    out_ref[...] = (sum_ref[...] + other_ref[...] + rest) * factor
-
-
-def add_kernel(left_ref, right_ref, known_ref, out_ref):
-    out_ref[...] = left_ref[...] + right_ref[...]
-
-
-def forward_kernel(far_ref, rest_ref, out_ref):
+    out_ref[...] = jnp.concatenate([sums, jnp.zeros((group_count, width - 2 * rows), jnp.float32)], axis=1)
+
+
+def pair_kernel(factor, sum_ref, other_ref, cross_ref, rest_ref, out_ref):
+    out_ref[...] = (sum_ref[...] + other_ref[...] + cross_ref[...]) * factor
+
+
+def add_kernel(*refs):
+    *terms, _, out_ref = refs
+    out_ref[...] = functools.reduce(jnp.add, [ref[...] for ref in terms])
+
+
+def forward_kernel(far_ref, sum_ref, out_ref):
     half = out_ref.shape[1]
     out_ref[...] = lax.select(is_odd(), far_ref[:, half:], far_ref[:, :half])
 
@@ -392,16 +397,24 @@
         in_specs=[WHOLE, ANYWHERE],
         out_specs=WHOLE,
         out_shape=half_block,
-    )(*in_vmem(far), rest)
+    )(*in_vmem(far), partial)
     forwarded = moved(forwarded, "ctx", (1, -1))
 
-    pair_sum = call(
-        functools.partial(pair_kernel, rows, factor),
-        "pair",
-        in_specs=[WHOLE] * 4,
+    cross = call(
+        functools.partial(cross_kernel, rows),
+        "cross",
+        in_specs=[WHOLE] * 2,
         out_specs=WHOLE,
         out_shape=sums,
-    )(*in_vmem(partial, other, across, swap))
+    )(*in_vmem(across, swap))
+    pair_sum = call(
+        functools.partial(pair_kernel, factor),
+        "pair",
+        in_specs=[WHOLE] * 3 + [ANYWHERE],
+        out_specs=WHOLE,
+        out_shape=sums,
+    )(*in_vmem(partial, other, cross), rest)
+
     gated, key_grad, value_grad, known_done = call(
         known_kernel,
         "known",
@@ -424,14 +437,16 @@
     )(*in_vmem(ready_tiles, rest, forwarded, query, keys, values), gated, key_grad, value_grad)
 
     def adder(out_shape, after):
-        add = call(
-            add_kernel,
-            "add",
-            in_specs=[WHOLE] * 2 + [ANYWHERE],
-            out_specs=WHOLE,
-            out_shape=out_shape,
-        )
-        return lambda left, right: add(*in_vmem(left, right), after)
+        def add(*terms):
+            return call(
+                add_kernel,
+                "add",
+                in_specs=[WHOLE] * len(terms) + [ANYWHERE],
+                out_specs=WHOLE,
+                out_shape=out_shape,
+            )(*in_vmem(*terms), after)
+
+        return add
 
     whole_sums = jax.ShapeDtypeStruct((group_count, taps), f32)
     filter_grad = summed(pair_sum, "ctx", adder(sums, known_done), adder(whole_sums, last_done))

time: 37.4 us -> 38.9 us (1.040)
  waiting for transfers between devices: 4.7 us -> 6.07 us
  Pallas kernels: 11.4 us -> 12 us
  starting transfers between devices: 20.2 us -> 19.8 us
    ppermute x2 -> x3, waiting for transfers between devices: 1.27 us -> 2.57 us  [summed(): arrived = [lax.ppermute(pair_sum, axis, route) for route in routes]]
    pallas_call x1, Pallas kernels: 1.4 us -> 1.98 us  [shards(): call(known_kernel, 'known', flops=4 * 10 ** 9, in_specs=[WHOLE] * 7 + [AN...]
    ppermute x2 -> x3, starting transfers between devices: 5.16 us -> 4.75 us  [summed(): arrived = [lax.ppermute(pair_sum, axis, route) for route in routes]]
  transfers between devices with their start and end apart: 8 -> 9, of which waited for: 4 -> 3; matrix products, arithmetic and copies ran while one was open for 0% -> 0% of each run, Pallas kernels for 25% -> 26%
where the time goes in v8:
time: 38.9 us; the launch traced here: 38.7 us
  starting transfers between devices  19.8 us (51%)
  Pallas kernels  12 us (31%)
  waiting for transfers between devices  6.07 us (16%)
  between operations  0.86 us (2%)
    ppermute x6, starting transfers between devices, moved(): lax.ppermute(block, axis, [pair for pair in route if 0 <= pair[1] < size])  15 us
    ppermute x3, starting transfers between devices, summed(): arrived = [lax.ppermute(pair_sum, axis, route) for route in routes]  4.75 us
    ppermute x6, waiting for transfers between devices, moved(): lax.ppermute(block, axis, [pair for pair in route if 0 <= pair[1] < size])  3.49 us
    ppermute x3, waiting for transfers between devices, summed(): arrived = [lax.ppermute(pair_sum, axis, route) for route in routes]  2.57 us
    pallas_call x1, Pallas kernels, shards(): call(functools.partial(tiles_kernel, rows), 'tiles', in_specs=[WHOLE], ou...  2.22 us
    pallas_call x1, Pallas kernels, shards(): call(known_kernel, 'known', flops=4 * 10 ** 9, in_specs=[WHOLE] * 7 + [AN...  1.98 us
    pallas_call x1, Pallas kernels, shards(): call(functools.partial(own_kernel, rows), 'own', flops=4 * 10 ** 9, in_sp...  1.66 us
    pallas_call x1, Pallas kernels, shards(): call(diagonal_kernel, 'diagonal', in_specs=[ANYWHERE] * 4, out_specs=WHOL...  1.28 us
  transfers between devices with their start and end apart: 9, of which 3 were waited for; matrix products, arithmetic and copies ran while one was open for 0% of the time, Pallas kernels for 26%

profile of v8, /device:TPU:0, one launch (start us, length us, event | category | flops | bytes accessed | tf_op | source)
XLA Modules:
  0.0 38.7 jit_solution(10461776439886992008)
XLA Ops:
  0.7 1.3 %diagonal.1.sent_ref = bf16[128,1024]{1,0:T(8,128)(2,1)S(1)} custom-call(bf16[128,2048]{1,0:T(8,128)(2,1)} %query_ref.7, bf16[128,2048]{1,0:T(8,128)(2,1)} %keys_ref.7, bf16[128,2048]{1,0:T(8,128)(2,1)} %values_ref.7, bf16[128,2048]{1,0:T(8,128)(2,1)} %cotangent_ref.1), custom_call_target="tpu_custom_call" | custom-call | flops 1000000 | bytes 100000 | tf_op jit(solution)/shard_map/diagonal/pallas_call | solution.py:340
  2.0 0.0 copy-start.4
  2.0 0.7 %collective-permute-start = (bf16[128,1024]{1,0:T(8,128)(2,1)S(1)}, bf16[128,1024]{1,0:T(8,128)(2,1)S(1)}, u32[]{:S(2)}, u32[]{:S(2)}) collective-permute-start(bf16[128,1024]{1,0:T(8,128)(2,1)S(1)} %diagonal.1.sent_ref), channel_id=1, source_target_pairs={{4,8},{8,4},{12,16},{16,12},{20,24},{24,20},{5,9},{9,5},{13,17},{1... | collective-permute-start | bytes 786440 | tf_op jit(solution)/shard_map/ppermute | solution.py:35
  2.7 0.3 products.1
  3.0 7.6 %collective-permute-start.1 = (bf16[128,2048]{1,0:T(8,128)(2,1)S(1)}, bf16[128,2048]{1,0:T(8,128)(2,1)S(1)}, u32[]{:S(2)}, u32[]{:S(2)}) collective-permute-start(bf16[128,2048]{1,0:T(8,128)(2,1)S(1)} %get-tuple-element.25.across_ref), channel_id=1, source_target_pairs={{0,8},{8,16},{12,4},{16,24},{20,12},{28,20},{1,9},{9,17},{13,5},{1... | collective-permute-start | bytes 1572872 | tf_op jit(solution)/shard_map/ppermute | solution.py:35
  10.6 1.3 %collective-permute-start.2 = (bf16[128,2048]{1,0:T(8,128)(2,1)S(1)}, bf16[128,2048]{1,0:T(8,128)(2,1)S(1)}, u32[]{:S(2)}, u32[]{:S(2)}) collective-permute-start(bf16[128,2048]{1,0:T(8,128)(2,1)S(1)} %get-tuple-element.24.near_ref), channel_id=1, source_target_pairs={{4,12},{8,0},{12,20},{16,8},{20,28},{24,16},{5,13},{9,1},{13,21},{... | collective-permute-start | bytes 1572872 | tf_op jit(solution)/shard_map/ppermute | solution.py:35
  11.9 2.8 %collective-permute-start.4 = (bf16[128,2048]{1,0:T(8,128)(2,1)S(1)}, bf16[128,2048]{1,0:T(8,128)(2,1)S(1)}, u32[]{:S(2)}, u32[]{:S(2)}) collective-permute-start(bf16[128,2048]{1,0:T(8,128)(2,1)S(1)} %get-tuple-element.25.across_ref), channel_id=1, source_target_pairs={{0,4},{4,0},{8,12},{12,8},{16,20},{20,16},{24,28},{28,24},{1,5},{5... | collective-permute-start | bytes 1572872 | tf_op jit(solution)/shard_map/ppermute | solution.py:35
  14.7 2.2 %tiles.1 = (bf16[16,128,384]{2,1,0:T(8,128)(2,1)S(1)}, bf16[16,128,384]{2,1,0:T(8,128)(2,1)S(1)}) custom-call(bf16[16,384]{1,0:T(8,128)(2,1)S(1)} %copy-done.4), custom_call_target="tpu_custom_call" | custom-call | flops 1000000 | bytes 100000 | tf_op jit(solution)/shard_map/tiles/pallas_call | solution.py:360
  16.9 1.7 %own.1 = (f32[16,384]{1,0:T(8,128)S(1)}, f32[128,2048]{1,0:T(8,128)S(1)}, f32[128,2048]{1,0:T(8,128)S(1)}) custom-call(bf16[16,128,384]{2,1,0:T(8,128)(2,1)S(1)} %get-tuple-element.22.ready_tiles.tiles_ref, bf16[16,128,384]{2,1,0:T(8,128)(2,1)S(1)} %get-tuple-element.23.late_tiles.tiles_ref, bf16[128,2048]{1,0:T(8,128)(2,1)S(1)} %get-tuple-element.24.near_ref, ...), custom_call_target="tpu_custom_call" | custom-call | flops 4000000000 | bytes 100000 | tf_op jit(solution)/shard_map/own/pallas_call | solution.py:367
  18.6 2.9 %collective-permute-done.1.two_ref = bf16[128,2048]{1,0:T(8,128)(2,1)S(1)} collective-permute-done((bf16[128,2048]{1,0:T(8,128)(2,1)S(1)}, bf16[128,2048]{1,0:T(8,128)(2,1)S(1)}, u32[]{:S(2)}, u32[]{:S(2)}) %collective-permute-start.1) | collective-permute-done | bytes 524320 | tf_op jit(solution)/shard_map/ppermute | solution.py:35
  21.5 0.9 %two.1.sum_ref = f32[16,384]{1,0:T(8,128)S(1)} custom-call(f32[16,384]{1,0:T(8,128)S(1)} %get-tuple-element.27.sum_ref, bf16[128,2048]{1,0:T(8,128)(2,1)S(1)} %get-tuple-element.24.near_ref, bf16[128,2048]{1,0:T(8,128)(2,1)S(1)} %collective-permute-done.1.two_ref), custom_call_target="tpu_custom_call" | custom-call | flops 1000000 | bytes 100000 | tf_op jit(solution)/shard_map/two/pallas_call | solution.py:376
  22.3 2.6 %collective-permute-start.5 = (f32[16,384]{1,0:T(8,128)S(1)}, f32[16,384]{1,0:T(8,128)S(1)}, u32[]{:S(2)}, u32[]{:S(2)}) collective-permute-start(f32[16,384]{1,0:T(8,128)S(1)} %two.1.sum_ref), channel_id=1, source_target_pairs={{0,4},{4,0},{8,12},{12,8},{16,20},{20,16},{24,28},{28,24},{1,5},{5... | collective-permute-start | bytes 73736 | tf_op jit(solution)/shard_map/ppermute | solution.py:35
  25.0 0.6 %collective-permute-done.2.far_ref = bf16[128,2048]{1,0:T(8,128)(2,1)S(1)} collective-permute-done((bf16[128,2048]{1,0:T(8,128)(2,1)S(1)}, bf16[128,2048]{1,0:T(8,128)(2,1)S(1)}, u32[]{:S(2)}, u32[]{:S(2)}) %collective-permute-start.2) | collective-permute-done | bytes 524320 | tf_op jit(solution)/shard_map/ppermute | solution.py:35
  25.6 0.1 collective-permute-start.3
  25.7 1.1 %ready.1 = (bf16[128,2048]{1,0:T(8,128)(2,1)}, bf16[128,2048]{1,0:T(8,128)(2,1)}, bf16[128,2048]{1,0:T(8,128)(2,1)}, f32[128,1024]{1,0:T(8,128)S(1)}) custom-call(bf16[16,128,384]{2,1,0:T(8,128)(2,1)S(1)} %get-tuple-element.22.ready_tiles.tiles_ref, f32[128,2048]{1,0:T(8,128)S(1)} %get-tuple-element.26.ready_ref, ...), custom_call_target="tpu_custom_call" | custom-call | flops 1000000 | bytes 100000 | tf_op jit(solution)/shard_map/ready/pallas_call | solution.py:385
  26.8 0.0 collective-permute-done.4.swap_ref
  26.8 0.9 %cross.1.cross_ref = f32[16,384]{1,0:T(8,128)S(1)} custom-call(bf16[128,2048]{1,0:T(8,128)(2,1)S(1)} %get-tuple-element.25.across_ref, bf16[128,2048]{1,0:T(8,128)(2,1)S(1)} %collective-permute-done.4.swap_ref), custom_call_target="tpu_custom_call" | custom-call | flops 1000000 | bytes 100000 | tf_op jit(solution)/shard_map/cross/pallas_call | solution.py:403
  27.7 0.0 collective-permute-done.5.other_ref
  27.7 2.1 %collective-permute-start.6 = (f32[16,384]{1,0:T(8,128)S(1)}, f32[16,384]{1,0:T(8,128)S(1)}, u32[]{:S(2)}, u32[]{:S(2)}) collective-permute-start(f32[16,384]{1,0:T(8,128)S(1)} %pair.1.refs_0_), channel_id=1, source_target_pairs={{0,8},{4,12},{8,0},{12,4},{16,24},{20,28},{24,16},{28,20},{1,9},{5... | collective-permute-start | bytes 73736 | tf_op jit(solution)/shard_map/ppermute | solution.py:47
  29.9 2.6 %collective-permute-start.7 = (f32[16,384]{1,0:T(8,128)S(1)}, f32[16,384]{1,0:T(8,128)S(1)}, u32[]{:S(2)}, u32[]{:S(2)}) collective-permute-start(f32[16,384]{1,0:T(8,128)S(1)} %pair.1.refs_0_), channel_id=1, source_target_pairs={{0,16},{4,20},{8,24},{12,28},{16,0},{20,4},{24,8},{28,12},{1,17},{... | collective-permute-start | bytes 73736 | tf_op jit(solution)/shard_map/ppermute | solution.py:47
  32.5 2.0 %known.1 = (bf16[128,2048]{1,0:T(8,128)(2,1)}, bf16[128,2048]{1,0:T(8,128)(2,1)}, bf16[128,2048]{1,0:T(8,128)(2,1)}, f32[8,128]{1,0:T(8,128)}) custom-call(bf16[16,128,384]{2,1,0:T(8,128)(2,1)S(1)} %get-tuple-element.23.late_tiles.tiles_ref, f32[128,2048]{1,0:T(8,128)S(1)} %get-tuple-element.29.late_ref, ...), custom_call_target="tpu_custom_call", output_to_operand_aliasing={{0}: (7, {}), {1}: (8, {}), {2}: (9, {})} | custom-call | flops 4000000000 | bytes 100000 | tf_op jit(solution)/shard_map/known/pallas_call | solution.py:418
  34.5 1.0 %last.1 = (bf16[128,2048]{1,0:T(8,128)(2,1)}, bf16[128,2048]{1,0:T(8,128)(2,1)}, bf16[128,2048]{1,0:T(8,128)(2,1)}, f32[8,128]{1,0:T(8,128)S(1)}) custom-call(bf16[16,128,384]{2,1,0:T(8,128)(2,1)S(1)} %get-tuple-element.22.ready_tiles.tiles_ref, ...), custom_call_target="tpu_custom_call", output_to_operand_aliasing={{0}: (6, {}), {1}: (7, {}), {2}: (8, {})} | custom-call | flops 1000000 | bytes 100000 | tf_op jit(solution)/shard_map/last/pallas_call | solution.py:429
  35.6 2.6 %collective-permute-done.8.refs_3_ = f32[16,384]{1,0:T(8,128)S(1)} collective-permute-done((f32[16,384]{1,0:T(8,128)S(1)}, f32[16,384]{1,0:T(8,128)S(1)}, u32[]{:S(2)}, u32[]{:S(2)}) %collective-permute-start.8) | collective-permute-done | bytes 24608 | tf_op jit(solution)/shard_map/ppermute | solution.py:47
  38.1 0.6 %add.1 = f32[16,384]{1,0:T(8,128)} custom-call(f32[16,384]{1,0:T(8,128)S(1)} %pair.1.refs_0_, f32[16,384]{1,0:T(8,128)S(1)} %collective-permute-done.6.refs_1_, f32[16,384]{1,0:T(8,128)S(1)} %collective-permute-done.7.refs_2_, f32[16,384]{1,0:T(8,128)S(1)} %collective-permute-done.8.refs_3_, f32[8,128]{1,0:T(8,128)S(1)} %get-tuple-element.39.refs_4_), custom_call_target="tpu_custom_call" | custom-call | flops 1000000 | bytes 100000 | tf_op jit(solution)/shard_map/add/pallas_call | solution.py:441
  (16 shorter events, 0.1 us)
Async XLA Ops:
  0.6 2.0 %copy-start = (bf16[128,2048]{1,0:T(8,128)(2,1)S(1)}, bf16[128,2048]{1,0:T(8,128)(2,1)}, u32[]{:S(2)}) copy-start(bf16[128,2048]{1,0:T(8,128)(2,1)} %query_ref.7) | copy-start | bytes 1572868
  0.6 2.0 %copy-start.1 = (bf16[128,2048]{1,0:T(8,128)(2,1)S(1)}, bf16[128,2048]{1,0:T(8,128)(2,1)}, u32[]{:S(2)}) copy-start(bf16[128,2048]{1,0:T(8,128)(2,1)} %keys_ref.7) | copy-start | bytes 1572868
  0.7 2.0 %copy-start.2 = (bf16[128,2048]{1,0:T(8,128)(2,1)S(1)}, bf16[128,2048]{1,0:T(8,128)(2,1)}, u32[]{:S(2)}) copy-start(bf16[128,2048]{1,0:T(8,128)(2,1)} %values_ref.7) | copy-start | bytes 1572868
  0.7 2.0 %copy-start.3 = (bf16[128,2048]{1,0:T(8,128)(2,1)S(1)}, bf16[128,2048]{1,0:T(8,128)(2,1)}, u32[]{:S(2)}) copy-start(bf16[128,2048]{1,0:T(8,128)(2,1)} %cotangent_ref.1) | copy-start | bytes 1572868
  2.0 12.7 %copy-start.4 = (bf16[16,384]{1,0:T(8,128)(2,1)S(1)}, bf16[16,384]{1,0:T(8,128)(2,1)}, u32[]{:S(2)}) copy-start(bf16[16,384]{1,0:T(8,128)(2,1)} %taps_ref.1) | copy-start | bytes 36868
  2.0 15.0 %collective-permute-start = (bf16[128,1024]{1,0:T(8,128)(2,1)S(1)}, bf16[128,1024]{1,0:T(8,128)(2,1)S(1)}, u32[]{:S(2)}, u32[]{:S(2)}) collective-permute-start(bf16[128,1024]{1,0:T(8,128)(2,1)S(1)} %diagonal.1.sent_ref), channel_id=1, source_target_pairs={{4,8},{8,4},{12,16},{16,12},{20,24},{24,20},{5,9},{9,5},{13,17},{1... | collective-permute-start | bytes 786440 | tf_op jit(solution)/shard_map/ppermute | solution.py:35
  3.0 18.4 %collective-permute-start.1 = (bf16[128,2048]{1,0:T(8,128)(2,1)S(1)}, bf16[128,2048]{1,0:T(8,128)(2,1)S(1)}, u32[]{:S(2)}, u32[]{:S(2)}) collective-permute-start(bf16[128,2048]{1,0:T(8,128)(2,1)S(1)} %get-tuple-element.25.across_ref), channel_id=1, source_target_pairs={{0,8},{8,16},{12,4},{16,24},{20,12},{28,20},{1,9},{9,17},{13,5},{1... | collective-permute-start | bytes 1572872 | tf_op jit(solution)/shard_map/ppermute | solution.py:35
  10.6 15.0 %collective-permute-start.2 = (bf16[128,2048]{1,0:T(8,128)(2,1)S(1)}, bf16[128,2048]{1,0:T(8,128)(2,1)S(1)}, u32[]{:S(2)}, u32[]{:S(2)}) collective-permute-start(bf16[128,2048]{1,0:T(8,128)(2,1)S(1)} %get-tuple-element.24.near_ref), channel_id=1, source_target_pairs={{4,12},{8,0},{12,20},{16,8},{20,28},{24,16},{5,13},{9,1},{13,21},{... | collective-permute-start | bytes 1572872 | tf_op jit(solution)/shard_map/ppermute | solution.py:35
  11.9 14.9 %collective-permute-start.4 = (bf16[128,2048]{1,0:T(8,128)(2,1)S(1)}, bf16[128,2048]{1,0:T(8,128)(2,1)S(1)}, u32[]{:S(2)}, u32[]{:S(2)}) collective-permute-start(bf16[128,2048]{1,0:T(8,128)(2,1)S(1)} %get-tuple-element.25.across_ref), channel_id=1, source_target_pairs={{0,4},{4,0},{8,12},{12,8},{16,20},{20,16},{24,28},{28,24},{1,5},{5... | collective-permute-start | bytes 1572872 | tf_op jit(solution)/shard_map/ppermute | solution.py:35
  22.3 5.4 %collective-permute-start.5 = (f32[16,384]{1,0:T(8,128)S(1)}, f32[16,384]{1,0:T(8,128)S(1)}, u32[]{:S(2)}, u32[]{:S(2)}) collective-permute-start(f32[16,384]{1,0:T(8,128)S(1)} %two.1.sum_ref), channel_id=1, source_target_pairs={{0,4},{4,0},{8,12},{12,8},{16,20},{20,16},{24,28},{28,24},{1,5},{5... | collective-permute-start | bytes 73736 | tf_op jit(solution)/shard_map/ppermute | solution.py:35
  25.6 8.9 %collective-permute-start.3 = (bf16[128,1024]{1,0:T(8,128)(2,1)S(1)}, bf16[128,1024]{1,0:T(8,128)(2,1)S(1)}, u32[]{:S(2)}, u32[]{:S(2)}) collective-permute-start(bf16[128,1024]{1,0:T(8,128)(2,1)S(1)} %forward.1), channel_id=1, source_target_pairs={{0,4},{4,0},{8,12},{12,8},{16,20},{20,16},{24,28},{28,24},{1,5},{5... | collective-permute-start | bytes 786440 | tf_op jit(solution)/shard_map/ppermute | solution.py:35
  27.7 7.8 %collective-permute-start.6 = (f32[16,384]{1,0:T(8,128)S(1)}, f32[16,384]{1,0:T(8,128)S(1)}, u32[]{:S(2)}, u32[]{:S(2)}) collective-permute-start(f32[16,384]{1,0:T(8,128)S(1)} %pair.1.refs_0_), channel_id=1, source_target_pairs={{0,8},{4,12},{8,0},{12,4},{16,24},{20,28},{24,16},{28,20},{1,9},{5... | collective-permute-start | bytes 73736 | tf_op jit(solution)/shard_map/ppermute | solution.py:47
  29.9 5.7 %collective-permute-start.7 = (f32[16,384]{1,0:T(8,128)S(1)}, f32[16,384]{1,0:T(8,128)S(1)}, u32[]{:S(2)}, u32[]{:S(2)}) collective-permute-start(f32[16,384]{1,0:T(8,128)S(1)} %pair.1.refs_0_), channel_id=1, source_target_pairs={{0,16},{4,20},{8,24},{12,28},{16,0},{20,4},{24,8},{28,12},{1,17},{... | collective-permute-start | bytes 73736 | tf_op jit(solution)/shard_map/ppermute | solution.py:47
  32.5 5.6 %collective-permute-start.8 = (f32[16,384]{1,0:T(8,128)S(1)}, f32[16,384]{1,0:T(8,128)S(1)}, u32[]{:S(2)}, u32[]{:S(2)}) collective-permute-start(f32[16,384]{1,0:T(8,128)S(1)} %pair.1.refs_0_), channel_id=1, source_target_pairs={{0,24},{4,28},{8,16},{12,20},{16,8},{20,12},{24,0},{28,4},{1,25},{... | collective-permute-start | bytes 73736 | tf_op jit(solution)/shard_map/ppermute | solution.py:47

commit v9 on v8

--- a/solution.py
+++ b/solution.py
@@ -9,7 +9,7 @@
 from jax.sharding import PartitionSpec as P
 
 SUBLANES = 8
-PARTS = 4
+PARTS = 2
 VMEM_LIMIT = 16 * 1024 * 1024
 WHOLE = pl.BlockSpec(memory_space=pltpu.VMEM)
 ANYWHERE = pl.BlockSpec(memory_space=pl.ANY)
@@ -35,19 +35,19 @@
     return lax.ppermute(block, axis, [pair for pair in route if 0 <= pair[1] < size])
 
 
-def summed(pair_sum, axis, add, add_last):
+def sum_terms(pair_sum, axis, add):
     size = lax.axis_size(axis)
     if size & (size - 1):
         even = lax.axis_index(axis) % 2 == 0
-        return lax.psum(jnp.where(even, pair_sum, 0.0), axis)
+        return [lax.psum(jnp.where(even, pair_sum, 0.0), axis)]
+    terms = [pair_sum]
     stride = 2
     while stride < size:
-        hops = (stride, 2 * stride, 3 * stride) if 4 * stride <= size else (stride,)
-        routes = [[(i, i ^ hop) for i in range(size)] for hop in hops]
-        arrived = [lax.ppermute(pair_sum, axis, route) for route in routes]
+        own = terms[0] if len(terms) == 1 else add(*terms)
+        hops = (3 * stride, 2 * stride, stride) if 4 * stride <= size else (stride,)
+        terms = [own] + [lax.ppermute(own, axis, [(i, i ^ hop) for i in range(size)]) for hop in hops]
         stride *= len(hops) + 1
-        pair_sum = (add if stride < size else add_last)(pair_sum, *arrived)
-    return pair_sum
+    return terms
 
 
 def is_odd():
@@ -214,7 +214,7 @@
 
 
 def add_kernel(*refs):
-    *terms, _, out_ref = refs
+    *terms, out_ref = refs
     out_ref[...] = functools.reduce(jnp.add, [ref[...] for ref in terms])
 
 
@@ -224,15 +224,12 @@
 
 
 def ready_kernel(
-    tiles_ref, ready_ref, two_ref, query_ref, keys_ref, values_ref, sum_ref,
-    gated_out, key_out, value_out, rest_ref, one, other, sems,
+    tiles_ref, ready_ref, two_ref, query_ref, keys_ref, values_ref, sum_ref, rest_ref, one, other
 ):
     odd = is_odd()
     group_count, rows, _ = tiles_ref.shape
     group_width = two_ref.shape[1] // group_count
     half = group_count // 2
-    step = max(1, half // 2)
-    copies = []
     for group in range(half):
         low, high = columns_of(group, group_width), columns_of(group + half, group_width)
         first = ready_ref[:, low] + DOT(tiles_ref[group, :, 2 * rows :], two_ref[:, low])
@@ -241,56 +238,46 @@
         known = lax.select(odd, second, first)
         one[:, low] = scaled(known, lax.select(odd, values_ref[:, high], query_ref[:, low]))
         other[:, low] = scaled(known, keys_ref[:, high])
-        if (group + 1) % step == 0:
-            start, size = (group + 1 - step) * group_width, step * group_width
-            part, place = pl.ds(start, size), pl.ds(start + half * group_width, size)
-            moves = [
-                (0, one.at[:, part], gated_out.at[:, part]),
-                (1, one.at[:, part], key_out.at[:, place]),
-                (1, other.at[:, part], value_out.at[:, place]),
-            ]
-            copies += launch(odd, moves, sems, len(copies))
-    finish(odd, copies)
-
-
-def known_kernel(
-    tiles_ref, late_ref, swap_ref, far_ref, query_ref, keys_ref, values_ref, gated_in, key_in, value_in,
-    gated_out, key_out, value_out, done_ref, one, other, sems,
-):
-    odd = is_odd()
-    done_ref[...] = jnp.zeros_like(done_ref)
+
+
+def known_kernel(tiles_ref, late_ref, swap_ref, far_ref, query_ref, keys_ref, values_ref, one, other):
+    odd = is_odd()
     group_count, rows, _ = tiles_ref.shape
     group_width = far_ref.shape[1] // group_count
-    step = max(1, group_count // PARTS)
-    copies = []
     for group in range(group_count):
         columns = columns_of(group, group_width)
         arrived = jnp.concatenate([swap_ref[:, columns], far_ref[:, columns]], axis=0)
         late = late_ref[:, columns] + DOT(tiles_ref[group, :, rows:], arrived)
         one[:, columns] = scaled(late, lax.select(odd, query_ref[:, columns], values_ref[:, columns]))
         other[:, columns] = scaled(late, keys_ref[:, columns])
-        if (group + 1) % step == 0:
-            part = pl.ds((group + 1 - step) * group_width, step * group_width)
-            moves = [
-                (0, one.at[:, part], key_out.at[:, part]),
-                (0, other.at[:, part], value_out.at[:, part]),
-                (1, one.at[:, part], gated_out.at[:, part]),
-            ]
-            copies += launch(odd, moves, sems, len(copies))
-    finish(odd, copies)
 
 
 def last_kernel(
-    tiles_ref, rest_ref, forwarded_ref, query_ref, keys_ref, values_ref, gated_in, key_in, value_in,
-    gated_out, key_out, value_out, done_ref, one, other, sems,
+    tiles_ref, rest_ref, forwarded_ref, query_ref, keys_ref, values_ref,
+    ready_one, ready_other, known_one, known_other, *refs,
 ):
-    odd = is_odd()
-    done_ref[...] = jnp.zeros_like(done_ref)
+    *terms, gated_out, key_out, value_out, filter_out, one, other, total, sems = refs
+    odd = is_odd()
     group_count, rows, _ = tiles_ref.shape
     half = group_count // 2
     group_width = forwarded_ref.shape[1] // half
-    step = max(1, half // 2)
-    copies = []
+    step = max(1, half // PARTS)
+    low_half, high_half = pl.ds(0, half * group_width), pl.ds(half * group_width, half * group_width)
+    copies = launch(
+        odd,
+        [
+            (0, known_one, key_out),
+            (0, known_other, value_out),
+            (0, ready_one, gated_out.at[:, low_half]),
+            (1, known_one, gated_out),
+            (1, ready_one, key_out.at[:, high_half]),
+            (1, ready_other, value_out.at[:, high_half]),
+        ],
+        sems,
+        0,
+    )
+    total[...] = functools.reduce(jnp.add, [term[...] for term in terms])
+    copies += launch(odd, [(0, total, filter_out), (1, total, filter_out)], sems, len(copies))
     for group in range(half):
         low, high = columns_of(group, group_width), columns_of(group + half, group_width)
         tile = lax.select(
@@ -327,14 +314,10 @@
             **options,
         )
 
-    def out_scratch(width, parts):
-        return [pltpu.VMEM((rows, width), jnp.bfloat16)] * 2 + [pltpu.SemaphoreType.DMA((3 * parts,))]
-
     bf16, f32 = jnp.bfloat16, jnp.float32
     block, half_block = pltpu.VMEM((rows, local_width), bf16), pltpu.VMEM((rows, half_width), bf16)
     wide, half_wide = pltpu.VMEM((rows, local_width), f32), pltpu.VMEM((rows, half_width), f32)
     tiles, sums = pltpu.VMEM((group_count, rows, taps), bf16), pltpu.VMEM((group_count, taps), f32)
-    mark = pltpu.VMEM((SUBLANES, group_width), f32)
     outs = [jax.ShapeDtypeStruct((rows, local_width), bf16)] * 3
 
     sent = call(
@@ -382,13 +365,12 @@
     )(*in_vmem(partial, near, two))
     other = moved(partial, "ctx", (1, -1))
 
-    gated, key_grad, value_grad, rest = call(
+    rest, ready_one, ready_other = call(
         ready_kernel,
         "ready",
         in_specs=[WHOLE] * 6 + [ANYWHERE],
-        out_specs=[ANYWHERE] * 3 + [WHOLE],
-        out_shape=outs + [half_wide],
-        scratch_shapes=out_scratch(half_width, 2),
+        out_specs=[WHOLE] * 3,
+        out_shape=[half_wide, half_block, half_block],
     )(*in_vmem(ready_tiles, ready, two, query, keys, values), partial)
 
     forwarded = call(
@@ -415,42 +397,36 @@
         out_shape=sums,
     )(*in_vmem(partial, other, cross), rest)
 
-    gated, key_grad, value_grad, known_done = call(
+    known_one, known_other = call(
         known_kernel,
         "known",
         flops=4 * 10**9,
-        in_specs=[WHOLE] * 7 + [ANYWHERE] * 3,
-        out_specs=[ANYWHERE] * 3 + [WHOLE],
-        out_shape=outs + [mark],
-        input_output_aliases={7: 0, 8: 1, 9: 2},
-        scratch_shapes=out_scratch(local_width, PARTS),
-    )(*in_vmem(late_tiles, late, swap, far, query, keys, values), gated, key_grad, value_grad)
-
-    gated, key_grad, value_grad, last_done = call(
+        in_specs=[WHOLE] * 7,
+        out_specs=[WHOLE] * 2,
+        out_shape=[block] * 2,
+    )(*in_vmem(late_tiles, late, swap, far, query, keys, values))
+
+    def add(*terms):
+        return call(
+            add_kernel,
+            "add",
+            in_specs=[WHOLE] * len(terms),
+            out_specs=WHOLE,
+            out_shape=sums,
+        )(*in_vmem(*terms))
+
+    terms = sum_terms(pair_sum, "ctx", add)
+    return call(
         last_kernel,
         "last",
-        in_specs=[WHOLE] * 6 + [ANYWHERE] * 3,
-        out_specs=[ANYWHERE] * 3 + [WHOLE],
-        out_shape=outs + [mark],
-        input_output_aliases={6: 0, 7: 1, 8: 2},
-        scratch_shapes=out_scratch(half_width, 2),
-    )(*in_vmem(ready_tiles, rest, forwarded, query, keys, values), gated, key_grad, value_grad)
-
-    def adder(out_shape, after):
-        def add(*terms):
-            return call(
-                add_kernel,
-                "add",
-                in_specs=[WHOLE] * len(terms) + [ANYWHERE],
-                out_specs=WHOLE,
-                out_shape=out_shape,
-            )(*in_vmem(*terms), after)
-
-        return add
-
-    whole_sums = jax.ShapeDtypeStruct((group_count, taps), f32)
-    filter_grad = summed(pair_sum, "ctx", adder(sums, known_done), adder(whole_sums, last_done))
-    return (gated, key_grad, value_grad, filter_grad)
+        in_specs=[WHOLE] * (10 + len(terms)),
+        out_specs=[ANYWHERE] * 4,
+        out_shape=outs + [jax.ShapeDtypeStruct((group_count, taps), f32)],
+        scratch_shapes=[half_block] * 2 + [sums, pltpu.SemaphoreType.DMA((8 + 3 * PARTS,))],
+    )(
+        *in_vmem(ready_tiles, rest, forwarded, query, keys, values),
+        *in_vmem(ready_one, ready_other, known_one, known_other, *terms),
+    )
 
 
 def solution(mesh):

time: 38.9 us -> 37.6 us (0.967)
  Pallas kernels: 12 us -> 9.5 us
  waiting for transfers between devices: 6.07 us -> 7.08 us
    pallas_call x3 -> x2, Pallas kernels: 3.62 us -> 1.9 us  [the longest x1 1.35 us: shards(): call(last_kernel, 'last', in_specs=[WHOLE] * (10 + len(terms)), out_specs...]
    ppermute x3, waiting for transfers between devices: 2.57 us -> 3.53 us  [sum_terms(): lax.ppermute(own, axis, [(i, i ^ hop) for i in range(size)])]
    pallas_call x1, Pallas kernels: 1.09 us -> 0.37 us  [shards(): call(ready_kernel, 'ready', in_specs=[WHOLE] * 6 + [ANYWHERE], out_specs=...]
  transfers between devices with their start and end apart: 9 -> 9, of which waited for: 3 -> 4; matrix products, arithmetic and copies ran while one was open for 0% -> 0% of each run, Pallas kernels for 26% -> 18%
where the time goes in v9:
time: 37.6 us; the launch traced here: 37.4 us
  starting transfers between devices  20 us (53%)
  Pallas kernels  9.5 us (25%)
  waiting for transfers between devices  7.08 us (19%)
  between operations  0.83 us (2%)
    ppermute x6, starting transfers between devices, moved(): lax.ppermute(block, axis, [pair for pair in route if 0 <= pair[1] < size])  15 us
    ppermute x3, starting transfers between devices, sum_terms(): lax.ppermute(own, axis, [(i, i ^ hop) for i in range(size)])  4.93 us
    ppermute x6, waiting for transfers between devices, moved(): lax.ppermute(block, axis, [pair for pair in route if 0 <= pair[1] < size])  3.55 us
    ppermute x3, waiting for transfers between devices, sum_terms(): lax.ppermute(own, axis, [(i, i ^ hop) for i in range(size)])  3.53 us
    pallas_call x1, Pallas kernels, shards(): call(functools.partial(tiles_kernel, rows), 'tiles', in_specs=[WHOLE], ou...  2.22 us
    pallas_call x1, Pallas kernels, shards(): call(functools.partial(own_kernel, rows), 'own', flops=4 * 10 ** 9, in_sp...  1.6 us
    pallas_call x1, Pallas kernels, shards(): call(last_kernel, 'last', in_specs=[WHOLE] * (10 + len(terms)), out_specs...  1.35 us
    pallas_call x1, Pallas kernels, shards(): call(diagonal_kernel, 'diagonal', in_specs=[ANYWHERE] * 4, out_specs=WHOL...  1.28 us
  transfers between devices with their start and end apart: 9, of which 4 were waited for; matrix products, arithmetic and copies ran while one was open for 0% of the time, Pallas kernels for 18%

profile of v9, /device:TPU:0, one launch (start us, length us, event | category | flops | bytes accessed | tf_op | source)
XLA Modules:
  0.0 37.4 jit_solution(7047556367522396608)
XLA Ops:
  0.7 1.3 %diagonal.1.sent_ref = bf16[128,1024]{1,0:T(8,128)(2,1)S(1)} custom-call(bf16[128,2048]{1,0:T(8,128)(2,1)} %query_ref.7, bf16[128,2048]{1,0:T(8,128)(2,1)} %keys_ref.7, bf16[128,2048]{1,0:T(8,128)(2,1)} %values_ref.7, bf16[128,2048]{1,0:T(8,128)(2,1)} %cotangent_ref.1), custom_call_target="tpu_custom_call" | custom-call | flops 1000000 | bytes 100000 | tf_op jit(solution)/shard_map/diagonal/pallas_call | solution.py:323
  2.0 0.0 copy-start.4
  2.0 0.7 %collective-permute-start = (bf16[128,1024]{1,0:T(8,128)(2,1)S(1)}, bf16[128,1024]{1,0:T(8,128)(2,1)S(1)}, u32[]{:S(2)}, u32[]{:S(2)}) collective-permute-start(bf16[128,1024]{1,0:T(8,128)(2,1)S(1)} %diagonal.1.sent_ref), channel_id=1, source_target_pairs={{4,8},{8,4},{12,16},{16,12},{20,24},{24,20},{5,9},{9,5},{13,17},{1... | collective-permute-start | bytes 786440 | tf_op jit(solution)/shard_map/ppermute | solution.py:35
  2.7 0.3 products.1
  3.0 7.6 %collective-permute-start.1 = (bf16[128,2048]{1,0:T(8,128)(2,1)S(1)}, bf16[128,2048]{1,0:T(8,128)(2,1)S(1)}, u32[]{:S(2)}, u32[]{:S(2)}) collective-permute-start(bf16[128,2048]{1,0:T(8,128)(2,1)S(1)} %get-tuple-element.19.across_ref), channel_id=1, source_target_pairs={{0,8},{8,16},{12,4},{16,24},{20,12},{28,20},{1,9},{9,17},{13,5},{1... | collective-permute-start | bytes 1572872 | tf_op jit(solution)/shard_map/ppermute | solution.py:35
  10.6 1.3 %collective-permute-start.2 = (bf16[128,2048]{1,0:T(8,128)(2,1)S(1)}, bf16[128,2048]{1,0:T(8,128)(2,1)S(1)}, u32[]{:S(2)}, u32[]{:S(2)}) collective-permute-start(bf16[128,2048]{1,0:T(8,128)(2,1)S(1)} %get-tuple-element.18.near_ref), channel_id=1, source_target_pairs={{4,12},{8,0},{12,20},{16,8},{20,28},{24,16},{5,13},{9,1},{13,21},{... | collective-permute-start | bytes 1572872 | tf_op jit(solution)/shard_map/ppermute | solution.py:35
  11.9 2.8 %collective-permute-start.4 = (bf16[128,2048]{1,0:T(8,128)(2,1)S(1)}, bf16[128,2048]{1,0:T(8,128)(2,1)S(1)}, u32[]{:S(2)}, u32[]{:S(2)}) collective-permute-start(bf16[128,2048]{1,0:T(8,128)(2,1)S(1)} %get-tuple-element.19.across_ref), channel_id=1, source_target_pairs={{0,4},{4,0},{8,12},{12,8},{16,20},{20,16},{24,28},{28,24},{1,5},{5... | collective-permute-start | bytes 1572872 | tf_op jit(solution)/shard_map/ppermute | solution.py:35
  14.7 2.2 %tiles.1 = (bf16[16,128,384]{2,1,0:T(8,128)(2,1)S(1)}, bf16[16,128,384]{2,1,0:T(8,128)(2,1)S(1)}) custom-call(bf16[16,384]{1,0:T(8,128)(2,1)S(1)} %copy-done.4), custom_call_target="tpu_custom_call" | custom-call | flops 1000000 | bytes 100000 | tf_op jit(solution)/shard_map/tiles/pallas_call | solution.py:343
  16.9 0.0 collective-permute-done.diagonal_ref
  16.9 1.6 %own.1 = (f32[16,384]{1,0:T(8,128)S(1)}, f32[128,2048]{1,0:T(8,128)S(1)}, f32[128,2048]{1,0:T(8,128)S(1)}) custom-call(bf16[16,128,384]{2,1,0:T(8,128)(2,1)S(1)} %get-tuple-element.16.ready_tiles.tiles_ref, bf16[16,128,384]{2,1,0:T(8,128)(2,1)S(1)} %get-tuple-element.17.late_tiles.tiles_ref, bf16[128,2048]{1,0:T(8,128)(2,1)S(1)} %get-tuple-element.18.near_ref, ...), custom_call_target="tpu_custom_call" | custom-call | flops 4000000000 | bytes 100000 | tf_op jit(solution)/shard_map/own/pallas_call | solution.py:350
  18.5 2.9 %collective-permute-done.1.two_ref = bf16[128,2048]{1,0:T(8,128)(2,1)S(1)} collective-permute-done((bf16[128,2048]{1,0:T(8,128)(2,1)S(1)}, bf16[128,2048]{1,0:T(8,128)(2,1)S(1)}, u32[]{:S(2)}, u32[]{:S(2)}) %collective-permute-start.1) | collective-permute-done | bytes 524320 | tf_op jit(solution)/shard_map/ppermute | solution.py:35
  21.5 0.9 %two.1.sum_ref = f32[16,384]{1,0:T(8,128)S(1)} custom-call(f32[16,384]{1,0:T(8,128)S(1)} %get-tuple-element.21.sum_ref, bf16[128,2048]{1,0:T(8,128)(2,1)S(1)} %get-tuple-element.18.near_ref, bf16[128,2048]{1,0:T(8,128)(2,1)S(1)} %collective-permute-done.1.two_ref), custom_call_target="tpu_custom_call" | custom-call | flops 1000000 | bytes 100000 | tf_op jit(solution)/shard_map/two/pallas_call | solution.py:359
  22.3 2.6 %collective-permute-start.5 = (f32[16,384]{1,0:T(8,128)S(1)}, f32[16,384]{1,0:T(8,128)S(1)}, u32[]{:S(2)}, u32[]{:S(2)}) collective-permute-start(f32[16,384]{1,0:T(8,128)S(1)} %two.1.sum_ref), channel_id=1, source_target_pairs={{0,4},{4,0},{8,12},{12,8},{16,20},{20,16},{24,28},{28,24},{1,5},{5... | collective-permute-start | bytes 73736 | tf_op jit(solution)/shard_map/ppermute | solution.py:35
  25.0 0.6 %collective-permute-done.2.far_ref = bf16[128,2048]{1,0:T(8,128)(2,1)S(1)} collective-permute-done((bf16[128,2048]{1,0:T(8,128)(2,1)S(1)}, bf16[128,2048]{1,0:T(8,128)(2,1)S(1)}, u32[]{:S(2)}, u32[]{:S(2)}) %collective-permute-start.2) | collective-permute-done | bytes 524320 | tf_op jit(solution)/shard_map/ppermute | solution.py:35
  25.6 0.1 collective-permute-start.3
  25.7 0.4 ready.1
  26.1 0.9 %cross.1.cross_ref = f32[16,384]{1,0:T(8,128)S(1)} custom-call(bf16[128,2048]{1,0:T(8,128)(2,1)S(1)} %get-tuple-element.19.across_ref, bf16[128,2048]{1,0:T(8,128)(2,1)S(1)} %collective-permute-done.4.swap_ref), custom_call_target="tpu_custom_call" | custom-call | flops 1000000 | bytes 100000 | tf_op jit(solution)/shard_map/cross/pallas_call | solution.py:385
  27.0 0.0 collective-permute-done.5.other_ref
  27.0 4.3 %collective-permute-start.6 = (f32[16,384]{1,0:T(8,128)S(1)}, f32[16,384]{1,0:T(8,128)S(1)}, u32[]{:S(2)}, u32[]{:S(2)}) collective-permute-start(f32[16,384]{1,0:T(8,128)S(1)} %pair.1.refs_0_), channel_id=1, source_target_pairs={{0,24},{4,28},{8,16},{12,20},{16,8},{20,12},{24,0},{28,4},{1,25},{... | collective-permute-start | bytes 73736 | tf_op jit(solution)/shard_map/ppermute | solution.py:48
  31.3 0.6 %collective-permute-start.8 = (f32[16,384]{1,0:T(8,128)S(1)}, f32[16,384]{1,0:T(8,128)S(1)}, u32[]{:S(2)}, u32[]{:S(2)}) collective-permute-start(f32[16,384]{1,0:T(8,128)S(1)} %pair.1.refs_0_), channel_id=1, source_target_pairs={{0,8},{4,12},{8,0},{12,4},{16,24},{20,28},{24,16},{28,20},{1,9},{5... | collective-permute-start | bytes 73736 | tf_op jit(solution)/shard_map/ppermute | solution.py:48
  32.0 0.5 %known.1 = (bf16[128,2048]{1,0:T(8,128)(2,1)S(1)}, bf16[128,2048]{1,0:T(8,128)(2,1)S(1)}) custom-call(bf16[16,128,384]{2,1,0:T(8,128)(2,1)S(1)} %get-tuple-element.17.late_tiles.tiles_ref, f32[128,2048]{1,0:T(8,128)S(1)} %get-tuple-element.25.late_ref, bf16[128,2048]{1,0:T(8,128)(2,1)S(1)} %collective-permute-done.4.swap_ref, ...), custom_call_target="tpu_custom_call" | custom-call | flops 4000000000 | bytes 100000 | tf_op jit(solution)/shard_map/known/pallas_call | solution.py:400
  32.5 0.6 %collective-permute-done.6.refs_1_ = f32[16,384]{1,0:T(8,128)S(1)} collective-permute-done((f32[16,384]{1,0:T(8,128)S(1)}, f32[16,384]{1,0:T(8,128)S(1)}, u32[]{:S(2)}, u32[]{:S(2)}) %collective-permute-start.6) | collective-permute-done | bytes 24608 | tf_op jit(solution)/shard_map/ppermute | solution.py:48
  33.1 2.9 %collective-permute-done.7.refs_2_ = f32[16,384]{1,0:T(8,128)S(1)} collective-permute-done((f32[16,384]{1,0:T(8,128)S(1)}, f32[16,384]{1,0:T(8,128)S(1)}, u32[]{:S(2)}, u32[]{:S(2)}) %collective-permute-start.7) | collective-permute-done | bytes 24608 | tf_op jit(solution)/shard_map/ppermute | solution.py:48
  36.0 1.4 %last.1 = (bf16[128,2048]{1,0:T(8,128)(2,1)}, bf16[128,2048]{1,0:T(8,128)(2,1)}, bf16[128,2048]{1,0:T(8,128)(2,1)}, f32[16,384]{1,0:T(8,128)}) custom-call(bf16[16,128,384]{2,1,0:T(8,128)(2,1)S(1)} %get-tuple-element.16.ready_tiles.tiles_ref, f32[128,1024]{1,0:T(8,128)S(1)} %get-tuple-element.22.rest_ref, ...), custom_call_target="tpu_custom_call" | custom-call | flops 1000000 | bytes 100000 | tf_op jit(solution)/shard_map/last/pallas_call | solution.py:419
  (15 shorter events, 0.1 us)
Async XLA Ops:
  0.6 2.0 %copy-start = (bf16[128,2048]{1,0:T(8,128)(2,1)S(1)}, bf16[128,2048]{1,0:T(8,128)(2,1)}, u32[]{:S(2)}) copy-start(bf16[128,2048]{1,0:T(8,128)(2,1)} %query_ref.7) | copy-start | bytes 1572868
  0.6 2.0 %copy-start.1 = (bf16[128,2048]{1,0:T(8,128)(2,1)S(1)}, bf16[128,2048]{1,0:T(8,128)(2,1)}, u32[]{:S(2)}) copy-start(bf16[128,2048]{1,0:T(8,128)(2,1)} %keys_ref.7) | copy-start | bytes 1572868
  0.7 2.0 %copy-start.2 = (bf16[128,2048]{1,0:T(8,128)(2,1)S(1)}, bf16[128,2048]{1,0:T(8,128)(2,1)}, u32[]{:S(2)}) copy-start(bf16[128,2048]{1,0:T(8,128)(2,1)} %values_ref.7) | copy-start | bytes 1572868
  0.7 2.0 %copy-start.3 = (bf16[128,2048]{1,0:T(8,128)(2,1)S(1)}, bf16[128,2048]{1,0:T(8,128)(2,1)}, u32[]{:S(2)}) copy-start(bf16[128,2048]{1,0:T(8,128)(2,1)} %cotangent_ref.1) | copy-start | bytes 1572868
  2.0 12.7 %copy-start.4 = (bf16[16,384]{1,0:T(8,128)(2,1)S(1)}, bf16[16,384]{1,0:T(8,128)(2,1)}, u32[]{:S(2)}) copy-start(bf16[16,384]{1,0:T(8,128)(2,1)} %taps_ref.1) | copy-start | bytes 36868
  2.0 15.0 %collective-permute-start = (bf16[128,1024]{1,0:T(8,128)(2,1)S(1)}, bf16[128,1024]{1,0:T(8,128)(2,1)S(1)}, u32[]{:S(2)}, u32[]{:S(2)}) collective-permute-start(bf16[128,1024]{1,0:T(8,128)(2,1)S(1)} %diagonal.1.sent_ref), channel_id=1, source_target_pairs={{4,8},{8,4},{12,16},{16,12},{20,24},{24,20},{5,9},{9,5},{13,17},{1... | collective-permute-start | bytes 786440 | tf_op jit(solution)/shard_map/ppermute | solution.py:35
  3.0 18.4 %collective-permute-start.1 = (bf16[128,2048]{1,0:T(8,128)(2,1)S(1)}, bf16[128,2048]{1,0:T(8,128)(2,1)S(1)}, u32[]{:S(2)}, u32[]{:S(2)}) collective-permute-start(bf16[128,2048]{1,0:T(8,128)(2,1)S(1)} %get-tuple-element.19.across_ref), channel_id=1, source_target_pairs={{0,8},{8,16},{12,4},{16,24},{20,12},{28,20},{1,9},{9,17},{13,5},{1... | collective-permute-start | bytes 1572872 | tf_op jit(solution)/shard_map/ppermute | solution.py:35
  10.6 15.0 %collective-permute-start.2 = (bf16[128,2048]{1,0:T(8,128)(2,1)S(1)}, bf16[128,2048]{1,0:T(8,128)(2,1)S(1)}, u32[]{:S(2)}, u32[]{:S(2)}) collective-permute-start(bf16[128,2048]{1,0:T(8,128)(2,1)S(1)} %get-tuple-element.18.near_ref), channel_id=1, source_target_pairs={{4,12},{8,0},{12,20},{16,8},{20,28},{24,16},{5,13},{9,1},{13,21},{... | collective-permute-start | bytes 1572872 | tf_op jit(solution)/shard_map/ppermute | solution.py:35
  11.9 14.2 %collective-permute-start.4 = (bf16[128,2048]{1,0:T(8,128)(2,1)S(1)}, bf16[128,2048]{1,0:T(8,128)(2,1)S(1)}, u32[]{:S(2)}, u32[]{:S(2)}) collective-permute-start(bf16[128,2048]{1,0:T(8,128)(2,1)S(1)} %get-tuple-element.19.across_ref), channel_id=1, source_target_pairs={{0,4},{4,0},{8,12},{12,8},{16,20},{20,16},{24,28},{28,24},{1,5},{5... | collective-permute-start | bytes 1572872 | tf_op jit(solution)/shard_map/ppermute | solution.py:35
  22.3 4.7 %collective-permute-start.5 = (f32[16,384]{1,0:T(8,128)S(1)}, f32[16,384]{1,0:T(8,128)S(1)}, u32[]{:S(2)}, u32[]{:S(2)}) collective-permute-start(f32[16,384]{1,0:T(8,128)S(1)} %two.1.sum_ref), channel_id=1, source_target_pairs={{0,4},{4,0},{8,12},{12,8},{16,20},{20,16},{24,28},{28,24},{1,5},{5... | collective-permute-start | bytes 73736 | tf_op jit(solution)/shard_map/ppermute | solution.py:35
  25.6 10.4 %collective-permute-start.3 = (bf16[128,1024]{1,0:T(8,128)(2,1)S(1)}, bf16[128,1024]{1,0:T(8,128)(2,1)S(1)}, u32[]{:S(2)}, u32[]{:S(2)}) collective-permute-start(bf16[128,1024]{1,0:T(8,128)(2,1)S(1)} %forward.1), channel_id=1, source_target_pairs={{0,4},{4,0},{8,12},{12,8},{16,20},{20,16},{24,28},{28,24},{1,5},{5... | collective-permute-start | bytes 786440 | tf_op jit(solution)/shard_map/ppermute | solution.py:35
  27.0 6.1 %collective-permute-start.6 = (f32[16,384]{1,0:T(8,128)S(1)}, f32[16,384]{1,0:T(8,128)S(1)}, u32[]{:S(2)}, u32[]{:S(2)}) collective-permute-start(f32[16,384]{1,0:T(8,128)S(1)} %pair.1.refs_0_), channel_id=1, source_target_pairs={{0,24},{4,28},{8,16},{12,20},{16,8},{20,12},{24,0},{28,4},{1,25},{... | collective-permute-start | bytes 73736 | tf_op jit(solution)/shard_map/ppermute | solution.py:48
  31.3 4.7 %collective-permute-start.7 = (f32[16,384]{1,0:T(8,128)S(1)}, f32[16,384]{1,0:T(8,128)S(1)}, u32[]{:S(2)}, u32[]{:S(2)}) collective-permute-start(f32[16,384]{1,0:T(8,128)S(1)} %pair.1.refs_0_), channel_id=1, source_target_pairs={{0,16},{4,20},{8,24},{12,28},{16,0},{20,4},{24,8},{28,12},{1,17},{... | collective-permute-start | bytes 73736 | tf_op jit(solution)/shard_map/ppermute | solution.py:48
  31.3 4.7 %collective-permute-start.8 = (f32[16,384]{1,0:T(8,128)S(1)}, f32[16,384]{1,0:T(8,128)S(1)}, u32[]{:S(2)}, u32[]{:S(2)}) collective-permute-start(f32[16,384]{1,0:T(8,128)S(1)} %pair.1.refs_0_), channel_id=1, source_target_pairs={{0,8},{4,12},{8,0},{12,4},{16,24},{20,28},{24,16},{28,20},{1,9},{5... | collective-permute-start | bytes 73736 | tf_op jit(solution)/shard_map/ppermute | solution.py:48

commit v10 on v9

--- a/solution.py
+++ b/solution.py
@@ -214,11 +214,11 @@
 
 
 def add_kernel(*refs):
-    *terms, out_ref = refs
+    *terms, _, out_ref = refs
     out_ref[...] = functools.reduce(jnp.add, [ref[...] for ref in terms])
 
 
-def forward_kernel(far_ref, sum_ref, out_ref):
+def forward_kernel(far_ref, rest_ref, out_ref):
     half = out_ref.shape[1]
     out_ref[...] = lax.select(is_odd(), far_ref[:, half:], far_ref[:, :half])
 
@@ -254,10 +254,11 @@
 
 def last_kernel(
     tiles_ref, rest_ref, forwarded_ref, query_ref, keys_ref, values_ref,
-    ready_one, ready_other, known_one, known_other, *refs,
+    ready_one, ready_other, known_one, known_other,
+    gated_out, key_out, value_out, mark_ref, one, other, sems,
 ):
-    *terms, gated_out, key_out, value_out, filter_out, one, other, total, sems = refs
-    odd = is_odd()
+    odd = is_odd()
+    mark_ref[...] = jnp.zeros_like(mark_ref)
     group_count, rows, _ = tiles_ref.shape
     half = group_count // 2
     group_width = forwarded_ref.shape[1] // half
@@ -276,8 +277,6 @@
         sems,
         0,
     )
-    total[...] = functools.reduce(jnp.add, [term[...] for term in terms])
-    copies += launch(odd, [(0, total, filter_out), (1, total, filter_out)], sems, len(copies))
     for group in range(half):
         low, high = columns_of(group, group_width), columns_of(group + half, group_width)
         tile = lax.select(
@@ -379,7 +378,7 @@
         in_specs=[WHOLE, ANYWHERE],
         out_specs=WHOLE,
         out_shape=half_block,
-    )(*in_vmem(far), partial)
+    )(*in_vmem(far), rest)
     forwarded = moved(forwarded, "ctx", (1, -1))
 
     cross = call(
@@ -406,27 +405,29 @@
         out_shape=[block] * 2,
     )(*in_vmem(late_tiles, late, swap, far, query, keys, values))
 
-    def add(*terms):
+    def add(*terms, out_shape=sums, after=known_one):
         return call(
             add_kernel,
             "add",
-            in_specs=[WHOLE] * len(terms),
+            in_specs=[WHOLE] * len(terms) + [ANYWHERE],
             out_specs=WHOLE,
-            out_shape=sums,
-        )(*in_vmem(*terms))
+            out_shape=out_shape,
+        )(*in_vmem(*terms), after)
 
     terms = sum_terms(pair_sum, "ctx", add)
-    return call(
+    gated, key_grad, value_grad, mark = call(
         last_kernel,
         "last",
-        in_specs=[WHOLE] * (10 + len(terms)),
-        out_specs=[ANYWHERE] * 4,
-        out_shape=outs + [jax.ShapeDtypeStruct((group_count, taps), f32)],
-        scratch_shapes=[half_block] * 2 + [sums, pltpu.SemaphoreType.DMA((8 + 3 * PARTS,))],
+        in_specs=[WHOLE] * 10,
+        out_specs=[ANYWHERE] * 3 + [WHOLE],
+        out_shape=outs + [pltpu.VMEM((SUBLANES, group_width), f32)],
+        scratch_shapes=[half_block] * 2 + [pltpu.SemaphoreType.DMA((6 + 3 * PARTS,))],
     )(
         *in_vmem(ready_tiles, rest, forwarded, query, keys, values),
-        *in_vmem(ready_one, ready_other, known_one, known_other, *terms),
+        *in_vmem(ready_one, ready_other, known_one, known_other),
     )
+    whole_sums = jax.ShapeDtypeStruct((group_count, taps), f32)
+    return (gated, key_grad, value_grad, add(*terms, out_shape=whole_sums, after=mark))
 
 
 def solution(mesh):

time: 37.6 us -> 36.9 us (0.981)
  waiting for transfers between devices: 7.08 us -> 5.69 us
  Pallas kernels: 9.5 us -> 10.1 us
    ppermute x3, waiting for transfers between devices: 3.53 us -> 2.16 us  [sum_terms(): lax.ppermute(own, axis, [(i, i ^ hop) for i in range(size)])]
    pallas_call x1 -> x2, Pallas kernels: 1.35 us -> 1.96 us  [the longest x1 1.35 us: shards(): call(last_kernel, 'last', in_specs=[WHOLE] * 10, out_specs=[ANYWHERE] * 3...]
  transfers between devices with their start and end apart: 9 -> 9, of which waited for: 4 -> 4; matrix products, arithmetic and copies ran while one was open for 0% -> 0% of each run, Pallas kernels for 18% -> 22%
where the time goes in v10:
time: 36.9 us; the launch traced here: 36.7 us
  starting transfers between devices  20 us (54%)
  Pallas kernels  10.1 us (27%)
  waiting for transfers between devices  5.69 us (15%)
  between operations  0.85 us (2%)
    ppermute x6, starting transfers between devices, moved(): lax.ppermute(block, axis, [pair for pair in route if 0 <= pair[1] < size])  15 us
    ppermute x3, starting transfers between devices, sum_terms(): lax.ppermute(own, axis, [(i, i ^ hop) for i in range(size)])  4.96 us
    ppermute x6, waiting for transfers between devices, moved(): lax.ppermute(block, axis, [pair for pair in route if 0 <= pair[1] < size])  3.53 us
    pallas_call x1, Pallas kernels, shards(): call(functools.partial(tiles_kernel, rows), 'tiles', in_specs=[WHOLE], ou...  2.22 us
    ppermute x3, waiting for transfers between devices, sum_terms(): lax.ppermute(own, axis, [(i, i ^ hop) for i in range(size)])  2.16 us
    pallas_call x1, Pallas kernels, shards(): call(functools.partial(own_kernel, rows), 'own', flops=4 * 10 ** 9, in_sp...  1.6 us
    pallas_call x1, Pallas kernels, shards(): call(last_kernel, 'last', in_specs=[WHOLE] * 10, out_specs=[ANYWHERE] * 3...  1.35 us
    pallas_call x1, Pallas kernels, shards(): call(diagonal_kernel, 'diagonal', in_specs=[ANYWHERE] * 4, out_specs=WHOL...  1.28 us
  transfers between devices with their start and end apart: 9, of which 4 were waited for; matrix products, arithmetic and copies ran while one was open for 0% of the time, Pallas kernels for 22%

profile of v10, /device:TPU:0, one launch (start us, length us, event | category | flops | bytes accessed | tf_op | source)
XLA Modules:
  0.0 36.7 jit_solution(2995997173944897903)
XLA Ops:
  0.7 1.3 %diagonal.1.sent_ref = bf16[128,1024]{1,0:T(8,128)(2,1)S(1)} custom-call(bf16[128,2048]{1,0:T(8,128)(2,1)} %query_ref.7, bf16[128,2048]{1,0:T(8,128)(2,1)} %keys_ref.7, bf16[128,2048]{1,0:T(8,128)(2,1)} %values_ref.7, bf16[128,2048]{1,0:T(8,128)(2,1)} %cotangent_ref.1), custom_call_target="tpu_custom_call" | custom-call | flops 1000000 | bytes 100000 | tf_op jit(solution)/shard_map/diagonal/pallas_call | solution.py:322
  2.0 0.0 copy-start.4
  2.0 0.7 %collective-permute-start = (bf16[128,1024]{1,0:T(8,128)(2,1)S(1)}, bf16[128,1024]{1,0:T(8,128)(2,1)S(1)}, u32[]{:S(2)}, u32[]{:S(2)}) collective-permute-start(bf16[128,1024]{1,0:T(8,128)(2,1)S(1)} %diagonal.1.sent_ref), channel_id=1, source_target_pairs={{4,8},{8,4},{12,16},{16,12},{20,24},{24,20},{5,9},{9,5},{13,17},{1... | collective-permute-start | bytes 786440 | tf_op jit(solution)/shard_map/ppermute | solution.py:35
  2.7 0.3 products.1
  3.0 7.6 %collective-permute-start.1 = (bf16[128,2048]{1,0:T(8,128)(2,1)S(1)}, bf16[128,2048]{1,0:T(8,128)(2,1)S(1)}, u32[]{:S(2)}, u32[]{:S(2)}) collective-permute-start(bf16[128,2048]{1,0:T(8,128)(2,1)S(1)} %get-tuple-element.23.across_ref), channel_id=1, source_target_pairs={{0,8},{8,16},{12,4},{16,24},{20,12},{28,20},{1,9},{9,17},{13,5},{1... | collective-permute-start | bytes 1572872 | tf_op jit(solution)/shard_map/ppermute | solution.py:35
  10.6 1.3 %collective-permute-start.2 = (bf16[128,2048]{1,0:T(8,128)(2,1)S(1)}, bf16[128,2048]{1,0:T(8,128)(2,1)S(1)}, u32[]{:S(2)}, u32[]{:S(2)}) collective-permute-start(bf16[128,2048]{1,0:T(8,128)(2,1)S(1)} %get-tuple-element.22.near_ref), channel_id=1, source_target_pairs={{4,12},{8,0},{12,20},{16,8},{20,28},{24,16},{5,13},{9,1},{13,21},{... | collective-permute-start | bytes 1572872 | tf_op jit(solution)/shard_map/ppermute | solution.py:35
  11.9 2.8 %collective-permute-start.4 = (bf16[128,2048]{1,0:T(8,128)(2,1)S(1)}, bf16[128,2048]{1,0:T(8,128)(2,1)S(1)}, u32[]{:S(2)}, u32[]{:S(2)}) collective-permute-start(bf16[128,2048]{1,0:T(8,128)(2,1)S(1)} %get-tuple-element.23.across_ref), channel_id=1, source_target_pairs={{0,4},{4,0},{8,12},{12,8},{16,20},{20,16},{24,28},{28,24},{1,5},{5... | collective-permute-start | bytes 1572872 | tf_op jit(solution)/shard_map/ppermute | solution.py:35
  14.7 2.2 %tiles.1 = (bf16[16,128,384]{2,1,0:T(8,128)(2,1)S(1)}, bf16[16,128,384]{2,1,0:T(8,128)(2,1)S(1)}) custom-call(bf16[16,384]{1,0:T(8,128)(2,1)S(1)} %copy-done.4), custom_call_target="tpu_custom_call" | custom-call | flops 1000000 | bytes 100000 | tf_op jit(solution)/shard_map/tiles/pallas_call | solution.py:342
  16.9 1.6 %own.1 = (f32[16,384]{1,0:T(8,128)S(1)}, f32[128,2048]{1,0:T(8,128)S(1)}, f32[128,2048]{1,0:T(8,128)S(1)}) custom-call(bf16[16,128,384]{2,1,0:T(8,128)(2,1)S(1)} %get-tuple-element.20.ready_tiles.tiles_ref, bf16[16,128,384]{2,1,0:T(8,128)(2,1)S(1)} %get-tuple-element.21.late_tiles.tiles_ref, bf16[128,2048]{1,0:T(8,128)(2,1)S(1)} %get-tuple-element.22.near_ref, ...), custom_call_target="tpu_custom_call" | custom-call | flops 4000000000 | bytes 100000 | tf_op jit(solution)/shard_map/own/pallas_call | solution.py:349
  18.5 2.9 %collective-permute-done.1.two_ref = bf16[128,2048]{1,0:T(8,128)(2,1)S(1)} collective-permute-done((bf16[128,2048]{1,0:T(8,128)(2,1)S(1)}, bf16[128,2048]{1,0:T(8,128)(2,1)S(1)}, u32[]{:S(2)}, u32[]{:S(2)}) %collective-permute-start.1) | collective-permute-done | bytes 524320 | tf_op jit(solution)/shard_map/ppermute | solution.py:35
  21.5 0.9 %two.1.sum_ref = f32[16,384]{1,0:T(8,128)S(1)} custom-call(f32[16,384]{1,0:T(8,128)S(1)} %get-tuple-element.25.sum_ref, bf16[128,2048]{1,0:T(8,128)(2,1)S(1)} %get-tuple-element.22.near_ref, bf16[128,2048]{1,0:T(8,128)(2,1)S(1)} %collective-permute-done.1.two_ref), custom_call_target="tpu_custom_call" | custom-call | flops 1000000 | bytes 100000 | tf_op jit(solution)/shard_map/two/pallas_call | solution.py:358
  22.3 2.6 %collective-permute-start.5 = (f32[16,384]{1,0:T(8,128)S(1)}, f32[16,384]{1,0:T(8,128)S(1)}, u32[]{:S(2)}, u32[]{:S(2)}) collective-permute-start(f32[16,384]{1,0:T(8,128)S(1)} %two.1.sum_ref), channel_id=1, source_target_pairs={{0,4},{4,0},{8,12},{12,8},{16,20},{20,16},{24,28},{28,24},{1,5},{5... | collective-permute-start | bytes 73736 | tf_op jit(solution)/shard_map/ppermute | solution.py:35
  25.0 0.4 %ready.1 = (f32[128,1024]{1,0:T(8,128)S(1)}, bf16[128,1024]{1,0:T(8,128)(2,1)S(1)}, bf16[128,1024]{1,0:T(8,128)(2,1)S(1)}) custom-call(bf16[16,128,384]{2,1,0:T(8,128)(2,1)S(1)} %get-tuple-element.20.ready_tiles.tiles_ref, f32[128,2048]{1,0:T(8,128)S(1)} %get-tuple-element.24.ready_ref, bf16[128,2048]{1,0:T(8,128)(2,1)S(1)} %collective-permute-done.1.two_ref, ...), custom_call_target="tpu_custom_call" | custom-call | flops 1000000 | bytes 100000 | tf_op jit(solution)/shard_map/ready/pallas_call | solution.py:367
  25.4 0.2 collective-permute-done.2.far_ref
  25.6 0.1 collective-permute-start.3
  25.7 0.4 collective-permute-done.4.swap_ref
  26.1 0.9 %cross.1.cross_ref = f32[16,384]{1,0:T(8,128)S(1)} custom-call(bf16[128,2048]{1,0:T(8,128)(2,1)S(1)} %get-tuple-element.23.across_ref, bf16[128,2048]{1,0:T(8,128)(2,1)S(1)} %collective-permute-done.4.swap_ref), custom_call_target="tpu_custom_call" | custom-call | flops 1000000 | bytes 100000 | tf_op jit(solution)/shard_map/cross/pallas_call | solution.py:384
  27.0 0.0 collective-permute-done.5.other_ref
  27.0 4.3 %collective-permute-start.6 = (f32[16,384]{1,0:T(8,128)S(1)}, f32[16,384]{1,0:T(8,128)S(1)}, u32[]{:S(2)}, u32[]{:S(2)}) collective-permute-start(f32[16,384]{1,0:T(8,128)S(1)} %pair.1.refs_0_), channel_id=1, source_target_pairs={{0,24},{4,28},{8,16},{12,20},{16,8},{20,12},{24,0},{28,4},{1,25},{... | collective-permute-start | bytes 73736 | tf_op jit(solution)/shard_map/ppermute | solution.py:48
  31.3 0.6 %collective-permute-start.8 = (f32[16,384]{1,0:T(8,128)S(1)}, f32[16,384]{1,0:T(8,128)S(1)}, u32[]{:S(2)}, u32[]{:S(2)}) collective-permute-start(f32[16,384]{1,0:T(8,128)S(1)} %pair.1.refs_0_), channel_id=1, source_target_pairs={{0,8},{4,12},{8,0},{12,4},{16,24},{20,28},{24,16},{28,20},{1,9},{5... | collective-permute-start | bytes 73736 | tf_op jit(solution)/shard_map/ppermute | solution.py:48
  32.0 0.5 %known.1 = (bf16[128,2048]{1,0:T(8,128)(2,1)S(1)}, bf16[128,2048]{1,0:T(8,128)(2,1)S(1)}) custom-call(bf16[16,128,384]{2,1,0:T(8,128)(2,1)S(1)} %get-tuple-element.21.late_tiles.tiles_ref, f32[128,2048]{1,0:T(8,128)S(1)} %get-tuple-element.29.late_ref, bf16[128,2048]{1,0:T(8,128)(2,1)S(1)} %collective-permute-done.4.swap_ref, ...), custom_call_target="tpu_custom_call" | custom-call | flops 4000000000 | bytes 100000 | tf_op jit(solution)/shard_map/known/pallas_call | solution.py:399
  32.5 1.3 %last.1 = (bf16[128,2048]{1,0:T(8,128)(2,1)}, bf16[128,2048]{1,0:T(8,128)(2,1)}, bf16[128,2048]{1,0:T(8,128)(2,1)}, f32[8,128]{1,0:T(8,128)S(1)}) custom-call(bf16[16,128,384]{2,1,0:T(8,128)(2,1)S(1)} %get-tuple-element.20.ready_tiles.tiles_ref, f32[128,1024]{1,0:T(8,128)S(1)} %get-tuple-element.26.rest_ref, ...), custom_call_target="tpu_custom_call" | custom-call | flops 1000000 | bytes 100000 | tf_op jit(solution)/shard_map/last/pallas_call | solution.py:418
  33.9 2.2 %collective-permute-done.7.refs_2_ = f32[16,384]{1,0:T(8,128)S(1)} collective-permute-done((f32[16,384]{1,0:T(8,128)S(1)}, f32[16,384]{1,0:T(8,128)S(1)}, u32[]{:S(2)}, u32[]{:S(2)}) %collective-permute-start.7) | collective-permute-done | bytes 24608 | tf_op jit(solution)/shard_map/ppermute | solution.py:48
  36.0 0.6 %add.1 = f32[16,384]{1,0:T(8,128)} custom-call(f32[16,384]{1,0:T(8,128)S(1)} %pair.1.refs_0_, f32[16,384]{1,0:T(8,128)S(1)} %collective-permute-done.6.refs_1_, f32[16,384]{1,0:T(8,128)S(1)} %collective-permute-done.7.refs_2_, f32[16,384]{1,0:T(8,128)S(1)} %collective-permute-done.8.refs_3_, f32[8,128]{1,0:T(8,128)S(1)} %get-tuple-element.35.refs_4_), custom_call_target="tpu_custom_call" | custom-call | flops 1000000 | bytes 100000 | tf_op jit(solution)/shard_map/add/pallas_call | solution.py:409
  (16 shorter events, 0.1 us)
Async XLA Ops:
  0.6 2.0 %copy-start = (bf16[128,2048]{1,0:T(8,128)(2,1)S(1)}, bf16[128,2048]{1,0:T(8,128)(2,1)}, u32[]{:S(2)}) copy-start(bf16[128,2048]{1,0:T(8,128)(2,1)} %query_ref.7) | copy-start | bytes 1572868
  0.6 2.0 %copy-start.1 = (bf16[128,2048]{1,0:T(8,128)(2,1)S(1)}, bf16[128,2048]{1,0:T(8,128)(2,1)}, u32[]{:S(2)}) copy-start(bf16[128,2048]{1,0:T(8,128)(2,1)} %keys_ref.7) | copy-start | bytes 1572868
  0.7 2.0 %copy-start.2 = (bf16[128,2048]{1,0:T(8,128)(2,1)S(1)}, bf16[128,2048]{1,0:T(8,128)(2,1)}, u32[]{:S(2)}) copy-start(bf16[128,2048]{1,0:T(8,128)(2,1)} %values_ref.7) | copy-start | bytes 1572868
  0.7 2.0 %copy-start.3 = (bf16[128,2048]{1,0:T(8,128)(2,1)S(1)}, bf16[128,2048]{1,0:T(8,128)(2,1)}, u32[]{:S(2)}) copy-start(bf16[128,2048]{1,0:T(8,128)(2,1)} %cotangent_ref.1) | copy-start | bytes 1572868
  2.0 12.7 %copy-start.4 = (bf16[16,384]{1,0:T(8,128)(2,1)S(1)}, bf16[16,384]{1,0:T(8,128)(2,1)}, u32[]{:S(2)}) copy-start(bf16[16,384]{1,0:T(8,128)(2,1)} %taps_ref.1) | copy-start | bytes 36868
  2.0 15.0 %collective-permute-start = (bf16[128,1024]{1,0:T(8,128)(2,1)S(1)}, bf16[128,1024]{1,0:T(8,128)(2,1)S(1)}, u32[]{:S(2)}, u32[]{:S(2)}) collective-permute-start(bf16[128,1024]{1,0:T(8,128)(2,1)S(1)} %diagonal.1.sent_ref), channel_id=1, source_target_pairs={{4,8},{8,4},{12,16},{16,12},{20,24},{24,20},{5,9},{9,5},{13,17},{1... | collective-permute-start | bytes 786440 | tf_op jit(solution)/shard_map/ppermute | solution.py:35
  3.0 18.4 %collective-permute-start.1 = (bf16[128,2048]{1,0:T(8,128)(2,1)S(1)}, bf16[128,2048]{1,0:T(8,128)(2,1)S(1)}, u32[]{:S(2)}, u32[]{:S(2)}) collective-permute-start(bf16[128,2048]{1,0:T(8,128)(2,1)S(1)} %get-tuple-element.23.across_ref), channel_id=1, source_target_pairs={{0,8},{8,16},{12,4},{16,24},{20,12},{28,20},{1,9},{9,17},{13,5},{1... | collective-permute-start | bytes 1572872 | tf_op jit(solution)/shard_map/ppermute | solution.py:35
  10.6 15.0 %collective-permute-start.2 = (bf16[128,2048]{1,0:T(8,128)(2,1)S(1)}, bf16[128,2048]{1,0:T(8,128)(2,1)S(1)}, u32[]{:S(2)}, u32[]{:S(2)}) collective-permute-start(bf16[128,2048]{1,0:T(8,128)(2,1)S(1)} %get-tuple-element.22.near_ref), channel_id=1, source_target_pairs={{4,12},{8,0},{12,20},{16,8},{20,28},{24,16},{5,13},{9,1},{13,21},{... | collective-permute-start | bytes 1572872 | tf_op jit(solution)/shard_map/ppermute | solution.py:35
  11.9 14.2 %collective-permute-start.4 = (bf16[128,2048]{1,0:T(8,128)(2,1)S(1)}, bf16[128,2048]{1,0:T(8,128)(2,1)S(1)}, u32[]{:S(2)}, u32[]{:S(2)}) collective-permute-start(bf16[128,2048]{1,0:T(8,128)(2,1)S(1)} %get-tuple-element.23.across_ref), channel_id=1, source_target_pairs={{0,4},{4,0},{8,12},{12,8},{16,20},{20,16},{24,28},{28,24},{1,5},{5... | collective-permute-start | bytes 1572872 | tf_op jit(solution)/shard_map/ppermute | solution.py:35
  22.3 4.6 %collective-permute-start.5 = (f32[16,384]{1,0:T(8,128)S(1)}, f32[16,384]{1,0:T(8,128)S(1)}, u32[]{:S(2)}, u32[]{:S(2)}) collective-permute-start(f32[16,384]{1,0:T(8,128)S(1)} %two.1.sum_ref), channel_id=1, source_target_pairs={{0,4},{4,0},{8,12},{12,8},{16,20},{20,16},{24,28},{28,24},{1,5},{5... | collective-permute-start | bytes 73736 | tf_op jit(solution)/shard_map/ppermute | solution.py:35
  25.6 6.9 %collective-permute-start.3 = (bf16[128,1024]{1,0:T(8,128)(2,1)S(1)}, bf16[128,1024]{1,0:T(8,128)(2,1)S(1)}, u32[]{:S(2)}, u32[]{:S(2)}) collective-permute-start(bf16[128,1024]{1,0:T(8,128)(2,1)S(1)} %forward.1), channel_id=1, source_target_pairs={{0,4},{4,0},{8,12},{12,8},{16,20},{20,16},{24,28},{28,24},{1,5},{5... | collective-permute-start | bytes 786440 | tf_op jit(solution)/shard_map/ppermute | solution.py:35
  27.0 6.9 %collective-permute-start.6 = (f32[16,384]{1,0:T(8,128)S(1)}, f32[16,384]{1,0:T(8,128)S(1)}, u32[]{:S(2)}, u32[]{:S(2)}) collective-permute-start(f32[16,384]{1,0:T(8,128)S(1)} %pair.1.refs_0_), channel_id=1, source_target_pairs={{0,24},{4,28},{8,16},{12,20},{16,8},{20,12},{24,0},{28,4},{1,25},{... | collective-permute-start | bytes 73736 | tf_op jit(solution)/shard_map/ppermute | solution.py:48
  31.3 4.7 %collective-permute-start.7 = (f32[16,384]{1,0:T(8,128)S(1)}, f32[16,384]{1,0:T(8,128)S(1)}, u32[]{:S(2)}, u32[]{:S(2)}) collective-permute-start(f32[16,384]{1,0:T(8,128)S(1)} %pair.1.refs_0_), channel_id=1, source_target_pairs={{0,16},{4,20},{8,24},{12,28},{16,0},{20,4},{24,8},{28,12},{1,17},{... | collective-permute-start | bytes 73736 | tf_op jit(solution)/shard_map/ppermute | solution.py:48
  31.3 4.7 %collective-permute-start.8 = (f32[16,384]{1,0:T(8,128)S(1)}, f32[16,384]{1,0:T(8,128)S(1)}, u32[]{:S(2)}, u32[]{:S(2)}) collective-permute-start(f32[16,384]{1,0:T(8,128)S(1)} %pair.1.refs_0_), channel_id=1, source_target_pairs={{0,8},{4,12},{8,0},{12,4},{16,24},{20,28},{24,16},{28,20},{1,9},{5... | collective-permute-start | bytes 73736 | tf_op jit(solution)/shard_map/ppermute | solution.py:48

commit v11 on v10

--- a/solution.py
+++ b/solution.py
@@ -66,12 +66,12 @@
     return slice(group * width, (group + 1) * width)
 
 
-def launch(odd, moves, sems, used):
+def launch(odd, moves, sems, used, priority=0):
     copies = [(*move, sems.at[used + place]) for place, move in enumerate(moves)]
     for parity, source, target, sem in copies:
         @pl.when(odd if parity else jnp.logical_not(odd))
         def _():
-            pltpu.make_async_copy(source, target, sem).start()
+            pltpu.make_async_copy(source, target, sem).start(priority=priority)
     return copies
 
 
@@ -93,21 +93,21 @@
 
 def diagonal_kernel(query_hbm, keys_hbm, values_hbm, cotangent_hbm, out_ref, left, right, sems):
     odd = is_odd()
-    half = out_ref.shape[1]
-    low, high = pl.ds(0, half), pl.ds(half, half)
-    copies = launch(
-        odd,
-        [
-            (1, keys_hbm.at[:, low], left),
-            (1, values_hbm.at[:, low], right),
-            (0, cotangent_hbm.at[:, high], left),
-            (0, query_hbm.at[:, high], right),
-        ],
-        sems,
-        0,
-    )
-    finish(odd, copies)
-    out_ref[...] = product(left[...], right[...])
+    rows, half = out_ref.shape
+    size = rows // PARTS
+    pieces = []
+    for piece in range(PARTS):
+        lines, low, high = pl.ds(piece * size, size), pl.ds(0, half), pl.ds(half, half)
+        moves = [
+            (1, keys_hbm.at[lines, low], left.at[lines]),
+            (1, values_hbm.at[lines, low], right.at[lines]),
+            (0, cotangent_hbm.at[lines, high], left.at[lines]),
+            (0, query_hbm.at[lines, high], right.at[lines]),
+        ]
+        pieces.append((lines, launch(odd, moves, sems, 4 * piece, priority=1)))
+    for lines, copies in pieces:
+        finish(odd, copies)
+        out_ref[lines, :] = product(left[lines, :], right[lines, :])
 
 
 def products_kernel(query_ref, keys_ref, values_ref, cotangent_ref, sent_ref, near_ref, across_ref):
@@ -325,7 +325,7 @@
         in_specs=[ANYWHERE] * 4,
         out_specs=WHOLE,
         out_shape=half_block,
-        scratch_shapes=[half_block] * 2 + [pltpu.SemaphoreType.DMA((4,))],
+        scratch_shapes=[half_block] * 2 + [pltpu.SemaphoreType.DMA((4 * PARTS,))],
     )(*in_hbm(query, keys, values, cotangent))
     diagonal = moved(sent, "ctx", (-1, 1))
     near, across = call(

time: 36.9 us -> 36.9 us (level)
  no operation moved by 1% of the time
where the time goes in v11:
time: 36.9 us; the launch traced here: 36.7 us
  starting transfers between devices  20 us (54%)
  Pallas kernels  10.2 us (28%)
  waiting for transfers between devices  5.69 us (15%)
  between operations  0.85 us (2%)
    ppermute x6, starting transfers between devices, moved(): lax.ppermute(block, axis, [pair for pair in route if 0 <= pair[1] < size])  15 us
    ppermute x3, starting transfers between devices, sum_terms(): lax.ppermute(own, axis, [(i, i ^ hop) for i in range(size)])  4.96 us
    ppermute x6, waiting for transfers between devices, moved(): lax.ppermute(block, axis, [pair for pair in route if 0 <= pair[1] < size])  3.53 us
    pallas_call x1, Pallas kernels, shards(): call(functools.partial(tiles_kernel, rows), 'tiles', in_specs=[WHOLE], ou...  2.22 us
    ppermute x3, waiting for transfers between devices, sum_terms(): lax.ppermute(own, axis, [(i, i ^ hop) for i in range(size)])  2.16 us
    pallas_call x1, Pallas kernels, shards(): call(functools.partial(own_kernel, rows), 'own', flops=4 * 10 ** 9, in_sp...  1.6 us
    pallas_call x1, Pallas kernels, shards(): call(diagonal_kernel, 'diagonal', in_specs=[ANYWHERE] * 4, out_specs=WHOL...  1.35 us
    pallas_call x1, Pallas kernels, shards(): call(last_kernel, 'last', in_specs=[WHOLE] * 10, out_specs=[ANYWHERE] * 3...  1.35 us
  transfers between devices with their start and end apart: 9, of which 4 were waited for; matrix products, arithmetic and copies ran while one was open for 0% of the time, Pallas kernels for 22%

profile of v11, /device:TPU:0, one launch (start us, length us, event | category | flops | bytes accessed | tf_op | source)
XLA Modules:
  0.0 36.7 jit_solution(8350827620664947289)
XLA Ops:
  0.7 1.3 %diagonal.1.sent_ref = bf16[128,1024]{1,0:T(8,128)(2,1)S(1)} custom-call(bf16[128,2048]{1,0:T(8,128)(2,1)} %query_ref.7, bf16[128,2048]{1,0:T(8,128)(2,1)} %keys_ref.7, bf16[128,2048]{1,0:T(8,128)(2,1)} %values_ref.7, bf16[128,2048]{1,0:T(8,128)(2,1)} %cotangent_ref.1), custom_call_target="tpu_custom_call" | custom-call | flops 1000000 | bytes 100000 | tf_op jit(solution)/shard_map/diagonal/pallas_call | solution.py:322
  2.0 0.0 copy-start.4
  2.0 0.7 %collective-permute-start = (bf16[128,1024]{1,0:T(8,128)(2,1)S(1)}, bf16[128,1024]{1,0:T(8,128)(2,1)S(1)}, u32[]{:S(2)}, u32[]{:S(2)}) collective-permute-start(bf16[128,1024]{1,0:T(8,128)(2,1)S(1)} %diagonal.1.sent_ref), channel_id=1, source_target_pairs={{4,8},{8,4},{12,16},{16,12},{20,24},{24,20},{5,9},{9,5},{13,17},{1... | collective-permute-start | bytes 786440 | tf_op jit(solution)/shard_map/ppermute | solution.py:35
  2.8 0.3 products.1
  3.1 7.6 %collective-permute-start.1 = (bf16[128,2048]{1,0:T(8,128)(2,1)S(1)}, bf16[128,2048]{1,0:T(8,128)(2,1)S(1)}, u32[]{:S(2)}, u32[]{:S(2)}) collective-permute-start(bf16[128,2048]{1,0:T(8,128)(2,1)S(1)} %get-tuple-element.23.across_ref), channel_id=1, source_target_pairs={{0,8},{8,16},{12,4},{16,24},{20,12},{28,20},{1,9},{9,17},{13,5},{1... | collective-permute-start | bytes 1572872 | tf_op jit(solution)/shard_map/ppermute | solution.py:35
  10.7 1.3 %collective-permute-start.2 = (bf16[128,2048]{1,0:T(8,128)(2,1)S(1)}, bf16[128,2048]{1,0:T(8,128)(2,1)S(1)}, u32[]{:S(2)}, u32[]{:S(2)}) collective-permute-start(bf16[128,2048]{1,0:T(8,128)(2,1)S(1)} %get-tuple-element.22.near_ref), channel_id=1, source_target_pairs={{4,12},{8,0},{12,20},{16,8},{20,28},{24,16},{5,13},{9,1},{13,21},{... | collective-permute-start | bytes 1572872 | tf_op jit(solution)/shard_map/ppermute | solution.py:35
  12.0 2.8 %collective-permute-start.4 = (bf16[128,2048]{1,0:T(8,128)(2,1)S(1)}, bf16[128,2048]{1,0:T(8,128)(2,1)S(1)}, u32[]{:S(2)}, u32[]{:S(2)}) collective-permute-start(bf16[128,2048]{1,0:T(8,128)(2,1)S(1)} %get-tuple-element.23.across_ref), channel_id=1, source_target_pairs={{0,4},{4,0},{8,12},{12,8},{16,20},{20,16},{24,28},{28,24},{1,5},{5... | collective-permute-start | bytes 1572872 | tf_op jit(solution)/shard_map/ppermute | solution.py:35
  14.8 2.2 %tiles.1 = (bf16[16,128,384]{2,1,0:T(8,128)(2,1)S(1)}, bf16[16,128,384]{2,1,0:T(8,128)(2,1)S(1)}) custom-call(bf16[16,384]{1,0:T(8,128)(2,1)S(1)} %copy-done.4), custom_call_target="tpu_custom_call" | custom-call | flops 1000000 | bytes 100000 | tf_op jit(solution)/shard_map/tiles/pallas_call | solution.py:342
  17.0 1.6 %own.1 = (f32[16,384]{1,0:T(8,128)S(1)}, f32[128,2048]{1,0:T(8,128)S(1)}, f32[128,2048]{1,0:T(8,128)S(1)}) custom-call(bf16[16,128,384]{2,1,0:T(8,128)(2,1)S(1)} %get-tuple-element.20.ready_tiles.tiles_ref, bf16[16,128,384]{2,1,0:T(8,128)(2,1)S(1)} %get-tuple-element.21.late_tiles.tiles_ref, bf16[128,2048]{1,0:T(8,128)(2,1)S(1)} %get-tuple-element.22.near_ref, ...), custom_call_target="tpu_custom_call" | custom-call | flops 4000000000 | bytes 100000 | tf_op jit(solution)/shard_map/own/pallas_call | solution.py:349
  18.6 2.9 %collective-permute-done.1.two_ref = bf16[128,2048]{1,0:T(8,128)(2,1)S(1)} collective-permute-done((bf16[128,2048]{1,0:T(8,128)(2,1)S(1)}, bf16[128,2048]{1,0:T(8,128)(2,1)S(1)}, u32[]{:S(2)}, u32[]{:S(2)}) %collective-permute-start.1) | collective-permute-done | bytes 524320 | tf_op jit(solution)/shard_map/ppermute | solution.py:35
  21.5 0.9 %two.1.sum_ref = f32[16,384]{1,0:T(8,128)S(1)} custom-call(f32[16,384]{1,0:T(8,128)S(1)} %get-tuple-element.25.sum_ref, bf16[128,2048]{1,0:T(8,128)(2,1)S(1)} %get-tuple-element.22.near_ref, bf16[128,2048]{1,0:T(8,128)(2,1)S(1)} %collective-permute-done.1.two_ref), custom_call_target="tpu_custom_call" | custom-call | flops 1000000 | bytes 100000 | tf_op jit(solution)/shard_map/two/pallas_call | solution.py:358
  22.4 2.6 %collective-permute-start.5 = (f32[16,384]{1,0:T(8,128)S(1)}, f32[16,384]{1,0:T(8,128)S(1)}, u32[]{:S(2)}, u32[]{:S(2)}) collective-permute-start(f32[16,384]{1,0:T(8,128)S(1)} %two.1.sum_ref), channel_id=1, source_target_pairs={{0,4},{4,0},{8,12},{12,8},{16,20},{20,16},{24,28},{28,24},{1,5},{5... | collective-permute-start | bytes 73736 | tf_op jit(solution)/shard_map/ppermute | solution.py:35
  25.0 0.4 %ready.1 = (f32[128,1024]{1,0:T(8,128)S(1)}, bf16[128,1024]{1,0:T(8,128)(2,1)S(1)}, bf16[128,1024]{1,0:T(8,128)(2,1)S(1)}) custom-call(bf16[16,128,384]{2,1,0:T(8,128)(2,1)S(1)} %get-tuple-element.20.ready_tiles.tiles_ref, f32[128,2048]{1,0:T(8,128)S(1)} %get-tuple-element.24.ready_ref, bf16[128,2048]{1,0:T(8,128)(2,1)S(1)} %collective-permute-done.1.two_ref, ...), custom_call_target="tpu_custom_call" | custom-call | flops 1000000 | bytes 100000 | tf_op jit(solution)/shard_map/ready/pallas_call | solution.py:367
  25.4 0.3 collective-permute-done.2.far_ref
  25.7 0.1 collective-permute-start.3
  25.8 0.4 collective-permute-done.4.swap_ref
  26.1 0.9 %cross.1.cross_ref = f32[16,384]{1,0:T(8,128)S(1)} custom-call(bf16[128,2048]{1,0:T(8,128)(2,1)S(1)} %get-tuple-element.23.across_ref, bf16[128,2048]{1,0:T(8,128)(2,1)S(1)} %collective-permute-done.4.swap_ref), custom_call_target="tpu_custom_call" | custom-call | flops 1000000 | bytes 100000 | tf_op jit(solution)/shard_map/cross/pallas_call | solution.py:384
  27.0 0.0 collective-permute-done.5.other_ref
  27.1 4.3 %collective-permute-start.6 = (f32[16,384]{1,0:T(8,128)S(1)}, f32[16,384]{1,0:T(8,128)S(1)}, u32[]{:S(2)}, u32[]{:S(2)}) collective-permute-start(f32[16,384]{1,0:T(8,128)S(1)} %pair.1.refs_0_), channel_id=1, source_target_pairs={{0,24},{4,28},{8,16},{12,20},{16,8},{20,12},{24,0},{28,4},{1,25},{... | collective-permute-start | bytes 73736 | tf_op jit(solution)/shard_map/ppermute | solution.py:48
  31.4 0.6 %collective-permute-start.8 = (f32[16,384]{1,0:T(8,128)S(1)}, f32[16,384]{1,0:T(8,128)S(1)}, u32[]{:S(2)}, u32[]{:S(2)}) collective-permute-start(f32[16,384]{1,0:T(8,128)S(1)} %pair.1.refs_0_), channel_id=1, source_target_pairs={{0,8},{4,12},{8,0},{12,4},{16,24},{20,28},{24,16},{28,20},{1,9},{5... | collective-permute-start | bytes 73736 | tf_op jit(solution)/shard_map/ppermute | solution.py:48
  32.0 0.5 %known.1 = (bf16[128,2048]{1,0:T(8,128)(2,1)S(1)}, bf16[128,2048]{1,0:T(8,128)(2,1)S(1)}) custom-call(bf16[16,128,384]{2,1,0:T(8,128)(2,1)S(1)} %get-tuple-element.21.late_tiles.tiles_ref, f32[128,2048]{1,0:T(8,128)S(1)} %get-tuple-element.29.late_ref, bf16[128,2048]{1,0:T(8,128)(2,1)S(1)} %collective-permute-done.4.swap_ref, ...), custom_call_target="tpu_custom_call" | custom-call | flops 4000000000 | bytes 100000 | tf_op jit(solution)/shard_map/known/pallas_call | solution.py:399
  32.6 1.3 %last.1 = (bf16[128,2048]{1,0:T(8,128)(2,1)}, bf16[128,2048]{1,0:T(8,128)(2,1)}, bf16[128,2048]{1,0:T(8,128)(2,1)}, f32[8,128]{1,0:T(8,128)S(1)}) custom-call(bf16[16,128,384]{2,1,0:T(8,128)(2,1)S(1)} %get-tuple-element.20.ready_tiles.tiles_ref, f32[128,1024]{1,0:T(8,128)S(1)} %get-tuple-element.26.rest_ref, ...), custom_call_target="tpu_custom_call" | custom-call | flops 1000000 | bytes 100000 | tf_op jit(solution)/shard_map/last/pallas_call | solution.py:418
  34.0 2.2 %collective-permute-done.7.refs_2_ = f32[16,384]{1,0:T(8,128)S(1)} collective-permute-done((f32[16,384]{1,0:T(8,128)S(1)}, f32[16,384]{1,0:T(8,128)S(1)}, u32[]{:S(2)}, u32[]{:S(2)}) %collective-permute-start.7) | collective-permute-done | bytes 24608 | tf_op jit(solution)/shard_map/ppermute | solution.py:48
  36.1 0.6 %add.1 = f32[16,384]{1,0:T(8,128)} custom-call(f32[16,384]{1,0:T(8,128)S(1)} %pair.1.refs_0_, f32[16,384]{1,0:T(8,128)S(1)} %collective-permute-done.6.refs_1_, f32[16,384]{1,0:T(8,128)S(1)} %collective-permute-done.7.refs_2_, f32[16,384]{1,0:T(8,128)S(1)} %collective-permute-done.8.refs_3_, f32[8,128]{1,0:T(8,128)S(1)} %get-tuple-element.35.refs_4_), custom_call_target="tpu_custom_call" | custom-call | flops 1000000 | bytes 100000 | tf_op jit(solution)/shard_map/add/pallas_call | solution.py:409
  (16 shorter events, 0.1 us)
Async XLA Ops:
  0.6 2.1 %copy-start = (bf16[128,2048]{1,0:T(8,128)(2,1)S(1)}, bf16[128,2048]{1,0:T(8,128)(2,1)}, u32[]{:S(2)}) copy-start(bf16[128,2048]{1,0:T(8,128)(2,1)} %query_ref.7) | copy-start | bytes 1572868
  0.6 2.1 %copy-start.1 = (bf16[128,2048]{1,0:T(8,128)(2,1)S(1)}, bf16[128,2048]{1,0:T(8,128)(2,1)}, u32[]{:S(2)}) copy-start(bf16[128,2048]{1,0:T(8,128)(2,1)} %keys_ref.7) | copy-start | bytes 1572868
  0.7 2.1 %copy-start.2 = (bf16[128,2048]{1,0:T(8,128)(2,1)S(1)}, bf16[128,2048]{1,0:T(8,128)(2,1)}, u32[]{:S(2)}) copy-start(bf16[128,2048]{1,0:T(8,128)(2,1)} %values_ref.7) | copy-start | bytes 1572868
  0.7 2.1 %copy-start.3 = (bf16[128,2048]{1,0:T(8,128)(2,1)S(1)}, bf16[128,2048]{1,0:T(8,128)(2,1)}, u32[]{:S(2)}) copy-start(bf16[128,2048]{1,0:T(8,128)(2,1)} %cotangent_ref.1) | copy-start | bytes 1572868
  2.0 12.7 %copy-start.4 = (bf16[16,384]{1,0:T(8,128)(2,1)S(1)}, bf16[16,384]{1,0:T(8,128)(2,1)}, u32[]{:S(2)}) copy-start(bf16[16,384]{1,0:T(8,128)(2,1)} %taps_ref.1) | copy-start | bytes 36868
  2.0 15.0 %collective-permute-start = (bf16[128,1024]{1,0:T(8,128)(2,1)S(1)}, bf16[128,1024]{1,0:T(8,128)(2,1)S(1)}, u32[]{:S(2)}, u32[]{:S(2)}) collective-permute-start(bf16[128,1024]{1,0:T(8,128)(2,1)S(1)} %diagonal.1.sent_ref), channel_id=1, source_target_pairs={{4,8},{8,4},{12,16},{16,12},{20,24},{24,20},{5,9},{9,5},{13,17},{1... | collective-permute-start | bytes 786440 | tf_op jit(solution)/shard_map/ppermute | solution.py:35
  3.1 18.4 %collective-permute-start.1 = (bf16[128,2048]{1,0:T(8,128)(2,1)S(1)}, bf16[128,2048]{1,0:T(8,128)(2,1)S(1)}, u32[]{:S(2)}, u32[]{:S(2)}) collective-permute-start(bf16[128,2048]{1,0:T(8,128)(2,1)S(1)} %get-tuple-element.23.across_ref), channel_id=1, source_target_pairs={{0,8},{8,16},{12,4},{16,24},{20,12},{28,20},{1,9},{9,17},{13,5},{1... | collective-permute-start | bytes 1572872 | tf_op jit(solution)/shard_map/ppermute | solution.py:35
  10.7 15.0 %collective-permute-start.2 = (bf16[128,2048]{1,0:T(8,128)(2,1)S(1)}, bf16[128,2048]{1,0:T(8,128)(2,1)S(1)}, u32[]{:S(2)}, u32[]{:S(2)}) collective-permute-start(bf16[128,2048]{1,0:T(8,128)(2,1)S(1)} %get-tuple-element.22.near_ref), channel_id=1, source_target_pairs={{4,12},{8,0},{12,20},{16,8},{20,28},{24,16},{5,13},{9,1},{13,21},{... | collective-permute-start | bytes 1572872 | tf_op jit(solution)/shard_map/ppermute | solution.py:35
  12.0 14.2 %collective-permute-start.4 = (bf16[128,2048]{1,0:T(8,128)(2,1)S(1)}, bf16[128,2048]{1,0:T(8,128)(2,1)S(1)}, u32[]{:S(2)}, u32[]{:S(2)}) collective-permute-start(bf16[128,2048]{1,0:T(8,128)(2,1)S(1)} %get-tuple-element.23.across_ref), channel_id=1, source_target_pairs={{0,4},{4,0},{8,12},{12,8},{16,20},{20,16},{24,28},{28,24},{1,5},{5... | collective-permute-start | bytes 1572872 | tf_op jit(solution)/shard_map/ppermute | solution.py:35
  22.4 4.6 %collective-permute-start.5 = (f32[16,384]{1,0:T(8,128)S(1)}, f32[16,384]{1,0:T(8,128)S(1)}, u32[]{:S(2)}, u32[]{:S(2)}) collective-permute-start(f32[16,384]{1,0:T(8,128)S(1)} %two.1.sum_ref), channel_id=1, source_target_pairs={{0,4},{4,0},{8,12},{12,8},{16,20},{20,16},{24,28},{28,24},{1,5},{5... | collective-permute-start | bytes 73736 | tf_op jit(solution)/shard_map/ppermute | solution.py:35
  25.7 6.9 %collective-permute-start.3 = (bf16[128,1024]{1,0:T(8,128)(2,1)S(1)}, bf16[128,1024]{1,0:T(8,128)(2,1)S(1)}, u32[]{:S(2)}, u32[]{:S(2)}) collective-permute-start(bf16[128,1024]{1,0:T(8,128)(2,1)S(1)} %forward.1), channel_id=1, source_target_pairs={{0,4},{4,0},{8,12},{12,8},{16,20},{20,16},{24,28},{28,24},{1,5},{5... | collective-permute-start | bytes 786440 | tf_op jit(solution)/shard_map/ppermute | solution.py:35
  27.1 6.9 %collective-permute-start.6 = (f32[16,384]{1,0:T(8,128)S(1)}, f32[16,384]{1,0:T(8,128)S(1)}, u32[]{:S(2)}, u32[]{:S(2)}) collective-permute-start(f32[16,384]{1,0:T(8,128)S(1)} %pair.1.refs_0_), channel_id=1, source_target_pairs={{0,24},{4,28},{8,16},{12,20},{16,8},{20,12},{24,0},{28,4},{1,25},{... | collective-permute-start | bytes 73736 | tf_op jit(solution)/shard_map/ppermute | solution.py:48
  31.4 4.7 %collective-permute-start.7 = (f32[16,384]{1,0:T(8,128)S(1)}, f32[16,384]{1,0:T(8,128)S(1)}, u32[]{:S(2)}, u32[]{:S(2)}) collective-permute-start(f32[16,384]{1,0:T(8,128)S(1)} %pair.1.refs_0_), channel_id=1, source_target_pairs={{0,16},{4,20},{8,24},{12,28},{16,0},{20,4},{24,8},{28,12},{1,17},{... | collective-permute-start | bytes 73736 | tf_op jit(solution)/shard_map/ppermute | solution.py:48
  31.4 4.7 %collective-permute-start.8 = (f32[16,384]{1,0:T(8,128)S(1)}, f32[16,384]{1,0:T(8,128)S(1)}, u32[]{:S(2)}, u32[]{:S(2)}) collective-permute-start(f32[16,384]{1,0:T(8,128)S(1)} %pair.1.refs_0_), channel_id=1, source_target_pairs={{0,8},{4,12},{8,0},{12,4},{16,24},{20,28},{24,16},{28,20},{1,9},{5... | collective-permute-start | bytes 73736 | tf_op jit(solution)/shard_map/ppermute | solution.py:48

commit v12 on v10

--- a/solution.py
+++ b/solution.py
@@ -54,6 +54,14 @@
     return lax.rem(lax.axis_index("ctx"), 2) == 1
 
 
+def is_ahead():
+    return lax.rem(lax.axis_index("grp"), 2) == 1
+
+
+def early_groups(group_count):
+    return 3 * group_count // 4
+
+
 def product(left, right):
     return (left.astype(jnp.float32) * right.astype(jnp.float32)).astype(jnp.bfloat16)
 
@@ -91,9 +99,13 @@
     return functools.reduce(jnp.add, lines)
 
 
-def diagonal_kernel(query_hbm, keys_hbm, values_hbm, cotangent_hbm, out_ref, left, right, sems):
-    odd = is_odd()
-    half = out_ref.shape[1]
+def diagonal_kernel(
+    query_hbm, keys_hbm, values_hbm, cotangent_hbm, taps_hbm, out_ref, ready_tiles, late_tiles,
+    left, right, taps_ref, sems,
+):
+    odd = is_odd()
+    rows, half = out_ref.shape
+    group_count = taps_ref.shape[0]
     low, high = pl.ds(0, half), pl.ds(half, half)
     copies = launch(
         odd,
@@ -106,6 +118,14 @@
         sems,
         0,
     )
+
+    @pl.when(is_ahead())
+    def _():
+        copy = pltpu.make_async_copy(taps_hbm, taps_ref, sems.at[4])
+        copy.start()
+        copy.wait()
+        build_tiles(odd, rows, taps_ref, ready_tiles, late_tiles, range(early_groups(group_count)))
+
     finish(odd, copies)
     out_ref[...] = product(left[...], right[...])
 
@@ -118,10 +138,9 @@
     across_ref[...] = lax.select(odd, grad, prod)
 
 
-def tiles_kernel(rows, taps_ref, ready_tiles, late_tiles):
-    odd = is_odd()
-    group_count, width = taps_ref.shape
-    for group in range(group_count):
+def build_tiles(odd, rows, taps_ref, ready_tiles, late_tiles, groups):
+    width = taps_ref.shape[1]
+    for group in groups:
         row = taps_ref[group : group + 1, :].astype(jnp.float32)
         spread = jnp.concatenate(
             [jnp.zeros((SUBLANES, rows), jnp.float32), jnp.broadcast_to(row, (SUBLANES, width))],
@@ -137,6 +156,23 @@
         turned = jnp.concatenate(turned, axis=1)
         ready_tiles[group] = lax.select(odd, band, turned).astype(jnp.bfloat16)
         late_tiles[group] = lax.select(odd, turned, band).astype(jnp.bfloat16)
+
+
+def tiles_kernel(rows, taps_ref, ready_in, late_in, ready_tiles, late_tiles):
+    odd = is_odd()
+    group_count = taps_ref.shape[0]
+    early = early_groups(group_count)
+
+    @pl.when(jnp.logical_not(is_ahead()))
+    def _():
+        build_tiles(odd, rows, taps_ref, ready_tiles, late_tiles, range(early))
+
+    @pl.when(is_ahead())
+    def _():
+        ready_tiles[:early] = ready_in[:early]
+        late_tiles[:early] = late_in[:early]
+
+    build_tiles(odd, rows, taps_ref, ready_tiles, late_tiles, range(early, group_count))
 
 
 def own_kernel(
@@ -319,14 +355,15 @@
     tiles, sums = pltpu.VMEM((group_count, rows, taps), bf16), pltpu.VMEM((group_count, taps), f32)
     outs = [jax.ShapeDtypeStruct((rows, local_width), bf16)] * 3
 
-    sent = call(
+    sent, ready_tiles, late_tiles = call(
         diagonal_kernel,
         "diagonal",
-        in_specs=[ANYWHERE] * 4,
-        out_specs=WHOLE,
-        out_shape=half_block,
-        scratch_shapes=[half_block] * 2 + [pltpu.SemaphoreType.DMA((4,))],
-    )(*in_hbm(query, keys, values, cotangent))
+        in_specs=[ANYWHERE] * 5,
+        out_specs=[WHOLE] * 3,
+        out_shape=[half_block, tiles, tiles],
+        scratch_shapes=[half_block] * 2
+        + [pltpu.VMEM((group_count, taps), bf16), pltpu.SemaphoreType.DMA((5,))],
+    )(*in_hbm(query, keys, values, cotangent, filter_taps))
     diagonal = moved(sent, "ctx", (-1, 1))
     near, across = call(
         products_kernel,
@@ -342,10 +379,10 @@
     ready_tiles, late_tiles = call(
         functools.partial(tiles_kernel, rows),
         "tiles",
-        in_specs=[WHOLE],
+        in_specs=[WHOLE] * 3,
         out_specs=[WHOLE] * 2,
         out_shape=[tiles] * 2,
-    )(*in_vmem(filter_taps))
+    )(*in_vmem(filter_taps, ready_tiles, late_tiles))
     partial, late, ready = call(
         functools.partial(own_kernel, rows),
         "own",

time: 36.9 us -> 38 us (1.030)
  waiting for transfers between devices: 5.69 us -> 6.87 us
    ppermute x6, waiting for transfers between devices: 3.53 us -> 6.49 us  [moved(): lax.ppermute(block, axis, [pair for pair in route if 0 <= pair[1] < size])]
    ppermute x3, waiting for transfers between devices: 2.16 us -> 0.38 us  [sum_terms(): lax.ppermute(own, axis, [(i, i ^ hop) for i in range(size)])]
  transfers between devices with their start and end apart: 9 -> 9, of which waited for: 4 -> 5; matrix products, arithmetic and copies ran while one was open for 0% -> 0% of each run, Pallas kernels for 22% -> 22%
where the time goes in v12:
time: 38 us; the launch traced here: 37.7 us
  starting transfers between devices  19.8 us (52%)
  Pallas kernels  10.2 us (27%)
  waiting for transfers between devices  6.87 us (18%)
  between operations  0.84 us (2%)
    ppermute x6, starting transfers between devices, moved(): lax.ppermute(block, axis, [pair for pair in route if 0 <= pair[1] < size])  15 us
    ppermute x6, waiting for transfers between devices, moved(): lax.ppermute(block, axis, [pair for pair in route if 0 <= pair[1] < size])  6.49 us
    ppermute x3, starting transfers between devices, sum_terms(): lax.ppermute(own, axis, [(i, i ^ hop) for i in range(size)])  4.77 us
    pallas_call x1, Pallas kernels, shards(): call(functools.partial(tiles_kernel, rows), 'tiles', in_specs=[WHOLE] * 3...  2.24 us
    pallas_call x1, Pallas kernels, shards(): call(functools.partial(own_kernel, rows), 'own', flops=4 * 10 ** 9, in_sp...  1.61 us
    pallas_call x1, Pallas kernels, shards(): call(last_kernel, 'last', in_specs=[WHOLE] * 10, out_specs=[ANYWHERE] * 3...  1.33 us
    pallas_call x1, Pallas kernels, shards(): call(diagonal_kernel, 'diagonal', in_specs=[ANYWHERE] * 5, out_specs=[WHO...  1.29 us
    pallas_call x1, Pallas kernels, shards(): call(functools.partial(two_kernel, rows), 'two', in_specs=[WHOLE] * 3, ou...  0.89 us
  transfers between devices with their start and end apart: 9, of which 5 were waited for; matrix products, arithmetic and copies ran while one was open for 0% of the time, Pallas kernels for 22%

profile of v12, /device:TPU:0, one launch (start us, length us, event | category | flops | bytes accessed | tf_op | source)
XLA Modules:
  0.0 37.7 jit_solution(5516494000253390707)
XLA Ops:
  0.7 1.3 %diagonal.1 = (bf16[128,1024]{1,0:T(8,128)(2,1)S(1)}, bf16[16,128,384]{2,1,0:T(8,128)(2,1)S(1)}, bf16[16,128,384]{2,1,0:T(8,128)(2,1)S(1)}) custom-call(bf16[128,2048]{1,0:T(8,128)(2,1)} %query_ref.7, bf16[128,2048]{1,0:T(8,128)(2,1)} %keys_ref.7, bf16[128,2048]{1,0:T(8,128)(2,1)} %values_ref.7, bf16[128,2048]{1,0:T(8,128)(2,1)} %cotangent_ref.1, ...), custom_call_target="tpu_custom_call" | custom-call | flops 1000000 | bytes 100000 | tf_op jit(solution)/shard_map/diagonal/pallas_call | solution.py:358
  2.0 0.0 copy-start.4
  2.0 0.7 %collective-permute-start = (bf16[128,1024]{1,0:T(8,128)(2,1)S(1)}, bf16[128,1024]{1,0:T(8,128)(2,1)S(1)}, u32[]{:S(2)}, u32[]{:S(2)}) collective-permute-start(bf16[128,1024]{1,0:T(8,128)(2,1)S(1)} %get-tuple-element.27.sent_ref), channel_id=1, source_target_pairs={{4,8},{8,4},{12,16},{16,12},{20,24},{24,20},{5,9},{9,5},{13,17},{1... | collective-permute-start | bytes 786440 | tf_op jit(solution)/shard_map/ppermute | solution.py:35
  2.7 0.3 products.1
  3.0 7.6 %collective-permute-start.1 = (bf16[128,2048]{1,0:T(8,128)(2,1)S(1)}, bf16[128,2048]{1,0:T(8,128)(2,1)S(1)}, u32[]{:S(2)}, u32[]{:S(2)}) collective-permute-start(bf16[128,2048]{1,0:T(8,128)(2,1)S(1)} %get-tuple-element.29.across_ref), channel_id=1, source_target_pairs={{0,8},{8,16},{12,4},{16,24},{20,12},{28,20},{1,9},{9,17},{13,5},{1... | collective-permute-start | bytes 1572872 | tf_op jit(solution)/shard_map/ppermute | solution.py:35
  10.6 1.3 %collective-permute-start.2 = (bf16[128,2048]{1,0:T(8,128)(2,1)S(1)}, bf16[128,2048]{1,0:T(8,128)(2,1)S(1)}, u32[]{:S(2)}, u32[]{:S(2)}) collective-permute-start(bf16[128,2048]{1,0:T(8,128)(2,1)S(1)} %get-tuple-element.28.near_ref), channel_id=1, source_target_pairs={{4,12},{8,0},{12,20},{16,8},{20,28},{24,16},{5,13},{9,1},{13,21},{... | collective-permute-start | bytes 1572872 | tf_op jit(solution)/shard_map/ppermute | solution.py:35
  11.9 2.8 %collective-permute-start.4 = (bf16[128,2048]{1,0:T(8,128)(2,1)S(1)}, bf16[128,2048]{1,0:T(8,128)(2,1)S(1)}, u32[]{:S(2)}, u32[]{:S(2)}) collective-permute-start(bf16[128,2048]{1,0:T(8,128)(2,1)S(1)} %get-tuple-element.29.across_ref), channel_id=1, source_target_pairs={{0,4},{4,0},{8,12},{12,8},{16,20},{20,16},{24,28},{28,24},{1,5},{5... | collective-permute-start | bytes 1572872 | tf_op jit(solution)/shard_map/ppermute | solution.py:35
  14.7 2.2 %tiles.1 = (bf16[16,128,384]{2,1,0:T(8,128)(2,1)S(1)}, bf16[16,128,384]{2,1,0:T(8,128)(2,1)S(1)}) custom-call(bf16[16,384]{1,0:T(8,128)(2,1)S(1)} %copy-done.4, bf16[16,128,384]{2,1,0:T(8,128)(2,1)S(1)} %get-tuple-element.23.ready_in, bf16[16,128,384]{2,1,0:T(8,128)(2,1)S(1)} %get-tuple-element.24.late_in), custom_call_target="tpu_custom_call" | custom-call | flops 1000000 | bytes 100000 | tf_op jit(solution)/shard_map/tiles/pallas_call | solution.py:379
  17.0 1.6 %own.1 = (f32[16,384]{1,0:T(8,128)S(1)}, f32[128,2048]{1,0:T(8,128)S(1)}, f32[128,2048]{1,0:T(8,128)S(1)}) custom-call(bf16[16,128,384]{2,1,0:T(8,128)(2,1)S(1)} %get-tuple-element.25.ready_tiles.tiles_ref, bf16[16,128,384]{2,1,0:T(8,128)(2,1)S(1)} %get-tuple-element.26.late_tiles.tiles_ref, bf16[128,2048]{1,0:T(8,128)(2,1)S(1)} %get-tuple-element.28.near_ref, ...), custom_call_target="tpu_custom_call" | custom-call | flops 4000000000 | bytes 100000 | tf_op jit(solution)/shard_map/own/pallas_call | solution.py:386
  18.6 4.2 %collective-permute-done.1.two_ref = bf16[128,2048]{1,0:T(8,128)(2,1)S(1)} collective-permute-done((bf16[128,2048]{1,0:T(8,128)(2,1)S(1)}, bf16[128,2048]{1,0:T(8,128)(2,1)S(1)}, u32[]{:S(2)}, u32[]{:S(2)}) %collective-permute-start.1) | collective-permute-done | bytes 524320 | tf_op jit(solution)/shard_map/ppermute | solution.py:35
  22.8 0.9 %two.1.sum_ref = f32[16,384]{1,0:T(8,128)S(1)} custom-call(f32[16,384]{1,0:T(8,128)S(1)} %get-tuple-element.31.sum_ref, bf16[128,2048]{1,0:T(8,128)(2,1)S(1)} %get-tuple-element.28.near_ref, bf16[128,2048]{1,0:T(8,128)(2,1)S(1)} %collective-permute-done.1.two_ref), custom_call_target="tpu_custom_call" | custom-call | flops 1000000 | bytes 100000 | tf_op jit(solution)/shard_map/two/pallas_call | solution.py:395
  23.7 2.6 %collective-permute-start.5 = (f32[16,384]{1,0:T(8,128)S(1)}, f32[16,384]{1,0:T(8,128)S(1)}, u32[]{:S(2)}, u32[]{:S(2)}) collective-permute-start(f32[16,384]{1,0:T(8,128)S(1)} %two.1.sum_ref), channel_id=1, source_target_pairs={{0,4},{4,0},{8,12},{12,8},{16,20},{20,16},{24,28},{28,24},{1,5},{5... | collective-permute-start | bytes 73736 | tf_op jit(solution)/shard_map/ppermute | solution.py:35
  26.3 0.4 %ready.1 = (f32[128,1024]{1,0:T(8,128)S(1)}, bf16[128,1024]{1,0:T(8,128)(2,1)S(1)}, bf16[128,1024]{1,0:T(8,128)(2,1)S(1)}) custom-call(bf16[16,128,384]{2,1,0:T(8,128)(2,1)S(1)} %get-tuple-element.25.ready_tiles.tiles_ref, f32[128,2048]{1,0:T(8,128)S(1)} %get-tuple-element.30.ready_ref, bf16[128,2048]{1,0:T(8,128)(2,1)S(1)} %collective-permute-done.1.two_ref, ...), custom_call_target="tpu_custom_call" | custom-call | flops 1000000 | bytes 100000 | tf_op jit(solution)/shard_map/ready/pallas_call | solution.py:404
  26.7 0.4 %collective-permute-done.2.far_ref = bf16[128,2048]{1,0:T(8,128)(2,1)S(1)} collective-permute-done((bf16[128,2048]{1,0:T(8,128)(2,1)S(1)}, bf16[128,2048]{1,0:T(8,128)(2,1)S(1)}, u32[]{:S(2)}, u32[]{:S(2)}) %collective-permute-start.2) | collective-permute-done | bytes 524320 | tf_op jit(solution)/shard_map/ppermute | solution.py:35
  27.2 0.1 collective-permute-start.3
  27.2 0.1 collective-permute-done.4.swap_ref
  27.3 0.9 %cross.1.cross_ref = f32[16,384]{1,0:T(8,128)S(1)} custom-call(bf16[128,2048]{1,0:T(8,128)(2,1)S(1)} %get-tuple-element.29.across_ref, bf16[128,2048]{1,0:T(8,128)(2,1)S(1)} %collective-permute-done.4.swap_ref), custom_call_target="tpu_custom_call" | custom-call | flops 1000000 | bytes 100000 | tf_op jit(solution)/shard_map/cross/pallas_call | solution.py:421
  28.2 4.1 %collective-permute-start.6 = (f32[16,384]{1,0:T(8,128)S(1)}, f32[16,384]{1,0:T(8,128)S(1)}, u32[]{:S(2)}, u32[]{:S(2)}) collective-permute-start(f32[16,384]{1,0:T(8,128)S(1)} %pair.1.refs_0_), channel_id=1, source_target_pairs={{0,24},{4,28},{8,16},{12,20},{16,8},{20,12},{24,0},{28,4},{1,25},{... | collective-permute-start | bytes 73736 | tf_op jit(solution)/shard_map/ppermute | solution.py:48
  32.3 0.6 %collective-permute-start.8 = (f32[16,384]{1,0:T(8,128)S(1)}, f32[16,384]{1,0:T(8,128)S(1)}, u32[]{:S(2)}, u32[]{:S(2)}) collective-permute-start(f32[16,384]{1,0:T(8,128)S(1)} %pair.1.refs_0_), channel_id=1, source_target_pairs={{0,8},{4,12},{8,0},{12,4},{16,24},{20,28},{24,16},{28,20},{1,9},{5... | collective-permute-start | bytes 73736 | tf_op jit(solution)/shard_map/ppermute | solution.py:48
  33.0 0.6 %known.1 = (bf16[128,2048]{1,0:T(8,128)(2,1)S(1)}, bf16[128,2048]{1,0:T(8,128)(2,1)S(1)}) custom-call(bf16[16,128,384]{2,1,0:T(8,128)(2,1)S(1)} %get-tuple-element.26.late_tiles.tiles_ref, f32[128,2048]{1,0:T(8,128)S(1)} %get-tuple-element.35.late_ref, bf16[128,2048]{1,0:T(8,128)(2,1)S(1)} %collective-permute-done.4.swap_ref, ...), custom_call_target="tpu_custom_call" | custom-call | flops 4000000000 | bytes 100000 | tf_op jit(solution)/shard_map/known/pallas_call | solution.py:436
  33.6 1.8 %collective-permute-done.3.forwarded_ref = bf16[128,1024]{1,0:T(8,128)(2,1)S(1)} collective-permute-done((bf16[128,1024]{1,0:T(8,128)(2,1)S(1)}, bf16[128,1024]{1,0:T(8,128)(2,1)S(1)}, u32[]{:S(2)}, u32[]{:S(2)}) %collective-permute-start.3) | collective-permute-done | bytes 262176 | tf_op jit(solution)/shard_map/ppermute | solution.py:35
  35.4 1.3 %last.1 = (bf16[128,2048]{1,0:T(8,128)(2,1)}, bf16[128,2048]{1,0:T(8,128)(2,1)}, bf16[128,2048]{1,0:T(8,128)(2,1)}, f32[8,128]{1,0:T(8,128)S(1)}) custom-call(bf16[16,128,384]{2,1,0:T(8,128)(2,1)S(1)} %get-tuple-element.25.ready_tiles.tiles_ref, f32[128,1024]{1,0:T(8,128)S(1)} %get-tuple-element.32.rest_ref, ...), custom_call_target="tpu_custom_call" | custom-call | flops 1000000 | bytes 100000 | tf_op jit(solution)/shard_map/last/pallas_call | solution.py:455
  36.7 0.4 collective-permute-done.7.refs_2_
  37.1 0.6 %add.1 = f32[16,384]{1,0:T(8,128)} custom-call(f32[16,384]{1,0:T(8,128)S(1)} %pair.1.refs_0_, f32[16,384]{1,0:T(8,128)S(1)} %collective-permute-done.6.refs_1_, f32[16,384]{1,0:T(8,128)S(1)} %collective-permute-done.7.refs_2_, f32[16,384]{1,0:T(8,128)S(1)} %collective-permute-done.8.refs_3_, f32[8,128]{1,0:T(8,128)S(1)} %get-tuple-element.41.refs_4_), custom_call_target="tpu_custom_call" | custom-call | flops 1000000 | bytes 100000 | tf_op jit(solution)/shard_map/add/pallas_call | solution.py:446
  (16 shorter events, 0.1 us)
Async XLA Ops:
  0.6 2.0 %copy-start = (bf16[128,2048]{1,0:T(8,128)(2,1)S(1)}, bf16[128,2048]{1,0:T(8,128)(2,1)}, u32[]{:S(2)}) copy-start(bf16[128,2048]{1,0:T(8,128)(2,1)} %query_ref.7) | copy-start | bytes 1572868
  0.6 2.0 %copy-start.1 = (bf16[128,2048]{1,0:T(8,128)(2,1)S(1)}, bf16[128,2048]{1,0:T(8,128)(2,1)}, u32[]{:S(2)}) copy-start(bf16[128,2048]{1,0:T(8,128)(2,1)} %keys_ref.7) | copy-start | bytes 1572868
  0.7 2.0 %copy-start.2 = (bf16[128,2048]{1,0:T(8,128)(2,1)S(1)}, bf16[128,2048]{1,0:T(8,128)(2,1)}, u32[]{:S(2)}) copy-start(bf16[128,2048]{1,0:T(8,128)(2,1)} %values_ref.7) | copy-start | bytes 1572868
  0.7 2.0 %copy-start.3 = (bf16[128,2048]{1,0:T(8,128)(2,1)S(1)}, bf16[128,2048]{1,0:T(8,128)(2,1)}, u32[]{:S(2)}) copy-start(bf16[128,2048]{1,0:T(8,128)(2,1)} %cotangent_ref.1) | copy-start | bytes 1572868
  2.0 12.7 %copy-start.4 = (bf16[16,384]{1,0:T(8,128)(2,1)S(1)}, bf16[16,384]{1,0:T(8,128)(2,1)}, u32[]{:S(2)}) copy-start(bf16[16,384]{1,0:T(8,128)(2,1)} %taps_ref.1) | copy-start | bytes 36868
  2.0 15.0 %collective-permute-start = (bf16[128,1024]{1,0:T(8,128)(2,1)S(1)}, bf16[128,1024]{1,0:T(8,128)(2,1)S(1)}, u32[]{:S(2)}, u32[]{:S(2)}) collective-permute-start(bf16[128,1024]{1,0:T(8,128)(2,1)S(1)} %get-tuple-element.27.sent_ref), channel_id=1, source_target_pairs={{4,8},{8,4},{12,16},{16,12},{20,24},{24,20},{5,9},{9,5},{13,17},{1... | collective-permute-start | bytes 786440 | tf_op jit(solution)/shard_map/ppermute | solution.py:35
  3.0 19.7 %collective-permute-start.1 = (bf16[128,2048]{1,0:T(8,128)(2,1)S(1)}, bf16[128,2048]{1,0:T(8,128)(2,1)S(1)}, u32[]{:S(2)}, u32[]{:S(2)}) collective-permute-start(bf16[128,2048]{1,0:T(8,128)(2,1)S(1)} %get-tuple-element.29.across_ref), channel_id=1, source_target_pairs={{0,8},{8,16},{12,4},{16,24},{20,12},{28,20},{1,9},{9,17},{13,5},{1... | collective-permute-start | bytes 1572872 | tf_op jit(solution)/shard_map/ppermute | solution.py:35
  10.6 16.5 %collective-permute-start.2 = (bf16[128,2048]{1,0:T(8,128)(2,1)S(1)}, bf16[128,2048]{1,0:T(8,128)(2,1)S(1)}, u32[]{:S(2)}, u32[]{:S(2)}) collective-permute-start(bf16[128,2048]{1,0:T(8,128)(2,1)S(1)} %get-tuple-element.28.near_ref), channel_id=1, source_target_pairs={{4,12},{8,0},{12,20},{16,8},{20,28},{24,16},{5,13},{9,1},{13,21},{... | collective-permute-start | bytes 1572872 | tf_op jit(solution)/shard_map/ppermute | solution.py:35
  11.9 15.4 %collective-permute-start.4 = (bf16[128,2048]{1,0:T(8,128)(2,1)S(1)}, bf16[128,2048]{1,0:T(8,128)(2,1)S(1)}, u32[]{:S(2)}, u32[]{:S(2)}) collective-permute-start(bf16[128,2048]{1,0:T(8,128)(2,1)S(1)} %get-tuple-element.29.across_ref), channel_id=1, source_target_pairs={{0,4},{4,0},{8,12},{12,8},{16,20},{20,16},{24,28},{28,24},{1,5},{5... | collective-permute-start | bytes 1572872 | tf_op jit(solution)/shard_map/ppermute | solution.py:35
  23.7 4.5 %collective-permute-start.5 = (f32[16,384]{1,0:T(8,128)S(1)}, f32[16,384]{1,0:T(8,128)S(1)}, u32[]{:S(2)}, u32[]{:S(2)}) collective-permute-start(f32[16,384]{1,0:T(8,128)S(1)} %two.1.sum_ref), channel_id=1, source_target_pairs={{0,4},{4,0},{8,12},{12,8},{16,20},{20,16},{24,28},{28,24},{1,5},{5... | collective-permute-start | bytes 73736 | tf_op jit(solution)/shard_map/ppermute | solution.py:35
  27.2 8.2 %collective-permute-start.3 = (bf16[128,1024]{1,0:T(8,128)(2,1)S(1)}, bf16[128,1024]{1,0:T(8,128)(2,1)S(1)}, u32[]{:S(2)}, u32[]{:S(2)}) collective-permute-start(bf16[128,1024]{1,0:T(8,128)(2,1)S(1)} %forward.1), channel_id=1, source_target_pairs={{0,4},{4,0},{8,12},{12,8},{16,20},{20,16},{24,28},{28,24},{1,5},{5... | collective-permute-start | bytes 786440 | tf_op jit(solution)/shard_map/ppermute | solution.py:35
  28.2 8.5 %collective-permute-start.6 = (f32[16,384]{1,0:T(8,128)S(1)}, f32[16,384]{1,0:T(8,128)S(1)}, u32[]{:S(2)}, u32[]{:S(2)}) collective-permute-start(f32[16,384]{1,0:T(8,128)S(1)} %pair.1.refs_0_), channel_id=1, source_target_pairs={{0,24},{4,28},{8,16},{12,20},{16,8},{20,12},{24,0},{28,4},{1,25},{... | collective-permute-start | bytes 73736 | tf_op jit(solution)/shard_map/ppermute | solution.py:48
  32.3 4.7 %collective-permute-start.7 = (f32[16,384]{1,0:T(8,128)S(1)}, f32[16,384]{1,0:T(8,128)S(1)}, u32[]{:S(2)}, u32[]{:S(2)}) collective-permute-start(f32[16,384]{1,0:T(8,128)S(1)} %pair.1.refs_0_), channel_id=1, source_target_pairs={{0,16},{4,20},{8,24},{12,28},{16,0},{20,4},{24,8},{28,12},{1,17},{... | collective-permute-start | bytes 73736 | tf_op jit(solution)/shard_map/ppermute | solution.py:48
  32.3 4.7 %collective-permute-start.8 = (f32[16,384]{1,0:T(8,128)S(1)}, f32[16,384]{1,0:T(8,128)S(1)}, u32[]{:S(2)}, u32[]{:S(2)}) collective-permute-start(f32[16,384]{1,0:T(8,128)S(1)} %pair.1.refs_0_), channel_id=1, source_target_pairs={{0,8},{4,12},{8,0},{12,4},{16,24},{20,28},{24,16},{28,20},{1,9},{5... | collective-permute-start | bytes 73736 | tf_op jit(solution)/shard_map/ppermute | solution.py:48

commit v13 on v10

--- a/solution.py
+++ b/solution.py
@@ -44,9 +44,13 @@
     stride = 2
     while stride < size:
         own = terms[0] if len(terms) == 1 else add(*terms)
-        hops = (3 * stride, 2 * stride, stride) if 4 * stride <= size else (stride,)
-        terms = [own] + [lax.ppermute(own, axis, [(i, i ^ hop) for i in range(size)]) for hop in hops]
-        stride *= len(hops) + 1
+        members = 4 if 4 * stride <= size else 2
+        terms = [own]
+        for turn in range(1, members):
+            places = [(i, i // stride % members) for i in range(size)]
+            route = [(i, i + ((place + turn) % members - place) * stride) for i, place in places]
+            terms.append(lax.ppermute(own, axis, route))
+        stride *= members
     return terms
 
 

time: 36.9 us -> 36.5 us (0.989)
  waiting for transfers between devices: 5.69 us -> 4.3 us
  starting transfers between devices: 20 us -> 21 us
    ppermute x3, waiting for transfers between devices: 2.16 us -> 0.77 us  [sum_terms(): terms.append(lax.ppermute(own, axis, route))]
    ppermute x3, starting transfers between devices: 4.96 us -> 5.99 us  [sum_terms(): terms.append(lax.ppermute(own, axis, route))]
  transfers between devices with their start and end apart: 9 -> 9, of which waited for: 4 -> 4; matrix products, arithmetic and copies ran while one was open for 0% -> 0% of each run, Pallas kernels for 22% -> 23%
where the time goes in v13:
time: 36.5 us; the launch traced here: 36.3 us
  starting transfers between devices  21 us (58%)
  Pallas kernels  10.1 us (28%)
  waiting for transfers between devices  4.3 us (12%)
  between operations  0.86 us (2%)
    ppermute x6, starting transfers between devices, moved(): lax.ppermute(block, axis, [pair for pair in route if 0 <= pair[1] < size])  15 us
    ppermute x3, starting transfers between devices, sum_terms(): terms.append(lax.ppermute(own, axis, route))  5.99 us
    ppermute x6, waiting for transfers between devices, moved(): lax.ppermute(block, axis, [pair for pair in route if 0 <= pair[1] < size])  3.53 us
    pallas_call x1, Pallas kernels, shards(): call(functools.partial(tiles_kernel, rows), 'tiles', in_specs=[WHOLE], ou...  2.22 us
    pallas_call x1, Pallas kernels, shards(): call(functools.partial(own_kernel, rows), 'own', flops=4 * 10 ** 9, in_sp...  1.6 us
    pallas_call x1, Pallas kernels, shards(): call(last_kernel, 'last', in_specs=[WHOLE] * 10, out_specs=[ANYWHERE] * 3...  1.35 us
    pallas_call x1, Pallas kernels, shards(): call(diagonal_kernel, 'diagonal', in_specs=[ANYWHERE] * 4, out_specs=WHOL...  1.28 us
    pallas_call x1, Pallas kernels, shards(): call(functools.partial(cross_kernel, rows), 'cross', in_specs=[WHOLE] * 2...  0.88 us
  transfers between devices with their start and end apart: 9, of which 4 were waited for; matrix products, arithmetic and copies ran while one was open for 0% of the time, Pallas kernels for 23%

profile of v13, /device:TPU:0, one launch (start us, length us, event | category | flops | bytes accessed | tf_op | source)
XLA Modules:
  0.0 36.3 jit_solution(850402966044361464)
XLA Ops:
  0.7 1.3 %diagonal.1.sent_ref = bf16[128,1024]{1,0:T(8,128)(2,1)S(1)} custom-call(bf16[128,2048]{1,0:T(8,128)(2,1)} %query_ref.7, bf16[128,2048]{1,0:T(8,128)(2,1)} %keys_ref.7, bf16[128,2048]{1,0:T(8,128)(2,1)} %values_ref.7, bf16[128,2048]{1,0:T(8,128)(2,1)} %cotangent_ref.1), custom_call_target="tpu_custom_call" | custom-call | flops 1000000 | bytes 100000 | tf_op jit(solution)/shard_map/diagonal/pallas_call | solution.py:326
  2.0 0.0 copy-start.4
  2.0 0.7 %collective-permute-start = (bf16[128,1024]{1,0:T(8,128)(2,1)S(1)}, bf16[128,1024]{1,0:T(8,128)(2,1)S(1)}, u32[]{:S(2)}, u32[]{:S(2)}) collective-permute-start(bf16[128,1024]{1,0:T(8,128)(2,1)S(1)} %diagonal.1.sent_ref), channel_id=1, source_target_pairs={{4,8},{8,4},{12,16},{16,12},{20,24},{24,20},{5,9},{9,5},{13,17},{1... | collective-permute-start | bytes 786440 | tf_op jit(solution)/shard_map/ppermute | solution.py:35
  2.7 0.3 products.1
  3.0 7.6 %collective-permute-start.1 = (bf16[128,2048]{1,0:T(8,128)(2,1)S(1)}, bf16[128,2048]{1,0:T(8,128)(2,1)S(1)}, u32[]{:S(2)}, u32[]{:S(2)}) collective-permute-start(bf16[128,2048]{1,0:T(8,128)(2,1)S(1)} %get-tuple-element.23.across_ref), channel_id=1, source_target_pairs={{0,8},{8,16},{12,4},{16,24},{20,12},{28,20},{1,9},{9,17},{13,5},{1... | collective-permute-start | bytes 1572872 | tf_op jit(solution)/shard_map/ppermute | solution.py:35
  10.6 1.3 %collective-permute-start.2 = (bf16[128,2048]{1,0:T(8,128)(2,1)S(1)}, bf16[128,2048]{1,0:T(8,128)(2,1)S(1)}, u32[]{:S(2)}, u32[]{:S(2)}) collective-permute-start(bf16[128,2048]{1,0:T(8,128)(2,1)S(1)} %get-tuple-element.22.near_ref), channel_id=1, source_target_pairs={{4,12},{8,0},{12,20},{16,8},{20,28},{24,16},{5,13},{9,1},{13,21},{... | collective-permute-start | bytes 1572872 | tf_op jit(solution)/shard_map/ppermute | solution.py:35
  11.9 2.8 %collective-permute-start.4 = (bf16[128,2048]{1,0:T(8,128)(2,1)S(1)}, bf16[128,2048]{1,0:T(8,128)(2,1)S(1)}, u32[]{:S(2)}, u32[]{:S(2)}) collective-permute-start(bf16[128,2048]{1,0:T(8,128)(2,1)S(1)} %get-tuple-element.23.across_ref), channel_id=1, source_target_pairs={{0,4},{4,0},{8,12},{12,8},{16,20},{20,16},{24,28},{28,24},{1,5},{5... | collective-permute-start | bytes 1572872 | tf_op jit(solution)/shard_map/ppermute | solution.py:35
  14.7 2.2 %tiles.1 = (bf16[16,128,384]{2,1,0:T(8,128)(2,1)S(1)}, bf16[16,128,384]{2,1,0:T(8,128)(2,1)S(1)}) custom-call(bf16[16,384]{1,0:T(8,128)(2,1)S(1)} %copy-done.4), custom_call_target="tpu_custom_call" | custom-call | flops 1000000 | bytes 100000 | tf_op jit(solution)/shard_map/tiles/pallas_call | solution.py:346
  16.9 1.6 %own.1 = (f32[16,384]{1,0:T(8,128)S(1)}, f32[128,2048]{1,0:T(8,128)S(1)}, f32[128,2048]{1,0:T(8,128)S(1)}) custom-call(bf16[16,128,384]{2,1,0:T(8,128)(2,1)S(1)} %get-tuple-element.20.ready_tiles.tiles_ref, bf16[16,128,384]{2,1,0:T(8,128)(2,1)S(1)} %get-tuple-element.21.late_tiles.tiles_ref, bf16[128,2048]{1,0:T(8,128)(2,1)S(1)} %get-tuple-element.22.near_ref, ...), custom_call_target="tpu_custom_call" | custom-call | flops 4000000000 | bytes 100000 | tf_op jit(solution)/shard_map/own/pallas_call | solution.py:353
  18.5 2.9 %collective-permute-done.1.two_ref = bf16[128,2048]{1,0:T(8,128)(2,1)S(1)} collective-permute-done((bf16[128,2048]{1,0:T(8,128)(2,1)S(1)}, bf16[128,2048]{1,0:T(8,128)(2,1)S(1)}, u32[]{:S(2)}, u32[]{:S(2)}) %collective-permute-start.1) | collective-permute-done | bytes 524320 | tf_op jit(solution)/shard_map/ppermute | solution.py:35
  21.5 0.9 %two.1.sum_ref = f32[16,384]{1,0:T(8,128)S(1)} custom-call(f32[16,384]{1,0:T(8,128)S(1)} %get-tuple-element.25.sum_ref, bf16[128,2048]{1,0:T(8,128)(2,1)S(1)} %get-tuple-element.22.near_ref, bf16[128,2048]{1,0:T(8,128)(2,1)S(1)} %collective-permute-done.1.two_ref), custom_call_target="tpu_custom_call" | custom-call | flops 1000000 | bytes 100000 | tf_op jit(solution)/shard_map/two/pallas_call | solution.py:362
  22.3 2.6 %collective-permute-start.5 = (f32[16,384]{1,0:T(8,128)S(1)}, f32[16,384]{1,0:T(8,128)S(1)}, u32[]{:S(2)}, u32[]{:S(2)}) collective-permute-start(f32[16,384]{1,0:T(8,128)S(1)} %two.1.sum_ref), channel_id=1, source_target_pairs={{0,4},{4,0},{8,12},{12,8},{16,20},{20,16},{24,28},{28,24},{1,5},{5... | collective-permute-start | bytes 73736 | tf_op jit(solution)/shard_map/ppermute | solution.py:35
  25.0 0.4 %ready.1 = (f32[128,1024]{1,0:T(8,128)S(1)}, bf16[128,1024]{1,0:T(8,128)(2,1)S(1)}, bf16[128,1024]{1,0:T(8,128)(2,1)S(1)}) custom-call(bf16[16,128,384]{2,1,0:T(8,128)(2,1)S(1)} %get-tuple-element.20.ready_tiles.tiles_ref, f32[128,2048]{1,0:T(8,128)S(1)} %get-tuple-element.24.ready_ref, bf16[128,2048]{1,0:T(8,128)(2,1)S(1)} %collective-permute-done.1.two_ref, ...), custom_call_target="tpu_custom_call" | custom-call | flops 1000000 | bytes 100000 | tf_op jit(solution)/shard_map/ready/pallas_call | solution.py:371
  25.4 0.2 collective-permute-done.2.far_ref
  25.6 0.1 collective-permute-start.3
  25.7 0.4 collective-permute-done.4.swap_ref
  26.1 0.9 %cross.1.cross_ref = f32[16,384]{1,0:T(8,128)S(1)} custom-call(bf16[128,2048]{1,0:T(8,128)(2,1)S(1)} %get-tuple-element.23.across_ref, bf16[128,2048]{1,0:T(8,128)(2,1)S(1)} %collective-permute-done.4.swap_ref), custom_call_target="tpu_custom_call" | custom-call | flops 1000000 | bytes 100000 | tf_op jit(solution)/shard_map/cross/pallas_call | solution.py:388
  27.0 2.0 %collective-permute-start.6 = (f32[16,384]{1,0:T(8,128)S(1)}, f32[16,384]{1,0:T(8,128)S(1)}, u32[]{:S(2)}, u32[]{:S(2)}) collective-permute-start(f32[16,384]{1,0:T(8,128)S(1)} %pair.1.refs_0_), channel_id=1, source_target_pairs={{0,8},{4,12},{8,16},{12,20},{16,24},{20,28},{24,0},{28,4},{1,9},{5... | collective-permute-start | bytes 73736 | tf_op jit(solution)/shard_map/ppermute | solution.py:52
  29.0 2.8 %collective-permute-start.7 = (f32[16,384]{1,0:T(8,128)S(1)}, f32[16,384]{1,0:T(8,128)S(1)}, u32[]{:S(2)}, u32[]{:S(2)}) collective-permute-start(f32[16,384]{1,0:T(8,128)S(1)} %pair.1.refs_0_), channel_id=1, source_target_pairs={{0,16},{4,20},{8,24},{12,28},{16,0},{20,4},{24,8},{28,12},{1,17},{... | collective-permute-start | bytes 73736 | tf_op jit(solution)/shard_map/ppermute | solution.py:52
  31.9 1.1 %collective-permute-start.8 = (f32[16,384]{1,0:T(8,128)S(1)}, f32[16,384]{1,0:T(8,128)S(1)}, u32[]{:S(2)}, u32[]{:S(2)}) collective-permute-start(f32[16,384]{1,0:T(8,128)S(1)} %pair.1.refs_0_), channel_id=1, source_target_pairs={{0,24},{4,28},{8,0},{12,4},{16,8},{20,12},{24,16},{28,20},{1,25},{... | collective-permute-start | bytes 73736 | tf_op jit(solution)/shard_map/ppermute | solution.py:52
  33.0 0.5 %known.1 = (bf16[128,2048]{1,0:T(8,128)(2,1)S(1)}, bf16[128,2048]{1,0:T(8,128)(2,1)S(1)}) custom-call(bf16[16,128,384]{2,1,0:T(8,128)(2,1)S(1)} %get-tuple-element.21.late_tiles.tiles_ref, f32[128,2048]{1,0:T(8,128)S(1)} %get-tuple-element.29.late_ref, bf16[128,2048]{1,0:T(8,128)(2,1)S(1)} %collective-permute-done.4.swap_ref, ...), custom_call_target="tpu_custom_call" | custom-call | flops 4000000000 | bytes 100000 | tf_op jit(solution)/shard_map/known/pallas_call | solution.py:403
  33.6 1.3 %last.1 = (bf16[128,2048]{1,0:T(8,128)(2,1)}, bf16[128,2048]{1,0:T(8,128)(2,1)}, bf16[128,2048]{1,0:T(8,128)(2,1)}, f32[8,128]{1,0:T(8,128)S(1)}) custom-call(bf16[16,128,384]{2,1,0:T(8,128)(2,1)S(1)} %get-tuple-element.20.ready_tiles.tiles_ref, f32[128,1024]{1,0:T(8,128)S(1)} %get-tuple-element.26.rest_ref, ...), custom_call_target="tpu_custom_call" | custom-call | flops 1000000 | bytes 100000 | tf_op jit(solution)/shard_map/last/pallas_call | solution.py:422
  34.9 0.8 %collective-permute-done.8.refs_3_ = f32[16,384]{1,0:T(8,128)S(1)} collective-permute-done((f32[16,384]{1,0:T(8,128)S(1)}, f32[16,384]{1,0:T(8,128)S(1)}, u32[]{:S(2)}, u32[]{:S(2)}) %collective-permute-start.8) | collective-permute-done | bytes 24608 | tf_op jit(solution)/shard_map/ppermute | solution.py:52
  35.7 0.6 %add.1 = f32[16,384]{1,0:T(8,128)} custom-call(f32[16,384]{1,0:T(8,128)S(1)} %pair.1.refs_0_, f32[16,384]{1,0:T(8,128)S(1)} %collective-permute-done.6.refs_1_, f32[16,384]{1,0:T(8,128)S(1)} %collective-permute-done.7.refs_2_, f32[16,384]{1,0:T(8,128)S(1)} %collective-permute-done.8.refs_3_, f32[8,128]{1,0:T(8,128)S(1)} %get-tuple-element.35.refs_4_), custom_call_target="tpu_custom_call" | custom-call | flops 1000000 | bytes 100000 | tf_op jit(solution)/shard_map/add/pallas_call | solution.py:413
  (16 shorter events, 0.1 us)
Async XLA Ops:
  0.6 2.0 %copy-start = (bf16[128,2048]{1,0:T(8,128)(2,1)S(1)}, bf16[128,2048]{1,0:T(8,128)(2,1)}, u32[]{:S(2)}) copy-start(bf16[128,2048]{1,0:T(8,128)(2,1)} %query_ref.7) | copy-start | bytes 1572868
  0.6 2.0 %copy-start.1 = (bf16[128,2048]{1,0:T(8,128)(2,1)S(1)}, bf16[128,2048]{1,0:T(8,128)(2,1)}, u32[]{:S(2)}) copy-start(bf16[128,2048]{1,0:T(8,128)(2,1)} %keys_ref.7) | copy-start | bytes 1572868
  0.7 2.0 %copy-start.2 = (bf16[128,2048]{1,0:T(8,128)(2,1)S(1)}, bf16[128,2048]{1,0:T(8,128)(2,1)}, u32[]{:S(2)}) copy-start(bf16[128,2048]{1,0:T(8,128)(2,1)} %values_ref.7) | copy-start | bytes 1572868
  0.7 2.0 %copy-start.3 = (bf16[128,2048]{1,0:T(8,128)(2,1)S(1)}, bf16[128,2048]{1,0:T(8,128)(2,1)}, u32[]{:S(2)}) copy-start(bf16[128,2048]{1,0:T(8,128)(2,1)} %cotangent_ref.1) | copy-start | bytes 1572868
  2.0 12.7 %copy-start.4 = (bf16[16,384]{1,0:T(8,128)(2,1)S(1)}, bf16[16,384]{1,0:T(8,128)(2,1)}, u32[]{:S(2)}) copy-start(bf16[16,384]{1,0:T(8,128)(2,1)} %taps_ref.1) | copy-start | bytes 36868
  2.0 15.0 %collective-permute-start = (bf16[128,1024]{1,0:T(8,128)(2,1)S(1)}, bf16[128,1024]{1,0:T(8,128)(2,1)S(1)}, u32[]{:S(2)}, u32[]{:S(2)}) collective-permute-start(bf16[128,1024]{1,0:T(8,128)(2,1)S(1)} %diagonal.1.sent_ref), channel_id=1, source_target_pairs={{4,8},{8,4},{12,16},{16,12},{20,24},{24,20},{5,9},{9,5},{13,17},{1... | collective-permute-start | bytes 786440 | tf_op jit(solution)/shard_map/ppermute | solution.py:35
  3.0 18.4 %collective-permute-start.1 = (bf16[128,2048]{1,0:T(8,128)(2,1)S(1)}, bf16[128,2048]{1,0:T(8,128)(2,1)S(1)}, u32[]{:S(2)}, u32[]{:S(2)}) collective-permute-start(bf16[128,2048]{1,0:T(8,128)(2,1)S(1)} %get-tuple-element.23.across_ref), channel_id=1, source_target_pairs={{0,8},{8,16},{12,4},{16,24},{20,12},{28,20},{1,9},{9,17},{13,5},{1... | collective-permute-start | bytes 1572872 | tf_op jit(solution)/shard_map/ppermute | solution.py:35
  10.6 15.0 %collective-permute-start.2 = (bf16[128,2048]{1,0:T(8,128)(2,1)S(1)}, bf16[128,2048]{1,0:T(8,128)(2,1)S(1)}, u32[]{:S(2)}, u32[]{:S(2)}) collective-permute-start(bf16[128,2048]{1,0:T(8,128)(2,1)S(1)} %get-tuple-element.22.near_ref), channel_id=1, source_target_pairs={{4,12},{8,0},{12,20},{16,8},{20,28},{24,16},{5,13},{9,1},{13,21},{... | collective-permute-start | bytes 1572872 | tf_op jit(solution)/shard_map/ppermute | solution.py:35
  11.9 14.2 %collective-permute-start.4 = (bf16[128,2048]{1,0:T(8,128)(2,1)S(1)}, bf16[128,2048]{1,0:T(8,128)(2,1)S(1)}, u32[]{:S(2)}, u32[]{:S(2)}) collective-permute-start(bf16[128,2048]{1,0:T(8,128)(2,1)S(1)} %get-tuple-element.23.across_ref), channel_id=1, source_target_pairs={{0,4},{4,0},{8,12},{12,8},{16,20},{20,16},{24,28},{28,24},{1,5},{5... | collective-permute-start | bytes 1572872 | tf_op jit(solution)/shard_map/ppermute | solution.py:35
  22.3 4.6 %collective-permute-start.5 = (f32[16,384]{1,0:T(8,128)S(1)}, f32[16,384]{1,0:T(8,128)S(1)}, u32[]{:S(2)}, u32[]{:S(2)}) collective-permute-start(f32[16,384]{1,0:T(8,128)S(1)} %two.1.sum_ref), channel_id=1, source_target_pairs={{0,4},{4,0},{8,12},{12,8},{16,20},{20,16},{24,28},{28,24},{1,5},{5... | collective-permute-start | bytes 73736 | tf_op jit(solution)/shard_map/ppermute | solution.py:35
  25.6 7.9 %collective-permute-start.3 = (bf16[128,1024]{1,0:T(8,128)(2,1)S(1)}, bf16[128,1024]{1,0:T(8,128)(2,1)S(1)}, u32[]{:S(2)}, u32[]{:S(2)}) collective-permute-start(bf16[128,1024]{1,0:T(8,128)(2,1)S(1)} %forward.1), channel_id=1, source_target_pairs={{0,4},{4,0},{8,12},{12,8},{16,20},{20,16},{24,28},{28,24},{1,5},{5... | collective-permute-start | bytes 786440 | tf_op jit(solution)/shard_map/ppermute | solution.py:35
  27.0 7.9 %collective-permute-start.6 = (f32[16,384]{1,0:T(8,128)S(1)}, f32[16,384]{1,0:T(8,128)S(1)}, u32[]{:S(2)}, u32[]{:S(2)}) collective-permute-start(f32[16,384]{1,0:T(8,128)S(1)} %pair.1.refs_0_), channel_id=1, source_target_pairs={{0,8},{4,12},{8,16},{12,20},{16,24},{20,28},{24,0},{28,4},{1,9},{5... | collective-permute-start | bytes 73736 | tf_op jit(solution)/shard_map/ppermute | solution.py:52
  29.0 5.9 %collective-permute-start.7 = (f32[16,384]{1,0:T(8,128)S(1)}, f32[16,384]{1,0:T(8,128)S(1)}, u32[]{:S(2)}, u32[]{:S(2)}) collective-permute-start(f32[16,384]{1,0:T(8,128)S(1)} %pair.1.refs_0_), channel_id=1, source_target_pairs={{0,16},{4,20},{8,24},{12,28},{16,0},{20,4},{24,8},{28,12},{1,17},{... | collective-permute-start | bytes 73736 | tf_op jit(solution)/shard_map/ppermute | solution.py:52
  31.9 3.8 %collective-permute-start.8 = (f32[16,384]{1,0:T(8,128)S(1)}, f32[16,384]{1,0:T(8,128)S(1)}, u32[]{:S(2)}, u32[]{:S(2)}) collective-permute-start(f32[16,384]{1,0:T(8,128)S(1)} %pair.1.refs_0_), channel_id=1, source_target_pairs={{0,24},{4,28},{8,0},{12,4},{16,8},{20,12},{24,16},{28,20},{1,25},{... | collective-permute-start | bytes 73736 | tf_op jit(solution)/shard_map/ppermute | solution.py:52

commit v14 on v13

--- a/solution.py
+++ b/solution.py
@@ -86,13 +86,34 @@
             pltpu.make_async_copy(source, target, sem).wait()
 
 
+def lines_summed(total):
+    line = lax.broadcasted_iota(jnp.int32, total.shape, 0)
+    bit = 1
+    while bit < SUBLANES:
+        total = jnp.where((line & bit) == bit, pltpu.roll(total, total.shape[1] - bit, 1), total)
+        bit *= 2
+    return jnp.sum(total, axis=0, keepdims=True)
+
+
 def skewed_sum(outer, rows):
     width = outer.shape[1]
     total = outer[:SUBLANES]
     for start in range(SUBLANES, rows, SUBLANES):
         total = total + pltpu.roll(outer[start : start + SUBLANES], width - start, 1)
-    lines = [total[:1]] + [pltpu.roll(total[s : s + 1], width - s, 1) for s in range(1, SUBLANES)]
-    return functools.reduce(jnp.add, lines)
+    return lines_summed(total)
+
+
+def skewed_pair(outer, rows):
+    width = outer.shape[1]
+    lane = lax.broadcasted_iota(jnp.int32, (SUBLANES, width), 1)
+    high = outer[:SUBLANES]
+    low = jnp.zeros_like(high)
+    for start in range(SUBLANES, rows, SUBLANES):
+        turned = pltpu.roll(outer[start : start + SUBLANES], width - start, 1)
+        above = lane < width - start
+        high = high + jnp.where(above, turned, 0.0)
+        low = low + jnp.where(above, 0.0, turned)
+    return lines_summed(jnp.concatenate([low, high], axis=1))
 
 
 def diagonal_kernel(query_hbm, keys_hbm, values_hbm, cotangent_hbm, out_ref, left, right, sems):
@@ -185,13 +206,12 @@
     odd = is_odd()
     group_count, width = out_ref.shape
     group_width = near_ref.shape[1] // group_count
-    blank = jnp.zeros((rows, rows), jnp.float32)
     sums = []
     for group in range(group_count):
         columns = columns_of(group, group_width)
         near, two = near_ref[:, columns], two_ref[:, columns]
         outer = DOT_ROWS(lax.select(odd, near, two), lax.select(odd, two, near))
-        sums.append(skewed_sum(jnp.concatenate([blank, outer], axis=1), rows))
+        sums.append(skewed_pair(outer, rows))
     sums = jnp.concatenate(sums, axis=0)
     out_ref[...] = sum_ref[...] + jnp.concatenate(
         [jnp.zeros((group_count, width - 2 * rows), jnp.float32), sums], axis=1
@@ -202,13 +222,12 @@
     odd = is_odd()
     group_count, width = out_ref.shape
     group_width = across_ref.shape[1] // group_count
-    blank = jnp.zeros((rows, rows), jnp.float32)
     sums = []
     for group in range(group_count):
         columns = columns_of(group, group_width)
         across, swap = across_ref[:, columns], swap_ref[:, columns]
         outer = DOT_ROWS(lax.select(odd, swap, across), lax.select(odd, across, swap))
-        sums.append(skewed_sum(jnp.concatenate([blank, outer], axis=1), rows))
+        sums.append(skewed_pair(outer, rows))
     sums = jnp.concatenate(sums, axis=0)
     out_ref[...] = jnp.concatenate([sums, jnp.zeros((group_count, width - 2 * rows), jnp.float32)], axis=1)
 

time: 36.5 us -> 36.4 us (level)
  transfers between devices with their start and end apart: 9 -> 9, of which waited for: 4 -> 4; matrix products, arithmetic and copies ran while one was open for 0% -> 0% of each run, Pallas kernels for 23% -> 22%
where the time goes in v14:
time: 36.4 us; the launch traced here: 36.2 us
  starting transfers between devices  21 us (58%)
  Pallas kernels  10 us (27%)
  waiting for transfers between devices  4.32 us (12%)
  between operations  0.85 us (2%)
    ppermute x6, starting transfers between devices, moved(): lax.ppermute(block, axis, [pair for pair in route if 0 <= pair[1] < size])  15 us
    ppermute x3, starting transfers between devices, sum_terms(): terms.append(lax.ppermute(own, axis, route))  5.99 us
    ppermute x6, waiting for transfers between devices, moved(): lax.ppermute(block, axis, [pair for pair in route if 0 <= pair[1] < size])  3.55 us
    pallas_call x1, Pallas kernels, shards(): call(functools.partial(tiles_kernel, rows), 'tiles', in_specs=[WHOLE], ou...  2.22 us
    pallas_call x1, Pallas kernels, shards(): call(functools.partial(own_kernel, rows), 'own', flops=4 * 10 ** 9, in_sp...  1.64 us
    pallas_call x1, Pallas kernels, shards(): call(last_kernel, 'last', in_specs=[WHOLE] * 10, out_specs=[ANYWHERE] * 3...  1.35 us
    pallas_call x1, Pallas kernels, shards(): call(diagonal_kernel, 'diagonal', in_specs=[ANYWHERE] * 4, out_specs=WHOL...  1.28 us
    pallas_call x1, Pallas kernels, shards(): call(functools.partial(cross_kernel, rows), 'cross', in_specs=[WHOLE] * 2...  0.83 us
  transfers between devices with their start and end apart: 9, of which 4 were waited for; matrix products, arithmetic and copies ran while one was open for 0% of the time, Pallas kernels for 22%

profile of v14, /device:TPU:0, one launch (start us, length us, event | category | flops | bytes accessed | tf_op | source)
XLA Modules:
  0.0 36.2 jit_solution(1499273538044615819)
XLA Ops:
  0.7 1.3 %diagonal.1.sent_ref = bf16[128,1024]{1,0:T(8,128)(2,1)S(1)} custom-call(bf16[128,2048]{1,0:T(8,128)(2,1)} %query_ref.7, bf16[128,2048]{1,0:T(8,128)(2,1)} %keys_ref.7, bf16[128,2048]{1,0:T(8,128)(2,1)} %values_ref.7, bf16[128,2048]{1,0:T(8,128)(2,1)} %cotangent_ref.1), custom_call_target="tpu_custom_call" | custom-call | flops 1000000 | bytes 100000 | tf_op jit(solution)/shard_map/diagonal/pallas_call | solution.py:345
  2.0 0.0 copy-start.4
  2.0 0.7 %collective-permute-start = (bf16[128,1024]{1,0:T(8,128)(2,1)S(1)}, bf16[128,1024]{1,0:T(8,128)(2,1)S(1)}, u32[]{:S(2)}, u32[]{:S(2)}) collective-permute-start(bf16[128,1024]{1,0:T(8,128)(2,1)S(1)} %diagonal.1.sent_ref), channel_id=1, source_target_pairs={{4,8},{8,4},{12,16},{16,12},{20,24},{24,20},{5,9},{9,5},{13,17},{1... | collective-permute-start | bytes 786440 | tf_op jit(solution)/shard_map/ppermute | solution.py:35
  2.7 0.3 products.1
  3.0 7.6 %collective-permute-start.1 = (bf16[128,2048]{1,0:T(8,128)(2,1)S(1)}, bf16[128,2048]{1,0:T(8,128)(2,1)S(1)}, u32[]{:S(2)}, u32[]{:S(2)}) collective-permute-start(bf16[128,2048]{1,0:T(8,128)(2,1)S(1)} %get-tuple-element.23.across_ref), channel_id=1, source_target_pairs={{0,8},{8,16},{12,4},{16,24},{20,12},{28,20},{1,9},{9,17},{13,5},{1... | collective-permute-start | bytes 1572872 | tf_op jit(solution)/shard_map/ppermute | solution.py:35
  10.6 1.3 %collective-permute-start.2 = (bf16[128,2048]{1,0:T(8,128)(2,1)S(1)}, bf16[128,2048]{1,0:T(8,128)(2,1)S(1)}, u32[]{:S(2)}, u32[]{:S(2)}) collective-permute-start(bf16[128,2048]{1,0:T(8,128)(2,1)S(1)} %get-tuple-element.22.near_ref), channel_id=1, source_target_pairs={{4,12},{8,0},{12,20},{16,8},{20,28},{24,16},{5,13},{9,1},{13,21},{... | collective-permute-start | bytes 1572872 | tf_op jit(solution)/shard_map/ppermute | solution.py:35
  11.9 2.8 %collective-permute-start.4 = (bf16[128,2048]{1,0:T(8,128)(2,1)S(1)}, bf16[128,2048]{1,0:T(8,128)(2,1)S(1)}, u32[]{:S(2)}, u32[]{:S(2)}) collective-permute-start(bf16[128,2048]{1,0:T(8,128)(2,1)S(1)} %get-tuple-element.23.across_ref), channel_id=1, source_target_pairs={{0,4},{4,0},{8,12},{12,8},{16,20},{20,16},{24,28},{28,24},{1,5},{5... | collective-permute-start | bytes 1572872 | tf_op jit(solution)/shard_map/ppermute | solution.py:35
  14.7 2.2 %tiles.1 = (bf16[16,128,384]{2,1,0:T(8,128)(2,1)S(1)}, bf16[16,128,384]{2,1,0:T(8,128)(2,1)S(1)}) custom-call(bf16[16,384]{1,0:T(8,128)(2,1)S(1)} %copy-done.4), custom_call_target="tpu_custom_call" | custom-call | flops 1000000 | bytes 100000 | tf_op jit(solution)/shard_map/tiles/pallas_call | solution.py:365
  16.9 1.6 %own.1 = (f32[16,384]{1,0:T(8,128)S(1)}, f32[128,2048]{1,0:T(8,128)S(1)}, f32[128,2048]{1,0:T(8,128)S(1)}) custom-call(bf16[16,128,384]{2,1,0:T(8,128)(2,1)S(1)} %get-tuple-element.20.ready_tiles.tiles_ref, bf16[16,128,384]{2,1,0:T(8,128)(2,1)S(1)} %get-tuple-element.21.late_tiles.tiles_ref, bf16[128,2048]{1,0:T(8,128)(2,1)S(1)} %get-tuple-element.22.near_ref, ...), custom_call_target="tpu_custom_call" | custom-call | flops 4000000000 | bytes 100000 | tf_op jit(solution)/shard_map/own/pallas_call | solution.py:372
  18.6 2.9 %collective-permute-done.1.two_ref = bf16[128,2048]{1,0:T(8,128)(2,1)S(1)} collective-permute-done((bf16[128,2048]{1,0:T(8,128)(2,1)S(1)}, bf16[128,2048]{1,0:T(8,128)(2,1)S(1)}, u32[]{:S(2)}, u32[]{:S(2)}) %collective-permute-start.1) | collective-permute-done | bytes 524320 | tf_op jit(solution)/shard_map/ppermute | solution.py:35
  21.5 0.8 %two.1.sum_ref = f32[16,384]{1,0:T(8,128)S(1)} custom-call(f32[16,384]{1,0:T(8,128)S(1)} %get-tuple-element.25.sum_ref, bf16[128,2048]{1,0:T(8,128)(2,1)S(1)} %get-tuple-element.22.near_ref, bf16[128,2048]{1,0:T(8,128)(2,1)S(1)} %collective-permute-done.1.two_ref), custom_call_target="tpu_custom_call" | custom-call | flops 1000000 | bytes 100000 | tf_op jit(solution)/shard_map/two/pallas_call | solution.py:381
  22.3 2.6 %collective-permute-start.5 = (f32[16,384]{1,0:T(8,128)S(1)}, f32[16,384]{1,0:T(8,128)S(1)}, u32[]{:S(2)}, u32[]{:S(2)}) collective-permute-start(f32[16,384]{1,0:T(8,128)S(1)} %two.1.sum_ref), channel_id=1, source_target_pairs={{0,4},{4,0},{8,12},{12,8},{16,20},{20,16},{24,28},{28,24},{1,5},{5... | collective-permute-start | bytes 73736 | tf_op jit(solution)/shard_map/ppermute | solution.py:35
  24.9 0.4 %ready.1 = (f32[128,1024]{1,0:T(8,128)S(1)}, bf16[128,1024]{1,0:T(8,128)(2,1)S(1)}, bf16[128,1024]{1,0:T(8,128)(2,1)S(1)}) custom-call(bf16[16,128,384]{2,1,0:T(8,128)(2,1)S(1)} %get-tuple-element.20.ready_tiles.tiles_ref, f32[128,2048]{1,0:T(8,128)S(1)} %get-tuple-element.24.ready_ref, bf16[128,2048]{1,0:T(8,128)(2,1)S(1)} %collective-permute-done.1.two_ref, ...), custom_call_target="tpu_custom_call" | custom-call | flops 1000000 | bytes 100000 | tf_op jit(solution)/shard_map/ready/pallas_call | solution.py:390
  25.3 0.3 collective-permute-done.2.far_ref
  25.6 0.1 collective-permute-start.3
  25.7 0.4 collective-permute-done.4.swap_ref
  26.1 0.8 %cross.1.cross_ref = f32[16,384]{1,0:T(8,128)S(1)} custom-call(bf16[128,2048]{1,0:T(8,128)(2,1)S(1)} %get-tuple-element.23.across_ref, bf16[128,2048]{1,0:T(8,128)(2,1)S(1)} %collective-permute-done.4.swap_ref), custom_call_target="tpu_custom_call" | custom-call | flops 1000000 | bytes 100000 | tf_op jit(solution)/shard_map/cross/pallas_call | solution.py:407
  26.9 2.0 %collective-permute-start.6 = (f32[16,384]{1,0:T(8,128)S(1)}, f32[16,384]{1,0:T(8,128)S(1)}, u32[]{:S(2)}, u32[]{:S(2)}) collective-permute-start(f32[16,384]{1,0:T(8,128)S(1)} %pair.1.refs_0_), channel_id=1, source_target_pairs={{0,8},{4,12},{8,16},{12,20},{16,24},{20,28},{24,0},{28,4},{1,9},{5... | collective-permute-start | bytes 73736 | tf_op jit(solution)/shard_map/ppermute | solution.py:52
  29.0 2.8 %collective-permute-start.7 = (f32[16,384]{1,0:T(8,128)S(1)}, f32[16,384]{1,0:T(8,128)S(1)}, u32[]{:S(2)}, u32[]{:S(2)}) collective-permute-start(f32[16,384]{1,0:T(8,128)S(1)} %pair.1.refs_0_), channel_id=1, source_target_pairs={{0,16},{4,20},{8,24},{12,28},{16,0},{20,4},{24,8},{28,12},{1,17},{... | collective-permute-start | bytes 73736 | tf_op jit(solution)/shard_map/ppermute | solution.py:52
  31.8 1.1 %collective-permute-start.8 = (f32[16,384]{1,0:T(8,128)S(1)}, f32[16,384]{1,0:T(8,128)S(1)}, u32[]{:S(2)}, u32[]{:S(2)}) collective-permute-start(f32[16,384]{1,0:T(8,128)S(1)} %pair.1.refs_0_), channel_id=1, source_target_pairs={{0,24},{4,28},{8,0},{12,4},{16,8},{20,12},{24,16},{28,20},{1,25},{... | collective-permute-start | bytes 73736 | tf_op jit(solution)/shard_map/ppermute | solution.py:52
  32.9 0.5 %known.1 = (bf16[128,2048]{1,0:T(8,128)(2,1)S(1)}, bf16[128,2048]{1,0:T(8,128)(2,1)S(1)}) custom-call(bf16[16,128,384]{2,1,0:T(8,128)(2,1)S(1)} %get-tuple-element.21.late_tiles.tiles_ref, f32[128,2048]{1,0:T(8,128)S(1)} %get-tuple-element.29.late_ref, bf16[128,2048]{1,0:T(8,128)(2,1)S(1)} %collective-permute-done.4.swap_ref, ...), custom_call_target="tpu_custom_call" | custom-call | flops 4000000000 | bytes 100000 | tf_op jit(solution)/shard_map/known/pallas_call | solution.py:422
  33.5 1.3 %last.1 = (bf16[128,2048]{1,0:T(8,128)(2,1)}, bf16[128,2048]{1,0:T(8,128)(2,1)}, bf16[128,2048]{1,0:T(8,128)(2,1)}, f32[8,128]{1,0:T(8,128)S(1)}) custom-call(bf16[16,128,384]{2,1,0:T(8,128)(2,1)S(1)} %get-tuple-element.20.ready_tiles.tiles_ref, f32[128,1024]{1,0:T(8,128)S(1)} %get-tuple-element.26.rest_ref, ...), custom_call_target="tpu_custom_call" | custom-call | flops 1000000 | bytes 100000 | tf_op jit(solution)/shard_map/last/pallas_call | solution.py:441
  34.9 0.8 %collective-permute-done.8.refs_3_ = f32[16,384]{1,0:T(8,128)S(1)} collective-permute-done((f32[16,384]{1,0:T(8,128)S(1)}, f32[16,384]{1,0:T(8,128)S(1)}, u32[]{:S(2)}, u32[]{:S(2)}) %collective-permute-start.8) | collective-permute-done | bytes 24608 | tf_op jit(solution)/shard_map/ppermute | solution.py:52
  35.6 0.6 %add.1 = f32[16,384]{1,0:T(8,128)} custom-call(f32[16,384]{1,0:T(8,128)S(1)} %pair.1.refs_0_, f32[16,384]{1,0:T(8,128)S(1)} %collective-permute-done.6.refs_1_, f32[16,384]{1,0:T(8,128)S(1)} %collective-permute-done.7.refs_2_, f32[16,384]{1,0:T(8,128)S(1)} %collective-permute-done.8.refs_3_, f32[8,128]{1,0:T(8,128)S(1)} %get-tuple-element.35.refs_4_), custom_call_target="tpu_custom_call" | custom-call | flops 1000000 | bytes 100000 | tf_op jit(solution)/shard_map/add/pallas_call | solution.py:432
  (16 shorter events, 0.1 us)
Async XLA Ops:
  0.6 2.0 %copy-start = (bf16[128,2048]{1,0:T(8,128)(2,1)S(1)}, bf16[128,2048]{1,0:T(8,128)(2,1)}, u32[]{:S(2)}) copy-start(bf16[128,2048]{1,0:T(8,128)(2,1)} %query_ref.7) | copy-start | bytes 1572868
  0.6 2.0 %copy-start.1 = (bf16[128,2048]{1,0:T(8,128)(2,1)S(1)}, bf16[128,2048]{1,0:T(8,128)(2,1)}, u32[]{:S(2)}) copy-start(bf16[128,2048]{1,0:T(8,128)(2,1)} %keys_ref.7) | copy-start | bytes 1572868
  0.7 2.0 %copy-start.2 = (bf16[128,2048]{1,0:T(8,128)(2,1)S(1)}, bf16[128,2048]{1,0:T(8,128)(2,1)}, u32[]{:S(2)}) copy-start(bf16[128,2048]{1,0:T(8,128)(2,1)} %values_ref.7) | copy-start | bytes 1572868
  0.7 2.0 %copy-start.3 = (bf16[128,2048]{1,0:T(8,128)(2,1)S(1)}, bf16[128,2048]{1,0:T(8,128)(2,1)}, u32[]{:S(2)}) copy-start(bf16[128,2048]{1,0:T(8,128)(2,1)} %cotangent_ref.1) | copy-start | bytes 1572868
  2.0 12.7 %copy-start.4 = (bf16[16,384]{1,0:T(8,128)(2,1)S(1)}, bf16[16,384]{1,0:T(8,128)(2,1)}, u32[]{:S(2)}) copy-start(bf16[16,384]{1,0:T(8,128)(2,1)} %taps_ref.1) | copy-start | bytes 36868
  2.0 15.0 %collective-permute-start = (bf16[128,1024]{1,0:T(8,128)(2,1)S(1)}, bf16[128,1024]{1,0:T(8,128)(2,1)S(1)}, u32[]{:S(2)}, u32[]{:S(2)}) collective-permute-start(bf16[128,1024]{1,0:T(8,128)(2,1)S(1)} %diagonal.1.sent_ref), channel_id=1, source_target_pairs={{4,8},{8,4},{12,16},{16,12},{20,24},{24,20},{5,9},{9,5},{13,17},{1... | collective-permute-start | bytes 786440 | tf_op jit(solution)/shard_map/ppermute | solution.py:35
  3.0 18.4 %collective-permute-start.1 = (bf16[128,2048]{1,0:T(8,128)(2,1)S(1)}, bf16[128,2048]{1,0:T(8,128)(2,1)S(1)}, u32[]{:S(2)}, u32[]{:S(2)}) collective-permute-start(bf16[128,2048]{1,0:T(8,128)(2,1)S(1)} %get-tuple-element.23.across_ref), channel_id=1, source_target_pairs={{0,8},{8,16},{12,4},{16,24},{20,12},{28,20},{1,9},{9,17},{13,5},{1... | collective-permute-start | bytes 1572872 | tf_op jit(solution)/shard_map/ppermute | solution.py:35
  10.6 15.0 %collective-permute-start.2 = (bf16[128,2048]{1,0:T(8,128)(2,1)S(1)}, bf16[128,2048]{1,0:T(8,128)(2,1)S(1)}, u32[]{:S(2)}, u32[]{:S(2)}) collective-permute-start(bf16[128,2048]{1,0:T(8,128)(2,1)S(1)} %get-tuple-element.22.near_ref), channel_id=1, source_target_pairs={{4,12},{8,0},{12,20},{16,8},{20,28},{24,16},{5,13},{9,1},{13,21},{... | collective-permute-start | bytes 1572872 | tf_op jit(solution)/shard_map/ppermute | solution.py:35
  11.9 14.2 %collective-permute-start.4 = (bf16[128,2048]{1,0:T(8,128)(2,1)S(1)}, bf16[128,2048]{1,0:T(8,128)(2,1)S(1)}, u32[]{:S(2)}, u32[]{:S(2)}) collective-permute-start(bf16[128,2048]{1,0:T(8,128)(2,1)S(1)} %get-tuple-element.23.across_ref), channel_id=1, source_target_pairs={{0,4},{4,0},{8,12},{12,8},{16,20},{20,16},{24,28},{28,24},{1,5},{5... | collective-permute-start | bytes 1572872 | tf_op jit(solution)/shard_map/ppermute | solution.py:35
  22.3 4.6 %collective-permute-start.5 = (f32[16,384]{1,0:T(8,128)S(1)}, f32[16,384]{1,0:T(8,128)S(1)}, u32[]{:S(2)}, u32[]{:S(2)}) collective-permute-start(f32[16,384]{1,0:T(8,128)S(1)} %two.1.sum_ref), channel_id=1, source_target_pairs={{0,4},{4,0},{8,12},{12,8},{16,20},{20,16},{24,28},{28,24},{1,5},{5... | collective-permute-start | bytes 73736 | tf_op jit(solution)/shard_map/ppermute | solution.py:35
  25.6 7.8 %collective-permute-start.3 = (bf16[128,1024]{1,0:T(8,128)(2,1)S(1)}, bf16[128,1024]{1,0:T(8,128)(2,1)S(1)}, u32[]{:S(2)}, u32[]{:S(2)}) collective-permute-start(bf16[128,1024]{1,0:T(8,128)(2,1)S(1)} %forward.1), channel_id=1, source_target_pairs={{0,4},{4,0},{8,12},{12,8},{16,20},{20,16},{24,28},{28,24},{1,5},{5... | collective-permute-start | bytes 786440 | tf_op jit(solution)/shard_map/ppermute | solution.py:35
  26.9 7.9 %collective-permute-start.6 = (f32[16,384]{1,0:T(8,128)S(1)}, f32[16,384]{1,0:T(8,128)S(1)}, u32[]{:S(2)}, u32[]{:S(2)}) collective-permute-start(f32[16,384]{1,0:T(8,128)S(1)} %pair.1.refs_0_), channel_id=1, source_target_pairs={{0,8},{4,12},{8,16},{12,20},{16,24},{20,28},{24,0},{28,4},{1,9},{5... | collective-permute-start | bytes 73736 | tf_op jit(solution)/shard_map/ppermute | solution.py:52
  29.0 5.9 %collective-permute-start.7 = (f32[16,384]{1,0:T(8,128)S(1)}, f32[16,384]{1,0:T(8,128)S(1)}, u32[]{:S(2)}, u32[]{:S(2)}) collective-permute-start(f32[16,384]{1,0:T(8,128)S(1)} %pair.1.refs_0_), channel_id=1, source_target_pairs={{0,16},{4,20},{8,24},{12,28},{16,0},{20,4},{24,8},{28,12},{1,17},{... | collective-permute-start | bytes 73736 | tf_op jit(solution)/shard_map/ppermute | solution.py:52
  31.8 3.8 %collective-permute-start.8 = (f32[16,384]{1,0:T(8,128)S(1)}, f32[16,384]{1,0:T(8,128)S(1)}, u32[]{:S(2)}, u32[]{:S(2)}) collective-permute-start(f32[16,384]{1,0:T(8,128)S(1)} %pair.1.refs_0_), channel_id=1, source_target_pairs={{0,24},{4,28},{8,0},{12,4},{16,8},{20,12},{24,16},{28,20},{1,25},{... | collective-permute-start | bytes 73736 | tf_op jit(solution)/shard_map/ppermute | solution.py:52

commit v15 on v14

--- a/solution.py
+++ b/solution.py
@@ -116,31 +116,42 @@
     return lines_summed(jnp.concatenate([low, high], axis=1))
 
 
-def diagonal_kernel(query_hbm, keys_hbm, values_hbm, cotangent_hbm, out_ref, left, right, sems):
-    odd = is_odd()
-    half = out_ref.shape[1]
-    low, high = pl.ds(0, half), pl.ds(half, half)
-    copies = launch(
-        odd,
-        [
-            (1, keys_hbm.at[:, low], left),
-            (1, values_hbm.at[:, low], right),
-            (0, cotangent_hbm.at[:, high], left),
-            (0, query_hbm.at[:, high], right),
-        ],
-        sems,
-        0,
+def load_kernel(
+    query_hbm, keys_hbm, values_hbm, cotangent_hbm,
+    query_ref, keys_ref, values_ref, near_ref, across_ref, sent_ref, cotangent_ref, sems,
+):
+    odd = is_odd()
+    half = sent_ref.shape[1]
+    pairs = (
+        ((keys_hbm, keys_ref), (values_hbm, values_ref)),
+        ((cotangent_hbm, cotangent_ref), (query_hbm, query_ref)),
     )
-    finish(odd, copies)
-    out_ref[...] = product(left[...], right[...])
-
-
-def products_kernel(query_ref, keys_ref, values_ref, cotangent_ref, sent_ref, near_ref, across_ref):
-    odd = is_odd()
-    prod = product(keys_ref[...], values_ref[...])
-    grad = product(cotangent_ref[...], query_ref[...])
-    near_ref[...] = lax.select(odd, prod, grad)
-    across_ref[...] = lax.select(odd, grad, prod)
+    parts = [pl.ds(0, half), pl.ds(half, half)]
+    moves = []
+    for parity in (0, 1):
+        first = 1 - parity
+        for part in (parts[first], parts[parity]):
+            for pair in (pairs[first], pairs[parity]):
+                moves.extend((parity, source.at[:, part], target.at[:, part]) for source, target in pair)
+    copies = launch(odd, moves, sems, 0)
+    sides = len(moves) // 2
+    for parity in (0, 1):
+        mine = copies[parity * sides : (parity + 1) * sides]
+
+        @pl.when(odd if parity else jnp.logical_not(odd))
+        def _():
+            order = (1 - parity, parity)
+            for place, part in enumerate(order):
+                columns = slice(part * half, (part + 1) * half)
+                for _, source, target, sem in mine[place * sides // 2 : (place + 1) * sides // 2]:
+                    pltpu.make_async_copy(source, target, sem).wait()
+                prod = product(keys_ref[:, columns], values_ref[:, columns])
+                grad = product(cotangent_ref[:, columns], query_ref[:, columns])
+                near = prod if parity else grad
+                near_ref[:, columns] = near
+                across_ref[:, columns] = grad if parity else prod
+                if place == 0:
+                    sent_ref[...] = near
 
 
 def tiles_kernel(rows, taps_ref, ready_tiles, late_tiles):
@@ -342,22 +353,15 @@
     tiles, sums = pltpu.VMEM((group_count, rows, taps), bf16), pltpu.VMEM((group_count, taps), f32)
     outs = [jax.ShapeDtypeStruct((rows, local_width), bf16)] * 3
 
-    sent = call(
-        diagonal_kernel,
-        "diagonal",
+    query, keys, values, near, across, sent = call(
+        load_kernel,
+        "load",
         in_specs=[ANYWHERE] * 4,
-        out_specs=WHOLE,
-        out_shape=half_block,
-        scratch_shapes=[half_block] * 2 + [pltpu.SemaphoreType.DMA((4,))],
+        out_specs=[WHOLE] * 6,
+        out_shape=[block] * 5 + [half_block],
+        scratch_shapes=[block, pltpu.SemaphoreType.DMA((16,))],
     )(*in_hbm(query, keys, values, cotangent))
     diagonal = moved(sent, "ctx", (-1, 1))
-    near, across = call(
-        products_kernel,
-        "products",
-        in_specs=[WHOLE] * 4 + [ANYWHERE],
-        out_specs=[WHOLE] * 2,
-        out_shape=[block] * 2,
-    )(*in_vmem(query, keys, values, cotangent), sent)
     two = moved(across, "ctx", (2, -2))
     far = moved(near, "ctx", (-2, 2))
     swap = moved(across, "ctx", (1, -1))

time: 36.4 us -> 36.3 us (level)
    pallas_call x2 -> x1, Pallas kernels: 1.6 us -> 1.78 us  [shards(): call(load_kernel, 'load', in_specs=[ANYWHERE] * 4, out_specs=[WHOLE] * 6,...]
  transfers between devices with their start and end apart: 9 -> 9, of which waited for: 4 -> 3; matrix products, arithmetic and copies ran while one was open for 0% -> 0% of each run, Pallas kernels for 22% -> 22%
where the time goes in v15:
time: 36.3 us; the launch traced here: 36.1 us
  starting transfers between devices  21.1 us (58%)
  Pallas kernels  10.2 us (28%)
  waiting for transfers between devices  4.06 us (11%)
  between operations  0.78 us (2%)
    ppermute x6, starting transfers between devices, moved(): lax.ppermute(block, axis, [pair for pair in route if 0 <= pair[1] < size])  15 us
    ppermute x3, starting transfers between devices, sum_terms(): terms.append(lax.ppermute(own, axis, route))  6.06 us
    ppermute x6, waiting for transfers between devices, moved(): lax.ppermute(block, axis, [pair for pair in route if 0 <= pair[1] < size])  3.5 us
    pallas_call x1, Pallas kernels, shards(): call(functools.partial(tiles_kernel, rows), 'tiles', in_specs=[WHOLE], ou...  2.22 us
    pallas_call x1, Pallas kernels, shards(): call(load_kernel, 'load', in_specs=[ANYWHERE] * 4, out_specs=[WHOLE] * 6,...  1.78 us
    pallas_call x1, Pallas kernels, shards(): call(functools.partial(own_kernel, rows), 'own', flops=4 * 10 ** 9, in_sp...  1.63 us
    pallas_call x1, Pallas kernels, shards(): call(last_kernel, 'last', in_specs=[WHOLE] * 10, out_specs=[ANYWHERE] * 3...  1.33 us
    pallas_call x1, Pallas kernels, shards(): call(functools.partial(two_kernel, rows), 'two', in_specs=[WHOLE] * 3, ou...  0.83 us
  transfers between devices with their start and end apart: 9, of which 3 were waited for; matrix products, arithmetic and copies ran while one was open for 0% of the time, Pallas kernels for 22%

profile of v15, /device:TPU:0, one launch (start us, length us, event | category | flops | bytes accessed | tf_op | source)
XLA Modules:
  0.0 36.1 jit_solution(7034791705414452584)
XLA Ops:
  0.6 1.8 %load.1 = (bf16[128,2048]{1,0:T(8,128)(2,1)S(1)}, bf16[128,2048]{1,0:T(8,128)(2,1)S(1)}, bf16[128,2048]{1,0:T(8,128)(2,1)S(1)}, bf16[128,2048]{1,0:T(8,128)(2,1)...) custom-call(bf16[128,2048]{1,0:T(8,128)(2,1)} %query_hbm.1, bf16[128,2048]{1,0:T(8,128)(2,1)} %keys_hbm.1, ...), custom_call_target="tpu_custom_call" | custom-call | flops 1000000 | bytes 100000 | tf_op jit(solution)/shard_map/load/pallas_call | solution.py:356
  2.4 0.7 %collective-permute-start = (bf16[128,1024]{1,0:T(8,128)(2,1)S(1)}, bf16[128,1024]{1,0:T(8,128)(2,1)S(1)}, u32[]{:S(2)}, u32[]{:S(2)}) collective-permute-start(bf16[128,1024]{1,0:T(8,128)(2,1)S(1)} %get-tuple-element.28), channel_id=1, source_target_pairs={{4,8},{8,4},{12,16},{16,12},{20,24},{24,20},{5,9},{9,5},{13,17},{1... | collective-permute-start | bytes 786440 | tf_op jit(solution)/shard_map/ppermute | solution.py:35
  3.1 7.6 %collective-permute-start.1 = (bf16[128,2048]{1,0:T(8,128)(2,1)S(1)}, bf16[128,2048]{1,0:T(8,128)(2,1)S(1)}, u32[]{:S(2)}, u32[]{:S(2)}) collective-permute-start(bf16[128,2048]{1,0:T(8,128)(2,1)S(1)} %get-tuple-element.27.across_ref), channel_id=1, source_target_pairs={{0,8},{8,16},{12,4},{16,24},{20,12},{28,20},{1,9},{9,17},{13,5},{1... | collective-permute-start | bytes 1572872 | tf_op jit(solution)/shard_map/ppermute | solution.py:35
  10.7 1.3 %collective-permute-start.2 = (bf16[128,2048]{1,0:T(8,128)(2,1)S(1)}, bf16[128,2048]{1,0:T(8,128)(2,1)S(1)}, u32[]{:S(2)}, u32[]{:S(2)}) collective-permute-start(bf16[128,2048]{1,0:T(8,128)(2,1)S(1)} %get-tuple-element.26.near_ref), channel_id=1, source_target_pairs={{4,12},{8,0},{12,20},{16,8},{20,28},{24,16},{5,13},{9,1},{13,21},{... | collective-permute-start | bytes 1572872 | tf_op jit(solution)/shard_map/ppermute | solution.py:35
  12.0 2.8 %collective-permute-start.4 = (bf16[128,2048]{1,0:T(8,128)(2,1)S(1)}, bf16[128,2048]{1,0:T(8,128)(2,1)S(1)}, u32[]{:S(2)}, u32[]{:S(2)}) collective-permute-start(bf16[128,2048]{1,0:T(8,128)(2,1)S(1)} %get-tuple-element.27.across_ref), channel_id=1, source_target_pairs={{0,4},{4,0},{8,12},{12,8},{16,20},{20,16},{24,28},{28,24},{1,5},{5... | collective-permute-start | bytes 1572872 | tf_op jit(solution)/shard_map/ppermute | solution.py:35
  14.8 2.2 %tiles.1 = (bf16[16,128,384]{2,1,0:T(8,128)(2,1)S(1)}, bf16[16,128,384]{2,1,0:T(8,128)(2,1)S(1)}) custom-call(bf16[16,384]{1,0:T(8,128)(2,1)S(1)} %copy-done), custom_call_target="tpu_custom_call" | custom-call | flops 1000000 | bytes 100000 | tf_op jit(solution)/shard_map/tiles/pallas_call | solution.py:369
  17.0 0.0 collective-permute-done.diagonal_ref
  17.0 1.6 %own.1 = (f32[16,384]{1,0:T(8,128)S(1)}, f32[128,2048]{1,0:T(8,128)S(1)}, f32[128,2048]{1,0:T(8,128)S(1)}) custom-call(bf16[16,128,384]{2,1,0:T(8,128)(2,1)S(1)} %get-tuple-element.24.ready_tiles.tiles_ref, bf16[16,128,384]{2,1,0:T(8,128)(2,1)S(1)} %get-tuple-element.25.late_tiles.tiles_ref, bf16[128,2048]{1,0:T(8,128)(2,1)S(1)} %get-tuple-element.26.near_ref, ...), custom_call_target="tpu_custom_call" | custom-call | flops 4000000000 | bytes 100000 | tf_op jit(solution)/shard_map/own/pallas_call | solution.py:376
  18.7 2.9 %collective-permute-done.1.two_ref = bf16[128,2048]{1,0:T(8,128)(2,1)S(1)} collective-permute-done((bf16[128,2048]{1,0:T(8,128)(2,1)S(1)}, bf16[128,2048]{1,0:T(8,128)(2,1)S(1)}, u32[]{:S(2)}, u32[]{:S(2)}) %collective-permute-start.1) | collective-permute-done | bytes 524320 | tf_op jit(solution)/shard_map/ppermute | solution.py:35
  21.5 0.8 %two.1.sum_ref = f32[16,384]{1,0:T(8,128)S(1)} custom-call(f32[16,384]{1,0:T(8,128)S(1)} %get-tuple-element.33.sum_ref, bf16[128,2048]{1,0:T(8,128)(2,1)S(1)} %get-tuple-element.26.near_ref, bf16[128,2048]{1,0:T(8,128)(2,1)S(1)} %collective-permute-done.1.two_ref), custom_call_target="tpu_custom_call" | custom-call | flops 1000000 | bytes 100000 | tf_op jit(solution)/shard_map/two/pallas_call | solution.py:385
  22.4 2.6 %collective-permute-start.5 = (f32[16,384]{1,0:T(8,128)S(1)}, f32[16,384]{1,0:T(8,128)S(1)}, u32[]{:S(2)}, u32[]{:S(2)}) collective-permute-start(f32[16,384]{1,0:T(8,128)S(1)} %two.1.sum_ref), channel_id=1, source_target_pairs={{0,4},{4,0},{8,12},{12,8},{16,20},{20,16},{24,28},{28,24},{1,5},{5... | collective-permute-start | bytes 73736 | tf_op jit(solution)/shard_map/ppermute | solution.py:35
  25.0 0.4 %ready.1 = (f32[128,1024]{1,0:T(8,128)S(1)}, bf16[128,1024]{1,0:T(8,128)(2,1)S(1)}, bf16[128,1024]{1,0:T(8,128)(2,1)S(1)}) custom-call(bf16[16,128,384]{2,1,0:T(8,128)(2,1)S(1)} %get-tuple-element.24.ready_tiles.tiles_ref, f32[128,2048]{1,0:T(8,128)S(1)} %get-tuple-element.29.ready_ref, bf16[128,2048]{1,0:T(8,128)(2,1)S(1)} %collective-permute-done.1.two_ref, ...), custom_call_target="tpu_custom_call" | custom-call | flops 1000000 | bytes 100000 | tf_op jit(solution)/shard_map/ready/pallas_call | solution.py:394
  25.4 0.6 %collective-permute-done.2.far_ref = bf16[128,2048]{1,0:T(8,128)(2,1)S(1)} collective-permute-done((bf16[128,2048]{1,0:T(8,128)(2,1)S(1)}, bf16[128,2048]{1,0:T(8,128)(2,1)S(1)}, u32[]{:S(2)}, u32[]{:S(2)}) %collective-permute-start.2) | collective-permute-done | bytes 524320 | tf_op jit(solution)/shard_map/ppermute | solution.py:35
  26.0 0.1 collective-permute-start.3
  26.1 0.0 collective-permute-done.4.swap_ref
  26.1 0.8 %cross.1.cross_ref = f32[16,384]{1,0:T(8,128)S(1)} custom-call(bf16[128,2048]{1,0:T(8,128)(2,1)S(1)} %get-tuple-element.27.across_ref, bf16[128,2048]{1,0:T(8,128)(2,1)S(1)} %collective-permute-done.4.swap_ref), custom_call_target="tpu_custom_call" | custom-call | flops 1000000 | bytes 100000 | tf_op jit(solution)/shard_map/cross/pallas_call | solution.py:411
  27.0 0.0 collective-permute-done.5.other_ref
  27.0 2.1 %collective-permute-start.6 = (f32[16,384]{1,0:T(8,128)S(1)}, f32[16,384]{1,0:T(8,128)S(1)}, u32[]{:S(2)}, u32[]{:S(2)}) collective-permute-start(f32[16,384]{1,0:T(8,128)S(1)} %pair.1.refs_0_), channel_id=1, source_target_pairs={{0,8},{4,12},{8,16},{12,20},{16,24},{20,28},{24,0},{28,4},{1,9},{5... | collective-permute-start | bytes 73736 | tf_op jit(solution)/shard_map/ppermute | solution.py:52
  29.1 2.6 %collective-permute-start.7 = (f32[16,384]{1,0:T(8,128)S(1)}, f32[16,384]{1,0:T(8,128)S(1)}, u32[]{:S(2)}, u32[]{:S(2)}) collective-permute-start(f32[16,384]{1,0:T(8,128)S(1)} %pair.1.refs_0_), channel_id=1, source_target_pairs={{0,16},{4,20},{8,24},{12,28},{16,0},{20,4},{24,8},{28,12},{1,17},{... | collective-permute-start | bytes 73736 | tf_op jit(solution)/shard_map/ppermute | solution.py:52
  31.7 1.4 %collective-permute-start.8 = (f32[16,384]{1,0:T(8,128)S(1)}, f32[16,384]{1,0:T(8,128)S(1)}, u32[]{:S(2)}, u32[]{:S(2)}) collective-permute-start(f32[16,384]{1,0:T(8,128)S(1)} %pair.1.refs_0_), channel_id=1, source_target_pairs={{0,24},{4,28},{8,0},{12,4},{16,8},{20,12},{24,16},{28,20},{1,25},{... | collective-permute-start | bytes 73736 | tf_op jit(solution)/shard_map/ppermute | solution.py:52
  33.0 0.5 %known.1 = (bf16[128,2048]{1,0:T(8,128)(2,1)S(1)}, bf16[128,2048]{1,0:T(8,128)(2,1)S(1)}) custom-call(bf16[16,128,384]{2,1,0:T(8,128)(2,1)S(1)} %get-tuple-element.25.late_tiles.tiles_ref, f32[128,2048]{1,0:T(8,128)S(1)} %get-tuple-element.37.late_ref, bf16[128,2048]{1,0:T(8,128)(2,1)S(1)} %collective-permute-done.4.swap_ref, ...), custom_call_target="tpu_custom_call" | custom-call | flops 4000000000 | bytes 100000 | tf_op jit(solution)/shard_map/known/pallas_call | solution.py:426
  33.6 1.3 %last.1 = (bf16[128,2048]{1,0:T(8,128)(2,1)}, bf16[128,2048]{1,0:T(8,128)(2,1)}, bf16[128,2048]{1,0:T(8,128)(2,1)}, f32[8,128]{1,0:T(8,128)S(1)}) custom-call(bf16[16,128,384]{2,1,0:T(8,128)(2,1)S(1)} %get-tuple-element.24.ready_tiles.tiles_ref, f32[128,1024]{1,0:T(8,128)S(1)} %get-tuple-element.34.rest_ref, ...), custom_call_target="tpu_custom_call" | custom-call | flops 1000000 | bytes 100000 | tf_op jit(solution)/shard_map/last/pallas_call | solution.py:445
  35.0 0.6 %collective-permute-done.8.refs_3_ = f32[16,384]{1,0:T(8,128)S(1)} collective-permute-done((f32[16,384]{1,0:T(8,128)S(1)}, f32[16,384]{1,0:T(8,128)S(1)}, u32[]{:S(2)}, u32[]{:S(2)}) %collective-permute-start.8) | collective-permute-done | bytes 24608 | tf_op jit(solution)/shard_map/ppermute | solution.py:52
  35.5 0.6 %add.1 = f32[16,384]{1,0:T(8,128)} custom-call(f32[16,384]{1,0:T(8,128)S(1)} %pair.1.refs_0_, f32[16,384]{1,0:T(8,128)S(1)} %collective-permute-done.6.refs_1_, f32[16,384]{1,0:T(8,128)S(1)} %collective-permute-done.7.refs_2_, f32[16,384]{1,0:T(8,128)S(1)} %collective-permute-done.8.refs_3_, f32[8,128]{1,0:T(8,128)S(1)} %get-tuple-element.43.refs_4_), custom_call_target="tpu_custom_call" | custom-call | flops 1000000 | bytes 100000 | tf_op jit(solution)/shard_map/add/pallas_call | solution.py:436
  (7 shorter events, 0.1 us)
Async XLA Ops:
  0.6 14.2 %copy-start = (bf16[16,384]{1,0:T(8,128)(2,1)S(1)}, bf16[16,384]{1,0:T(8,128)(2,1)}, u32[]{:S(2)}) copy-start(bf16[16,384]{1,0:T(8,128)(2,1)} %taps_ref.1) | copy-start | bytes 36868
  2.4 14.6 %collective-permute-start = (bf16[128,1024]{1,0:T(8,128)(2,1)S(1)}, bf16[128,1024]{1,0:T(8,128)(2,1)S(1)}, u32[]{:S(2)}, u32[]{:S(2)}) collective-permute-start(bf16[128,1024]{1,0:T(8,128)(2,1)S(1)} %get-tuple-element.28), channel_id=1, source_target_pairs={{4,8},{8,4},{12,16},{16,12},{20,24},{24,20},{5,9},{9,5},{13,17},{1... | collective-permute-start | bytes 786440 | tf_op jit(solution)/shard_map/ppermute | solution.py:35
  3.1 18.4 %collective-permute-start.1 = (bf16[128,2048]{1,0:T(8,128)(2,1)S(1)}, bf16[128,2048]{1,0:T(8,128)(2,1)S(1)}, u32[]{:S(2)}, u32[]{:S(2)}) collective-permute-start(bf16[128,2048]{1,0:T(8,128)(2,1)S(1)} %get-tuple-element.27.across_ref), channel_id=1, source_target_pairs={{0,8},{8,16},{12,4},{16,24},{20,12},{28,20},{1,9},{9,17},{13,5},{1... | collective-permute-start | bytes 1572872 | tf_op jit(solution)/shard_map/ppermute | solution.py:35
  10.7 15.3 %collective-permute-start.2 = (bf16[128,2048]{1,0:T(8,128)(2,1)S(1)}, bf16[128,2048]{1,0:T(8,128)(2,1)S(1)}, u32[]{:S(2)}, u32[]{:S(2)}) collective-permute-start(bf16[128,2048]{1,0:T(8,128)(2,1)S(1)} %get-tuple-element.26.near_ref), channel_id=1, source_target_pairs={{4,12},{8,0},{12,20},{16,8},{20,28},{24,16},{5,13},{9,1},{13,21},{... | collective-permute-start | bytes 1572872 | tf_op jit(solution)/shard_map/ppermute | solution.py:35
  12.0 14.1 %collective-permute-start.4 = (bf16[128,2048]{1,0:T(8,128)(2,1)S(1)}, bf16[128,2048]{1,0:T(8,128)(2,1)S(1)}, u32[]{:S(2)}, u32[]{:S(2)}) collective-permute-start(bf16[128,2048]{1,0:T(8,128)(2,1)S(1)} %get-tuple-element.27.across_ref), channel_id=1, source_target_pairs={{0,4},{4,0},{8,12},{12,8},{16,20},{20,16},{24,28},{28,24},{1,5},{5... | collective-permute-start | bytes 1572872 | tf_op jit(solution)/shard_map/ppermute | solution.py:35
  22.4 4.6 %collective-permute-start.5 = (f32[16,384]{1,0:T(8,128)S(1)}, f32[16,384]{1,0:T(8,128)S(1)}, u32[]{:S(2)}, u32[]{:S(2)}) collective-permute-start(f32[16,384]{1,0:T(8,128)S(1)} %two.1.sum_ref), channel_id=1, source_target_pairs={{0,4},{4,0},{8,12},{12,8},{16,20},{20,16},{24,28},{28,24},{1,5},{5... | collective-permute-start | bytes 73736 | tf_op jit(solution)/shard_map/ppermute | solution.py:35
  26.0 7.6 %collective-permute-start.3 = (bf16[128,1024]{1,0:T(8,128)(2,1)S(1)}, bf16[128,1024]{1,0:T(8,128)(2,1)S(1)}, u32[]{:S(2)}, u32[]{:S(2)}) collective-permute-start(bf16[128,1024]{1,0:T(8,128)(2,1)S(1)} %forward.1), channel_id=1, source_target_pairs={{0,4},{4,0},{8,12},{12,8},{16,20},{20,16},{24,28},{28,24},{1,5},{5... | collective-permute-start | bytes 786440 | tf_op jit(solution)/shard_map/ppermute | solution.py:35
  27.0 8.0 %collective-permute-start.6 = (f32[16,384]{1,0:T(8,128)S(1)}, f32[16,384]{1,0:T(8,128)S(1)}, u32[]{:S(2)}, u32[]{:S(2)}) collective-permute-start(f32[16,384]{1,0:T(8,128)S(1)} %pair.1.refs_0_), channel_id=1, source_target_pairs={{0,8},{4,12},{8,16},{12,20},{16,24},{20,28},{24,0},{28,4},{1,9},{5... | collective-permute-start | bytes 73736 | tf_op jit(solution)/shard_map/ppermute | solution.py:52
  29.1 5.9 %collective-permute-start.7 = (f32[16,384]{1,0:T(8,128)S(1)}, f32[16,384]{1,0:T(8,128)S(1)}, u32[]{:S(2)}, u32[]{:S(2)}) collective-permute-start(f32[16,384]{1,0:T(8,128)S(1)} %pair.1.refs_0_), channel_id=1, source_target_pairs={{0,16},{4,20},{8,24},{12,28},{16,0},{20,4},{24,8},{28,12},{1,17},{... | collective-permute-start | bytes 73736 | tf_op jit(solution)/shard_map/ppermute | solution.py:52
  31.7 3.8 %collective-permute-start.8 = (f32[16,384]{1,0:T(8,128)S(1)}, f32[16,384]{1,0:T(8,128)S(1)}, u32[]{:S(2)}, u32[]{:S(2)}) collective-permute-start(f32[16,384]{1,0:T(8,128)S(1)} %pair.1.refs_0_), channel_id=1, source_target_pairs={{0,24},{4,28},{8,0},{12,4},{16,8},{20,12},{24,16},{28,20},{1,25},{... | collective-permute-start | bytes 73736 | tf_op jit(solution)/shard_map/ppermute | solution.py:52

commit v16 on v14

--- a/solution.py
+++ b/solution.py
@@ -45,10 +45,13 @@
     while stride < size:
         own = terms[0] if len(terms) == 1 else add(*terms)
         members = 4 if 4 * stride <= size else 2
+        rounds = [(1, (0, 3)), (2, range(4)), (3, range(4)), (1, (1, 2))] if members == 4 else [(1, range(2))]
         terms = [own]
-        for turn in range(1, members):
+        for turn, senders in rounds:
             places = [(i, i // stride % members) for i in range(size)]
-            route = [(i, i + ((place + turn) % members - place) * stride) for i, place in places]
+            route = [
+                (i, i + ((place + turn) % members - place) * stride) for i, place in places if place in senders
+            ]
             terms.append(lax.ppermute(own, axis, route))
         stride *= members
     return terms

time: 36.4 us -> 38.3 us (1.052)
  the two profiles are of different devices: /device:TPU:0 before, /device:TPU:18 now
where the time goes in v16:
time: 38.3 us; the launch traced here: 38 us
  starting transfers between devices  19.5 us (51%)
  Pallas kernels  10 us (26%)
  waiting for transfers between devices  7.66 us (20%)
  between operations  0.87 us (2%)
    ppermute x6, starting transfers between devices, moved(): lax.ppermute(block, axis, [pair for pair in route if 0 <= pair[1] < size])  11.7 us
    ppermute x4, starting transfers between devices, sum_terms(): terms.append(lax.ppermute(own, axis, route))  7.75 us
    ppermute x6, waiting for transfers between devices, moved(): lax.ppermute(block, axis, [pair for pair in route if 0 <= pair[1] < size])  6.2 us
    pallas_call x1, Pallas kernels, shards(): call(functools.partial(tiles_kernel, rows), 'tiles', in_specs=[WHOLE], ou...  2.22 us
    pallas_call x1, Pallas kernels, shards(): call(functools.partial(own_kernel, rows), 'own', flops=4 * 10 ** 9, in_sp...  1.64 us
    ppermute x4, waiting for transfers between devices, sum_terms(): terms.append(lax.ppermute(own, axis, route))  1.46 us
    pallas_call x1, Pallas kernels, shards(): call(last_kernel, 'last', in_specs=[WHOLE] * 10, out_specs=[ANYWHERE] * 3...  1.34 us
    pallas_call x1, Pallas kernels, shards(): call(diagonal_kernel, 'diagonal', in_specs=[ANYWHERE] * 4, out_specs=WHOL...  1.28 us
  transfers between devices with their start and end apart: 10, of which 4 were waited for; matrix products, arithmetic and copies ran while one was open for 0% of the time, Pallas kernels for 21%

profile of v16, /device:TPU:18, one launch (start us, length us, event | category | flops | bytes accessed | tf_op | source)
XLA Modules:
  0.0 38.0 jit_solution(12002615471581232423)
XLA Ops:
  0.7 1.3 %diagonal.1.sent_ref = bf16[128,1024]{1,0:T(8,128)(2,1)S(1)} custom-call(bf16[128,2048]{1,0:T(8,128)(2,1)} %query_ref.7, bf16[128,2048]{1,0:T(8,128)(2,1)} %keys_ref.7, bf16[128,2048]{1,0:T(8,128)(2,1)} %values_ref.7, bf16[128,2048]{1,0:T(8,128)(2,1)} %cotangent_ref.1), custom_call_target="tpu_custom_call" | custom-call | flops 1000000 | bytes 100000 | tf_op jit(solution)/shard_map/diagonal/pallas_call | solution.py:348
  2.0 3.5 %collective-permute-start = (bf16[128,1024]{1,0:T(8,128)(2,1)S(1)}, bf16[128,1024]{1,0:T(8,128)(2,1)S(1)}, u32[]{:S(2)}, u32[]{:S(2)}) collective-permute-start(bf16[128,1024]{1,0:T(8,128)(2,1)S(1)} %diagonal.1.sent_ref), channel_id=1, source_target_pairs={{4,8},{8,4},{12,16},{16,12},{20,24},{24,20},{5,9},{9,5},{13,17},{1... | collective-permute-start | bytes 786440 | tf_op jit(solution)/shard_map/ppermute | solution.py:35
  5.5 0.3 products.1
  5.8 2.4 %collective-permute-start.1 = (bf16[128,2048]{1,0:T(8,128)(2,1)S(1)}, bf16[128,2048]{1,0:T(8,128)(2,1)S(1)}, u32[]{:S(2)}, u32[]{:S(2)}) collective-permute-start(bf16[128,2048]{1,0:T(8,128)(2,1)S(1)} %get-tuple-element.23.across_ref), channel_id=1, source_target_pairs={{0,8},{8,16},{12,4},{16,24},{20,12},{28,20},{1,9},{9,17},{13,5},{1... | collective-permute-start | bytes 1572872 | tf_op jit(solution)/shard_map/ppermute | solution.py:35
  8.2 3.5 %collective-permute-start.2 = (bf16[128,2048]{1,0:T(8,128)(2,1)S(1)}, bf16[128,2048]{1,0:T(8,128)(2,1)S(1)}, u32[]{:S(2)}, u32[]{:S(2)}) collective-permute-start(bf16[128,2048]{1,0:T(8,128)(2,1)S(1)} %get-tuple-element.22.near_ref), channel_id=1, source_target_pairs={{4,12},{8,0},{12,20},{16,8},{20,28},{24,16},{5,13},{9,1},{13,21},{... | collective-permute-start | bytes 1572872 | tf_op jit(solution)/shard_map/ppermute | solution.py:35
  11.7 0.4 %collective-permute-start.4 = (bf16[128,2048]{1,0:T(8,128)(2,1)S(1)}, bf16[128,2048]{1,0:T(8,128)(2,1)S(1)}, u32[]{:S(2)}, u32[]{:S(2)}) collective-permute-start(bf16[128,2048]{1,0:T(8,128)(2,1)S(1)} %get-tuple-element.23.across_ref), channel_id=1, source_target_pairs={{0,4},{4,0},{8,12},{12,8},{16,20},{20,16},{24,28},{28,24},{1,5},{5... | collective-permute-start | bytes 1572872 | tf_op jit(solution)/shard_map/ppermute | solution.py:35
  12.1 2.2 %tiles.1 = (bf16[16,128,384]{2,1,0:T(8,128)(2,1)S(1)}, bf16[16,128,384]{2,1,0:T(8,128)(2,1)S(1)}) custom-call(bf16[16,384]{1,0:T(8,128)(2,1)S(1)} %copy-done.4), custom_call_target="tpu_custom_call" | custom-call | flops 1000000 | bytes 100000 | tf_op jit(solution)/shard_map/tiles/pallas_call | solution.py:368
  14.3 1.6 %own.1 = (f32[16,384]{1,0:T(8,128)S(1)}, f32[128,2048]{1,0:T(8,128)S(1)}, f32[128,2048]{1,0:T(8,128)S(1)}) custom-call(bf16[16,128,384]{2,1,0:T(8,128)(2,1)S(1)} %get-tuple-element.20.ready_tiles.tiles_ref, bf16[16,128,384]{2,1,0:T(8,128)(2,1)S(1)} %get-tuple-element.21.late_tiles.tiles_ref, bf16[128,2048]{1,0:T(8,128)(2,1)S(1)} %get-tuple-element.22.near_ref, ...), custom_call_target="tpu_custom_call" | custom-call | flops 4000000000 | bytes 100000 | tf_op jit(solution)/shard_map/own/pallas_call | solution.py:375
  16.0 5.1 %collective-permute-done.1.two_ref = bf16[128,2048]{1,0:T(8,128)(2,1)S(1)} collective-permute-done((bf16[128,2048]{1,0:T(8,128)(2,1)S(1)}, bf16[128,2048]{1,0:T(8,128)(2,1)S(1)}, u32[]{:S(2)}, u32[]{:S(2)}) %collective-permute-start.1) | collective-permute-done | bytes 524320 | tf_op jit(solution)/shard_map/ppermute | solution.py:35
  21.1 0.8 %two.1.sum_ref = f32[16,384]{1,0:T(8,128)S(1)} custom-call(f32[16,384]{1,0:T(8,128)S(1)} %get-tuple-element.25.sum_ref, bf16[128,2048]{1,0:T(8,128)(2,1)S(1)} %get-tuple-element.22.near_ref, bf16[128,2048]{1,0:T(8,128)(2,1)S(1)} %collective-permute-done.1.two_ref), custom_call_target="tpu_custom_call" | custom-call | flops 1000000 | bytes 100000 | tf_op jit(solution)/shard_map/two/pallas_call | solution.py:384
  21.9 0.4 %collective-permute-start.5 = (f32[16,384]{1,0:T(8,128)S(1)}, f32[16,384]{1,0:T(8,128)S(1)}, u32[]{:S(2)}, u32[]{:S(2)}) collective-permute-start(f32[16,384]{1,0:T(8,128)S(1)} %two.1.sum_ref), channel_id=1, source_target_pairs={{0,4},{4,0},{8,12},{12,8},{16,20},{20,16},{24,28},{28,24},{1,5},{5... | collective-permute-start | bytes 73736 | tf_op jit(solution)/shard_map/ppermute | solution.py:35
  22.3 0.4 ready.1
  22.7 0.5 %collective-permute-done.2.far_ref = bf16[128,2048]{1,0:T(8,128)(2,1)S(1)} collective-permute-done((bf16[128,2048]{1,0:T(8,128)(2,1)S(1)}, bf16[128,2048]{1,0:T(8,128)(2,1)S(1)}, u32[]{:S(2)}, u32[]{:S(2)}) %collective-permute-start.2) | collective-permute-done | bytes 524320 | tf_op jit(solution)/shard_map/ppermute | solution.py:35
  23.2 1.6 %collective-permute-start.3 = (bf16[128,1024]{1,0:T(8,128)(2,1)S(1)}, bf16[128,1024]{1,0:T(8,128)(2,1)S(1)}, u32[]{:S(2)}, u32[]{:S(2)}) collective-permute-start(bf16[128,1024]{1,0:T(8,128)(2,1)S(1)} %forward.1), channel_id=1, source_target_pairs={{0,4},{4,0},{8,12},{12,8},{16,20},{20,16},{24,28},{28,24},{1,5},{5... | collective-permute-start | bytes 786440 | tf_op jit(solution)/shard_map/ppermute | solution.py:35
  24.8 0.6 %collective-permute-done.4.swap_ref = bf16[128,2048]{1,0:T(8,128)(2,1)S(1)} collective-permute-done((bf16[128,2048]{1,0:T(8,128)(2,1)S(1)}, bf16[128,2048]{1,0:T(8,128)(2,1)S(1)}, u32[]{:S(2)}, u32[]{:S(2)}) %collective-permute-start.4) | collective-permute-done | bytes 524320 | tf_op jit(solution)/shard_map/ppermute | solution.py:35
  25.4 0.8 %cross.1.cross_ref = f32[16,384]{1,0:T(8,128)S(1)} custom-call(bf16[128,2048]{1,0:T(8,128)(2,1)S(1)} %get-tuple-element.23.across_ref, bf16[128,2048]{1,0:T(8,128)(2,1)S(1)} %collective-permute-done.4.swap_ref), custom_call_target="tpu_custom_call" | custom-call | flops 1000000 | bytes 100000 | tf_op jit(solution)/shard_map/cross/pallas_call | solution.py:410
  26.3 0.7 %collective-permute-start.6 = (f32[16,384]{1,0:T(8,128)S(1)}, f32[16,384]{1,0:T(8,128)S(1)}, u32[]{:S(2)}, u32[]{:S(2)}) collective-permute-start(f32[16,384]{1,0:T(8,128)S(1)} %pair.1.refs_0_), channel_id=1, source_target_pairs={{0,8},{4,12},{24,0},{28,4},{1,9},{5,13},{25,1},{29,5},{2,10},{6,14... | collective-permute-start | bytes 73736 | tf_op jit(solution)/shard_map/ppermute | solution.py:55
  26.9 3.2 %collective-permute-start.7 = (f32[16,384]{1,0:T(8,128)S(1)}, f32[16,384]{1,0:T(8,128)S(1)}, u32[]{:S(2)}, u32[]{:S(2)}) collective-permute-start(f32[16,384]{1,0:T(8,128)S(1)} %pair.1.refs_0_), channel_id=1, source_target_pairs={{0,16},{4,20},{8,24},{12,28},{16,0},{20,4},{24,8},{28,12},{1,17},{... | collective-permute-start | bytes 73736 | tf_op jit(solution)/shard_map/ppermute | solution.py:55
  30.1 1.6 %collective-permute-start.8 = (f32[16,384]{1,0:T(8,128)S(1)}, f32[16,384]{1,0:T(8,128)S(1)}, u32[]{:S(2)}, u32[]{:S(2)}) collective-permute-start(f32[16,384]{1,0:T(8,128)S(1)} %pair.1.refs_0_), channel_id=1, source_target_pairs={{0,24},{4,28},{8,0},{12,4},{16,8},{20,12},{24,16},{28,20},{1,25},{... | collective-permute-start | bytes 73736 | tf_op jit(solution)/shard_map/ppermute | solution.py:55
  31.7 2.3 %collective-permute-start.9 = (f32[16,384]{1,0:T(8,128)S(1)}, f32[16,384]{1,0:T(8,128)S(1)}, u32[]{:S(2)}, u32[]{:S(2)}) collective-permute-start(f32[16,384]{1,0:T(8,128)S(1)} %pair.1.refs_0_), channel_id=1, source_target_pairs={{8,16},{12,20},{16,24},{20,28},{9,17},{13,21},{17,25},{21,29},{10,... | collective-permute-start | bytes 73736 | tf_op jit(solution)/shard_map/ppermute | solution.py:55
  34.0 0.5 %known.1 = (bf16[128,2048]{1,0:T(8,128)(2,1)S(1)}, bf16[128,2048]{1,0:T(8,128)(2,1)S(1)}) custom-call(bf16[16,128,384]{2,1,0:T(8,128)(2,1)S(1)} %get-tuple-element.21.late_tiles.tiles_ref, f32[128,2048]{1,0:T(8,128)S(1)} %get-tuple-element.29.late_ref, bf16[128,2048]{1,0:T(8,128)(2,1)S(1)} %collective-permute-done.4.swap_ref, ...), custom_call_target="tpu_custom_call" | custom-call | flops 4000000000 | bytes 100000 | tf_op jit(solution)/shard_map/known/pallas_call | solution.py:425
  34.6 1.3 %last.1 = (bf16[128,2048]{1,0:T(8,128)(2,1)}, bf16[128,2048]{1,0:T(8,128)(2,1)}, bf16[128,2048]{1,0:T(8,128)(2,1)}, f32[8,128]{1,0:T(8,128)S(1)}) custom-call(bf16[16,128,384]{2,1,0:T(8,128)(2,1)S(1)} %get-tuple-element.20.ready_tiles.tiles_ref, f32[128,1024]{1,0:T(8,128)S(1)} %get-tuple-element.26.rest_ref, ...), custom_call_target="tpu_custom_call" | custom-call | flops 1000000 | bytes 100000 | tf_op jit(solution)/shard_map/last/pallas_call | solution.py:444
  36.0 1.4 %collective-permute-done.9.refs_4_ = f32[16,384]{1,0:T(8,128)S(1)} collective-permute-done((f32[16,384]{1,0:T(8,128)S(1)}, f32[16,384]{1,0:T(8,128)S(1)}, u32[]{:S(2)}, u32[]{:S(2)}) %collective-permute-start.9) | collective-permute-done | bytes 24608 | tf_op jit(solution)/shard_map/ppermute | solution.py:55
  37.4 0.6 %add.1 = f32[16,384]{1,0:T(8,128)} custom-call(f32[16,384]{1,0:T(8,128)S(1)} %pair.1.refs_0_, f32[16,384]{1,0:T(8,128)S(1)} %collective-permute-done.6.refs_1_, f32[16,384]{1,0:T(8,128)S(1)} %collective-permute-done.7.refs_2_, f32[16,384]{1,0:T(8,128)S(1)} %collective-permute-done.8.refs_3_, f32[16,384]{1,0:T(8,128)S(1)} %collective-permute-done.9.refs_4_, ...), custom_call_target="tpu_custom_call" | custom-call | flops 1000000 | bytes 100000 | tf_op jit(solution)/shard_map/add/pallas_call | solution.py:435
  (18 shorter events, 0.1 us)
Async XLA Ops:
  0.6 4.8 %copy-start = (bf16[128,2048]{1,0:T(8,128)(2,1)S(1)}, bf16[128,2048]{1,0:T(8,128)(2,1)}, u32[]{:S(2)}) copy-start(bf16[128,2048]{1,0:T(8,128)(2,1)} %query_ref.7) | copy-start | bytes 1572868
  0.6 4.8 %copy-start.1 = (bf16[128,2048]{1,0:T(8,128)(2,1)S(1)}, bf16[128,2048]{1,0:T(8,128)(2,1)}, u32[]{:S(2)}) copy-start(bf16[128,2048]{1,0:T(8,128)(2,1)} %keys_ref.7) | copy-start | bytes 1572868
  0.7 4.8 %copy-start.2 = (bf16[128,2048]{1,0:T(8,128)(2,1)S(1)}, bf16[128,2048]{1,0:T(8,128)(2,1)}, u32[]{:S(2)}) copy-start(bf16[128,2048]{1,0:T(8,128)(2,1)} %values_ref.7) | copy-start | bytes 1572868
  0.7 4.8 %copy-start.3 = (bf16[128,2048]{1,0:T(8,128)(2,1)S(1)}, bf16[128,2048]{1,0:T(8,128)(2,1)}, u32[]{:S(2)}) copy-start(bf16[128,2048]{1,0:T(8,128)(2,1)} %cotangent_ref.1) | copy-start | bytes 1572868
  2.0 10.1 %copy-start.4 = (bf16[16,384]{1,0:T(8,128)(2,1)S(1)}, bf16[16,384]{1,0:T(8,128)(2,1)}, u32[]{:S(2)}) copy-start(bf16[16,384]{1,0:T(8,128)(2,1)} %taps_ref.1) | copy-start | bytes 36868
  2.0 12.4 %collective-permute-start = (bf16[128,1024]{1,0:T(8,128)(2,1)S(1)}, bf16[128,1024]{1,0:T(8,128)(2,1)S(1)}, u32[]{:S(2)}, u32[]{:S(2)}) collective-permute-start(bf16[128,1024]{1,0:T(8,128)(2,1)S(1)} %diagonal.1.sent_ref), channel_id=1, source_target_pairs={{4,8},{8,4},{12,16},{16,12},{20,24},{24,20},{5,9},{9,5},{13,17},{1... | collective-permute-start | bytes 786440 | tf_op jit(solution)/shard_map/ppermute | solution.py:35
  5.8 15.3 %collective-permute-start.1 = (bf16[128,2048]{1,0:T(8,128)(2,1)S(1)}, bf16[128,2048]{1,0:T(8,128)(2,1)S(1)}, u32[]{:S(2)}, u32[]{:S(2)}) collective-permute-start(bf16[128,2048]{1,0:T(8,128)(2,1)S(1)} %get-tuple-element.23.across_ref), channel_id=1, source_target_pairs={{0,8},{8,16},{12,4},{16,24},{20,12},{28,20},{1,9},{9,17},{13,5},{1... | collective-permute-start | bytes 1572872 | tf_op jit(solution)/shard_map/ppermute | solution.py:35
  8.2 15.0 %collective-permute-start.2 = (bf16[128,2048]{1,0:T(8,128)(2,1)S(1)}, bf16[128,2048]{1,0:T(8,128)(2,1)S(1)}, u32[]{:S(2)}, u32[]{:S(2)}) collective-permute-start(bf16[128,2048]{1,0:T(8,128)(2,1)S(1)} %get-tuple-element.22.near_ref), channel_id=1, source_target_pairs={{4,12},{8,0},{12,20},{16,8},{20,28},{24,16},{5,13},{9,1},{13,21},{... | collective-permute-start | bytes 1572872 | tf_op jit(solution)/shard_map/ppermute | solution.py:35
  11.7 13.7 %collective-permute-start.4 = (bf16[128,2048]{1,0:T(8,128)(2,1)S(1)}, bf16[128,2048]{1,0:T(8,128)(2,1)S(1)}, u32[]{:S(2)}, u32[]{:S(2)}) collective-permute-start(bf16[128,2048]{1,0:T(8,128)(2,1)S(1)} %get-tuple-element.23.across_ref), channel_id=1, source_target_pairs={{0,4},{4,0},{8,12},{12,8},{16,20},{20,16},{24,28},{28,24},{1,5},{5... | collective-permute-start | bytes 1572872 | tf_op jit(solution)/shard_map/ppermute | solution.py:35
  21.9 4.3 %collective-permute-start.5 = (f32[16,384]{1,0:T(8,128)S(1)}, f32[16,384]{1,0:T(8,128)S(1)}, u32[]{:S(2)}, u32[]{:S(2)}) collective-permute-start(f32[16,384]{1,0:T(8,128)S(1)} %two.1.sum_ref), channel_id=1, source_target_pairs={{0,4},{4,0},{8,12},{12,8},{16,20},{20,16},{24,28},{28,24},{1,5},{5... | collective-permute-start | bytes 73736 | tf_op jit(solution)/shard_map/ppermute | solution.py:35
  23.2 11.4 %collective-permute-start.3 = (bf16[128,1024]{1,0:T(8,128)(2,1)S(1)}, bf16[128,1024]{1,0:T(8,128)(2,1)S(1)}, u32[]{:S(2)}, u32[]{:S(2)}) collective-permute-start(bf16[128,1024]{1,0:T(8,128)(2,1)S(1)} %forward.1), channel_id=1, source_target_pairs={{0,4},{4,0},{8,12},{12,8},{16,20},{20,16},{24,28},{28,24},{1,5},{5... | collective-permute-start | bytes 786440 | tf_op jit(solution)/shard_map/ppermute | solution.py:35
  26.3 9.7 %collective-permute-start.6 = (f32[16,384]{1,0:T(8,128)S(1)}, f32[16,384]{1,0:T(8,128)S(1)}, u32[]{:S(2)}, u32[]{:S(2)}) collective-permute-start(f32[16,384]{1,0:T(8,128)S(1)} %pair.1.refs_0_), channel_id=1, source_target_pairs={{0,8},{4,12},{24,0},{28,4},{1,9},{5,13},{25,1},{29,5},{2,10},{6,14... | collective-permute-start | bytes 73736 | tf_op jit(solution)/shard_map/ppermute | solution.py:55
  26.9 9.0 %collective-permute-start.7 = (f32[16,384]{1,0:T(8,128)S(1)}, f32[16,384]{1,0:T(8,128)S(1)}, u32[]{:S(2)}, u32[]{:S(2)}) collective-permute-start(f32[16,384]{1,0:T(8,128)S(1)} %pair.1.refs_0_), channel_id=1, source_target_pairs={{0,16},{4,20},{8,24},{12,28},{16,0},{20,4},{24,8},{28,12},{1,17},{... | collective-permute-start | bytes 73736 | tf_op jit(solution)/shard_map/ppermute | solution.py:55
  30.1 5.9 %collective-permute-start.8 = (f32[16,384]{1,0:T(8,128)S(1)}, f32[16,384]{1,0:T(8,128)S(1)}, u32[]{:S(2)}, u32[]{:S(2)}) collective-permute-start(f32[16,384]{1,0:T(8,128)S(1)} %pair.1.refs_0_), channel_id=1, source_target_pairs={{0,24},{4,28},{8,0},{12,4},{16,8},{20,12},{24,16},{28,20},{1,25},{... | collective-permute-start | bytes 73736 | tf_op jit(solution)/shard_map/ppermute | solution.py:55
  31.7 5.7 %collective-permute-start.9 = (f32[16,384]{1,0:T(8,128)S(1)}, f32[16,384]{1,0:T(8,128)S(1)}, u32[]{:S(2)}, u32[]{:S(2)}) collective-permute-start(f32[16,384]{1,0:T(8,128)S(1)} %pair.1.refs_0_), channel_id=1, source_target_pairs={{8,16},{12,20},{16,24},{20,28},{9,17},{13,21},{17,25},{21,29},{10,... | collective-permute-start | bytes 73736 | tf_op jit(solution)/shard_map/ppermute | solution.py:55

commit v17 on v14

--- a/solution.py
+++ b/solution.py
@@ -135,12 +135,18 @@
     out_ref[...] = product(left[...], right[...])
 
 
-def products_kernel(query_ref, keys_ref, values_ref, cotangent_ref, sent_ref, near_ref, across_ref):
-    odd = is_odd()
+def products_kernel(
+    query_ref, keys_ref, values_ref, cotangent_ref, sent_ref, near_ref, across_ref, low_ref, high_ref
+):
+    odd = is_odd()
+    half = low_ref.shape[1]
     prod = product(keys_ref[...], values_ref[...])
     grad = product(cotangent_ref[...], query_ref[...])
     near_ref[...] = lax.select(odd, prod, grad)
-    across_ref[...] = lax.select(odd, grad, prod)
+    across = lax.select(odd, grad, prod)
+    across_ref[...] = across
+    low_ref[...] = across[:, :half]
+    high_ref[...] = across[:, half:]
 
 
 def tiles_kernel(rows, taps_ref, ready_tiles, late_tiles):
@@ -202,7 +208,7 @@
     sum_ref[...] = jnp.concatenate([sums, jnp.zeros((group_count, width - 2 * rows), jnp.float32)], axis=1)
 
 
-def two_kernel(rows, sum_ref, near_ref, two_ref, out_ref):
+def two_kernel(rows, sum_ref, near_ref, two_ref, cross_ref, out_ref):
     odd = is_odd()
     group_count, width = out_ref.shape
     group_width = near_ref.shape[1] // group_count
@@ -218,7 +224,7 @@
     )
 
 
-def cross_kernel(rows, across_ref, swap_ref, out_ref):
+def cross_kernel(rows, across_ref, swap_ref, after_ref, out_ref):
     odd = is_odd()
     group_count, width = out_ref.shape
     group_width = across_ref.shape[1] // group_count
@@ -232,8 +238,10 @@
     out_ref[...] = jnp.concatenate([sums, jnp.zeros((group_count, width - 2 * rows), jnp.float32)], axis=1)
 
 
-def pair_kernel(factor, sum_ref, other_ref, cross_ref, rest_ref, out_ref):
-    out_ref[...] = (sum_ref[...] + other_ref[...] + cross_ref[...]) * factor
+def pair_kernel(factor, sum_ref, other_ref, low_ref, high_ref, rest_ref, out_ref):
+    half = low_ref.shape[0]
+    out_ref[:half] = (sum_ref[:half] + other_ref[:half] + low_ref[...]) * factor
+    out_ref[half:] = (sum_ref[half:] + other_ref[half:] + high_ref[...]) * factor
 
 
 def add_kernel(*refs):
@@ -263,13 +271,18 @@
         other[:, low] = scaled(known, keys_ref[:, high])
 
 
-def known_kernel(tiles_ref, late_ref, swap_ref, far_ref, query_ref, keys_ref, values_ref, one, other):
+def known_kernel(
+    tiles_ref, late_ref, low_ref, high_ref, far_ref, query_ref, keys_ref, values_ref, one, other
+):
     odd = is_odd()
     group_count, rows, _ = tiles_ref.shape
     group_width = far_ref.shape[1] // group_count
+    half = group_count // 2
     for group in range(group_count):
         columns = columns_of(group, group_width)
-        arrived = jnp.concatenate([swap_ref[:, columns], far_ref[:, columns]], axis=0)
+        inner = columns_of(group % half, group_width)
+        swap = (low_ref if group < half else high_ref)[:, inner]
+        arrived = jnp.concatenate([swap, far_ref[:, columns]], axis=0)
         late = late_ref[:, columns] + DOT(tiles_ref[group, :, rows:], arrived)
         one[:, columns] = scaled(late, lax.select(odd, query_ref[:, columns], values_ref[:, columns]))
         other[:, columns] = scaled(late, keys_ref[:, columns])
@@ -340,6 +353,7 @@
     block, half_block = pltpu.VMEM((rows, local_width), bf16), pltpu.VMEM((rows, half_width), bf16)
     wide, half_wide = pltpu.VMEM((rows, local_width), f32), pltpu.VMEM((rows, half_width), f32)
     tiles, sums = pltpu.VMEM((group_count, rows, taps), bf16), pltpu.VMEM((group_count, taps), f32)
+    half_sums = pltpu.VMEM((group_count // 2, taps), f32)
     outs = [jax.ShapeDtypeStruct((rows, local_width), bf16)] * 3
 
     sent = call(
@@ -351,16 +365,17 @@
         scratch_shapes=[half_block] * 2 + [pltpu.SemaphoreType.DMA((4,))],
     )(*in_hbm(query, keys, values, cotangent))
     diagonal = moved(sent, "ctx", (-1, 1))
-    near, across = call(
+    near, across, across_low, across_high = call(
         products_kernel,
         "products",
         in_specs=[WHOLE] * 4 + [ANYWHERE],
-        out_specs=[WHOLE] * 2,
-        out_shape=[block] * 2,
+        out_specs=[WHOLE] * 4,
+        out_shape=[block, block, half_block, half_block],
     )(*in_vmem(query, keys, values, cotangent), sent)
     two = moved(across, "ctx", (2, -2))
     far = moved(near, "ctx", (-2, 2))
-    swap = moved(across, "ctx", (1, -1))
+    swap_low = moved(across_low, "ctx", (1, -1))
+    swap_high = moved(across_high, "ctx", (1, -1))
 
     ready_tiles, late_tiles = call(
         functools.partial(tiles_kernel, rows),
@@ -378,13 +393,23 @@
         out_shape=[sums, wide, wide],
     )(*in_vmem(ready_tiles, late_tiles, near, across, diagonal))
 
+    def cross_of(own, swap, after):
+        return call(
+            functools.partial(cross_kernel, rows),
+            "cross",
+            in_specs=[WHOLE] * 2 + [ANYWHERE],
+            out_specs=WHOLE,
+            out_shape=half_sums,
+        )(*in_vmem(own, swap), after)
+
+    cross_low = cross_of(across_low, swap_low, partial)
     partial = call(
         functools.partial(two_kernel, rows),
         "two",
-        in_specs=[WHOLE] * 3,
+        in_specs=[WHOLE] * 3 + [ANYWHERE],
         out_specs=WHOLE,
         out_shape=sums,
-    )(*in_vmem(partial, near, two))
+    )(*in_vmem(partial, near, two), cross_low)
     other = moved(partial, "ctx", (1, -1))
 
     rest, ready_one, ready_other = call(
@@ -395,38 +420,31 @@
         out_shape=[half_wide, half_block, half_block],
     )(*in_vmem(ready_tiles, ready, two, query, keys, values), partial)
 
-    forwarded = call(
+    sent_on = call(
         forward_kernel,
         "forward",
         in_specs=[WHOLE, ANYWHERE],
         out_specs=WHOLE,
         out_shape=half_block,
     )(*in_vmem(far), rest)
-    forwarded = moved(forwarded, "ctx", (1, -1))
-
-    cross = call(
-        functools.partial(cross_kernel, rows),
-        "cross",
-        in_specs=[WHOLE] * 2,
-        out_specs=WHOLE,
-        out_shape=sums,
-    )(*in_vmem(across, swap))
+    forwarded = moved(sent_on, "ctx", (1, -1))
+
     pair_sum = call(
         functools.partial(pair_kernel, factor),
         "pair",
-        in_specs=[WHOLE] * 3 + [ANYWHERE],
+        in_specs=[WHOLE] * 4 + [ANYWHERE],
         out_specs=WHOLE,
         out_shape=sums,
-    )(*in_vmem(partial, other, cross), rest)
+    )(*in_vmem(partial, other, cross_low, cross_of(across_high, swap_high, sent_on)), rest)
 
     known_one, known_other = call(
         known_kernel,
         "known",
         flops=4 * 10**9,
-        in_specs=[WHOLE] * 7,
+        in_specs=[WHOLE] * 8,
         out_specs=[WHOLE] * 2,
         out_shape=[block] * 2,
-    )(*in_vmem(late_tiles, late, swap, far, query, keys, values))
+    )(*in_vmem(late_tiles, late, swap_low, swap_high, far, query, keys, values))
 
     def add(*terms, out_shape=sums, after=known_one):
         return call(

time: 36.4 us -> 36.9 us (1.014)
  Pallas kernels: 10 us -> 10.5 us
  starting transfers between devices: 21 us -> 20.5 us
  waiting for transfers between devices: 4.32 us -> 4.74 us
    ppermute x6 -> x7, waiting for transfers between devices: 3.55 us -> 4.04 us  [moved(): lax.ppermute(block, axis, [pair for pair in route if 0 <= pair[1] < size])]
    ppermute x6 -> x7, starting transfers between devices: 15 us -> 14.6 us  [moved(): lax.ppermute(block, axis, [pair for pair in route if 0 <= pair[1] < size])]
    pallas_call x4 -> x5, Pallas kernels: 2.21 us -> 2.6 us  [the longest x2 1.24 us: cross_of(): call(functools.partial(cross_kernel, rows), 'cross', in_specs=[WHOLE] * 2...]
  transfers between devices with their start and end apart: 9 -> 10, of which waited for: 4 -> 4; matrix products, arithmetic and copies ran while one was open for 0% -> 0% of each run, Pallas kernels for 22% -> 24%
where the time goes in v17:
time: 36.9 us; the launch traced here: 36.7 us
  starting transfers between devices  20.5 us (56%)
  Pallas kernels  10.5 us (28%)
  waiting for transfers between devices  4.74 us (13%)
  between operations  0.86 us (2%)
    ppermute x7, starting transfers between devices, moved(): lax.ppermute(block, axis, [pair for pair in route if 0 <= pair[1] < size])  14.6 us
    ppermute x3, starting transfers between devices, sum_terms(): terms.append(lax.ppermute(own, axis, route))  5.94 us
    ppermute x7, waiting for transfers between devices, moved(): lax.ppermute(block, axis, [pair for pair in route if 0 <= pair[1] < size])  4.04 us
    pallas_call x1, Pallas kernels, shards(): call(functools.partial(tiles_kernel, rows), 'tiles', in_specs=[WHOLE], ou...  2.22 us
    pallas_call x1, Pallas kernels, shards(): call(functools.partial(own_kernel, rows), 'own', flops=4 * 10 ** 9, in_sp...  1.71 us
    pallas_call x1, Pallas kernels, shards(): call(last_kernel, 'last', in_specs=[WHOLE] * 10, out_specs=[ANYWHERE] * 3...  1.35 us
    pallas_call x1, Pallas kernels, shards(): call(diagonal_kernel, 'diagonal', in_specs=[ANYWHERE] * 4, out_specs=WHOL...  1.28 us
    pallas_call x2, Pallas kernels, cross_of(): call(functools.partial(cross_kernel, rows), 'cross', in_specs=[WHOLE] * 2...  1.24 us
  transfers between devices with their start and end apart: 10, of which 4 were waited for; matrix products, arithmetic and copies ran while one was open for 0% of the time, Pallas kernels for 24%

profile of v17, /device:TPU:0, one launch (start us, length us, event | category | flops | bytes accessed | tf_op | source)
XLA Modules:
  0.0 36.7 jit_solution(2338782041477195728)
XLA Ops:
  0.7 1.3 %diagonal.1.sent_ref = bf16[128,1024]{1,0:T(8,128)(2,1)S(1)} custom-call(bf16[128,2048]{1,0:T(8,128)(2,1)} %query_ref.7, bf16[128,2048]{1,0:T(8,128)(2,1)} %keys_ref.7, bf16[128,2048]{1,0:T(8,128)(2,1)} %values_ref.7, bf16[128,2048]{1,0:T(8,128)(2,1)} %cotangent_ref.1), custom_call_target="tpu_custom_call" | custom-call | flops 1000000 | bytes 100000 | tf_op jit(solution)/shard_map/diagonal/pallas_call | solution.py:359
  2.0 0.7 %collective-permute-start = (bf16[128,1024]{1,0:T(8,128)(2,1)S(1)}, bf16[128,1024]{1,0:T(8,128)(2,1)S(1)}, u32[]{:S(2)}, u32[]{:S(2)}) collective-permute-start(bf16[128,1024]{1,0:T(8,128)(2,1)S(1)} %diagonal.1.sent_ref), channel_id=1, source_target_pairs={{4,8},{8,4},{12,16},{16,12},{20,24},{24,20},{5,9},{9,5},{13,17},{1... | collective-permute-start | bytes 786440 | tf_op jit(solution)/shard_map/ppermute | solution.py:35
  2.7 0.3 products.1
  3.0 7.6 %collective-permute-start.1 = (bf16[128,2048]{1,0:T(8,128)(2,1)S(1)}, bf16[128,2048]{1,0:T(8,128)(2,1)S(1)}, u32[]{:S(2)}, u32[]{:S(2)}) collective-permute-start(bf16[128,2048]{1,0:T(8,128)(2,1)S(1)} %get-tuple-element.25.across_ref), channel_id=1, source_target_pairs={{0,8},{8,16},{12,4},{16,24},{20,12},{28,20},{1,9},{9,17},{13,5},{1... | collective-permute-start | bytes 1572872 | tf_op jit(solution)/shard_map/ppermute | solution.py:35
  10.6 1.3 %collective-permute-start.3 = (bf16[128,2048]{1,0:T(8,128)(2,1)S(1)}, bf16[128,2048]{1,0:T(8,128)(2,1)S(1)}, u32[]{:S(2)}, u32[]{:S(2)}) collective-permute-start(bf16[128,2048]{1,0:T(8,128)(2,1)S(1)} %get-tuple-element.24.near_ref), channel_id=1, source_target_pairs={{4,12},{8,0},{12,20},{16,8},{20,28},{24,16},{5,13},{9,1},{13,21},{... | collective-permute-start | bytes 1572872 | tf_op jit(solution)/shard_map/ppermute | solution.py:35
  11.9 2.8 %collective-permute-start.2 = (bf16[128,1024]{1,0:T(8,128)(2,1)S(1)}, bf16[128,1024]{1,0:T(8,128)(2,1)S(1)}, u32[]{:S(2)}, u32[]{:S(2)}) collective-permute-start(bf16[128,1024]{1,0:T(8,128)(2,1)S(1)} %get-tuple-element.28.across_ref), channel_id=1, source_target_pairs={{0,4},{4,0},{8,12},{12,8},{16,20},{20,16},{24,28},{28,24},{1,5},{5... | collective-permute-start | bytes 786440 | tf_op jit(solution)/shard_map/ppermute | solution.py:35
  14.8 2.2 %tiles.1 = (bf16[16,128,384]{2,1,0:T(8,128)(2,1)S(1)}, bf16[16,128,384]{2,1,0:T(8,128)(2,1)S(1)}) custom-call(bf16[16,384]{1,0:T(8,128)(2,1)S(1)} %copy-done.4), custom_call_target="tpu_custom_call" | custom-call | flops 1000000 | bytes 100000 | tf_op jit(solution)/shard_map/tiles/pallas_call | solution.py:380
  17.0 1.7 %own.1 = (f32[16,384]{1,0:T(8,128)S(1)}, f32[128,2048]{1,0:T(8,128)S(1)}, f32[128,2048]{1,0:T(8,128)S(1)}) custom-call(bf16[16,128,384]{2,1,0:T(8,128)(2,1)S(1)} %get-tuple-element.22.ready_tiles.tiles_ref, bf16[16,128,384]{2,1,0:T(8,128)(2,1)S(1)} %get-tuple-element.23.late_tiles.tiles_ref, bf16[128,2048]{1,0:T(8,128)(2,1)S(1)} %get-tuple-element.24.near_ref, ...), custom_call_target="tpu_custom_call" | custom-call | flops 4000000000 | bytes 100000 | tf_op jit(solution)/shard_map/own/pallas_call | solution.py:387
  18.8 3.2 %collective-permute-done.2.swap_ref.low_ref = bf16[128,1024]{1,0:T(8,128)(2,1)S(1)} collective-permute-done((bf16[128,1024]{1,0:T(8,128)(2,1)S(1)}, bf16[128,1024]{1,0:T(8,128)(2,1)S(1)}, u32[]{:S(2)}, u32[]{:S(2)}) %collective-permute-start.2) | collective-permute-done | bytes 262176 | tf_op jit(solution)/shard_map/ppermute | solution.py:35
  21.9 0.6 %cross.2.cross_ref.low_ref = f32[8,384]{1,0:T(8,128)S(1)} custom-call(bf16[128,1024]{1,0:T(8,128)(2,1)S(1)} %get-tuple-element.28.across_ref, bf16[128,1024]{1,0:T(8,128)(2,1)S(1)} %collective-permute-done.2.swap_ref.low_ref, f32[16,384]{1,0:T(8,128)S(1)} %get-tuple-element.27.after_ref.sum_ref), custom_call_target="tpu_custom_call" | custom-call | flops 1000000 | bytes 100000 | tf_op jit(solution)/shard_map/cross/pallas_call | solution.py:397
  22.6 0.8 %two.1.sum_ref = f32[16,384]{1,0:T(8,128)S(1)} custom-call(f32[16,384]{1,0:T(8,128)S(1)} %get-tuple-element.27.after_ref.sum_ref, bf16[128,2048]{1,0:T(8,128)(2,1)S(1)} %get-tuple-element.24.near_ref, bf16[128,2048]{1,0:T(8,128)(2,1)S(1)} %collective-permute-done.1.two_ref, f32[8,384]{1,0:T(8,128)S(1)} %cross.2.cross_ref.low_ref), custom_call_target="tpu_custom_call" | custom-call | flops 1000000 | bytes 100000 | tf_op jit(solution)/shard_map/two/pallas_call | solution.py:406
  23.4 2.1 %collective-permute-start.6 = (f32[16,384]{1,0:T(8,128)S(1)}, f32[16,384]{1,0:T(8,128)S(1)}, u32[]{:S(2)}, u32[]{:S(2)}) collective-permute-start(f32[16,384]{1,0:T(8,128)S(1)} %two.1.sum_ref), channel_id=1, source_target_pairs={{0,4},{4,0},{8,12},{12,8},{16,20},{20,16},{24,28},{28,24},{1,5},{5... | collective-permute-start | bytes 73736 | tf_op jit(solution)/shard_map/ppermute | solution.py:35
  25.5 0.4 %ready.1 = (f32[128,1024]{1,0:T(8,128)S(1)}, bf16[128,1024]{1,0:T(8,128)(2,1)S(1)}, bf16[128,1024]{1,0:T(8,128)(2,1)S(1)}) custom-call(bf16[16,128,384]{2,1,0:T(8,128)(2,1)S(1)} %get-tuple-element.22.ready_tiles.tiles_ref, f32[128,2048]{1,0:T(8,128)S(1)} %get-tuple-element.26.ready_ref, bf16[128,2048]{1,0:T(8,128)(2,1)S(1)} %collective-permute-done.1.two_ref, ...), custom_call_target="tpu_custom_call" | custom-call | flops 1000000 | bytes 100000 | tf_op jit(solution)/shard_map/ready/pallas_call | solution.py:415
  25.9 0.1 collective-permute-start.4
  26.0 0.1 collective-permute-done.5.high_ref.swap_ref
  26.1 0.6 %cross.3.high_ref = f32[8,384]{1,0:T(8,128)S(1)} custom-call(bf16[128,1024]{1,0:T(8,128)(2,1)S(1)} %get-tuple-element.33.across_ref, bf16[128,1024]{1,0:T(8,128)(2,1)S(1)} %collective-permute-done.5.high_ref.swap_ref, bf16[128,1024]{1,0:T(8,128)(2,1)S(1)} %forward.1.after_ref), custom_call_target="tpu_custom_call" | custom-call | flops 1000000 | bytes 100000 | tf_op jit(solution)/shard_map/cross/pallas_call | solution.py:397
  26.7 0.8 %collective-permute-done.6.other_ref = f32[16,384]{1,0:T(8,128)S(1)} collective-permute-done((f32[16,384]{1,0:T(8,128)S(1)}, f32[16,384]{1,0:T(8,128)S(1)}, u32[]{:S(2)}, u32[]{:S(2)}) %collective-permute-start.6) | collective-permute-done | bytes 24608 | tf_op jit(solution)/shard_map/ppermute | solution.py:35
  27.5 2.0 %collective-permute-start.7 = (f32[16,384]{1,0:T(8,128)S(1)}, f32[16,384]{1,0:T(8,128)S(1)}, u32[]{:S(2)}, u32[]{:S(2)}) collective-permute-start(f32[16,384]{1,0:T(8,128)S(1)} %pair.1.refs_0_), channel_id=1, source_target_pairs={{0,8},{4,12},{8,16},{12,20},{16,24},{20,28},{24,0},{28,4},{1,9},{5... | collective-permute-start | bytes 73736 | tf_op jit(solution)/shard_map/ppermute | solution.py:52
  29.5 2.7 %collective-permute-start.8 = (f32[16,384]{1,0:T(8,128)S(1)}, f32[16,384]{1,0:T(8,128)S(1)}, u32[]{:S(2)}, u32[]{:S(2)}) collective-permute-start(f32[16,384]{1,0:T(8,128)S(1)} %pair.1.refs_0_), channel_id=1, source_target_pairs={{0,16},{4,20},{8,24},{12,28},{16,0},{20,4},{24,8},{28,12},{1,17},{... | collective-permute-start | bytes 73736 | tf_op jit(solution)/shard_map/ppermute | solution.py:52
  32.2 1.2 %collective-permute-start.9 = (f32[16,384]{1,0:T(8,128)S(1)}, f32[16,384]{1,0:T(8,128)S(1)}, u32[]{:S(2)}, u32[]{:S(2)}) collective-permute-start(f32[16,384]{1,0:T(8,128)S(1)} %pair.1.refs_0_), channel_id=1, source_target_pairs={{0,24},{4,28},{8,0},{12,4},{16,8},{20,12},{24,16},{28,20},{1,25},{... | collective-permute-start | bytes 73736 | tf_op jit(solution)/shard_map/ppermute | solution.py:52
  33.4 0.5 %known.1 = (bf16[128,2048]{1,0:T(8,128)(2,1)S(1)}, bf16[128,2048]{1,0:T(8,128)(2,1)S(1)}) custom-call(bf16[16,128,384]{2,1,0:T(8,128)(2,1)S(1)} %get-tuple-element.23.late_tiles.tiles_ref, f32[128,2048]{1,0:T(8,128)S(1)} %get-tuple-element.32.late_ref, bf16[128,1024]{1,0:T(8,128)(2,1)S(1)} %collective-permute-done.2.swap_ref.low_ref, ...), custom_call_target="tpu_custom_call" | custom-call | flops 4000000000 | bytes 100000 | tf_op jit(solution)/shard_map/known/pallas_call | solution.py:440
  34.0 1.3 %last.1 = (bf16[128,2048]{1,0:T(8,128)(2,1)}, bf16[128,2048]{1,0:T(8,128)(2,1)}, bf16[128,2048]{1,0:T(8,128)(2,1)}, f32[8,128]{1,0:T(8,128)S(1)}) custom-call(bf16[16,128,384]{2,1,0:T(8,128)(2,1)S(1)} %get-tuple-element.22.ready_tiles.tiles_ref, f32[128,1024]{1,0:T(8,128)S(1)} %get-tuple-element.29.rest_ref, ...), custom_call_target="tpu_custom_call" | custom-call | flops 1000000 | bytes 100000 | tf_op jit(solution)/shard_map/last/pallas_call | solution.py:459
  35.4 0.7 %collective-permute-done.9.refs_3_ = f32[16,384]{1,0:T(8,128)S(1)} collective-permute-done((f32[16,384]{1,0:T(8,128)S(1)}, f32[16,384]{1,0:T(8,128)S(1)}, u32[]{:S(2)}, u32[]{:S(2)}) %collective-permute-start.9) | collective-permute-done | bytes 24608 | tf_op jit(solution)/shard_map/ppermute | solution.py:52
  36.1 0.6 %add.1 = f32[16,384]{1,0:T(8,128)} custom-call(f32[16,384]{1,0:T(8,128)S(1)} %pair.1.refs_0_, f32[16,384]{1,0:T(8,128)S(1)} %collective-permute-done.7.refs_1_, f32[16,384]{1,0:T(8,128)S(1)} %collective-permute-done.8.refs_2_, f32[16,384]{1,0:T(8,128)S(1)} %collective-permute-done.9.refs_3_, f32[8,128]{1,0:T(8,128)S(1)} %get-tuple-element.39.refs_4_), custom_call_target="tpu_custom_call" | custom-call | flops 1000000 | bytes 100000 | tf_op jit(solution)/shard_map/add/pallas_call | solution.py:450
  (19 shorter events, 0.2 us)
Async XLA Ops:
  0.6 2.0 %copy-start = (bf16[128,2048]{1,0:T(8,128)(2,1)S(1)}, bf16[128,2048]{1,0:T(8,128)(2,1)}, u32[]{:S(2)}) copy-start(bf16[128,2048]{1,0:T(8,128)(2,1)} %query_ref.7) | copy-start | bytes 1572868
  0.6 2.0 %copy-start.1 = (bf16[128,2048]{1,0:T(8,128)(2,1)S(1)}, bf16[128,2048]{1,0:T(8,128)(2,1)}, u32[]{:S(2)}) copy-start(bf16[128,2048]{1,0:T(8,128)(2,1)} %keys_ref.7) | copy-start | bytes 1572868
  0.7 2.0 %copy-start.2 = (bf16[128,2048]{1,0:T(8,128)(2,1)S(1)}, bf16[128,2048]{1,0:T(8,128)(2,1)}, u32[]{:S(2)}) copy-start(bf16[128,2048]{1,0:T(8,128)(2,1)} %values_ref.7) | copy-start | bytes 1572868
  0.7 2.0 %copy-start.3 = (bf16[128,2048]{1,0:T(8,128)(2,1)S(1)}, bf16[128,2048]{1,0:T(8,128)(2,1)}, u32[]{:S(2)}) copy-start(bf16[128,2048]{1,0:T(8,128)(2,1)} %cotangent_ref.1) | copy-start | bytes 1572868
  2.0 12.8 %copy-start.4 = (bf16[16,384]{1,0:T(8,128)(2,1)S(1)}, bf16[16,384]{1,0:T(8,128)(2,1)}, u32[]{:S(2)}) copy-start(bf16[16,384]{1,0:T(8,128)(2,1)} %taps_ref.1) | copy-start | bytes 36868
  2.0 15.1 %collective-permute-start = (bf16[128,1024]{1,0:T(8,128)(2,1)S(1)}, bf16[128,1024]{1,0:T(8,128)(2,1)S(1)}, u32[]{:S(2)}, u32[]{:S(2)}) collective-permute-start(bf16[128,1024]{1,0:T(8,128)(2,1)S(1)} %diagonal.1.sent_ref), channel_id=1, source_target_pairs={{4,8},{8,4},{12,16},{16,12},{20,24},{24,20},{5,9},{9,5},{13,17},{1... | collective-permute-start | bytes 786440 | tf_op jit(solution)/shard_map/ppermute | solution.py:35
  3.0 19.5 %collective-permute-start.1 = (bf16[128,2048]{1,0:T(8,128)(2,1)S(1)}, bf16[128,2048]{1,0:T(8,128)(2,1)S(1)}, u32[]{:S(2)}, u32[]{:S(2)}) collective-permute-start(bf16[128,2048]{1,0:T(8,128)(2,1)S(1)} %get-tuple-element.25.across_ref), channel_id=1, source_target_pairs={{0,8},{8,16},{12,4},{16,24},{20,12},{28,20},{1,9},{9,17},{13,5},{1... | collective-permute-start | bytes 1572872 | tf_op jit(solution)/shard_map/ppermute | solution.py:35
  10.6 15.3 %collective-permute-start.3 = (bf16[128,2048]{1,0:T(8,128)(2,1)S(1)}, bf16[128,2048]{1,0:T(8,128)(2,1)S(1)}, u32[]{:S(2)}, u32[]{:S(2)}) collective-permute-start(bf16[128,2048]{1,0:T(8,128)(2,1)S(1)} %get-tuple-element.24.near_ref), channel_id=1, source_target_pairs={{4,12},{8,0},{12,20},{16,8},{20,28},{24,16},{5,13},{9,1},{13,21},{... | collective-permute-start | bytes 1572872 | tf_op jit(solution)/shard_map/ppermute | solution.py:35
  11.9 10.0 %collective-permute-start.2 = (bf16[128,1024]{1,0:T(8,128)(2,1)S(1)}, bf16[128,1024]{1,0:T(8,128)(2,1)S(1)}, u32[]{:S(2)}, u32[]{:S(2)}) collective-permute-start(bf16[128,1024]{1,0:T(8,128)(2,1)S(1)} %get-tuple-element.28.across_ref), channel_id=1, source_target_pairs={{0,4},{4,0},{8,12},{12,8},{16,20},{20,16},{24,28},{28,24},{1,5},{5... | collective-permute-start | bytes 786440 | tf_op jit(solution)/shard_map/ppermute | solution.py:35
  14.7 11.4 %collective-permute-start.5 = (bf16[128,1024]{1,0:T(8,128)(2,1)S(1)}, bf16[128,1024]{1,0:T(8,128)(2,1)S(1)}, u32[]{:S(2)}, u32[]{:S(2)}) collective-permute-start(bf16[128,1024]{1,0:T(8,128)(2,1)S(1)} %get-tuple-element.33.across_ref), channel_id=1, source_target_pairs={{0,4},{4,0},{8,12},{12,8},{16,20},{20,16},{24,28},{28,24},{1,5},{5... | collective-permute-start | bytes 786440 | tf_op jit(solution)/shard_map/ppermute | solution.py:35
  23.4 4.1 %collective-permute-start.6 = (f32[16,384]{1,0:T(8,128)S(1)}, f32[16,384]{1,0:T(8,128)S(1)}, u32[]{:S(2)}, u32[]{:S(2)}) collective-permute-start(f32[16,384]{1,0:T(8,128)S(1)} %two.1.sum_ref), channel_id=1, source_target_pairs={{0,4},{4,0},{8,12},{12,8},{16,20},{20,16},{24,28},{28,24},{1,5},{5... | collective-permute-start | bytes 73736 | tf_op jit(solution)/shard_map/ppermute | solution.py:35
  25.9 8.0 %collective-permute-start.4 = (bf16[128,1024]{1,0:T(8,128)(2,1)S(1)}, bf16[128,1024]{1,0:T(8,128)(2,1)S(1)}, u32[]{:S(2)}, u32[]{:S(2)}) collective-permute-start(bf16[128,1024]{1,0:T(8,128)(2,1)S(1)} %forward.1.after_ref), channel_id=1, source_target_pairs={{0,4},{4,0},{8,12},{12,8},{16,20},{20,16},{24,28},{28,24},{1,5},{5... | collective-permute-start | bytes 786440 | tf_op jit(solution)/shard_map/ppermute | solution.py:35
  27.5 7.8 %collective-permute-start.7 = (f32[16,384]{1,0:T(8,128)S(1)}, f32[16,384]{1,0:T(8,128)S(1)}, u32[]{:S(2)}, u32[]{:S(2)}) collective-permute-start(f32[16,384]{1,0:T(8,128)S(1)} %pair.1.refs_0_), channel_id=1, source_target_pairs={{0,8},{4,12},{8,16},{12,20},{16,24},{20,28},{24,0},{28,4},{1,9},{5... | collective-permute-start | bytes 73736 | tf_op jit(solution)/shard_map/ppermute | solution.py:52
  29.5 5.8 %collective-permute-start.8 = (f32[16,384]{1,0:T(8,128)S(1)}, f32[16,384]{1,0:T(8,128)S(1)}, u32[]{:S(2)}, u32[]{:S(2)}) collective-permute-start(f32[16,384]{1,0:T(8,128)S(1)} %pair.1.refs_0_), channel_id=1, source_target_pairs={{0,16},{4,20},{8,24},{12,28},{16,0},{20,4},{24,8},{28,12},{1,17},{... | collective-permute-start | bytes 73736 | tf_op jit(solution)/shard_map/ppermute | solution.py:52
  32.2 3.8 %collective-permute-start.9 = (f32[16,384]{1,0:T(8,128)S(1)}, f32[16,384]{1,0:T(8,128)S(1)}, u32[]{:S(2)}, u32[]{:S(2)}) collective-permute-start(f32[16,384]{1,0:T(8,128)S(1)} %pair.1.refs_0_), channel_id=1, source_target_pairs={{0,24},{4,28},{8,0},{12,4},{16,8},{20,12},{24,16},{28,20},{1,25},{... | collective-permute-start | bytes 73736 | tf_op jit(solution)/shard_map/ppermute | solution.py:52

commit v18 on v14

--- a/solution.py
+++ b/solution.py
@@ -103,17 +103,27 @@
     return lines_summed(total)
 
 
-def skewed_pair(outer, rows):
-    width = outer.shape[1]
-    lane = lax.broadcasted_iota(jnp.int32, (SUBLANES, width), 1)
-    high = outer[:SUBLANES]
+def skewed_pairs(outer_ref):
+    group_count, rows, width = outer_ref.shape
+
+    def lines(start):
+        return outer_ref[:, start : start + SUBLANES, :].reshape(group_count * SUBLANES, width)
+
+    high = lines(0)
     low = jnp.zeros_like(high)
+    lane = lax.broadcasted_iota(jnp.int32, high.shape, 1)
     for start in range(SUBLANES, rows, SUBLANES):
-        turned = pltpu.roll(outer[start : start + SUBLANES], width - start, 1)
+        turned = pltpu.roll(lines(start), width - start, 1)
         above = lane < width - start
         high = high + jnp.where(above, turned, 0.0)
         low = low + jnp.where(above, 0.0, turned)
-    return lines_summed(jnp.concatenate([low, high], axis=1))
+    total = jnp.concatenate([low, high], axis=1)
+    line = lax.broadcasted_iota(jnp.int32, total.shape, 0)
+    bit = 1
+    while bit < SUBLANES:
+        total = jnp.where((line & bit) == bit, pltpu.roll(total, 2 * width - bit, 1), total)
+        bit *= 2
+    return jnp.sum(total.reshape(group_count, SUBLANES, 2 * width), axis=1)
 
 
 def diagonal_kernel(query_hbm, keys_hbm, values_hbm, cotangent_hbm, out_ref, left, right, sems):
@@ -202,33 +212,29 @@
     sum_ref[...] = jnp.concatenate([sums, jnp.zeros((group_count, width - 2 * rows), jnp.float32)], axis=1)
 
 
-def two_kernel(rows, sum_ref, near_ref, two_ref, out_ref):
+def two_kernel(rows, sum_ref, near_ref, two_ref, out_ref, outer_ref):
     odd = is_odd()
     group_count, width = out_ref.shape
     group_width = near_ref.shape[1] // group_count
-    sums = []
     for group in range(group_count):
         columns = columns_of(group, group_width)
         near, two = near_ref[:, columns], two_ref[:, columns]
-        outer = DOT_ROWS(lax.select(odd, near, two), lax.select(odd, two, near))
-        sums.append(skewed_pair(outer, rows))
-    sums = jnp.concatenate(sums, axis=0)
+        outer_ref[group] = DOT_ROWS(lax.select(odd, near, two), lax.select(odd, two, near))
+    sums = skewed_pairs(outer_ref)
     out_ref[...] = sum_ref[...] + jnp.concatenate(
         [jnp.zeros((group_count, width - 2 * rows), jnp.float32), sums], axis=1
     )
 
 
-def cross_kernel(rows, across_ref, swap_ref, out_ref):
+def cross_kernel(rows, across_ref, swap_ref, out_ref, outer_ref):
     odd = is_odd()
     group_count, width = out_ref.shape
     group_width = across_ref.shape[1] // group_count
-    sums = []
     for group in range(group_count):
         columns = columns_of(group, group_width)
         across, swap = across_ref[:, columns], swap_ref[:, columns]
-        outer = DOT_ROWS(lax.select(odd, swap, across), lax.select(odd, across, swap))
-        sums.append(skewed_pair(outer, rows))
-    sums = jnp.concatenate(sums, axis=0)
+        outer_ref[group] = DOT_ROWS(lax.select(odd, swap, across), lax.select(odd, across, swap))
+    sums = skewed_pairs(outer_ref)
     out_ref[...] = jnp.concatenate([sums, jnp.zeros((group_count, width - 2 * rows), jnp.float32)], axis=1)
 
 
@@ -384,6 +390,7 @@
         in_specs=[WHOLE] * 3,
         out_specs=WHOLE,
         out_shape=sums,
+        scratch_shapes=[pltpu.VMEM((group_count, rows, rows), f32)],
     )(*in_vmem(partial, near, two))
     other = moved(partial, "ctx", (1, -1))
 
@@ -410,6 +417,7 @@
         in_specs=[WHOLE] * 2,
         out_specs=WHOLE,
         out_shape=sums,
+        scratch_shapes=[pltpu.VMEM((group_count, rows, rows), f32)],
     )(*in_vmem(across, swap))
     pair_sum = call(
         functools.partial(pair_kernel, factor),

time: 36.4 us -> 36.4 us (level)
  no operation moved by 1% of the time
where the time goes in v18:
time: 36.4 us; the launch traced here: 36.2 us
  starting transfers between devices  21 us (58%)
  Pallas kernels  10 us (27%)
  waiting for transfers between devices  4.34 us (12%)
  between operations  0.86 us (2%)
    ppermute x6, starting transfers between devices, moved(): lax.ppermute(block, axis, [pair for pair in route if 0 <= pair[1] < size])  15 us
    ppermute x3, starting transfers between devices, sum_terms(): terms.append(lax.ppermute(own, axis, route))  5.98 us
    ppermute x6, waiting for transfers between devices, moved(): lax.ppermute(block, axis, [pair for pair in route if 0 <= pair[1] < size])  3.56 us
    pallas_call x1, Pallas kernels, shards(): call(functools.partial(tiles_kernel, rows), 'tiles', in_specs=[WHOLE], ou...  2.22 us
    pallas_call x1, Pallas kernels, shards(): call(functools.partial(own_kernel, rows), 'own', flops=4 * 10 ** 9, in_sp...  1.64 us
    pallas_call x1, Pallas kernels, shards(): call(last_kernel, 'last', in_specs=[WHOLE] * 10, out_specs=[ANYWHERE] * 3...  1.35 us
    pallas_call x1, Pallas kernels, shards(): call(diagonal_kernel, 'diagonal', in_specs=[ANYWHERE] * 4, out_specs=WHOL...  1.28 us
    pallas_call x1, Pallas kernels, shards(): call(functools.partial(cross_kernel, rows), 'cross', in_specs=[WHOLE] * 2...  0.82 us
  transfers between devices with their start and end apart: 9, of which 4 were waited for; matrix products, arithmetic and copies ran while one was open for 0% of the time, Pallas kernels for 22%

profile of v18, /device:TPU:0, one launch (start us, length us, event | category | flops | bytes accessed | tf_op | source)
XLA Modules:
  0.0 36.2 jit_solution(11259870281156670224)
XLA Ops:
  0.7 1.3 %diagonal.1.sent_ref = bf16[128,1024]{1,0:T(8,128)(2,1)S(1)} custom-call(bf16[128,2048]{1,0:T(8,128)(2,1)} %query_ref.7, bf16[128,2048]{1,0:T(8,128)(2,1)} %keys_ref.7, bf16[128,2048]{1,0:T(8,128)(2,1)} %values_ref.7, bf16[128,2048]{1,0:T(8,128)(2,1)} %cotangent_ref.1), custom_call_target="tpu_custom_call" | custom-call | flops 1000000 | bytes 100000 | tf_op jit(solution)/shard_map/diagonal/pallas_call | solution.py:351
  2.0 0.0 copy-start.4
  2.0 0.7 %collective-permute-start = (bf16[128,1024]{1,0:T(8,128)(2,1)S(1)}, bf16[128,1024]{1,0:T(8,128)(2,1)S(1)}, u32[]{:S(2)}, u32[]{:S(2)}) collective-permute-start(bf16[128,1024]{1,0:T(8,128)(2,1)S(1)} %diagonal.1.sent_ref), channel_id=1, source_target_pairs={{4,8},{8,4},{12,16},{16,12},{20,24},{24,20},{5,9},{9,5},{13,17},{1... | collective-permute-start | bytes 786440 | tf_op jit(solution)/shard_map/ppermute | solution.py:35
  2.7 0.3 products.1
  3.0 7.6 %collective-permute-start.1 = (bf16[128,2048]{1,0:T(8,128)(2,1)S(1)}, bf16[128,2048]{1,0:T(8,128)(2,1)S(1)}, u32[]{:S(2)}, u32[]{:S(2)}) collective-permute-start(bf16[128,2048]{1,0:T(8,128)(2,1)S(1)} %get-tuple-element.23.across_ref), channel_id=1, source_target_pairs={{0,8},{8,16},{12,4},{16,24},{20,12},{28,20},{1,9},{9,17},{13,5},{1... | collective-permute-start | bytes 1572872 | tf_op jit(solution)/shard_map/ppermute | solution.py:35
  10.6 1.3 %collective-permute-start.2 = (bf16[128,2048]{1,0:T(8,128)(2,1)S(1)}, bf16[128,2048]{1,0:T(8,128)(2,1)S(1)}, u32[]{:S(2)}, u32[]{:S(2)}) collective-permute-start(bf16[128,2048]{1,0:T(8,128)(2,1)S(1)} %get-tuple-element.22.near_ref), channel_id=1, source_target_pairs={{4,12},{8,0},{12,20},{16,8},{20,28},{24,16},{5,13},{9,1},{13,21},{... | collective-permute-start | bytes 1572872 | tf_op jit(solution)/shard_map/ppermute | solution.py:35
  11.9 2.8 %collective-permute-start.4 = (bf16[128,2048]{1,0:T(8,128)(2,1)S(1)}, bf16[128,2048]{1,0:T(8,128)(2,1)S(1)}, u32[]{:S(2)}, u32[]{:S(2)}) collective-permute-start(bf16[128,2048]{1,0:T(8,128)(2,1)S(1)} %get-tuple-element.23.across_ref), channel_id=1, source_target_pairs={{0,4},{4,0},{8,12},{12,8},{16,20},{20,16},{24,28},{28,24},{1,5},{5... | collective-permute-start | bytes 1572872 | tf_op jit(solution)/shard_map/ppermute | solution.py:35
  14.7 2.2 %tiles.1 = (bf16[16,128,384]{2,1,0:T(8,128)(2,1)S(1)}, bf16[16,128,384]{2,1,0:T(8,128)(2,1)S(1)}) custom-call(bf16[16,384]{1,0:T(8,128)(2,1)S(1)} %copy-done.4), custom_call_target="tpu_custom_call" | custom-call | flops 1000000 | bytes 100000 | tf_op jit(solution)/shard_map/tiles/pallas_call | solution.py:371
  16.9 1.6 %own.1 = (f32[16,384]{1,0:T(8,128)S(1)}, f32[128,2048]{1,0:T(8,128)S(1)}, f32[128,2048]{1,0:T(8,128)S(1)}) custom-call(bf16[16,128,384]{2,1,0:T(8,128)(2,1)S(1)} %get-tuple-element.20.ready_tiles.tiles_ref, bf16[16,128,384]{2,1,0:T(8,128)(2,1)S(1)} %get-tuple-element.21.late_tiles.tiles_ref, bf16[128,2048]{1,0:T(8,128)(2,1)S(1)} %get-tuple-element.22.near_ref, ...), custom_call_target="tpu_custom_call" | custom-call | flops 4000000000 | bytes 100000 | tf_op jit(solution)/shard_map/own/pallas_call | solution.py:378
  18.6 2.9 %collective-permute-done.1.two_ref = bf16[128,2048]{1,0:T(8,128)(2,1)S(1)} collective-permute-done((bf16[128,2048]{1,0:T(8,128)(2,1)S(1)}, bf16[128,2048]{1,0:T(8,128)(2,1)S(1)}, u32[]{:S(2)}, u32[]{:S(2)}) %collective-permute-start.1) | collective-permute-done | bytes 524320 | tf_op jit(solution)/shard_map/ppermute | solution.py:35
  21.5 0.8 %two.1.sum_ref = f32[16,384]{1,0:T(8,128)S(1)} custom-call(f32[16,384]{1,0:T(8,128)S(1)} %get-tuple-element.25.sum_ref, bf16[128,2048]{1,0:T(8,128)(2,1)S(1)} %get-tuple-element.22.near_ref, bf16[128,2048]{1,0:T(8,128)(2,1)S(1)} %collective-permute-done.1.two_ref), custom_call_target="tpu_custom_call" | custom-call | flops 1000000 | bytes 100000 | tf_op jit(solution)/shard_map/two/pallas_call | solution.py:387
  22.3 2.6 %collective-permute-start.5 = (f32[16,384]{1,0:T(8,128)S(1)}, f32[16,384]{1,0:T(8,128)S(1)}, u32[]{:S(2)}, u32[]{:S(2)}) collective-permute-start(f32[16,384]{1,0:T(8,128)S(1)} %two.1.sum_ref), channel_id=1, source_target_pairs={{0,4},{4,0},{8,12},{12,8},{16,20},{20,16},{24,28},{28,24},{1,5},{5... | collective-permute-start | bytes 73736 | tf_op jit(solution)/shard_map/ppermute | solution.py:35
  24.9 0.4 %ready.1 = (f32[128,1024]{1,0:T(8,128)S(1)}, bf16[128,1024]{1,0:T(8,128)(2,1)S(1)}, bf16[128,1024]{1,0:T(8,128)(2,1)S(1)}) custom-call(bf16[16,128,384]{2,1,0:T(8,128)(2,1)S(1)} %get-tuple-element.20.ready_tiles.tiles_ref, f32[128,2048]{1,0:T(8,128)S(1)} %get-tuple-element.24.ready_ref, bf16[128,2048]{1,0:T(8,128)(2,1)S(1)} %collective-permute-done.1.two_ref, ...), custom_call_target="tpu_custom_call" | custom-call | flops 1000000 | bytes 100000 | tf_op jit(solution)/shard_map/ready/pallas_call | solution.py:397
  25.3 0.3 collective-permute-done.2.far_ref
  25.6 0.1 collective-permute-start.3
  25.7 0.4 collective-permute-done.4.swap_ref
  26.1 0.8 %cross.1.cross_ref = f32[16,384]{1,0:T(8,128)S(1)} custom-call(bf16[128,2048]{1,0:T(8,128)(2,1)S(1)} %get-tuple-element.23.across_ref, bf16[128,2048]{1,0:T(8,128)(2,1)S(1)} %collective-permute-done.4.swap_ref), custom_call_target="tpu_custom_call" | custom-call | flops 1000000 | bytes 100000 | tf_op jit(solution)/shard_map/cross/pallas_call | solution.py:414
  26.9 2.0 %collective-permute-start.6 = (f32[16,384]{1,0:T(8,128)S(1)}, f32[16,384]{1,0:T(8,128)S(1)}, u32[]{:S(2)}, u32[]{:S(2)}) collective-permute-start(f32[16,384]{1,0:T(8,128)S(1)} %pair.1.refs_0_), channel_id=1, source_target_pairs={{0,8},{4,12},{8,16},{12,20},{16,24},{20,28},{24,0},{28,4},{1,9},{5... | collective-permute-start | bytes 73736 | tf_op jit(solution)/shard_map/ppermute | solution.py:52
  29.0 2.8 %collective-permute-start.7 = (f32[16,384]{1,0:T(8,128)S(1)}, f32[16,384]{1,0:T(8,128)S(1)}, u32[]{:S(2)}, u32[]{:S(2)}) collective-permute-start(f32[16,384]{1,0:T(8,128)S(1)} %pair.1.refs_0_), channel_id=1, source_target_pairs={{0,16},{4,20},{8,24},{12,28},{16,0},{20,4},{24,8},{28,12},{1,17},{... | collective-permute-start | bytes 73736 | tf_op jit(solution)/shard_map/ppermute | solution.py:52
  31.8 1.1 %collective-permute-start.8 = (f32[16,384]{1,0:T(8,128)S(1)}, f32[16,384]{1,0:T(8,128)S(1)}, u32[]{:S(2)}, u32[]{:S(2)}) collective-permute-start(f32[16,384]{1,0:T(8,128)S(1)} %pair.1.refs_0_), channel_id=1, source_target_pairs={{0,24},{4,28},{8,0},{12,4},{16,8},{20,12},{24,16},{28,20},{1,25},{... | collective-permute-start | bytes 73736 | tf_op jit(solution)/shard_map/ppermute | solution.py:52
  32.9 0.5 %known.1 = (bf16[128,2048]{1,0:T(8,128)(2,1)S(1)}, bf16[128,2048]{1,0:T(8,128)(2,1)S(1)}) custom-call(bf16[16,128,384]{2,1,0:T(8,128)(2,1)S(1)} %get-tuple-element.21.late_tiles.tiles_ref, f32[128,2048]{1,0:T(8,128)S(1)} %get-tuple-element.29.late_ref, bf16[128,2048]{1,0:T(8,128)(2,1)S(1)} %collective-permute-done.4.swap_ref, ...), custom_call_target="tpu_custom_call" | custom-call | flops 4000000000 | bytes 100000 | tf_op jit(solution)/shard_map/known/pallas_call | solution.py:430
  33.5 1.3 %last.1 = (bf16[128,2048]{1,0:T(8,128)(2,1)}, bf16[128,2048]{1,0:T(8,128)(2,1)}, bf16[128,2048]{1,0:T(8,128)(2,1)}, f32[8,128]{1,0:T(8,128)S(1)}) custom-call(bf16[16,128,384]{2,1,0:T(8,128)(2,1)S(1)} %get-tuple-element.20.ready_tiles.tiles_ref, f32[128,1024]{1,0:T(8,128)S(1)} %get-tuple-element.26.rest_ref, ...), custom_call_target="tpu_custom_call" | custom-call | flops 1000000 | bytes 100000 | tf_op jit(solution)/shard_map/last/pallas_call | solution.py:449
  34.9 0.8 %collective-permute-done.8.refs_3_ = f32[16,384]{1,0:T(8,128)S(1)} collective-permute-done((f32[16,384]{1,0:T(8,128)S(1)}, f32[16,384]{1,0:T(8,128)S(1)}, u32[]{:S(2)}, u32[]{:S(2)}) %collective-permute-start.8) | collective-permute-done | bytes 24608 | tf_op jit(solution)/shard_map/ppermute | solution.py:52
  35.6 0.6 %add.1 = f32[16,384]{1,0:T(8,128)} custom-call(f32[16,384]{1,0:T(8,128)S(1)} %pair.1.refs_0_, f32[16,384]{1,0:T(8,128)S(1)} %collective-permute-done.6.refs_1_, f32[16,384]{1,0:T(8,128)S(1)} %collective-permute-done.7.refs_2_, f32[16,384]{1,0:T(8,128)S(1)} %collective-permute-done.8.refs_3_, f32[8,128]{1,0:T(8,128)S(1)} %get-tuple-element.35.refs_4_), custom_call_target="tpu_custom_call" | custom-call | flops 1000000 | bytes 100000 | tf_op jit(solution)/shard_map/add/pallas_call | solution.py:440
  (16 shorter events, 0.1 us)
Async XLA Ops:
  0.6 2.0 %copy-start = (bf16[128,2048]{1,0:T(8,128)(2,1)S(1)}, bf16[128,2048]{1,0:T(8,128)(2,1)}, u32[]{:S(2)}) copy-start(bf16[128,2048]{1,0:T(8,128)(2,1)} %query_ref.7) | copy-start | bytes 1572868
  0.6 2.0 %copy-start.1 = (bf16[128,2048]{1,0:T(8,128)(2,1)S(1)}, bf16[128,2048]{1,0:T(8,128)(2,1)}, u32[]{:S(2)}) copy-start(bf16[128,2048]{1,0:T(8,128)(2,1)} %keys_ref.7) | copy-start | bytes 1572868
  0.7 2.0 %copy-start.2 = (bf16[128,2048]{1,0:T(8,128)(2,1)S(1)}, bf16[128,2048]{1,0:T(8,128)(2,1)}, u32[]{:S(2)}) copy-start(bf16[128,2048]{1,0:T(8,128)(2,1)} %values_ref.7) | copy-start | bytes 1572868
  0.7 2.0 %copy-start.3 = (bf16[128,2048]{1,0:T(8,128)(2,1)S(1)}, bf16[128,2048]{1,0:T(8,128)(2,1)}, u32[]{:S(2)}) copy-start(bf16[128,2048]{1,0:T(8,128)(2,1)} %cotangent_ref.1) | copy-start | bytes 1572868
  2.0 12.7 %copy-start.4 = (bf16[16,384]{1,0:T(8,128)(2,1)S(1)}, bf16[16,384]{1,0:T(8,128)(2,1)}, u32[]{:S(2)}) copy-start(bf16[16,384]{1,0:T(8,128)(2,1)} %taps_ref.1) | copy-start | bytes 36868
  2.0 15.0 %collective-permute-start = (bf16[128,1024]{1,0:T(8,128)(2,1)S(1)}, bf16[128,1024]{1,0:T(8,128)(2,1)S(1)}, u32[]{:S(2)}, u32[]{:S(2)}) collective-permute-start(bf16[128,1024]{1,0:T(8,128)(2,1)S(1)} %diagonal.1.sent_ref), channel_id=1, source_target_pairs={{4,8},{8,4},{12,16},{16,12},{20,24},{24,20},{5,9},{9,5},{13,17},{1... | collective-permute-start | bytes 786440 | tf_op jit(solution)/shard_map/ppermute | solution.py:35
  3.0 18.4 %collective-permute-start.1 = (bf16[128,2048]{1,0:T(8,128)(2,1)S(1)}, bf16[128,2048]{1,0:T(8,128)(2,1)S(1)}, u32[]{:S(2)}, u32[]{:S(2)}) collective-permute-start(bf16[128,2048]{1,0:T(8,128)(2,1)S(1)} %get-tuple-element.23.across_ref), channel_id=1, source_target_pairs={{0,8},{8,16},{12,4},{16,24},{20,12},{28,20},{1,9},{9,17},{13,5},{1... | collective-permute-start | bytes 1572872 | tf_op jit(solution)/shard_map/ppermute | solution.py:35
  10.6 15.0 %collective-permute-start.2 = (bf16[128,2048]{1,0:T(8,128)(2,1)S(1)}, bf16[128,2048]{1,0:T(8,128)(2,1)S(1)}, u32[]{:S(2)}, u32[]{:S(2)}) collective-permute-start(bf16[128,2048]{1,0:T(8,128)(2,1)S(1)} %get-tuple-element.22.near_ref), channel_id=1, source_target_pairs={{4,12},{8,0},{12,20},{16,8},{20,28},{24,16},{5,13},{9,1},{13,21},{... | collective-permute-start | bytes 1572872 | tf_op jit(solution)/shard_map/ppermute | solution.py:35
  11.9 14.2 %collective-permute-start.4 = (bf16[128,2048]{1,0:T(8,128)(2,1)S(1)}, bf16[128,2048]{1,0:T(8,128)(2,1)S(1)}, u32[]{:S(2)}, u32[]{:S(2)}) collective-permute-start(bf16[128,2048]{1,0:T(8,128)(2,1)S(1)} %get-tuple-element.23.across_ref), channel_id=1, source_target_pairs={{0,4},{4,0},{8,12},{12,8},{16,20},{20,16},{24,28},{28,24},{1,5},{5... | collective-permute-start | bytes 1572872 | tf_op jit(solution)/shard_map/ppermute | solution.py:35
  22.3 4.6 %collective-permute-start.5 = (f32[16,384]{1,0:T(8,128)S(1)}, f32[16,384]{1,0:T(8,128)S(1)}, u32[]{:S(2)}, u32[]{:S(2)}) collective-permute-start(f32[16,384]{1,0:T(8,128)S(1)} %two.1.sum_ref), channel_id=1, source_target_pairs={{0,4},{4,0},{8,12},{12,8},{16,20},{20,16},{24,28},{28,24},{1,5},{5... | collective-permute-start | bytes 73736 | tf_op jit(solution)/shard_map/ppermute | solution.py:35
  25.6 7.8 %collective-permute-start.3 = (bf16[128,1024]{1,0:T(8,128)(2,1)S(1)}, bf16[128,1024]{1,0:T(8,128)(2,1)S(1)}, u32[]{:S(2)}, u32[]{:S(2)}) collective-permute-start(bf16[128,1024]{1,0:T(8,128)(2,1)S(1)} %forward.1), channel_id=1, source_target_pairs={{0,4},{4,0},{8,12},{12,8},{16,20},{20,16},{24,28},{28,24},{1,5},{5... | collective-permute-start | bytes 786440 | tf_op jit(solution)/shard_map/ppermute | solution.py:35
  26.9 7.9 %collective-permute-start.6 = (f32[16,384]{1,0:T(8,128)S(1)}, f32[16,384]{1,0:T(8,128)S(1)}, u32[]{:S(2)}, u32[]{:S(2)}) collective-permute-start(f32[16,384]{1,0:T(8,128)S(1)} %pair.1.refs_0_), channel_id=1, source_target_pairs={{0,8},{4,12},{8,16},{12,20},{16,24},{20,28},{24,0},{28,4},{1,9},{5... | collective-permute-start | bytes 73736 | tf_op jit(solution)/shard_map/ppermute | solution.py:52
  29.0 5.9 %collective-permute-start.7 = (f32[16,384]{1,0:T(8,128)S(1)}, f32[16,384]{1,0:T(8,128)S(1)}, u32[]{:S(2)}, u32[]{:S(2)}) collective-permute-start(f32[16,384]{1,0:T(8,128)S(1)} %pair.1.refs_0_), channel_id=1, source_target_pairs={{0,16},{4,20},{8,24},{12,28},{16,0},{20,4},{24,8},{28,12},{1,17},{... | collective-permute-start | bytes 73736 | tf_op jit(solution)/shard_map/ppermute | solution.py:52
  31.8 3.8 %collective-permute-start.8 = (f32[16,384]{1,0:T(8,128)S(1)}, f32[16,384]{1,0:T(8,128)S(1)}, u32[]{:S(2)}, u32[]{:S(2)}) collective-permute-start(f32[16,384]{1,0:T(8,128)S(1)} %pair.1.refs_0_), channel_id=1, source_target_pairs={{0,24},{4,28},{8,0},{12,4},{16,8},{20,12},{24,16},{28,20},{1,25},{... | collective-permute-start | bytes 73736 | tf_op jit(solution)/shard_map/ppermute | solution.py:52

commit v19 on v18

--- a/solution.py
+++ b/solution.py
@@ -103,27 +103,42 @@
     return lines_summed(total)
 
 
-def skewed_pairs(outer_ref):
+def skewed_pairs(outer_ref, right):
     group_count, rows, width = outer_ref.shape
 
     def lines(start):
         return outer_ref[:, start : start + SUBLANES, :].reshape(group_count * SUBLANES, width)
 
-    high = lines(0)
-    low = jnp.zeros_like(high)
-    lane = lax.broadcasted_iota(jnp.int32, high.shape, 1)
+    first = lines(0)
+    blank = jnp.zeros_like(first)
+    high = lax.select(right, blank, first)
+    low = lax.select(right, first, blank)
+    lane = lax.broadcasted_iota(jnp.int32, first.shape, 1)
     for start in range(SUBLANES, rows, SUBLANES):
-        turned = pltpu.roll(lines(start), width - start, 1)
-        above = lane < width - start
+        shift = jnp.where(right, start, width - start)
+        turned = pltpu.roll(lines(start), shift, 1)
+        above = lane < shift
         high = high + jnp.where(above, turned, 0.0)
         low = low + jnp.where(above, 0.0, turned)
     total = jnp.concatenate([low, high], axis=1)
     line = lax.broadcasted_iota(jnp.int32, total.shape, 0)
     bit = 1
     while bit < SUBLANES:
-        total = jnp.where((line & bit) == bit, pltpu.roll(total, 2 * width - bit, 1), total)
+        turned = pltpu.roll(total, jnp.where(right, bit, 2 * width - bit), 1)
+        total = jnp.where((line & bit) == bit, turned, total)
         bit *= 2
-    return jnp.sum(total.reshape(group_count, SUBLANES, 2 * width), axis=1)
+    sums = jnp.sum(total.reshape(group_count, SUBLANES, 2 * width), axis=1)
+    return lax.select(right, pltpu.roll(sums, 1, 1), sums)
+
+
+def turned_columns(block, reverse):
+    rows = block.shape[0]
+    row = lax.broadcasted_iota(jnp.int32, (rows, rows), 0)
+    column = lax.broadcasted_iota(jnp.int32, (rows, rows), 1)
+    place = lax.select(reverse, rows - 1 - column, column)
+    order = jnp.where(row == place, 1.0, 0.0).astype(block.dtype)
+    moved_block = lax.dot_general(block, order, (((0,), (0,)), ((), ())), preferred_element_type=jnp.float32)
+    return moved_block.astype(block.dtype)
 
 
 def diagonal_kernel(query_hbm, keys_hbm, values_hbm, cotangent_hbm, out_ref, left, right, sems):
@@ -175,7 +190,8 @@
 
 
 def own_kernel(
-    rows, ready_tiles, late_tiles, near_ref, across_ref, diagonal_ref, sum_ref, late_ref, ready_ref
+    rows, ready_tiles, late_tiles, near_ref, across_ref, diagonal_ref, sum_ref, late_ref, ready_ref,
+    near_turned, across_turned,
 ):
     odd = is_odd()
     group_count, width = sum_ref.shape
@@ -186,6 +202,10 @@
         columns = columns_of(group, group_width)
         late_ref[:, columns] = DOT(late_tiles[group, :, :rows], near_ref[:, columns])
         ready_ref[:, columns] = DOT(ready_tiles[group, :, :rows], across_ref[:, columns])
+    for group in range(group_count):
+        columns, places = columns_of(group, group_width), columns_of(group, rows)
+        near_turned[:, places] = turned_columns(near_ref[:, columns], odd)
+        across_turned[:, places] = turned_columns(across_ref[:, columns], jnp.logical_not(odd))
     middles = []
     for group in range(half):
         low, high = columns_of(group, group_width), columns_of(group + half, group_width)
@@ -212,29 +232,27 @@
     sum_ref[...] = jnp.concatenate([sums, jnp.zeros((group_count, width - 2 * rows), jnp.float32)], axis=1)
 
 
-def two_kernel(rows, sum_ref, near_ref, two_ref, out_ref, outer_ref):
+def two_kernel(rows, sum_ref, turned_ref, two_ref, out_ref, outer_ref):
     odd = is_odd()
     group_count, width = out_ref.shape
-    group_width = near_ref.shape[1] // group_count
+    group_width = two_ref.shape[1] // group_count
     for group in range(group_count):
         columns = columns_of(group, group_width)
-        near, two = near_ref[:, columns], two_ref[:, columns]
-        outer_ref[group] = DOT_ROWS(lax.select(odd, near, two), lax.select(odd, two, near))
-    sums = skewed_pairs(outer_ref)
+        outer_ref[group] = DOT(two_ref[:, columns], turned_ref[:, columns_of(group, rows)])
+    sums = skewed_pairs(outer_ref, odd)
     out_ref[...] = sum_ref[...] + jnp.concatenate(
         [jnp.zeros((group_count, width - 2 * rows), jnp.float32), sums], axis=1
     )
 
 
-def cross_kernel(rows, across_ref, swap_ref, out_ref, outer_ref):
+def cross_kernel(rows, turned_ref, swap_ref, out_ref, outer_ref):
     odd = is_odd()
     group_count, width = out_ref.shape
-    group_width = across_ref.shape[1] // group_count
+    group_width = swap_ref.shape[1] // group_count
     for group in range(group_count):
         columns = columns_of(group, group_width)
-        across, swap = across_ref[:, columns], swap_ref[:, columns]
-        outer_ref[group] = DOT_ROWS(lax.select(odd, swap, across), lax.select(odd, across, swap))
-    sums = skewed_pairs(outer_ref)
+        outer_ref[group] = DOT(swap_ref[:, columns], turned_ref[:, columns_of(group, rows)])
+    sums = skewed_pairs(outer_ref, jnp.logical_not(odd))
     out_ref[...] = jnp.concatenate([sums, jnp.zeros((group_count, width - 2 * rows), jnp.float32)], axis=1)
 
 
@@ -346,6 +364,7 @@
     block, half_block = pltpu.VMEM((rows, local_width), bf16), pltpu.VMEM((rows, half_width), bf16)
     wide, half_wide = pltpu.VMEM((rows, local_width), f32), pltpu.VMEM((rows, half_width), f32)
     tiles, sums = pltpu.VMEM((group_count, rows, taps), bf16), pltpu.VMEM((group_count, taps), f32)
+    turned = pltpu.VMEM((group_width, group_count * rows), bf16)
     outs = [jax.ShapeDtypeStruct((rows, local_width), bf16)] * 3
 
     sent = call(
@@ -375,13 +394,13 @@
         out_specs=[WHOLE] * 2,
         out_shape=[tiles] * 2,
     )(*in_vmem(filter_taps))
-    partial, late, ready = call(
+    partial, late, ready, near_turned, across_turned = call(
         functools.partial(own_kernel, rows),
         "own",
         flops=4 * 10**9,
         in_specs=[WHOLE] * 5,
-        out_specs=[WHOLE] * 3,
-        out_shape=[sums, wide, wide],
+        out_specs=[WHOLE] * 5,
+        out_shape=[sums, wide, wide, turned, turned],
     )(*in_vmem(ready_tiles, late_tiles, near, across, diagonal))
 
     partial = call(
@@ -391,7 +410,7 @@
         out_specs=WHOLE,
         out_shape=sums,
         scratch_shapes=[pltpu.VMEM((group_count, rows, rows), f32)],
-    )(*in_vmem(partial, near, two))
+    )(*in_vmem(partial, near_turned, two))
     other = moved(partial, "ctx", (1, -1))
 
     rest, ready_one, ready_other = call(
@@ -418,7 +437,7 @@
         out_specs=WHOLE,
         out_shape=sums,
         scratch_shapes=[pltpu.VMEM((group_count, rows, rows), f32)],
-    )(*in_vmem(across, swap))
+    )(*in_vmem(across_turned, swap))
     pair_sum = call(
         functools.partial(pair_kernel, factor),
         "pair",

time: 36.4 us -> 36.4 us (level)
  transfers between devices with their start and end apart: 9 -> 9, of which waited for: 4 -> 4; matrix products, arithmetic and copies ran while one was open for 0% -> 0% of each run, Pallas kernels for 22% -> 23%
where the time goes in v19:
time: 36.4 us; the launch traced here: 36.2 us
  starting transfers between devices  20.9 us (57%)
  Pallas kernels  10.3 us (28%)
  waiting for transfers between devices  4.16 us (11%)
  between operations  0.84 us (2%)
    ppermute x6, starting transfers between devices, moved(): lax.ppermute(block, axis, [pair for pair in route if 0 <= pair[1] < size])  15 us
    ppermute x3, starting transfers between devices, sum_terms(): terms.append(lax.ppermute(own, axis, route))  5.94 us
    ppermute x6, waiting for transfers between devices, moved(): lax.ppermute(block, axis, [pair for pair in route if 0 <= pair[1] < size])  3.34 us
    pallas_call x1, Pallas kernels, shards(): call(functools.partial(tiles_kernel, rows), 'tiles', in_specs=[WHOLE], ou...  2.22 us
    pallas_call x1, Pallas kernels, shards(): call(functools.partial(own_kernel, rows), 'own', flops=4 * 10 ** 9, in_sp...  1.96 us
    pallas_call x1, Pallas kernels, shards(): call(last_kernel, 'last', in_specs=[WHOLE] * 10, out_specs=[ANYWHERE] * 3...  1.35 us
    pallas_call x1, Pallas kernels, shards(): call(diagonal_kernel, 'diagonal', in_specs=[ANYWHERE] * 4, out_specs=WHOL...  1.28 us
    ppermute x3, waiting for transfers between devices, sum_terms(): terms.append(lax.ppermute(own, axis, route))  0.82 us
  transfers between devices with their start and end apart: 9, of which 4 were waited for; matrix products, arithmetic and copies ran while one was open for 0% of the time, Pallas kernels for 23%

profile of v19, /device:TPU:0, one launch (start us, length us, event | category | flops | bytes accessed | tf_op | source)
XLA Modules:
  0.0 36.2 jit_solution(11756514924051218195)
XLA Ops:
  0.7 1.3 %diagonal.1.sent_ref = bf16[128,1024]{1,0:T(8,128)(2,1)S(1)} custom-call(bf16[128,2048]{1,0:T(8,128)(2,1)} %query_ref.7, bf16[128,2048]{1,0:T(8,128)(2,1)} %keys_ref.7, bf16[128,2048]{1,0:T(8,128)(2,1)} %values_ref.7, bf16[128,2048]{1,0:T(8,128)(2,1)} %cotangent_ref.1), custom_call_target="tpu_custom_call" | custom-call | flops 1000000 | bytes 100000 | tf_op jit(solution)/shard_map/diagonal/pallas_call | solution.py:370
  2.0 0.0 copy-start.4
  2.0 0.7 %collective-permute-start = (bf16[128,1024]{1,0:T(8,128)(2,1)S(1)}, bf16[128,1024]{1,0:T(8,128)(2,1)S(1)}, u32[]{:S(2)}, u32[]{:S(2)}) collective-permute-start(bf16[128,1024]{1,0:T(8,128)(2,1)S(1)} %diagonal.1.sent_ref), channel_id=1, source_target_pairs={{4,8},{8,4},{12,16},{16,12},{20,24},{24,20},{5,9},{9,5},{13,17},{1... | collective-permute-start | bytes 786440 | tf_op jit(solution)/shard_map/ppermute | solution.py:35
  2.7 0.3 products.1
  3.0 7.6 %collective-permute-start.1 = (bf16[128,2048]{1,0:T(8,128)(2,1)S(1)}, bf16[128,2048]{1,0:T(8,128)(2,1)S(1)}, u32[]{:S(2)}, u32[]{:S(2)}) collective-permute-start(bf16[128,2048]{1,0:T(8,128)(2,1)S(1)} %get-tuple-element.25.across_ref), channel_id=1, source_target_pairs={{0,8},{8,16},{12,4},{16,24},{20,12},{28,20},{1,9},{9,17},{13,5},{1... | collective-permute-start | bytes 1572872 | tf_op jit(solution)/shard_map/ppermute | solution.py:35
  10.6 1.3 %collective-permute-start.2 = (bf16[128,2048]{1,0:T(8,128)(2,1)S(1)}, bf16[128,2048]{1,0:T(8,128)(2,1)S(1)}, u32[]{:S(2)}, u32[]{:S(2)}) collective-permute-start(bf16[128,2048]{1,0:T(8,128)(2,1)S(1)} %get-tuple-element.24.near_ref), channel_id=1, source_target_pairs={{4,12},{8,0},{12,20},{16,8},{20,28},{24,16},{5,13},{9,1},{13,21},{... | collective-permute-start | bytes 1572872 | tf_op jit(solution)/shard_map/ppermute | solution.py:35
  11.9 2.8 %collective-permute-start.4 = (bf16[128,2048]{1,0:T(8,128)(2,1)S(1)}, bf16[128,2048]{1,0:T(8,128)(2,1)S(1)}, u32[]{:S(2)}, u32[]{:S(2)}) collective-permute-start(bf16[128,2048]{1,0:T(8,128)(2,1)S(1)} %get-tuple-element.25.across_ref), channel_id=1, source_target_pairs={{0,4},{4,0},{8,12},{12,8},{16,20},{20,16},{24,28},{28,24},{1,5},{5... | collective-permute-start | bytes 1572872 | tf_op jit(solution)/shard_map/ppermute | solution.py:35
  14.7 2.2 %tiles.1 = (bf16[16,128,384]{2,1,0:T(8,128)(2,1)S(1)}, bf16[16,128,384]{2,1,0:T(8,128)(2,1)S(1)}) custom-call(bf16[16,384]{1,0:T(8,128)(2,1)S(1)} %copy-done.4), custom_call_target="tpu_custom_call" | custom-call | flops 1000000 | bytes 100000 | tf_op jit(solution)/shard_map/tiles/pallas_call | solution.py:390
  16.9 2.0 %own.1 = (f32[16,384]{1,0:T(8,128)S(1)}, f32[128,2048]{1,0:T(8,128)S(1)}, f32[128,2048]{1,0:T(8,128)S(1)}, bf16[128,2048]{1,0:T(8,128)(2,1)S(1)}, bf16[128,2048]{1,0:T(8,128)(2,1)S(1)}) custom-call(bf16[16,128,384]{2,1,0:T(8,128)(2,1)S(1)} %get-tuple-element.22.ready_tiles.tiles_ref, bf16[16,128,384]{2,1,0:T(8,128)(2,1)S(1)} %get-tuple-element.23.late_tiles.tiles_ref, ...), custom_call_target="tpu_custom_call" | custom-call | flops 4000000000 | bytes 100000 | tf_op jit(solution)/shard_map/own/pallas_call | solution.py:397
  18.9 2.5 %collective-permute-done.1.two_ref = bf16[128,2048]{1,0:T(8,128)(2,1)S(1)} collective-permute-done((bf16[128,2048]{1,0:T(8,128)(2,1)S(1)}, bf16[128,2048]{1,0:T(8,128)(2,1)S(1)}, u32[]{:S(2)}, u32[]{:S(2)}) %collective-permute-start.1) | collective-permute-done | bytes 524320 | tf_op jit(solution)/shard_map/ppermute | solution.py:35
  21.5 0.8 %two.1.sum_ref = f32[16,384]{1,0:T(8,128)S(1)} custom-call(f32[16,384]{1,0:T(8,128)S(1)} %get-tuple-element.27.sum_ref, bf16[128,2048]{1,0:T(8,128)(2,1)S(1)} %get-tuple-element.28.turned_ref, bf16[128,2048]{1,0:T(8,128)(2,1)S(1)} %collective-permute-done.1.two_ref), custom_call_target="tpu_custom_call" | custom-call | flops 1000000 | bytes 100000 | tf_op jit(solution)/shard_map/two/pallas_call | solution.py:406
  22.2 2.6 %collective-permute-start.5 = (f32[16,384]{1,0:T(8,128)S(1)}, f32[16,384]{1,0:T(8,128)S(1)}, u32[]{:S(2)}, u32[]{:S(2)}) collective-permute-start(f32[16,384]{1,0:T(8,128)S(1)} %two.1.sum_ref), channel_id=1, source_target_pairs={{0,4},{4,0},{8,12},{12,8},{16,20},{20,16},{24,28},{28,24},{1,5},{5... | collective-permute-start | bytes 73736 | tf_op jit(solution)/shard_map/ppermute | solution.py:35
  24.8 0.4 %ready.1 = (f32[128,1024]{1,0:T(8,128)S(1)}, bf16[128,1024]{1,0:T(8,128)(2,1)S(1)}, bf16[128,1024]{1,0:T(8,128)(2,1)S(1)}) custom-call(bf16[16,128,384]{2,1,0:T(8,128)(2,1)S(1)} %get-tuple-element.22.ready_tiles.tiles_ref, f32[128,2048]{1,0:T(8,128)S(1)} %get-tuple-element.26.ready_ref, bf16[128,2048]{1,0:T(8,128)(2,1)S(1)} %collective-permute-done.1.two_ref, ...), custom_call_target="tpu_custom_call" | custom-call | flops 1000000 | bytes 100000 | tf_op jit(solution)/shard_map/ready/pallas_call | solution.py:416
  25.2 0.4 %collective-permute-done.2.far_ref = bf16[128,2048]{1,0:T(8,128)(2,1)S(1)} collective-permute-done((bf16[128,2048]{1,0:T(8,128)(2,1)S(1)}, bf16[128,2048]{1,0:T(8,128)(2,1)S(1)}, u32[]{:S(2)}, u32[]{:S(2)}) %collective-permute-start.2) | collective-permute-done | bytes 524320 | tf_op jit(solution)/shard_map/ppermute | solution.py:35
  25.6 0.1 collective-permute-start.3
  25.7 0.4 %collective-permute-done.4.swap_ref = bf16[128,2048]{1,0:T(8,128)(2,1)S(1)} collective-permute-done((bf16[128,2048]{1,0:T(8,128)(2,1)S(1)}, bf16[128,2048]{1,0:T(8,128)(2,1)S(1)}, u32[]{:S(2)}, u32[]{:S(2)}) %collective-permute-start.4) | collective-permute-done | bytes 524320 | tf_op jit(solution)/shard_map/ppermute | solution.py:35
  26.1 0.8 %cross.1.cross_ref = f32[16,384]{1,0:T(8,128)S(1)} custom-call(bf16[128,2048]{1,0:T(8,128)(2,1)S(1)} %get-tuple-element.38.turned_ref, bf16[128,2048]{1,0:T(8,128)(2,1)S(1)} %collective-permute-done.4.swap_ref), custom_call_target="tpu_custom_call" | custom-call | flops 1000000 | bytes 100000 | tf_op jit(solution)/shard_map/cross/pallas_call | solution.py:433
  26.9 2.0 %collective-permute-start.6 = (f32[16,384]{1,0:T(8,128)S(1)}, f32[16,384]{1,0:T(8,128)S(1)}, u32[]{:S(2)}, u32[]{:S(2)}) collective-permute-start(f32[16,384]{1,0:T(8,128)S(1)} %pair.1.refs_0_), channel_id=1, source_target_pairs={{0,8},{4,12},{8,16},{12,20},{16,24},{20,28},{24,0},{28,4},{1,9},{5... | collective-permute-start | bytes 73736 | tf_op jit(solution)/shard_map/ppermute | solution.py:52
  28.9 2.9 %collective-permute-start.7 = (f32[16,384]{1,0:T(8,128)S(1)}, f32[16,384]{1,0:T(8,128)S(1)}, u32[]{:S(2)}, u32[]{:S(2)}) collective-permute-start(f32[16,384]{1,0:T(8,128)S(1)} %pair.1.refs_0_), channel_id=1, source_target_pairs={{0,16},{4,20},{8,24},{12,28},{16,0},{20,4},{24,8},{28,12},{1,17},{... | collective-permute-start | bytes 73736 | tf_op jit(solution)/shard_map/ppermute | solution.py:52
  31.7 1.1 %collective-permute-start.8 = (f32[16,384]{1,0:T(8,128)S(1)}, f32[16,384]{1,0:T(8,128)S(1)}, u32[]{:S(2)}, u32[]{:S(2)}) collective-permute-start(f32[16,384]{1,0:T(8,128)S(1)} %pair.1.refs_0_), channel_id=1, source_target_pairs={{0,24},{4,28},{8,0},{12,4},{16,8},{20,12},{24,16},{28,20},{1,25},{... | collective-permute-start | bytes 73736 | tf_op jit(solution)/shard_map/ppermute | solution.py:52
  32.8 0.5 %known.1 = (bf16[128,2048]{1,0:T(8,128)(2,1)S(1)}, bf16[128,2048]{1,0:T(8,128)(2,1)S(1)}) custom-call(bf16[16,128,384]{2,1,0:T(8,128)(2,1)S(1)} %get-tuple-element.23.late_tiles.tiles_ref, f32[128,2048]{1,0:T(8,128)S(1)} %get-tuple-element.32.late_ref, bf16[128,2048]{1,0:T(8,128)(2,1)S(1)} %collective-permute-done.4.swap_ref, ...), custom_call_target="tpu_custom_call" | custom-call | flops 4000000000 | bytes 100000 | tf_op jit(solution)/shard_map/known/pallas_call | solution.py:449
  33.4 1.3 %last.1 = (bf16[128,2048]{1,0:T(8,128)(2,1)}, bf16[128,2048]{1,0:T(8,128)(2,1)}, bf16[128,2048]{1,0:T(8,128)(2,1)}, f32[8,128]{1,0:T(8,128)S(1)}) custom-call(bf16[16,128,384]{2,1,0:T(8,128)(2,1)S(1)} %get-tuple-element.22.ready_tiles.tiles_ref, f32[128,1024]{1,0:T(8,128)S(1)} %get-tuple-element.29.rest_ref, ...), custom_call_target="tpu_custom_call" | custom-call | flops 1000000 | bytes 100000 | tf_op jit(solution)/shard_map/last/pallas_call | solution.py:468
  34.8 0.8 %collective-permute-done.8.refs_3_ = f32[16,384]{1,0:T(8,128)S(1)} collective-permute-done((f32[16,384]{1,0:T(8,128)S(1)}, f32[16,384]{1,0:T(8,128)S(1)}, u32[]{:S(2)}, u32[]{:S(2)}) %collective-permute-start.8) | collective-permute-done | bytes 24608 | tf_op jit(solution)/shard_map/ppermute | solution.py:52
  35.6 0.6 %add.1 = f32[16,384]{1,0:T(8,128)} custom-call(f32[16,384]{1,0:T(8,128)S(1)} %pair.1.refs_0_, f32[16,384]{1,0:T(8,128)S(1)} %collective-permute-done.6.refs_1_, f32[16,384]{1,0:T(8,128)S(1)} %collective-permute-done.7.refs_2_, f32[16,384]{1,0:T(8,128)S(1)} %collective-permute-done.8.refs_3_, f32[8,128]{1,0:T(8,128)S(1)} %get-tuple-element.39.refs_4_), custom_call_target="tpu_custom_call" | custom-call | flops 1000000 | bytes 100000 | tf_op jit(solution)/shard_map/add/pallas_call | solution.py:459
  (16 shorter events, 0.1 us)
Async XLA Ops:
  0.6 2.0 %copy-start = (bf16[128,2048]{1,0:T(8,128)(2,1)S(1)}, bf16[128,2048]{1,0:T(8,128)(2,1)}, u32[]{:S(2)}) copy-start(bf16[128,2048]{1,0:T(8,128)(2,1)} %query_ref.7) | copy-start | bytes 1572868
  0.6 2.0 %copy-start.1 = (bf16[128,2048]{1,0:T(8,128)(2,1)S(1)}, bf16[128,2048]{1,0:T(8,128)(2,1)}, u32[]{:S(2)}) copy-start(bf16[128,2048]{1,0:T(8,128)(2,1)} %keys_ref.7) | copy-start | bytes 1572868
  0.7 2.0 %copy-start.2 = (bf16[128,2048]{1,0:T(8,128)(2,1)S(1)}, bf16[128,2048]{1,0:T(8,128)(2,1)}, u32[]{:S(2)}) copy-start(bf16[128,2048]{1,0:T(8,128)(2,1)} %values_ref.7) | copy-start | bytes 1572868
  0.7 2.0 %copy-start.3 = (bf16[128,2048]{1,0:T(8,128)(2,1)S(1)}, bf16[128,2048]{1,0:T(8,128)(2,1)}, u32[]{:S(2)}) copy-start(bf16[128,2048]{1,0:T(8,128)(2,1)} %cotangent_ref.1) | copy-start | bytes 1572868
  2.0 12.7 %copy-start.4 = (bf16[16,384]{1,0:T(8,128)(2,1)S(1)}, bf16[16,384]{1,0:T(8,128)(2,1)}, u32[]{:S(2)}) copy-start(bf16[16,384]{1,0:T(8,128)(2,1)} %taps_ref.1) | copy-start | bytes 36868
  2.0 15.0 %collective-permute-start = (bf16[128,1024]{1,0:T(8,128)(2,1)S(1)}, bf16[128,1024]{1,0:T(8,128)(2,1)S(1)}, u32[]{:S(2)}, u32[]{:S(2)}) collective-permute-start(bf16[128,1024]{1,0:T(8,128)(2,1)S(1)} %diagonal.1.sent_ref), channel_id=1, source_target_pairs={{4,8},{8,4},{12,16},{16,12},{20,24},{24,20},{5,9},{9,5},{13,17},{1... | collective-permute-start | bytes 786440 | tf_op jit(solution)/shard_map/ppermute | solution.py:35
  3.0 18.4 %collective-permute-start.1 = (bf16[128,2048]{1,0:T(8,128)(2,1)S(1)}, bf16[128,2048]{1,0:T(8,128)(2,1)S(1)}, u32[]{:S(2)}, u32[]{:S(2)}) collective-permute-start(bf16[128,2048]{1,0:T(8,128)(2,1)S(1)} %get-tuple-element.25.across_ref), channel_id=1, source_target_pairs={{0,8},{8,16},{12,4},{16,24},{20,12},{28,20},{1,9},{9,17},{13,5},{1... | collective-permute-start | bytes 1572872 | tf_op jit(solution)/shard_map/ppermute | solution.py:35
  10.6 15.0 %collective-permute-start.2 = (bf16[128,2048]{1,0:T(8,128)(2,1)S(1)}, bf16[128,2048]{1,0:T(8,128)(2,1)S(1)}, u32[]{:S(2)}, u32[]{:S(2)}) collective-permute-start(bf16[128,2048]{1,0:T(8,128)(2,1)S(1)} %get-tuple-element.24.near_ref), channel_id=1, source_target_pairs={{4,12},{8,0},{12,20},{16,8},{20,28},{24,16},{5,13},{9,1},{13,21},{... | collective-permute-start | bytes 1572872 | tf_op jit(solution)/shard_map/ppermute | solution.py:35
  11.9 14.2 %collective-permute-start.4 = (bf16[128,2048]{1,0:T(8,128)(2,1)S(1)}, bf16[128,2048]{1,0:T(8,128)(2,1)S(1)}, u32[]{:S(2)}, u32[]{:S(2)}) collective-permute-start(bf16[128,2048]{1,0:T(8,128)(2,1)S(1)} %get-tuple-element.25.across_ref), channel_id=1, source_target_pairs={{0,4},{4,0},{8,12},{12,8},{16,20},{20,16},{24,28},{28,24},{1,5},{5... | collective-permute-start | bytes 1572872 | tf_op jit(solution)/shard_map/ppermute | solution.py:35
  22.2 4.6 %collective-permute-start.5 = (f32[16,384]{1,0:T(8,128)S(1)}, f32[16,384]{1,0:T(8,128)S(1)}, u32[]{:S(2)}, u32[]{:S(2)}) collective-permute-start(f32[16,384]{1,0:T(8,128)S(1)} %two.1.sum_ref), channel_id=1, source_target_pairs={{0,4},{4,0},{8,12},{12,8},{16,20},{20,16},{24,28},{28,24},{1,5},{5... | collective-permute-start | bytes 73736 | tf_op jit(solution)/shard_map/ppermute | solution.py:35
  25.6 7.7 %collective-permute-start.3 = (bf16[128,1024]{1,0:T(8,128)(2,1)S(1)}, bf16[128,1024]{1,0:T(8,128)(2,1)S(1)}, u32[]{:S(2)}, u32[]{:S(2)}) collective-permute-start(bf16[128,1024]{1,0:T(8,128)(2,1)S(1)} %forward.1), channel_id=1, source_target_pairs={{0,4},{4,0},{8,12},{12,8},{16,20},{20,16},{24,28},{28,24},{1,5},{5... | collective-permute-start | bytes 786440 | tf_op jit(solution)/shard_map/ppermute | solution.py:35
  26.9 7.9 %collective-permute-start.6 = (f32[16,384]{1,0:T(8,128)S(1)}, f32[16,384]{1,0:T(8,128)S(1)}, u32[]{:S(2)}, u32[]{:S(2)}) collective-permute-start(f32[16,384]{1,0:T(8,128)S(1)} %pair.1.refs_0_), channel_id=1, source_target_pairs={{0,8},{4,12},{8,16},{12,20},{16,24},{20,28},{24,0},{28,4},{1,9},{5... | collective-permute-start | bytes 73736 | tf_op jit(solution)/shard_map/ppermute | solution.py:52
  28.9 5.9 %collective-permute-start.7 = (f32[16,384]{1,0:T(8,128)S(1)}, f32[16,384]{1,0:T(8,128)S(1)}, u32[]{:S(2)}, u32[]{:S(2)}) collective-permute-start(f32[16,384]{1,0:T(8,128)S(1)} %pair.1.refs_0_), channel_id=1, source_target_pairs={{0,16},{4,20},{8,24},{12,28},{16,0},{20,4},{24,8},{28,12},{1,17},{... | collective-permute-start | bytes 73736 | tf_op jit(solution)/shard_map/ppermute | solution.py:52
  31.7 3.8 %collective-permute-start.8 = (f32[16,384]{1,0:T(8,128)S(1)}, f32[16,384]{1,0:T(8,128)S(1)}, u32[]{:S(2)}, u32[]{:S(2)}) collective-permute-start(f32[16,384]{1,0:T(8,128)S(1)} %pair.1.refs_0_), channel_id=1, source_target_pairs={{0,24},{4,28},{8,0},{12,4},{16,8},{20,12},{24,16},{28,20},{1,25},{... | collective-permute-start | bytes 73736 | tf_op jit(solution)/shard_map/ppermute | solution.py:52

commit v20 on v14

--- a/solution.py
+++ b/solution.py
@@ -45,10 +45,11 @@
     while stride < size:
         own = terms[0] if len(terms) == 1 else add(*terms)
         members = 4 if 4 * stride <= size else 2
+        rounds = ((2, 3, 1, 0), (3, 2, 0, 1), (1, 0, 3, 2)) if members == 4 else ((1, 0),)
         terms = [own]
-        for turn in range(1, members):
+        for targets in rounds:
             places = [(i, i // stride % members) for i in range(size)]
-            route = [(i, i + ((place + turn) % members - place) * stride) for i, place in places]
+            route = [(i, i + (targets[place] - place) * stride) for i, place in places]
             terms.append(lax.ppermute(own, axis, route))
         stride *= members
     return terms

time: 36.4 us -> 35.9 us (0.986)
  starting transfers between devices: 21 us -> 19.9 us
  waiting for transfers between devices: 4.32 us -> 4.95 us
    ppermute x3, starting transfers between devices: 5.99 us -> 4.87 us  [sum_terms(): terms.append(lax.ppermute(own, axis, route))]
    ppermute x3, waiting for transfers between devices: 0.77 us -> 1.4 us  [sum_terms(): terms.append(lax.ppermute(own, axis, route))]
  transfers between devices with their start and end apart: 9 -> 9, of which waited for: 4 -> 5; matrix products, arithmetic and copies ran while one was open for 0% -> 0% of each run, Pallas kernels for 22% -> 23%
where the time goes in v20:
time: 35.9 us; the launch traced here: 35.7 us
  starting transfers between devices  19.9 us (55%)
  Pallas kernels  10 us (28%)
  waiting for transfers between devices  4.95 us (14%)
  between operations  0.84 us (2%)
    ppermute x6, starting transfers between devices, moved(): lax.ppermute(block, axis, [pair for pair in route if 0 <= pair[1] < size])  15 us
    ppermute x3, starting transfers between devices, sum_terms(): terms.append(lax.ppermute(own, axis, route))  4.87 us
    ppermute x6, waiting for transfers between devices, moved(): lax.ppermute(block, axis, [pair for pair in route if 0 <= pair[1] < size])  3.55 us
    pallas_call x1, Pallas kernels, shards(): call(functools.partial(tiles_kernel, rows), 'tiles', in_specs=[WHOLE], ou...  2.22 us
    pallas_call x1, Pallas kernels, shards(): call(functools.partial(own_kernel, rows), 'own', flops=4 * 10 ** 9, in_sp...  1.64 us
    ppermute x3, waiting for transfers between devices, sum_terms(): terms.append(lax.ppermute(own, axis, route))  1.4 us
    pallas_call x1, Pallas kernels, shards(): call(last_kernel, 'last', in_specs=[WHOLE] * 10, out_specs=[ANYWHERE] * 3...  1.35 us
    pallas_call x1, Pallas kernels, shards(): call(diagonal_kernel, 'diagonal', in_specs=[ANYWHERE] * 4, out_specs=WHOL...  1.28 us
  transfers between devices with their start and end apart: 9, of which 5 were waited for; matrix products, arithmetic and copies ran while one was open for 0% of the time, Pallas kernels for 23%

profile of v20, /device:TPU:0, one launch (start us, length us, event | category | flops | bytes accessed | tf_op | source)
XLA Modules:
  0.0 35.7 jit_solution(13217860838667639892)
XLA Ops:
  0.7 1.3 %diagonal.1.sent_ref = bf16[128,1024]{1,0:T(8,128)(2,1)S(1)} custom-call(bf16[128,2048]{1,0:T(8,128)(2,1)} %query_ref.7, bf16[128,2048]{1,0:T(8,128)(2,1)} %keys_ref.7, bf16[128,2048]{1,0:T(8,128)(2,1)} %values_ref.7, bf16[128,2048]{1,0:T(8,128)(2,1)} %cotangent_ref.1), custom_call_target="tpu_custom_call" | custom-call | flops 1000000 | bytes 100000 | tf_op jit(solution)/shard_map/diagonal/pallas_call | solution.py:346
  2.0 0.7 %collective-permute-start = (bf16[128,1024]{1,0:T(8,128)(2,1)S(1)}, bf16[128,1024]{1,0:T(8,128)(2,1)S(1)}, u32[]{:S(2)}, u32[]{:S(2)}) collective-permute-start(bf16[128,1024]{1,0:T(8,128)(2,1)S(1)} %diagonal.1.sent_ref), channel_id=1, source_target_pairs={{4,8},{8,4},{12,16},{16,12},{20,24},{24,20},{5,9},{9,5},{13,17},{1... | collective-permute-start | bytes 786440 | tf_op jit(solution)/shard_map/ppermute | solution.py:35
  2.7 0.3 products.1
  3.0 7.6 %collective-permute-start.1 = (bf16[128,2048]{1,0:T(8,128)(2,1)S(1)}, bf16[128,2048]{1,0:T(8,128)(2,1)S(1)}, u32[]{:S(2)}, u32[]{:S(2)}) collective-permute-start(bf16[128,2048]{1,0:T(8,128)(2,1)S(1)} %get-tuple-element.23.across_ref), channel_id=1, source_target_pairs={{0,8},{8,16},{12,4},{16,24},{20,12},{28,20},{1,9},{9,17},{13,5},{1... | collective-permute-start | bytes 1572872 | tf_op jit(solution)/shard_map/ppermute | solution.py:35
  10.6 1.3 %collective-permute-start.2 = (bf16[128,2048]{1,0:T(8,128)(2,1)S(1)}, bf16[128,2048]{1,0:T(8,128)(2,1)S(1)}, u32[]{:S(2)}, u32[]{:S(2)}) collective-permute-start(bf16[128,2048]{1,0:T(8,128)(2,1)S(1)} %get-tuple-element.22.near_ref), channel_id=1, source_target_pairs={{4,12},{8,0},{12,20},{16,8},{20,28},{24,16},{5,13},{9,1},{13,21},{... | collective-permute-start | bytes 1572872 | tf_op jit(solution)/shard_map/ppermute | solution.py:35
  11.9 2.8 %collective-permute-start.4 = (bf16[128,2048]{1,0:T(8,128)(2,1)S(1)}, bf16[128,2048]{1,0:T(8,128)(2,1)S(1)}, u32[]{:S(2)}, u32[]{:S(2)}) collective-permute-start(bf16[128,2048]{1,0:T(8,128)(2,1)S(1)} %get-tuple-element.23.across_ref), channel_id=1, source_target_pairs={{0,4},{4,0},{8,12},{12,8},{16,20},{20,16},{24,28},{28,24},{1,5},{5... | collective-permute-start | bytes 1572872 | tf_op jit(solution)/shard_map/ppermute | solution.py:35
  14.7 2.2 %tiles.1 = (bf16[16,128,384]{2,1,0:T(8,128)(2,1)S(1)}, bf16[16,128,384]{2,1,0:T(8,128)(2,1)S(1)}) custom-call(bf16[16,384]{1,0:T(8,128)(2,1)S(1)} %copy-done.4), custom_call_target="tpu_custom_call" | custom-call | flops 1000000 | bytes 100000 | tf_op jit(solution)/shard_map/tiles/pallas_call | solution.py:366
  16.9 1.6 %own.1 = (f32[16,384]{1,0:T(8,128)S(1)}, f32[128,2048]{1,0:T(8,128)S(1)}, f32[128,2048]{1,0:T(8,128)S(1)}) custom-call(bf16[16,128,384]{2,1,0:T(8,128)(2,1)S(1)} %get-tuple-element.20.ready_tiles.tiles_ref, bf16[16,128,384]{2,1,0:T(8,128)(2,1)S(1)} %get-tuple-element.21.late_tiles.tiles_ref, bf16[128,2048]{1,0:T(8,128)(2,1)S(1)} %get-tuple-element.22.near_ref, ...), custom_call_target="tpu_custom_call" | custom-call | flops 4000000000 | bytes 100000 | tf_op jit(solution)/shard_map/own/pallas_call | solution.py:373
  18.6 2.9 %collective-permute-done.1.two_ref = bf16[128,2048]{1,0:T(8,128)(2,1)S(1)} collective-permute-done((bf16[128,2048]{1,0:T(8,128)(2,1)S(1)}, bf16[128,2048]{1,0:T(8,128)(2,1)S(1)}, u32[]{:S(2)}, u32[]{:S(2)}) %collective-permute-start.1) | collective-permute-done | bytes 524320 | tf_op jit(solution)/shard_map/ppermute | solution.py:35
  21.5 0.8 %two.1.sum_ref = f32[16,384]{1,0:T(8,128)S(1)} custom-call(f32[16,384]{1,0:T(8,128)S(1)} %get-tuple-element.25.sum_ref, bf16[128,2048]{1,0:T(8,128)(2,1)S(1)} %get-tuple-element.22.near_ref, bf16[128,2048]{1,0:T(8,128)(2,1)S(1)} %collective-permute-done.1.two_ref), custom_call_target="tpu_custom_call" | custom-call | flops 1000000 | bytes 100000 | tf_op jit(solution)/shard_map/two/pallas_call | solution.py:382
  22.3 2.6 %collective-permute-start.5 = (f32[16,384]{1,0:T(8,128)S(1)}, f32[16,384]{1,0:T(8,128)S(1)}, u32[]{:S(2)}, u32[]{:S(2)}) collective-permute-start(f32[16,384]{1,0:T(8,128)S(1)} %two.1.sum_ref), channel_id=1, source_target_pairs={{0,4},{4,0},{8,12},{12,8},{16,20},{20,16},{24,28},{28,24},{1,5},{5... | collective-permute-start | bytes 73736 | tf_op jit(solution)/shard_map/ppermute | solution.py:35
  24.9 0.4 %ready.1 = (f32[128,1024]{1,0:T(8,128)S(1)}, bf16[128,1024]{1,0:T(8,128)(2,1)S(1)}, bf16[128,1024]{1,0:T(8,128)(2,1)S(1)}) custom-call(bf16[16,128,384]{2,1,0:T(8,128)(2,1)S(1)} %get-tuple-element.20.ready_tiles.tiles_ref, f32[128,2048]{1,0:T(8,128)S(1)} %get-tuple-element.24.ready_ref, bf16[128,2048]{1,0:T(8,128)(2,1)S(1)} %collective-permute-done.1.two_ref, ...), custom_call_target="tpu_custom_call" | custom-call | flops 1000000 | bytes 100000 | tf_op jit(solution)/shard_map/ready/pallas_call | solution.py:391
  25.3 0.3 collective-permute-done.2.far_ref
  25.6 0.1 collective-permute-start.3
  25.7 0.4 %collective-permute-done.4.swap_ref = bf16[128,2048]{1,0:T(8,128)(2,1)S(1)} collective-permute-done((bf16[128,2048]{1,0:T(8,128)(2,1)S(1)}, bf16[128,2048]{1,0:T(8,128)(2,1)S(1)}, u32[]{:S(2)}, u32[]{:S(2)}) %collective-permute-start.4) | collective-permute-done | bytes 524320 | tf_op jit(solution)/shard_map/ppermute | solution.py:35
  26.1 0.8 %cross.1.cross_ref = f32[16,384]{1,0:T(8,128)S(1)} custom-call(bf16[128,2048]{1,0:T(8,128)(2,1)S(1)} %get-tuple-element.23.across_ref, bf16[128,2048]{1,0:T(8,128)(2,1)S(1)} %collective-permute-done.4.swap_ref), custom_call_target="tpu_custom_call" | custom-call | flops 1000000 | bytes 100000 | tf_op jit(solution)/shard_map/cross/pallas_call | solution.py:408
  26.9 3.1 %collective-permute-start.6 = (f32[16,384]{1,0:T(8,128)S(1)}, f32[16,384]{1,0:T(8,128)S(1)}, u32[]{:S(2)}, u32[]{:S(2)}) collective-permute-start(f32[16,384]{1,0:T(8,128)S(1)} %pair.1.refs_0_), channel_id=1, source_target_pairs={{0,16},{4,20},{8,24},{12,28},{16,8},{20,12},{24,0},{28,4},{1,17},{... | collective-permute-start | bytes 73736 | tf_op jit(solution)/shard_map/ppermute | solution.py:53
  30.0 1.3 %collective-permute-start.7 = (f32[16,384]{1,0:T(8,128)S(1)}, f32[16,384]{1,0:T(8,128)S(1)}, u32[]{:S(2)}, u32[]{:S(2)}) collective-permute-start(f32[16,384]{1,0:T(8,128)S(1)} %pair.1.refs_0_), channel_id=1, source_target_pairs={{0,24},{4,28},{8,16},{12,20},{16,0},{20,4},{24,8},{28,12},{1,25},{... | collective-permute-start | bytes 73736 | tf_op jit(solution)/shard_map/ppermute | solution.py:53
  31.3 0.5 %collective-permute-start.8 = (f32[16,384]{1,0:T(8,128)S(1)}, f32[16,384]{1,0:T(8,128)S(1)}, u32[]{:S(2)}, u32[]{:S(2)}) collective-permute-start(f32[16,384]{1,0:T(8,128)S(1)} %pair.1.refs_0_), channel_id=1, source_target_pairs={{0,8},{4,12},{8,0},{12,4},{16,24},{20,28},{24,16},{28,20},{1,9},{5... | collective-permute-start | bytes 73736 | tf_op jit(solution)/shard_map/ppermute | solution.py:53
  31.8 0.5 %known.1 = (bf16[128,2048]{1,0:T(8,128)(2,1)S(1)}, bf16[128,2048]{1,0:T(8,128)(2,1)S(1)}) custom-call(bf16[16,128,384]{2,1,0:T(8,128)(2,1)S(1)} %get-tuple-element.21.late_tiles.tiles_ref, f32[128,2048]{1,0:T(8,128)S(1)} %get-tuple-element.29.late_ref, bf16[128,2048]{1,0:T(8,128)(2,1)S(1)} %collective-permute-done.4.swap_ref, ...), custom_call_target="tpu_custom_call" | custom-call | flops 4000000000 | bytes 100000 | tf_op jit(solution)/shard_map/known/pallas_call | solution.py:423
  32.4 1.3 %last.1 = (bf16[128,2048]{1,0:T(8,128)(2,1)}, bf16[128,2048]{1,0:T(8,128)(2,1)}, bf16[128,2048]{1,0:T(8,128)(2,1)}, f32[8,128]{1,0:T(8,128)S(1)}) custom-call(bf16[16,128,384]{2,1,0:T(8,128)(2,1)S(1)} %get-tuple-element.20.ready_tiles.tiles_ref, f32[128,1024]{1,0:T(8,128)S(1)} %get-tuple-element.26.rest_ref, ...), custom_call_target="tpu_custom_call" | custom-call | flops 1000000 | bytes 100000 | tf_op jit(solution)/shard_map/last/pallas_call | solution.py:442
  33.7 1.0 %collective-permute-done.7.refs_2_ = f32[16,384]{1,0:T(8,128)S(1)} collective-permute-done((f32[16,384]{1,0:T(8,128)S(1)}, f32[16,384]{1,0:T(8,128)S(1)}, u32[]{:S(2)}, u32[]{:S(2)}) %collective-permute-start.7) | collective-permute-done | bytes 24608 | tf_op jit(solution)/shard_map/ppermute | solution.py:53
  34.7 0.4 %collective-permute-done.8.refs_3_ = f32[16,384]{1,0:T(8,128)S(1)} collective-permute-done((f32[16,384]{1,0:T(8,128)S(1)}, f32[16,384]{1,0:T(8,128)S(1)}, u32[]{:S(2)}, u32[]{:S(2)}) %collective-permute-start.8) | collective-permute-done | bytes 24608 | tf_op jit(solution)/shard_map/ppermute | solution.py:53
  35.1 0.6 %add.1 = f32[16,384]{1,0:T(8,128)} custom-call(f32[16,384]{1,0:T(8,128)S(1)} %pair.1.refs_0_, f32[16,384]{1,0:T(8,128)S(1)} %collective-permute-done.6.refs_1_, f32[16,384]{1,0:T(8,128)S(1)} %collective-permute-done.7.refs_2_, f32[16,384]{1,0:T(8,128)S(1)} %collective-permute-done.8.refs_3_, f32[8,128]{1,0:T(8,128)S(1)} %get-tuple-element.35.refs_4_), custom_call_target="tpu_custom_call" | custom-call | flops 1000000 | bytes 100000 | tf_op jit(solution)/shard_map/add/pallas_call | solution.py:433
  (16 shorter events, 0.1 us)
Async XLA Ops:
  0.6 2.0 %copy-start = (bf16[128,2048]{1,0:T(8,128)(2,1)S(1)}, bf16[128,2048]{1,0:T(8,128)(2,1)}, u32[]{:S(2)}) copy-start(bf16[128,2048]{1,0:T(8,128)(2,1)} %query_ref.7) | copy-start | bytes 1572868
  0.6 2.0 %copy-start.1 = (bf16[128,2048]{1,0:T(8,128)(2,1)S(1)}, bf16[128,2048]{1,0:T(8,128)(2,1)}, u32[]{:S(2)}) copy-start(bf16[128,2048]{1,0:T(8,128)(2,1)} %keys_ref.7) | copy-start | bytes 1572868
  0.7 2.0 %copy-start.2 = (bf16[128,2048]{1,0:T(8,128)(2,1)S(1)}, bf16[128,2048]{1,0:T(8,128)(2,1)}, u32[]{:S(2)}) copy-start(bf16[128,2048]{1,0:T(8,128)(2,1)} %values_ref.7) | copy-start | bytes 1572868
  0.7 2.0 %copy-start.3 = (bf16[128,2048]{1,0:T(8,128)(2,1)S(1)}, bf16[128,2048]{1,0:T(8,128)(2,1)}, u32[]{:S(2)}) copy-start(bf16[128,2048]{1,0:T(8,128)(2,1)} %cotangent_ref.1) | copy-start | bytes 1572868
  2.0 12.7 %copy-start.4 = (bf16[16,384]{1,0:T(8,128)(2,1)S(1)}, bf16[16,384]{1,0:T(8,128)(2,1)}, u32[]{:S(2)}) copy-start(bf16[16,384]{1,0:T(8,128)(2,1)} %taps_ref.1) | copy-start | bytes 36868
  2.0 15.0 %collective-permute-start = (bf16[128,1024]{1,0:T(8,128)(2,1)S(1)}, bf16[128,1024]{1,0:T(8,128)(2,1)S(1)}, u32[]{:S(2)}, u32[]{:S(2)}) collective-permute-start(bf16[128,1024]{1,0:T(8,128)(2,1)S(1)} %diagonal.1.sent_ref), channel_id=1, source_target_pairs={{4,8},{8,4},{12,16},{16,12},{20,24},{24,20},{5,9},{9,5},{13,17},{1... | collective-permute-start | bytes 786440 | tf_op jit(solution)/shard_map/ppermute | solution.py:35
  3.0 18.4 %collective-permute-start.1 = (bf16[128,2048]{1,0:T(8,128)(2,1)S(1)}, bf16[128,2048]{1,0:T(8,128)(2,1)S(1)}, u32[]{:S(2)}, u32[]{:S(2)}) collective-permute-start(bf16[128,2048]{1,0:T(8,128)(2,1)S(1)} %get-tuple-element.23.across_ref), channel_id=1, source_target_pairs={{0,8},{8,16},{12,4},{16,24},{20,12},{28,20},{1,9},{9,17},{13,5},{1... | collective-permute-start | bytes 1572872 | tf_op jit(solution)/shard_map/ppermute | solution.py:35
  10.6 15.0 %collective-permute-start.2 = (bf16[128,2048]{1,0:T(8,128)(2,1)S(1)}, bf16[128,2048]{1,0:T(8,128)(2,1)S(1)}, u32[]{:S(2)}, u32[]{:S(2)}) collective-permute-start(bf16[128,2048]{1,0:T(8,128)(2,1)S(1)} %get-tuple-element.22.near_ref), channel_id=1, source_target_pairs={{4,12},{8,0},{12,20},{16,8},{20,28},{24,16},{5,13},{9,1},{13,21},{... | collective-permute-start | bytes 1572872 | tf_op jit(solution)/shard_map/ppermute | solution.py:35
  11.9 14.2 %collective-permute-start.4 = (bf16[128,2048]{1,0:T(8,128)(2,1)S(1)}, bf16[128,2048]{1,0:T(8,128)(2,1)S(1)}, u32[]{:S(2)}, u32[]{:S(2)}) collective-permute-start(bf16[128,2048]{1,0:T(8,128)(2,1)S(1)} %get-tuple-element.23.across_ref), channel_id=1, source_target_pairs={{0,4},{4,0},{8,12},{12,8},{16,20},{20,16},{24,28},{28,24},{1,5},{5... | collective-permute-start | bytes 1572872 | tf_op jit(solution)/shard_map/ppermute | solution.py:35
  22.3 4.6 %collective-permute-start.5 = (f32[16,384]{1,0:T(8,128)S(1)}, f32[16,384]{1,0:T(8,128)S(1)}, u32[]{:S(2)}, u32[]{:S(2)}) collective-permute-start(f32[16,384]{1,0:T(8,128)S(1)} %two.1.sum_ref), channel_id=1, source_target_pairs={{0,4},{4,0},{8,12},{12,8},{16,20},{20,16},{24,28},{28,24},{1,5},{5... | collective-permute-start | bytes 73736 | tf_op jit(solution)/shard_map/ppermute | solution.py:35
  25.6 6.7 %collective-permute-start.3 = (bf16[128,1024]{1,0:T(8,128)(2,1)S(1)}, bf16[128,1024]{1,0:T(8,128)(2,1)S(1)}, u32[]{:S(2)}, u32[]{:S(2)}) collective-permute-start(bf16[128,1024]{1,0:T(8,128)(2,1)S(1)} %forward.1), channel_id=1, source_target_pairs={{0,4},{4,0},{8,12},{12,8},{16,20},{20,16},{24,28},{28,24},{1,5},{5... | collective-permute-start | bytes 786440 | tf_op jit(solution)/shard_map/ppermute | solution.py:35
  26.9 6.8 %collective-permute-start.6 = (f32[16,384]{1,0:T(8,128)S(1)}, f32[16,384]{1,0:T(8,128)S(1)}, u32[]{:S(2)}, u32[]{:S(2)}) collective-permute-start(f32[16,384]{1,0:T(8,128)S(1)} %pair.1.refs_0_), channel_id=1, source_target_pairs={{0,16},{4,20},{8,24},{12,28},{16,8},{20,12},{24,0},{28,4},{1,17},{... | collective-permute-start | bytes 73736 | tf_op jit(solution)/shard_map/ppermute | solution.py:53
  30.0 4.7 %collective-permute-start.7 = (f32[16,384]{1,0:T(8,128)S(1)}, f32[16,384]{1,0:T(8,128)S(1)}, u32[]{:S(2)}, u32[]{:S(2)}) collective-permute-start(f32[16,384]{1,0:T(8,128)S(1)} %pair.1.refs_0_), channel_id=1, source_target_pairs={{0,24},{4,28},{8,16},{12,20},{16,0},{20,4},{24,8},{28,12},{1,25},{... | collective-permute-start | bytes 73736 | tf_op jit(solution)/shard_map/ppermute | solution.py:53
  31.3 3.8 %collective-permute-start.8 = (f32[16,384]{1,0:T(8,128)S(1)}, f32[16,384]{1,0:T(8,128)S(1)}, u32[]{:S(2)}, u32[]{:S(2)}) collective-permute-start(f32[16,384]{1,0:T(8,128)S(1)} %pair.1.refs_0_), channel_id=1, source_target_pairs={{0,8},{4,12},{8,0},{12,4},{16,24},{20,28},{24,16},{28,20},{1,9},{5... | collective-permute-start | bytes 73736 | tf_op jit(solution)/shard_map/ppermute | solution.py:53

commit v21 on v19

--- a/solution.py
+++ b/solution.py
@@ -45,10 +45,11 @@
     while stride < size:
         own = terms[0] if len(terms) == 1 else add(*terms)
         members = 4 if 4 * stride <= size else 2
+        rounds = ((2, 3, 1, 0), (3, 2, 0, 1), (1, 0, 3, 2)) if members == 4 else ((1, 0),)
         terms = [own]
-        for turn in range(1, members):
+        for targets in rounds:
             places = [(i, i // stride % members) for i in range(size)]
-            route = [(i, i + ((place + turn) % members - place) * stride) for i, place in places]
+            route = [(i, i + (targets[place] - place) * stride) for i, place in places]
             terms.append(lax.ppermute(own, axis, route))
         stride *= members
     return terms

time: 36.4 us -> 35.9 us (0.986)
  starting transfers between devices: 20.9 us -> 19.8 us
  waiting for transfers between devices: 4.16 us -> 4.73 us
    ppermute x3, starting transfers between devices: 5.94 us -> 4.87 us  [sum_terms(): terms.append(lax.ppermute(own, axis, route))]
    ppermute x3, waiting for transfers between devices: 0.82 us -> 1.39 us  [sum_terms(): terms.append(lax.ppermute(own, axis, route))]
  transfers between devices with their start and end apart: 9 -> 9, of which waited for: 4 -> 5; matrix products, arithmetic and copies ran while one was open for 0% -> 0% of each run, Pallas kernels for 23% -> 23%
where the time goes in v21:
time: 35.9 us; the launch traced here: 35.7 us
  starting transfers between devices  19.8 us (55%)
  Pallas kernels  10.3 us (29%)
  waiting for transfers between devices  4.73 us (13%)
  between operations  0.83 us (2%)
    ppermute x6, starting transfers between devices, moved(): lax.ppermute(block, axis, [pair for pair in route if 0 <= pair[1] < size])  15 us
    ppermute x3, starting transfers between devices, sum_terms(): terms.append(lax.ppermute(own, axis, route))  4.87 us
    ppermute x6, waiting for transfers between devices, moved(): lax.ppermute(block, axis, [pair for pair in route if 0 <= pair[1] < size])  3.34 us
    pallas_call x1, Pallas kernels, shards(): call(functools.partial(tiles_kernel, rows), 'tiles', in_specs=[WHOLE], ou...  2.22 us
    pallas_call x1, Pallas kernels, shards(): call(functools.partial(own_kernel, rows), 'own', flops=4 * 10 ** 9, in_sp...  1.96 us
    ppermute x3, waiting for transfers between devices, sum_terms(): terms.append(lax.ppermute(own, axis, route))  1.39 us
    pallas_call x1, Pallas kernels, shards(): call(last_kernel, 'last', in_specs=[WHOLE] * 10, out_specs=[ANYWHERE] * 3...  1.35 us
    pallas_call x1, Pallas kernels, shards(): call(diagonal_kernel, 'diagonal', in_specs=[ANYWHERE] * 4, out_specs=WHOL...  1.28 us
  transfers between devices with their start and end apart: 9, of which 5 were waited for; matrix products, arithmetic and copies ran while one was open for 0% of the time, Pallas kernels for 23%

profile of v21, /device:TPU:0, one launch (start us, length us, event | category | flops | bytes accessed | tf_op | source)
XLA Modules:
  0.0 35.7 jit_solution(85280049747235640)
XLA Ops:
  0.7 1.3 %diagonal.1.sent_ref = bf16[128,1024]{1,0:T(8,128)(2,1)S(1)} custom-call(bf16[128,2048]{1,0:T(8,128)(2,1)} %query_ref.7, bf16[128,2048]{1,0:T(8,128)(2,1)} %keys_ref.7, bf16[128,2048]{1,0:T(8,128)(2,1)} %values_ref.7, bf16[128,2048]{1,0:T(8,128)(2,1)} %cotangent_ref.1), custom_call_target="tpu_custom_call" | custom-call | flops 1000000 | bytes 100000 | tf_op jit(solution)/shard_map/diagonal/pallas_call | solution.py:371
  2.0 0.7 %collective-permute-start = (bf16[128,1024]{1,0:T(8,128)(2,1)S(1)}, bf16[128,1024]{1,0:T(8,128)(2,1)S(1)}, u32[]{:S(2)}, u32[]{:S(2)}) collective-permute-start(bf16[128,1024]{1,0:T(8,128)(2,1)S(1)} %diagonal.1.sent_ref), channel_id=1, source_target_pairs={{4,8},{8,4},{12,16},{16,12},{20,24},{24,20},{5,9},{9,5},{13,17},{1... | collective-permute-start | bytes 786440 | tf_op jit(solution)/shard_map/ppermute | solution.py:35
  2.7 0.3 products.1
  3.0 7.6 %collective-permute-start.1 = (bf16[128,2048]{1,0:T(8,128)(2,1)S(1)}, bf16[128,2048]{1,0:T(8,128)(2,1)S(1)}, u32[]{:S(2)}, u32[]{:S(2)}) collective-permute-start(bf16[128,2048]{1,0:T(8,128)(2,1)S(1)} %get-tuple-element.25.across_ref), channel_id=1, source_target_pairs={{0,8},{8,16},{12,4},{16,24},{20,12},{28,20},{1,9},{9,17},{13,5},{1... | collective-permute-start | bytes 1572872 | tf_op jit(solution)/shard_map/ppermute | solution.py:35
  10.6 1.3 %collective-permute-start.2 = (bf16[128,2048]{1,0:T(8,128)(2,1)S(1)}, bf16[128,2048]{1,0:T(8,128)(2,1)S(1)}, u32[]{:S(2)}, u32[]{:S(2)}) collective-permute-start(bf16[128,2048]{1,0:T(8,128)(2,1)S(1)} %get-tuple-element.24.near_ref), channel_id=1, source_target_pairs={{4,12},{8,0},{12,20},{16,8},{20,28},{24,16},{5,13},{9,1},{13,21},{... | collective-permute-start | bytes 1572872 | tf_op jit(solution)/shard_map/ppermute | solution.py:35
  11.9 2.8 %collective-permute-start.4 = (bf16[128,2048]{1,0:T(8,128)(2,1)S(1)}, bf16[128,2048]{1,0:T(8,128)(2,1)S(1)}, u32[]{:S(2)}, u32[]{:S(2)}) collective-permute-start(bf16[128,2048]{1,0:T(8,128)(2,1)S(1)} %get-tuple-element.25.across_ref), channel_id=1, source_target_pairs={{0,4},{4,0},{8,12},{12,8},{16,20},{20,16},{24,28},{28,24},{1,5},{5... | collective-permute-start | bytes 1572872 | tf_op jit(solution)/shard_map/ppermute | solution.py:35
  14.7 2.2 %tiles.1 = (bf16[16,128,384]{2,1,0:T(8,128)(2,1)S(1)}, bf16[16,128,384]{2,1,0:T(8,128)(2,1)S(1)}) custom-call(bf16[16,384]{1,0:T(8,128)(2,1)S(1)} %copy-done.4), custom_call_target="tpu_custom_call" | custom-call | flops 1000000 | bytes 100000 | tf_op jit(solution)/shard_map/tiles/pallas_call | solution.py:391
  16.9 2.0 %own.1 = (f32[16,384]{1,0:T(8,128)S(1)}, f32[128,2048]{1,0:T(8,128)S(1)}, f32[128,2048]{1,0:T(8,128)S(1)}, bf16[128,2048]{1,0:T(8,128)(2,1)S(1)}, bf16[128,2048]{1,0:T(8,128)(2,1)S(1)}) custom-call(bf16[16,128,384]{2,1,0:T(8,128)(2,1)S(1)} %get-tuple-element.22.ready_tiles.tiles_ref, bf16[16,128,384]{2,1,0:T(8,128)(2,1)S(1)} %get-tuple-element.23.late_tiles.tiles_ref, ...), custom_call_target="tpu_custom_call" | custom-call | flops 4000000000 | bytes 100000 | tf_op jit(solution)/shard_map/own/pallas_call | solution.py:398
  18.9 2.5 %collective-permute-done.1.two_ref = bf16[128,2048]{1,0:T(8,128)(2,1)S(1)} collective-permute-done((bf16[128,2048]{1,0:T(8,128)(2,1)S(1)}, bf16[128,2048]{1,0:T(8,128)(2,1)S(1)}, u32[]{:S(2)}, u32[]{:S(2)}) %collective-permute-start.1) | collective-permute-done | bytes 524320 | tf_op jit(solution)/shard_map/ppermute | solution.py:35
  21.5 0.8 %two.1.sum_ref = f32[16,384]{1,0:T(8,128)S(1)} custom-call(f32[16,384]{1,0:T(8,128)S(1)} %get-tuple-element.27.sum_ref, bf16[128,2048]{1,0:T(8,128)(2,1)S(1)} %get-tuple-element.28.turned_ref, bf16[128,2048]{1,0:T(8,128)(2,1)S(1)} %collective-permute-done.1.two_ref), custom_call_target="tpu_custom_call" | custom-call | flops 1000000 | bytes 100000 | tf_op jit(solution)/shard_map/two/pallas_call | solution.py:407
  22.2 2.6 %collective-permute-start.5 = (f32[16,384]{1,0:T(8,128)S(1)}, f32[16,384]{1,0:T(8,128)S(1)}, u32[]{:S(2)}, u32[]{:S(2)}) collective-permute-start(f32[16,384]{1,0:T(8,128)S(1)} %two.1.sum_ref), channel_id=1, source_target_pairs={{0,4},{4,0},{8,12},{12,8},{16,20},{20,16},{24,28},{28,24},{1,5},{5... | collective-permute-start | bytes 73736 | tf_op jit(solution)/shard_map/ppermute | solution.py:35
  24.8 0.4 %ready.1 = (f32[128,1024]{1,0:T(8,128)S(1)}, bf16[128,1024]{1,0:T(8,128)(2,1)S(1)}, bf16[128,1024]{1,0:T(8,128)(2,1)S(1)}) custom-call(bf16[16,128,384]{2,1,0:T(8,128)(2,1)S(1)} %get-tuple-element.22.ready_tiles.tiles_ref, f32[128,2048]{1,0:T(8,128)S(1)} %get-tuple-element.26.ready_ref, bf16[128,2048]{1,0:T(8,128)(2,1)S(1)} %collective-permute-done.1.two_ref, ...), custom_call_target="tpu_custom_call" | custom-call | flops 1000000 | bytes 100000 | tf_op jit(solution)/shard_map/ready/pallas_call | solution.py:417
  25.2 0.4 %collective-permute-done.2.far_ref = bf16[128,2048]{1,0:T(8,128)(2,1)S(1)} collective-permute-done((bf16[128,2048]{1,0:T(8,128)(2,1)S(1)}, bf16[128,2048]{1,0:T(8,128)(2,1)S(1)}, u32[]{:S(2)}, u32[]{:S(2)}) %collective-permute-start.2) | collective-permute-done | bytes 524320 | tf_op jit(solution)/shard_map/ppermute | solution.py:35
  25.6 0.1 collective-permute-start.3
  25.7 0.4 %collective-permute-done.4.swap_ref = bf16[128,2048]{1,0:T(8,128)(2,1)S(1)} collective-permute-done((bf16[128,2048]{1,0:T(8,128)(2,1)S(1)}, bf16[128,2048]{1,0:T(8,128)(2,1)S(1)}, u32[]{:S(2)}, u32[]{:S(2)}) %collective-permute-start.4) | collective-permute-done | bytes 524320 | tf_op jit(solution)/shard_map/ppermute | solution.py:35
  26.1 0.8 %cross.1.cross_ref = f32[16,384]{1,0:T(8,128)S(1)} custom-call(bf16[128,2048]{1,0:T(8,128)(2,1)S(1)} %get-tuple-element.38.turned_ref, bf16[128,2048]{1,0:T(8,128)(2,1)S(1)} %collective-permute-done.4.swap_ref), custom_call_target="tpu_custom_call" | custom-call | flops 1000000 | bytes 100000 | tf_op jit(solution)/shard_map/cross/pallas_call | solution.py:434
  26.9 3.0 %collective-permute-start.6 = (f32[16,384]{1,0:T(8,128)S(1)}, f32[16,384]{1,0:T(8,128)S(1)}, u32[]{:S(2)}, u32[]{:S(2)}) collective-permute-start(f32[16,384]{1,0:T(8,128)S(1)} %pair.1.refs_0_), channel_id=1, source_target_pairs={{0,16},{4,20},{8,24},{12,28},{16,8},{20,12},{24,0},{28,4},{1,17},{... | collective-permute-start | bytes 73736 | tf_op jit(solution)/shard_map/ppermute | solution.py:53
  29.9 1.4 %collective-permute-start.7 = (f32[16,384]{1,0:T(8,128)S(1)}, f32[16,384]{1,0:T(8,128)S(1)}, u32[]{:S(2)}, u32[]{:S(2)}) collective-permute-start(f32[16,384]{1,0:T(8,128)S(1)} %pair.1.refs_0_), channel_id=1, source_target_pairs={{0,24},{4,28},{8,16},{12,20},{16,0},{20,4},{24,8},{28,12},{1,25},{... | collective-permute-start | bytes 73736 | tf_op jit(solution)/shard_map/ppermute | solution.py:53
  31.2 0.5 %collective-permute-start.8 = (f32[16,384]{1,0:T(8,128)S(1)}, f32[16,384]{1,0:T(8,128)S(1)}, u32[]{:S(2)}, u32[]{:S(2)}) collective-permute-start(f32[16,384]{1,0:T(8,128)S(1)} %pair.1.refs_0_), channel_id=1, source_target_pairs={{0,8},{4,12},{8,0},{12,4},{16,24},{20,28},{24,16},{28,20},{1,9},{5... | collective-permute-start | bytes 73736 | tf_op jit(solution)/shard_map/ppermute | solution.py:53
  31.8 0.6 %known.1 = (bf16[128,2048]{1,0:T(8,128)(2,1)S(1)}, bf16[128,2048]{1,0:T(8,128)(2,1)S(1)}) custom-call(bf16[16,128,384]{2,1,0:T(8,128)(2,1)S(1)} %get-tuple-element.23.late_tiles.tiles_ref, f32[128,2048]{1,0:T(8,128)S(1)} %get-tuple-element.32.late_ref, bf16[128,2048]{1,0:T(8,128)(2,1)S(1)} %collective-permute-done.4.swap_ref, ...), custom_call_target="tpu_custom_call" | custom-call | flops 4000000000 | bytes 100000 | tf_op jit(solution)/shard_map/known/pallas_call | solution.py:450
  32.3 1.3 %last.1 = (bf16[128,2048]{1,0:T(8,128)(2,1)}, bf16[128,2048]{1,0:T(8,128)(2,1)}, bf16[128,2048]{1,0:T(8,128)(2,1)}, f32[8,128]{1,0:T(8,128)S(1)}) custom-call(bf16[16,128,384]{2,1,0:T(8,128)(2,1)S(1)} %get-tuple-element.22.ready_tiles.tiles_ref, f32[128,1024]{1,0:T(8,128)S(1)} %get-tuple-element.29.rest_ref, ...), custom_call_target="tpu_custom_call" | custom-call | flops 1000000 | bytes 100000 | tf_op jit(solution)/shard_map/last/pallas_call | solution.py:469
  33.7 0.9 %collective-permute-done.7.refs_2_ = f32[16,384]{1,0:T(8,128)S(1)} collective-permute-done((f32[16,384]{1,0:T(8,128)S(1)}, f32[16,384]{1,0:T(8,128)S(1)}, u32[]{:S(2)}, u32[]{:S(2)}) %collective-permute-start.7) | collective-permute-done | bytes 24608 | tf_op jit(solution)/shard_map/ppermute | solution.py:53
  34.6 0.5 %collective-permute-done.8.refs_3_ = f32[16,384]{1,0:T(8,128)S(1)} collective-permute-done((f32[16,384]{1,0:T(8,128)S(1)}, f32[16,384]{1,0:T(8,128)S(1)}, u32[]{:S(2)}, u32[]{:S(2)}) %collective-permute-start.8) | collective-permute-done | bytes 24608 | tf_op jit(solution)/shard_map/ppermute | solution.py:53
  35.1 0.6 %add.1 = f32[16,384]{1,0:T(8,128)} custom-call(f32[16,384]{1,0:T(8,128)S(1)} %pair.1.refs_0_, f32[16,384]{1,0:T(8,128)S(1)} %collective-permute-done.6.refs_1_, f32[16,384]{1,0:T(8,128)S(1)} %collective-permute-done.7.refs_2_, f32[16,384]{1,0:T(8,128)S(1)} %collective-permute-done.8.refs_3_, f32[8,128]{1,0:T(8,128)S(1)} %get-tuple-element.39.refs_4_), custom_call_target="tpu_custom_call" | custom-call | flops 1000000 | bytes 100000 | tf_op jit(solution)/shard_map/add/pallas_call | solution.py:460
  (16 shorter events, 0.1 us)
Async XLA Ops:
  0.6 2.0 %copy-start = (bf16[128,2048]{1,0:T(8,128)(2,1)S(1)}, bf16[128,2048]{1,0:T(8,128)(2,1)}, u32[]{:S(2)}) copy-start(bf16[128,2048]{1,0:T(8,128)(2,1)} %query_ref.7) | copy-start | bytes 1572868
  0.6 2.0 %copy-start.1 = (bf16[128,2048]{1,0:T(8,128)(2,1)S(1)}, bf16[128,2048]{1,0:T(8,128)(2,1)}, u32[]{:S(2)}) copy-start(bf16[128,2048]{1,0:T(8,128)(2,1)} %keys_ref.7) | copy-start | bytes 1572868
  0.7 2.0 %copy-start.2 = (bf16[128,2048]{1,0:T(8,128)(2,1)S(1)}, bf16[128,2048]{1,0:T(8,128)(2,1)}, u32[]{:S(2)}) copy-start(bf16[128,2048]{1,0:T(8,128)(2,1)} %values_ref.7) | copy-start | bytes 1572868
  0.7 2.0 %copy-start.3 = (bf16[128,2048]{1,0:T(8,128)(2,1)S(1)}, bf16[128,2048]{1,0:T(8,128)(2,1)}, u32[]{:S(2)}) copy-start(bf16[128,2048]{1,0:T(8,128)(2,1)} %cotangent_ref.1) | copy-start | bytes 1572868
  2.0 12.7 %copy-start.4 = (bf16[16,384]{1,0:T(8,128)(2,1)S(1)}, bf16[16,384]{1,0:T(8,128)(2,1)}, u32[]{:S(2)}) copy-start(bf16[16,384]{1,0:T(8,128)(2,1)} %taps_ref.1) | copy-start | bytes 36868
  2.0 15.0 %collective-permute-start = (bf16[128,1024]{1,0:T(8,128)(2,1)S(1)}, bf16[128,1024]{1,0:T(8,128)(2,1)S(1)}, u32[]{:S(2)}, u32[]{:S(2)}) collective-permute-start(bf16[128,1024]{1,0:T(8,128)(2,1)S(1)} %diagonal.1.sent_ref), channel_id=1, source_target_pairs={{4,8},{8,4},{12,16},{16,12},{20,24},{24,20},{5,9},{9,5},{13,17},{1... | collective-permute-start | bytes 786440 | tf_op jit(solution)/shard_map/ppermute | solution.py:35
  3.0 18.4 %collective-permute-start.1 = (bf16[128,2048]{1,0:T(8,128)(2,1)S(1)}, bf16[128,2048]{1,0:T(8,128)(2,1)S(1)}, u32[]{:S(2)}, u32[]{:S(2)}) collective-permute-start(bf16[128,2048]{1,0:T(8,128)(2,1)S(1)} %get-tuple-element.25.across_ref), channel_id=1, source_target_pairs={{0,8},{8,16},{12,4},{16,24},{20,12},{28,20},{1,9},{9,17},{13,5},{1... | collective-permute-start | bytes 1572872 | tf_op jit(solution)/shard_map/ppermute | solution.py:35
  10.6 15.0 %collective-permute-start.2 = (bf16[128,2048]{1,0:T(8,128)(2,1)S(1)}, bf16[128,2048]{1,0:T(8,128)(2,1)S(1)}, u32[]{:S(2)}, u32[]{:S(2)}) collective-permute-start(bf16[128,2048]{1,0:T(8,128)(2,1)S(1)} %get-tuple-element.24.near_ref), channel_id=1, source_target_pairs={{4,12},{8,0},{12,20},{16,8},{20,28},{24,16},{5,13},{9,1},{13,21},{... | collective-permute-start | bytes 1572872 | tf_op jit(solution)/shard_map/ppermute | solution.py:35
  11.9 14.2 %collective-permute-start.4 = (bf16[128,2048]{1,0:T(8,128)(2,1)S(1)}, bf16[128,2048]{1,0:T(8,128)(2,1)S(1)}, u32[]{:S(2)}, u32[]{:S(2)}) collective-permute-start(bf16[128,2048]{1,0:T(8,128)(2,1)S(1)} %get-tuple-element.25.across_ref), channel_id=1, source_target_pairs={{0,4},{4,0},{8,12},{12,8},{16,20},{20,16},{24,28},{28,24},{1,5},{5... | collective-permute-start | bytes 1572872 | tf_op jit(solution)/shard_map/ppermute | solution.py:35
  22.2 4.6 %collective-permute-start.5 = (f32[16,384]{1,0:T(8,128)S(1)}, f32[16,384]{1,0:T(8,128)S(1)}, u32[]{:S(2)}, u32[]{:S(2)}) collective-permute-start(f32[16,384]{1,0:T(8,128)S(1)} %two.1.sum_ref), channel_id=1, source_target_pairs={{0,4},{4,0},{8,12},{12,8},{16,20},{20,16},{24,28},{28,24},{1,5},{5... | collective-permute-start | bytes 73736 | tf_op jit(solution)/shard_map/ppermute | solution.py:35
  25.6 6.7 %collective-permute-start.3 = (bf16[128,1024]{1,0:T(8,128)(2,1)S(1)}, bf16[128,1024]{1,0:T(8,128)(2,1)S(1)}, u32[]{:S(2)}, u32[]{:S(2)}) collective-permute-start(bf16[128,1024]{1,0:T(8,128)(2,1)S(1)} %forward.1), channel_id=1, source_target_pairs={{0,4},{4,0},{8,12},{12,8},{16,20},{20,16},{24,28},{28,24},{1,5},{5... | collective-permute-start | bytes 786440 | tf_op jit(solution)/shard_map/ppermute | solution.py:35
  26.9 6.8 %collective-permute-start.6 = (f32[16,384]{1,0:T(8,128)S(1)}, f32[16,384]{1,0:T(8,128)S(1)}, u32[]{:S(2)}, u32[]{:S(2)}) collective-permute-start(f32[16,384]{1,0:T(8,128)S(1)} %pair.1.refs_0_), channel_id=1, source_target_pairs={{0,16},{4,20},{8,24},{12,28},{16,8},{20,12},{24,0},{28,4},{1,17},{... | collective-permute-start | bytes 73736 | tf_op jit(solution)/shard_map/ppermute | solution.py:53
  29.9 4.7 %collective-permute-start.7 = (f32[16,384]{1,0:T(8,128)S(1)}, f32[16,384]{1,0:T(8,128)S(1)}, u32[]{:S(2)}, u32[]{:S(2)}) collective-permute-start(f32[16,384]{1,0:T(8,128)S(1)} %pair.1.refs_0_), channel_id=1, source_target_pairs={{0,24},{4,28},{8,16},{12,20},{16,0},{20,4},{24,8},{28,12},{1,25},{... | collective-permute-start | bytes 73736 | tf_op jit(solution)/shard_map/ppermute | solution.py:53
  31.2 3.8 %collective-permute-start.8 = (f32[16,384]{1,0:T(8,128)S(1)}, f32[16,384]{1,0:T(8,128)S(1)}, u32[]{:S(2)}, u32[]{:S(2)}) collective-permute-start(f32[16,384]{1,0:T(8,128)S(1)} %pair.1.refs_0_), channel_id=1, source_target_pairs={{0,8},{4,12},{8,0},{12,4},{16,24},{20,28},{24,16},{28,20},{1,9},{5... | collective-permute-start | bytes 73736 | tf_op jit(solution)/shard_map/ppermute | solution.py:53

commit v22 on v21

--- a/solution.py
+++ b/solution.py
@@ -45,7 +45,7 @@
     while stride < size:
         own = terms[0] if len(terms) == 1 else add(*terms)
         members = 4 if 4 * stride <= size else 2
-        rounds = ((2, 3, 1, 0), (3, 2, 0, 1), (1, 0, 3, 2)) if members == 4 else ((1, 0),)
+        rounds = ((1, 3, 0, 2), (3, 2, 1, 0), (2, 0, 3, 1)) if members == 4 else ((1, 0),)
         terms = [own]
         for targets in rounds:
             places = [(i, i // stride % members) for i in range(size)]

time: 35.9 us -> 36 us (level)
  starting transfers between devices: 19.8 us -> 21.3 us
  waiting for transfers between devices: 4.73 us -> 3.37 us
    ppermute x3, starting transfers between devices: 4.87 us -> 6.33 us  [sum_terms(): terms.append(lax.ppermute(own, axis, route))]
    ppermute x3, waiting for transfers between devices: 1.39 us -> 0.04 us  [sum_terms(): terms.append(lax.ppermute(own, axis, route))]
  transfers between devices with their start and end apart: 9 -> 9, of which waited for: 5 -> 3; matrix products, arithmetic and copies ran while one was open for 0% -> 0% of each run, Pallas kernels for 23% -> 23%
where the time goes in v22:
time: 36 us; the launch traced here: 35.8 us
  starting transfers between devices  21.3 us (59%)
  Pallas kernels  10.3 us (29%)
  waiting for transfers between devices  3.37 us (9%)
  between operations  0.84 us (2%)
    ppermute x6, starting transfers between devices, moved(): lax.ppermute(block, axis, [pair for pair in route if 0 <= pair[1] < size])  15 us
    ppermute x3, starting transfers between devices, sum_terms(): terms.append(lax.ppermute(own, axis, route))  6.33 us
    ppermute x6, waiting for transfers between devices, moved(): lax.ppermute(block, axis, [pair for pair in route if 0 <= pair[1] < size])  3.34 us
    pallas_call x1, Pallas kernels, shards(): call(functools.partial(tiles_kernel, rows), 'tiles', in_specs=[WHOLE], ou...  2.22 us
    pallas_call x1, Pallas kernels, shards(): call(functools.partial(own_kernel, rows), 'own', flops=4 * 10 ** 9, in_sp...  1.96 us
    pallas_call x1, Pallas kernels, shards(): call(last_kernel, 'last', in_specs=[WHOLE] * 10, out_specs=[ANYWHERE] * 3...  1.35 us
    pallas_call x1, Pallas kernels, shards(): call(diagonal_kernel, 'diagonal', in_specs=[ANYWHERE] * 4, out_specs=WHOL...  1.28 us
    pallas_call x1, Pallas kernels, shards(): call(functools.partial(two_kernel, rows), 'two', in_specs=[WHOLE] * 3, ou...  0.78 us
  transfers between devices with their start and end apart: 9, of which 3 were waited for; matrix products, arithmetic and copies ran while one was open for 0% of the time, Pallas kernels for 23%

profile of v22, /device:TPU:0, one launch (start us, length us, event | category | flops | bytes accessed | tf_op | source)
XLA Modules:
  0.0 35.8 jit_solution(9228179047768078050)
XLA Ops:
  0.7 1.3 %diagonal.1.sent_ref = bf16[128,1024]{1,0:T(8,128)(2,1)S(1)} custom-call(bf16[128,2048]{1,0:T(8,128)(2,1)} %query_ref.7, bf16[128,2048]{1,0:T(8,128)(2,1)} %keys_ref.7, bf16[128,2048]{1,0:T(8,128)(2,1)} %values_ref.7, bf16[128,2048]{1,0:T(8,128)(2,1)} %cotangent_ref.1), custom_call_target="tpu_custom_call" | custom-call | flops 1000000 | bytes 100000 | tf_op jit(solution)/shard_map/diagonal/pallas_call | solution.py:371
  2.0 0.0 copy-start.4
  2.0 0.7 %collective-permute-start = (bf16[128,1024]{1,0:T(8,128)(2,1)S(1)}, bf16[128,1024]{1,0:T(8,128)(2,1)S(1)}, u32[]{:S(2)}, u32[]{:S(2)}) collective-permute-start(bf16[128,1024]{1,0:T(8,128)(2,1)S(1)} %diagonal.1.sent_ref), channel_id=1, source_target_pairs={{4,8},{8,4},{12,16},{16,12},{20,24},{24,20},{5,9},{9,5},{13,17},{1... | collective-permute-start | bytes 786440 | tf_op jit(solution)/shard_map/ppermute | solution.py:35
  2.7 0.3 products.1
  3.0 7.6 %collective-permute-start.1 = (bf16[128,2048]{1,0:T(8,128)(2,1)S(1)}, bf16[128,2048]{1,0:T(8,128)(2,1)S(1)}, u32[]{:S(2)}, u32[]{:S(2)}) collective-permute-start(bf16[128,2048]{1,0:T(8,128)(2,1)S(1)} %get-tuple-element.25.across_ref), channel_id=1, source_target_pairs={{0,8},{8,16},{12,4},{16,24},{20,12},{28,20},{1,9},{9,17},{13,5},{1... | collective-permute-start | bytes 1572872 | tf_op jit(solution)/shard_map/ppermute | solution.py:35
  10.6 1.3 %collective-permute-start.2 = (bf16[128,2048]{1,0:T(8,128)(2,1)S(1)}, bf16[128,2048]{1,0:T(8,128)(2,1)S(1)}, u32[]{:S(2)}, u32[]{:S(2)}) collective-permute-start(bf16[128,2048]{1,0:T(8,128)(2,1)S(1)} %get-tuple-element.24.near_ref), channel_id=1, source_target_pairs={{4,12},{8,0},{12,20},{16,8},{20,28},{24,16},{5,13},{9,1},{13,21},{... | collective-permute-start | bytes 1572872 | tf_op jit(solution)/shard_map/ppermute | solution.py:35
  11.9 2.8 %collective-permute-start.4 = (bf16[128,2048]{1,0:T(8,128)(2,1)S(1)}, bf16[128,2048]{1,0:T(8,128)(2,1)S(1)}, u32[]{:S(2)}, u32[]{:S(2)}) collective-permute-start(bf16[128,2048]{1,0:T(8,128)(2,1)S(1)} %get-tuple-element.25.across_ref), channel_id=1, source_target_pairs={{0,4},{4,0},{8,12},{12,8},{16,20},{20,16},{24,28},{28,24},{1,5},{5... | collective-permute-start | bytes 1572872 | tf_op jit(solution)/shard_map/ppermute | solution.py:35
  14.7 2.2 %tiles.1 = (bf16[16,128,384]{2,1,0:T(8,128)(2,1)S(1)}, bf16[16,128,384]{2,1,0:T(8,128)(2,1)S(1)}) custom-call(bf16[16,384]{1,0:T(8,128)(2,1)S(1)} %copy-done.4), custom_call_target="tpu_custom_call" | custom-call | flops 1000000 | bytes 100000 | tf_op jit(solution)/shard_map/tiles/pallas_call | solution.py:391
  16.9 2.0 %own.1 = (f32[16,384]{1,0:T(8,128)S(1)}, f32[128,2048]{1,0:T(8,128)S(1)}, f32[128,2048]{1,0:T(8,128)S(1)}, bf16[128,2048]{1,0:T(8,128)(2,1)S(1)}, bf16[128,2048]{1,0:T(8,128)(2,1)S(1)}) custom-call(bf16[16,128,384]{2,1,0:T(8,128)(2,1)S(1)} %get-tuple-element.22.ready_tiles.tiles_ref, bf16[16,128,384]{2,1,0:T(8,128)(2,1)S(1)} %get-tuple-element.23.late_tiles.tiles_ref, ...), custom_call_target="tpu_custom_call" | custom-call | flops 4000000000 | bytes 100000 | tf_op jit(solution)/shard_map/own/pallas_call | solution.py:398
  18.9 2.5 %collective-permute-done.1.two_ref = bf16[128,2048]{1,0:T(8,128)(2,1)S(1)} collective-permute-done((bf16[128,2048]{1,0:T(8,128)(2,1)S(1)}, bf16[128,2048]{1,0:T(8,128)(2,1)S(1)}, u32[]{:S(2)}, u32[]{:S(2)}) %collective-permute-start.1) | collective-permute-done | bytes 524320 | tf_op jit(solution)/shard_map/ppermute | solution.py:35
  21.5 0.8 %two.1.sum_ref = f32[16,384]{1,0:T(8,128)S(1)} custom-call(f32[16,384]{1,0:T(8,128)S(1)} %get-tuple-element.27.sum_ref, bf16[128,2048]{1,0:T(8,128)(2,1)S(1)} %get-tuple-element.28.turned_ref, bf16[128,2048]{1,0:T(8,128)(2,1)S(1)} %collective-permute-done.1.two_ref), custom_call_target="tpu_custom_call" | custom-call | flops 1000000 | bytes 100000 | tf_op jit(solution)/shard_map/two/pallas_call | solution.py:407
  22.2 2.6 %collective-permute-start.5 = (f32[16,384]{1,0:T(8,128)S(1)}, f32[16,384]{1,0:T(8,128)S(1)}, u32[]{:S(2)}, u32[]{:S(2)}) collective-permute-start(f32[16,384]{1,0:T(8,128)S(1)} %two.1.sum_ref), channel_id=1, source_target_pairs={{0,4},{4,0},{8,12},{12,8},{16,20},{20,16},{24,28},{28,24},{1,5},{5... | collective-permute-start | bytes 73736 | tf_op jit(solution)/shard_map/ppermute | solution.py:35
  24.8 0.4 %ready.1 = (f32[128,1024]{1,0:T(8,128)S(1)}, bf16[128,1024]{1,0:T(8,128)(2,1)S(1)}, bf16[128,1024]{1,0:T(8,128)(2,1)S(1)}) custom-call(bf16[16,128,384]{2,1,0:T(8,128)(2,1)S(1)} %get-tuple-element.22.ready_tiles.tiles_ref, f32[128,2048]{1,0:T(8,128)S(1)} %get-tuple-element.26.ready_ref, bf16[128,2048]{1,0:T(8,128)(2,1)S(1)} %collective-permute-done.1.two_ref, ...), custom_call_target="tpu_custom_call" | custom-call | flops 1000000 | bytes 100000 | tf_op jit(solution)/shard_map/ready/pallas_call | solution.py:417
  25.2 0.4 %collective-permute-done.2.far_ref = bf16[128,2048]{1,0:T(8,128)(2,1)S(1)} collective-permute-done((bf16[128,2048]{1,0:T(8,128)(2,1)S(1)}, bf16[128,2048]{1,0:T(8,128)(2,1)S(1)}, u32[]{:S(2)}, u32[]{:S(2)}) %collective-permute-start.2) | collective-permute-done | bytes 524320 | tf_op jit(solution)/shard_map/ppermute | solution.py:35
  25.6 0.1 collective-permute-start.3
  25.7 0.4 %collective-permute-done.4.swap_ref = bf16[128,2048]{1,0:T(8,128)(2,1)S(1)} collective-permute-done((bf16[128,2048]{1,0:T(8,128)(2,1)S(1)}, bf16[128,2048]{1,0:T(8,128)(2,1)S(1)}, u32[]{:S(2)}, u32[]{:S(2)}) %collective-permute-start.4) | collective-permute-done | bytes 524320 | tf_op jit(solution)/shard_map/ppermute | solution.py:35
  26.1 0.8 %cross.1.cross_ref = f32[16,384]{1,0:T(8,128)S(1)} custom-call(bf16[128,2048]{1,0:T(8,128)(2,1)S(1)} %get-tuple-element.38.turned_ref, bf16[128,2048]{1,0:T(8,128)(2,1)S(1)} %collective-permute-done.4.swap_ref), custom_call_target="tpu_custom_call" | custom-call | flops 1000000 | bytes 100000 | tf_op jit(solution)/shard_map/cross/pallas_call | solution.py:434
  26.9 2.0 %collective-permute-start.6 = (f32[16,384]{1,0:T(8,128)S(1)}, f32[16,384]{1,0:T(8,128)S(1)}, u32[]{:S(2)}, u32[]{:S(2)}) collective-permute-start(f32[16,384]{1,0:T(8,128)S(1)} %pair.1.refs_0_), channel_id=1, source_target_pairs={{0,8},{4,12},{8,24},{12,28},{16,0},{20,4},{24,16},{28,20},{1,9},{5... | collective-permute-start | bytes 73736 | tf_op jit(solution)/shard_map/ppermute | solution.py:53
  28.9 2.5 %collective-permute-start.7 = (f32[16,384]{1,0:T(8,128)S(1)}, f32[16,384]{1,0:T(8,128)S(1)}, u32[]{:S(2)}, u32[]{:S(2)}) collective-permute-start(f32[16,384]{1,0:T(8,128)S(1)} %pair.1.refs_0_), channel_id=1, source_target_pairs={{0,24},{4,28},{8,16},{12,20},{16,8},{20,12},{24,0},{28,4},{1,25},{... | collective-permute-start | bytes 73736 | tf_op jit(solution)/shard_map/ppermute | solution.py:53
  31.4 1.9 %collective-permute-start.8 = (f32[16,384]{1,0:T(8,128)S(1)}, f32[16,384]{1,0:T(8,128)S(1)}, u32[]{:S(2)}, u32[]{:S(2)}) collective-permute-start(f32[16,384]{1,0:T(8,128)S(1)} %pair.1.refs_0_), channel_id=1, source_target_pairs={{0,16},{4,20},{8,0},{12,4},{16,24},{20,28},{24,8},{28,12},{1,17},{... | collective-permute-start | bytes 73736 | tf_op jit(solution)/shard_map/ppermute | solution.py:53
  33.2 0.5 %known.1 = (bf16[128,2048]{1,0:T(8,128)(2,1)S(1)}, bf16[128,2048]{1,0:T(8,128)(2,1)S(1)}) custom-call(bf16[16,128,384]{2,1,0:T(8,128)(2,1)S(1)} %get-tuple-element.23.late_tiles.tiles_ref, f32[128,2048]{1,0:T(8,128)S(1)} %get-tuple-element.32.late_ref, bf16[128,2048]{1,0:T(8,128)(2,1)S(1)} %collective-permute-done.4.swap_ref, ...), custom_call_target="tpu_custom_call" | custom-call | flops 4000000000 | bytes 100000 | tf_op jit(solution)/shard_map/known/pallas_call | solution.py:450
  33.8 1.3 %last.1 = (bf16[128,2048]{1,0:T(8,128)(2,1)}, bf16[128,2048]{1,0:T(8,128)(2,1)}, bf16[128,2048]{1,0:T(8,128)(2,1)}, f32[8,128]{1,0:T(8,128)S(1)}) custom-call(bf16[16,128,384]{2,1,0:T(8,128)(2,1)S(1)} %get-tuple-element.22.ready_tiles.tiles_ref, f32[128,1024]{1,0:T(8,128)S(1)} %get-tuple-element.29.rest_ref, ...), custom_call_target="tpu_custom_call" | custom-call | flops 1000000 | bytes 100000 | tf_op jit(solution)/shard_map/last/pallas_call | solution.py:469
  35.1 0.0 collective-permute-done.8.refs_3_
  35.2 0.6 %add.1 = f32[16,384]{1,0:T(8,128)} custom-call(f32[16,384]{1,0:T(8,128)S(1)} %pair.1.refs_0_, f32[16,384]{1,0:T(8,128)S(1)} %collective-permute-done.6.refs_1_, f32[16,384]{1,0:T(8,128)S(1)} %collective-permute-done.7.refs_2_, f32[16,384]{1,0:T(8,128)S(1)} %collective-permute-done.8.refs_3_, f32[8,128]{1,0:T(8,128)S(1)} %get-tuple-element.39.refs_4_), custom_call_target="tpu_custom_call" | custom-call | flops 1000000 | bytes 100000 | tf_op jit(solution)/shard_map/add/pallas_call | solution.py:460
  (16 shorter events, 0.1 us)
Async XLA Ops:
  0.6 2.0 %copy-start = (bf16[128,2048]{1,0:T(8,128)(2,1)S(1)}, bf16[128,2048]{1,0:T(8,128)(2,1)}, u32[]{:S(2)}) copy-start(bf16[128,2048]{1,0:T(8,128)(2,1)} %query_ref.7) | copy-start | bytes 1572868
  0.6 2.0 %copy-start.1 = (bf16[128,2048]{1,0:T(8,128)(2,1)S(1)}, bf16[128,2048]{1,0:T(8,128)(2,1)}, u32[]{:S(2)}) copy-start(bf16[128,2048]{1,0:T(8,128)(2,1)} %keys_ref.7) | copy-start | bytes 1572868
  0.7 2.0 %copy-start.2 = (bf16[128,2048]{1,0:T(8,128)(2,1)S(1)}, bf16[128,2048]{1,0:T(8,128)(2,1)}, u32[]{:S(2)}) copy-start(bf16[128,2048]{1,0:T(8,128)(2,1)} %values_ref.7) | copy-start | bytes 1572868
  0.7 2.0 %copy-start.3 = (bf16[128,2048]{1,0:T(8,128)(2,1)S(1)}, bf16[128,2048]{1,0:T(8,128)(2,1)}, u32[]{:S(2)}) copy-start(bf16[128,2048]{1,0:T(8,128)(2,1)} %cotangent_ref.1) | copy-start | bytes 1572868
  2.0 12.7 %copy-start.4 = (bf16[16,384]{1,0:T(8,128)(2,1)S(1)}, bf16[16,384]{1,0:T(8,128)(2,1)}, u32[]{:S(2)}) copy-start(bf16[16,384]{1,0:T(8,128)(2,1)} %taps_ref.1) | copy-start | bytes 36868
  2.0 15.0 %collective-permute-start = (bf16[128,1024]{1,0:T(8,128)(2,1)S(1)}, bf16[128,1024]{1,0:T(8,128)(2,1)S(1)}, u32[]{:S(2)}, u32[]{:S(2)}) collective-permute-start(bf16[128,1024]{1,0:T(8,128)(2,1)S(1)} %diagonal.1.sent_ref), channel_id=1, source_target_pairs={{4,8},{8,4},{12,16},{16,12},{20,24},{24,20},{5,9},{9,5},{13,17},{1... | collective-permute-start | bytes 786440 | tf_op jit(solution)/shard_map/ppermute | solution.py:35
  3.0 18.4 %collective-permute-start.1 = (bf16[128,2048]{1,0:T(8,128)(2,1)S(1)}, bf16[128,2048]{1,0:T(8,128)(2,1)S(1)}, u32[]{:S(2)}, u32[]{:S(2)}) collective-permute-start(bf16[128,2048]{1,0:T(8,128)(2,1)S(1)} %get-tuple-element.25.across_ref), channel_id=1, source_target_pairs={{0,8},{8,16},{12,4},{16,24},{20,12},{28,20},{1,9},{9,17},{13,5},{1... | collective-permute-start | bytes 1572872 | tf_op jit(solution)/shard_map/ppermute | solution.py:35
  10.6 15.0 %collective-permute-start.2 = (bf16[128,2048]{1,0:T(8,128)(2,1)S(1)}, bf16[128,2048]{1,0:T(8,128)(2,1)S(1)}, u32[]{:S(2)}, u32[]{:S(2)}) collective-permute-start(bf16[128,2048]{1,0:T(8,128)(2,1)S(1)} %get-tuple-element.24.near_ref), channel_id=1, source_target_pairs={{4,12},{8,0},{12,20},{16,8},{20,28},{24,16},{5,13},{9,1},{13,21},{... | collective-permute-start | bytes 1572872 | tf_op jit(solution)/shard_map/ppermute | solution.py:35
  11.9 14.2 %collective-permute-start.4 = (bf16[128,2048]{1,0:T(8,128)(2,1)S(1)}, bf16[128,2048]{1,0:T(8,128)(2,1)S(1)}, u32[]{:S(2)}, u32[]{:S(2)}) collective-permute-start(bf16[128,2048]{1,0:T(8,128)(2,1)S(1)} %get-tuple-element.25.across_ref), channel_id=1, source_target_pairs={{0,4},{4,0},{8,12},{12,8},{16,20},{20,16},{24,28},{28,24},{1,5},{5... | collective-permute-start | bytes 1572872 | tf_op jit(solution)/shard_map/ppermute | solution.py:35
  22.2 4.6 %collective-permute-start.5 = (f32[16,384]{1,0:T(8,128)S(1)}, f32[16,384]{1,0:T(8,128)S(1)}, u32[]{:S(2)}, u32[]{:S(2)}) collective-permute-start(f32[16,384]{1,0:T(8,128)S(1)} %two.1.sum_ref), channel_id=1, source_target_pairs={{0,4},{4,0},{8,12},{12,8},{16,20},{20,16},{24,28},{28,24},{1,5},{5... | collective-permute-start | bytes 73736 | tf_op jit(solution)/shard_map/ppermute | solution.py:35
  25.6 8.1 %collective-permute-start.3 = (bf16[128,1024]{1,0:T(8,128)(2,1)S(1)}, bf16[128,1024]{1,0:T(8,128)(2,1)S(1)}, u32[]{:S(2)}, u32[]{:S(2)}) collective-permute-start(bf16[128,1024]{1,0:T(8,128)(2,1)S(1)} %forward.1), channel_id=1, source_target_pairs={{0,4},{4,0},{8,12},{12,8},{16,20},{20,16},{24,28},{28,24},{1,5},{5... | collective-permute-start | bytes 786440 | tf_op jit(solution)/shard_map/ppermute | solution.py:35
  26.9 8.3 %collective-permute-start.6 = (f32[16,384]{1,0:T(8,128)S(1)}, f32[16,384]{1,0:T(8,128)S(1)}, u32[]{:S(2)}, u32[]{:S(2)}) collective-permute-start(f32[16,384]{1,0:T(8,128)S(1)} %pair.1.refs_0_), channel_id=1, source_target_pairs={{0,8},{4,12},{8,24},{12,28},{16,0},{20,4},{24,16},{28,20},{1,9},{5... | collective-permute-start | bytes 73736 | tf_op jit(solution)/shard_map/ppermute | solution.py:53
  28.9 6.3 %collective-permute-start.7 = (f32[16,384]{1,0:T(8,128)S(1)}, f32[16,384]{1,0:T(8,128)S(1)}, u32[]{:S(2)}, u32[]{:S(2)}) collective-permute-start(f32[16,384]{1,0:T(8,128)S(1)} %pair.1.refs_0_), channel_id=1, source_target_pairs={{0,24},{4,28},{8,16},{12,20},{16,8},{20,12},{24,0},{28,4},{1,25},{... | collective-permute-start | bytes 73736 | tf_op jit(solution)/shard_map/ppermute | solution.py:53
  31.4 3.8 %collective-permute-start.8 = (f32[16,384]{1,0:T(8,128)S(1)}, f32[16,384]{1,0:T(8,128)S(1)}, u32[]{:S(2)}, u32[]{:S(2)}) collective-permute-start(f32[16,384]{1,0:T(8,128)S(1)} %pair.1.refs_0_), channel_id=1, source_target_pairs={{0,16},{4,20},{8,0},{12,4},{16,24},{20,28},{24,8},{28,12},{1,17},{... | collective-permute-start | bytes 73736 | tf_op jit(solution)/shard_map/ppermute | solution.py:53

commit v23 on v22

--- a/solution.py
+++ b/solution.py
@@ -9,7 +9,7 @@
 from jax.sharding import PartitionSpec as P
 
 SUBLANES = 8
-PARTS = 2
+PARTS = 4
 VMEM_LIMIT = 16 * 1024 * 1024
 WHOLE = pl.BlockSpec(memory_space=pltpu.VMEM)
 ANYWHERE = pl.BlockSpec(memory_space=pl.ANY)

time: 36 us -> 36 us (level)
  no operation moved by 1% of the time
where the time goes in v23:
time: 36 us; the launch traced here: 35.8 us
  starting transfers between devices  21.3 us (59%)
  Pallas kernels  10.3 us (29%)
  waiting for transfers between devices  3.34 us (9%)
  between operations  0.85 us (2%)
    ppermute x6, starting transfers between devices, moved(): lax.ppermute(block, axis, [pair for pair in route if 0 <= pair[1] < size])  15 us
    ppermute x3, starting transfers between devices, sum_terms(): terms.append(lax.ppermute(own, axis, route))  6.33 us
    ppermute x6, waiting for transfers between devices, moved(): lax.ppermute(block, axis, [pair for pair in route if 0 <= pair[1] < size])  3.34 us
    pallas_call x1, Pallas kernels, shards(): call(functools.partial(tiles_kernel, rows), 'tiles', in_specs=[WHOLE], ou...  2.22 us
    pallas_call x1, Pallas kernels, shards(): call(functools.partial(own_kernel, rows), 'own', flops=4 * 10 ** 9, in_sp...  1.96 us
    pallas_call x1, Pallas kernels, shards(): call(last_kernel, 'last', in_specs=[WHOLE] * 10, out_specs=[ANYWHERE] * 3...  1.39 us
    pallas_call x1, Pallas kernels, shards(): call(diagonal_kernel, 'diagonal', in_specs=[ANYWHERE] * 4, out_specs=WHOL...  1.28 us
    pallas_call x1, Pallas kernels, shards(): call(functools.partial(two_kernel, rows), 'two', in_specs=[WHOLE] * 3, ou...  0.78 us
  transfers between devices with their start and end apart: 9, of which 3 were waited for; matrix products, arithmetic and copies ran while one was open for 0% of the time, Pallas kernels for 23%

profile of v23, /device:TPU:0, one launch (start us, length us, event | category | flops | bytes accessed | tf_op | source)
XLA Modules:
  0.0 35.8 jit_solution(12570927689943930329)
XLA Ops:
  0.7 1.3 %diagonal.1.sent_ref = bf16[128,1024]{1,0:T(8,128)(2,1)S(1)} custom-call(bf16[128,2048]{1,0:T(8,128)(2,1)} %query_ref.7, bf16[128,2048]{1,0:T(8,128)(2,1)} %keys_ref.7, bf16[128,2048]{1,0:T(8,128)(2,1)} %values_ref.7, bf16[128,2048]{1,0:T(8,128)(2,1)} %cotangent_ref.1), custom_call_target="tpu_custom_call" | custom-call | flops 1000000 | bytes 100000 | tf_op jit(solution)/shard_map/diagonal/pallas_call | solution.py:371
  2.0 0.0 copy-start.4
  2.0 0.7 %collective-permute-start = (bf16[128,1024]{1,0:T(8,128)(2,1)S(1)}, bf16[128,1024]{1,0:T(8,128)(2,1)S(1)}, u32[]{:S(2)}, u32[]{:S(2)}) collective-permute-start(bf16[128,1024]{1,0:T(8,128)(2,1)S(1)} %diagonal.1.sent_ref), channel_id=1, source_target_pairs={{4,8},{8,4},{12,16},{16,12},{20,24},{24,20},{5,9},{9,5},{13,17},{1... | collective-permute-start | bytes 786440 | tf_op jit(solution)/shard_map/ppermute | solution.py:35
  2.7 0.3 products.1
  3.0 7.6 %collective-permute-start.1 = (bf16[128,2048]{1,0:T(8,128)(2,1)S(1)}, bf16[128,2048]{1,0:T(8,128)(2,1)S(1)}, u32[]{:S(2)}, u32[]{:S(2)}) collective-permute-start(bf16[128,2048]{1,0:T(8,128)(2,1)S(1)} %get-tuple-element.25.across_ref), channel_id=1, source_target_pairs={{0,8},{8,16},{12,4},{16,24},{20,12},{28,20},{1,9},{9,17},{13,5},{1... | collective-permute-start | bytes 1572872 | tf_op jit(solution)/shard_map/ppermute | solution.py:35
  10.6 1.3 %collective-permute-start.2 = (bf16[128,2048]{1,0:T(8,128)(2,1)S(1)}, bf16[128,2048]{1,0:T(8,128)(2,1)S(1)}, u32[]{:S(2)}, u32[]{:S(2)}) collective-permute-start(bf16[128,2048]{1,0:T(8,128)(2,1)S(1)} %get-tuple-element.24.near_ref), channel_id=1, source_target_pairs={{4,12},{8,0},{12,20},{16,8},{20,28},{24,16},{5,13},{9,1},{13,21},{... | collective-permute-start | bytes 1572872 | tf_op jit(solution)/shard_map/ppermute | solution.py:35
  11.9 2.8 %collective-permute-start.4 = (bf16[128,2048]{1,0:T(8,128)(2,1)S(1)}, bf16[128,2048]{1,0:T(8,128)(2,1)S(1)}, u32[]{:S(2)}, u32[]{:S(2)}) collective-permute-start(bf16[128,2048]{1,0:T(8,128)(2,1)S(1)} %get-tuple-element.25.across_ref), channel_id=1, source_target_pairs={{0,4},{4,0},{8,12},{12,8},{16,20},{20,16},{24,28},{28,24},{1,5},{5... | collective-permute-start | bytes 1572872 | tf_op jit(solution)/shard_map/ppermute | solution.py:35
  14.7 2.2 %tiles.1 = (bf16[16,128,384]{2,1,0:T(8,128)(2,1)S(1)}, bf16[16,128,384]{2,1,0:T(8,128)(2,1)S(1)}) custom-call(bf16[16,384]{1,0:T(8,128)(2,1)S(1)} %copy-done.4), custom_call_target="tpu_custom_call" | custom-call | flops 1000000 | bytes 100000 | tf_op jit(solution)/shard_map/tiles/pallas_call | solution.py:391
  16.9 0.0 collective-permute-done.diagonal_ref
  16.9 2.0 %own.1 = (f32[16,384]{1,0:T(8,128)S(1)}, f32[128,2048]{1,0:T(8,128)S(1)}, f32[128,2048]{1,0:T(8,128)S(1)}, bf16[128,2048]{1,0:T(8,128)(2,1)S(1)}, bf16[128,2048]{1,0:T(8,128)(2,1)S(1)}) custom-call(bf16[16,128,384]{2,1,0:T(8,128)(2,1)S(1)} %get-tuple-element.22.ready_tiles.tiles_ref, bf16[16,128,384]{2,1,0:T(8,128)(2,1)S(1)} %get-tuple-element.23.late_tiles.tiles_ref, ...), custom_call_target="tpu_custom_call" | custom-call | flops 4000000000 | bytes 100000 | tf_op jit(solution)/shard_map/own/pallas_call | solution.py:398
  18.9 2.5 %collective-permute-done.1.two_ref = bf16[128,2048]{1,0:T(8,128)(2,1)S(1)} collective-permute-done((bf16[128,2048]{1,0:T(8,128)(2,1)S(1)}, bf16[128,2048]{1,0:T(8,128)(2,1)S(1)}, u32[]{:S(2)}, u32[]{:S(2)}) %collective-permute-start.1) | collective-permute-done | bytes 524320 | tf_op jit(solution)/shard_map/ppermute | solution.py:35
  21.5 0.8 %two.1.sum_ref = f32[16,384]{1,0:T(8,128)S(1)} custom-call(f32[16,384]{1,0:T(8,128)S(1)} %get-tuple-element.27.sum_ref, bf16[128,2048]{1,0:T(8,128)(2,1)S(1)} %get-tuple-element.28.turned_ref, bf16[128,2048]{1,0:T(8,128)(2,1)S(1)} %collective-permute-done.1.two_ref), custom_call_target="tpu_custom_call" | custom-call | flops 1000000 | bytes 100000 | tf_op jit(solution)/shard_map/two/pallas_call | solution.py:407
  22.2 2.6 %collective-permute-start.5 = (f32[16,384]{1,0:T(8,128)S(1)}, f32[16,384]{1,0:T(8,128)S(1)}, u32[]{:S(2)}, u32[]{:S(2)}) collective-permute-start(f32[16,384]{1,0:T(8,128)S(1)} %two.1.sum_ref), channel_id=1, source_target_pairs={{0,4},{4,0},{8,12},{12,8},{16,20},{20,16},{24,28},{28,24},{1,5},{5... | collective-permute-start | bytes 73736 | tf_op jit(solution)/shard_map/ppermute | solution.py:35
  24.8 0.4 %ready.1 = (f32[128,1024]{1,0:T(8,128)S(1)}, bf16[128,1024]{1,0:T(8,128)(2,1)S(1)}, bf16[128,1024]{1,0:T(8,128)(2,1)S(1)}) custom-call(bf16[16,128,384]{2,1,0:T(8,128)(2,1)S(1)} %get-tuple-element.22.ready_tiles.tiles_ref, f32[128,2048]{1,0:T(8,128)S(1)} %get-tuple-element.26.ready_ref, bf16[128,2048]{1,0:T(8,128)(2,1)S(1)} %collective-permute-done.1.two_ref, ...), custom_call_target="tpu_custom_call" | custom-call | flops 1000000 | bytes 100000 | tf_op jit(solution)/shard_map/ready/pallas_call | solution.py:417
  25.2 0.4 %collective-permute-done.2.far_ref = bf16[128,2048]{1,0:T(8,128)(2,1)S(1)} collective-permute-done((bf16[128,2048]{1,0:T(8,128)(2,1)S(1)}, bf16[128,2048]{1,0:T(8,128)(2,1)S(1)}, u32[]{:S(2)}, u32[]{:S(2)}) %collective-permute-start.2) | collective-permute-done | bytes 524320 | tf_op jit(solution)/shard_map/ppermute | solution.py:35
  25.6 0.1 collective-permute-start.3
  25.7 0.4 %collective-permute-done.4.swap_ref = bf16[128,2048]{1,0:T(8,128)(2,1)S(1)} collective-permute-done((bf16[128,2048]{1,0:T(8,128)(2,1)S(1)}, bf16[128,2048]{1,0:T(8,128)(2,1)S(1)}, u32[]{:S(2)}, u32[]{:S(2)}) %collective-permute-start.4) | collective-permute-done | bytes 524320 | tf_op jit(solution)/shard_map/ppermute | solution.py:35
  26.1 0.8 %cross.1.cross_ref = f32[16,384]{1,0:T(8,128)S(1)} custom-call(bf16[128,2048]{1,0:T(8,128)(2,1)S(1)} %get-tuple-element.38.turned_ref, bf16[128,2048]{1,0:T(8,128)(2,1)S(1)} %collective-permute-done.4.swap_ref), custom_call_target="tpu_custom_call" | custom-call | flops 1000000 | bytes 100000 | tf_op jit(solution)/shard_map/cross/pallas_call | solution.py:434
  26.9 2.0 %collective-permute-start.6 = (f32[16,384]{1,0:T(8,128)S(1)}, f32[16,384]{1,0:T(8,128)S(1)}, u32[]{:S(2)}, u32[]{:S(2)}) collective-permute-start(f32[16,384]{1,0:T(8,128)S(1)} %pair.1.refs_0_), channel_id=1, source_target_pairs={{0,8},{4,12},{8,24},{12,28},{16,0},{20,4},{24,16},{28,20},{1,9},{5... | collective-permute-start | bytes 73736 | tf_op jit(solution)/shard_map/ppermute | solution.py:53
  28.9 2.5 %collective-permute-start.7 = (f32[16,384]{1,0:T(8,128)S(1)}, f32[16,384]{1,0:T(8,128)S(1)}, u32[]{:S(2)}, u32[]{:S(2)}) collective-permute-start(f32[16,384]{1,0:T(8,128)S(1)} %pair.1.refs_0_), channel_id=1, source_target_pairs={{0,24},{4,28},{8,16},{12,20},{16,8},{20,12},{24,0},{28,4},{1,25},{... | collective-permute-start | bytes 73736 | tf_op jit(solution)/shard_map/ppermute | solution.py:53
  31.4 1.9 %collective-permute-start.8 = (f32[16,384]{1,0:T(8,128)S(1)}, f32[16,384]{1,0:T(8,128)S(1)}, u32[]{:S(2)}, u32[]{:S(2)}) collective-permute-start(f32[16,384]{1,0:T(8,128)S(1)} %pair.1.refs_0_), channel_id=1, source_target_pairs={{0,16},{4,20},{8,0},{12,4},{16,24},{20,28},{24,8},{28,12},{1,17},{... | collective-permute-start | bytes 73736 | tf_op jit(solution)/shard_map/ppermute | solution.py:53
  33.2 0.5 %known.1 = (bf16[128,2048]{1,0:T(8,128)(2,1)S(1)}, bf16[128,2048]{1,0:T(8,128)(2,1)S(1)}) custom-call(bf16[16,128,384]{2,1,0:T(8,128)(2,1)S(1)} %get-tuple-element.23.late_tiles.tiles_ref, f32[128,2048]{1,0:T(8,128)S(1)} %get-tuple-element.32.late_ref, bf16[128,2048]{1,0:T(8,128)(2,1)S(1)} %collective-permute-done.4.swap_ref, ...), custom_call_target="tpu_custom_call" | custom-call | flops 4000000000 | bytes 100000 | tf_op jit(solution)/shard_map/known/pallas_call | solution.py:450
  33.8 1.4 %last.1 = (bf16[128,2048]{1,0:T(8,128)(2,1)}, bf16[128,2048]{1,0:T(8,128)(2,1)}, bf16[128,2048]{1,0:T(8,128)(2,1)}, f32[8,128]{1,0:T(8,128)S(1)}) custom-call(bf16[16,128,384]{2,1,0:T(8,128)(2,1)S(1)} %get-tuple-element.22.ready_tiles.tiles_ref, f32[128,1024]{1,0:T(8,128)S(1)} %get-tuple-element.29.rest_ref, ...), custom_call_target="tpu_custom_call" | custom-call | flops 1000000 | bytes 100000 | tf_op jit(solution)/shard_map/last/pallas_call | solution.py:469
  35.2 0.6 %add.1 = f32[16,384]{1,0:T(8,128)} custom-call(f32[16,384]{1,0:T(8,128)S(1)} %pair.1.refs_0_, f32[16,384]{1,0:T(8,128)S(1)} %collective-permute-done.6.refs_1_, f32[16,384]{1,0:T(8,128)S(1)} %collective-permute-done.7.refs_2_, f32[16,384]{1,0:T(8,128)S(1)} %collective-permute-done.8.refs_3_, f32[8,128]{1,0:T(8,128)S(1)} %get-tuple-element.39.refs_4_), custom_call_target="tpu_custom_call" | custom-call | flops 1000000 | bytes 100000 | tf_op jit(solution)/shard_map/add/pallas_call | solution.py:460
  (16 shorter events, 0.1 us)
Async XLA Ops:
  0.6 2.0 %copy-start = (bf16[128,2048]{1,0:T(8,128)(2,1)S(1)}, bf16[128,2048]{1,0:T(8,128)(2,1)}, u32[]{:S(2)}) copy-start(bf16[128,2048]{1,0:T(8,128)(2,1)} %query_ref.7) | copy-start | bytes 1572868
  0.6 2.0 %copy-start.1 = (bf16[128,2048]{1,0:T(8,128)(2,1)S(1)}, bf16[128,2048]{1,0:T(8,128)(2,1)}, u32[]{:S(2)}) copy-start(bf16[128,2048]{1,0:T(8,128)(2,1)} %keys_ref.7) | copy-start | bytes 1572868
  0.7 2.0 %copy-start.2 = (bf16[128,2048]{1,0:T(8,128)(2,1)S(1)}, bf16[128,2048]{1,0:T(8,128)(2,1)}, u32[]{:S(2)}) copy-start(bf16[128,2048]{1,0:T(8,128)(2,1)} %values_ref.7) | copy-start | bytes 1572868
  0.7 2.0 %copy-start.3 = (bf16[128,2048]{1,0:T(8,128)(2,1)S(1)}, bf16[128,2048]{1,0:T(8,128)(2,1)}, u32[]{:S(2)}) copy-start(bf16[128,2048]{1,0:T(8,128)(2,1)} %cotangent_ref.1) | copy-start | bytes 1572868
  2.0 12.7 %copy-start.4 = (bf16[16,384]{1,0:T(8,128)(2,1)S(1)}, bf16[16,384]{1,0:T(8,128)(2,1)}, u32[]{:S(2)}) copy-start(bf16[16,384]{1,0:T(8,128)(2,1)} %taps_ref.1) | copy-start | bytes 36868
  2.0 15.0 %collective-permute-start = (bf16[128,1024]{1,0:T(8,128)(2,1)S(1)}, bf16[128,1024]{1,0:T(8,128)(2,1)S(1)}, u32[]{:S(2)}, u32[]{:S(2)}) collective-permute-start(bf16[128,1024]{1,0:T(8,128)(2,1)S(1)} %diagonal.1.sent_ref), channel_id=1, source_target_pairs={{4,8},{8,4},{12,16},{16,12},{20,24},{24,20},{5,9},{9,5},{13,17},{1... | collective-permute-start | bytes 786440 | tf_op jit(solution)/shard_map/ppermute | solution.py:35
  3.0 18.4 %collective-permute-start.1 = (bf16[128,2048]{1,0:T(8,128)(2,1)S(1)}, bf16[128,2048]{1,0:T(8,128)(2,1)S(1)}, u32[]{:S(2)}, u32[]{:S(2)}) collective-permute-start(bf16[128,2048]{1,0:T(8,128)(2,1)S(1)} %get-tuple-element.25.across_ref), channel_id=1, source_target_pairs={{0,8},{8,16},{12,4},{16,24},{20,12},{28,20},{1,9},{9,17},{13,5},{1... | collective-permute-start | bytes 1572872 | tf_op jit(solution)/shard_map/ppermute | solution.py:35
  10.6 15.0 %collective-permute-start.2 = (bf16[128,2048]{1,0:T(8,128)(2,1)S(1)}, bf16[128,2048]{1,0:T(8,128)(2,1)S(1)}, u32[]{:S(2)}, u32[]{:S(2)}) collective-permute-start(bf16[128,2048]{1,0:T(8,128)(2,1)S(1)} %get-tuple-element.24.near_ref), channel_id=1, source_target_pairs={{4,12},{8,0},{12,20},{16,8},{20,28},{24,16},{5,13},{9,1},{13,21},{... | collective-permute-start | bytes 1572872 | tf_op jit(solution)/shard_map/ppermute | solution.py:35
  11.9 14.2 %collective-permute-start.4 = (bf16[128,2048]{1,0:T(8,128)(2,1)S(1)}, bf16[128,2048]{1,0:T(8,128)(2,1)S(1)}, u32[]{:S(2)}, u32[]{:S(2)}) collective-permute-start(bf16[128,2048]{1,0:T(8,128)(2,1)S(1)} %get-tuple-element.25.across_ref), channel_id=1, source_target_pairs={{0,4},{4,0},{8,12},{12,8},{16,20},{20,16},{24,28},{28,24},{1,5},{5... | collective-permute-start | bytes 1572872 | tf_op jit(solution)/shard_map/ppermute | solution.py:35
  22.2 4.6 %collective-permute-start.5 = (f32[16,384]{1,0:T(8,128)S(1)}, f32[16,384]{1,0:T(8,128)S(1)}, u32[]{:S(2)}, u32[]{:S(2)}) collective-permute-start(f32[16,384]{1,0:T(8,128)S(1)} %two.1.sum_ref), channel_id=1, source_target_pairs={{0,4},{4,0},{8,12},{12,8},{16,20},{20,16},{24,28},{28,24},{1,5},{5... | collective-permute-start | bytes 73736 | tf_op jit(solution)/shard_map/ppermute | solution.py:35
  25.6 8.1 %collective-permute-start.3 = (bf16[128,1024]{1,0:T(8,128)(2,1)S(1)}, bf16[128,1024]{1,0:T(8,128)(2,1)S(1)}, u32[]{:S(2)}, u32[]{:S(2)}) collective-permute-start(bf16[128,1024]{1,0:T(8,128)(2,1)S(1)} %forward.1), channel_id=1, source_target_pairs={{0,4},{4,0},{8,12},{12,8},{16,20},{20,16},{24,28},{28,24},{1,5},{5... | collective-permute-start | bytes 786440 | tf_op jit(solution)/shard_map/ppermute | solution.py:35
  26.9 8.3 %collective-permute-start.6 = (f32[16,384]{1,0:T(8,128)S(1)}, f32[16,384]{1,0:T(8,128)S(1)}, u32[]{:S(2)}, u32[]{:S(2)}) collective-permute-start(f32[16,384]{1,0:T(8,128)S(1)} %pair.1.refs_0_), channel_id=1, source_target_pairs={{0,8},{4,12},{8,24},{12,28},{16,0},{20,4},{24,16},{28,20},{1,9},{5... | collective-permute-start | bytes 73736 | tf_op jit(solution)/shard_map/ppermute | solution.py:53
  28.9 6.3 %collective-permute-start.7 = (f32[16,384]{1,0:T(8,128)S(1)}, f32[16,384]{1,0:T(8,128)S(1)}, u32[]{:S(2)}, u32[]{:S(2)}) collective-permute-start(f32[16,384]{1,0:T(8,128)S(1)} %pair.1.refs_0_), channel_id=1, source_target_pairs={{0,24},{4,28},{8,16},{12,20},{16,8},{20,12},{24,0},{28,4},{1,25},{... | collective-permute-start | bytes 73736 | tf_op jit(solution)/shard_map/ppermute | solution.py:53
  31.4 3.8 %collective-permute-start.8 = (f32[16,384]{1,0:T(8,128)S(1)}, f32[16,384]{1,0:T(8,128)S(1)}, u32[]{:S(2)}, u32[]{:S(2)}) collective-permute-start(f32[16,384]{1,0:T(8,128)S(1)} %pair.1.refs_0_), channel_id=1, source_target_pairs={{0,16},{4,20},{8,0},{12,4},{16,24},{20,28},{24,8},{28,12},{1,17},{... | collective-permute-start | bytes 73736 | tf_op jit(solution)/shard_map/ppermute | solution.py:53
